TPU v7x, 512 devices: a whole 4x8x8 slice. The times are simulated.
512 devices in a mesh: gz: 8 (over z), xy: 64 (over y, x, core).
Axes of the slice: x: 4, y: 8, z: 8, core: 2. Of those that a mesh axis runs over, the one named last changes fastest.
Arguments:
- right_side: float32 [256, 512, 128], P('gz', 'xy'), may hold values from -12 to 12
- labels: int32 [256, 512, 128], P('gz', 'xy'), may hold values from 0 to 1, as said below
Outputs:
- pressure: float32 [256, 512, 128], P('gz', 'xy')
- remain: float32 [256, 512, 128], P('gz', 'xy')
Inputs may be any that keep to these rules, and one draw needn't show every extreme that they name: `labels`: 1 marks a gas cell inside a bubble, 0 a liquid cell.
All inputs are finite; a program needn't handle non-finite values.
Results may differ from a plain program's by a relative error of at most 0.0003.
Values sent between devices are 32-bit elements; how exact they have to be, the bound alone decides.
No kernel may reach another device: no remote copies, remote signals or barrier semaphores. Data moves between devices by JAX's collectives and lax.ppermute only.
A program may use at most 64 MiB of HBM per device.

v0:
```python
from functools import partial

import jax
import jax.numpy as jnp
from jax import lax
from jax.sharding import PartitionSpec as P

LEVELS = 3
SWEEPS = 2
COARSE_SWEEPS = 12


gas_density = 0.001


def padded(array, sides, width):
    for axis, dim in sides:
        devices, length = (lax.axis_size(axis), array.shape[dim])
        up = [(i, (i + 1) % devices) for i in range(devices - 1)]
        down = [(j, i) for i, j in up]
        last = lax.slice_in_dim(array, length - width, length, axis=dim)
        leading = lax.slice_in_dim(array, 0, width, axis=dim)
        before = lax.ppermute(last, axis, up)
        after = lax.ppermute(leading, axis, down)
        array = jnp.concatenate([before, array, after], axis=dim)
    return array


def density_of(labels):
    return jnp.where(labels == 1, gas_density, 1.0).astype(jnp.float32)


def coarsen(values):
    extent_z, extent_y, extent_x = values.shape
    blocks = values.reshape(extent_z // 2, 2, extent_y // 2, 2, extent_x // 2, 2)
    return jnp.mean(blocks, axis=(1, 3, 5))


def prolong(values):
    extent_z, extent_y, extent_x = values.shape
    spread = jnp.broadcast_to(
        values[:, None, :, None, :, None], (extent_z, 2, extent_y, 2, extent_x, 2)
    )
    return spread.reshape(2 * extent_z, 2 * extent_y, 2 * extent_x)


def coefficients(density, rimmed):
    lower_z = 2.0 / (density + rimmed[:-2, 1:-1, 1:-1])
    upper_z = 2.0 / (density + rimmed[2:, 1:-1, 1:-1])
    lower_y = 2.0 / (density + rimmed[1:-1, :-2, 1:-1])
    upper_y = 2.0 / (density + rimmed[1:-1, 2:, 1:-1])
    lower_x = 2.0 / (density + rimmed[1:-1, 1:-1, :-2])
    upper_x = 2.0 / (density + rimmed[1:-1, 1:-1, 2:])
    diagonal = lower_z + upper_z + lower_y + upper_y + lower_x + upper_x
    return ((lower_z, upper_z, lower_y, upper_y, lower_x, upper_x), diagonal)


def neighbours(faces, rimmed):
    lower_z, upper_z, lower_y, upper_y, lower_x, upper_x = faces
    return (
        lower_z * rimmed[:-2, 1:-1, 1:-1]
        + upper_z * rimmed[2:, 1:-1, 1:-1]
        + lower_y * rimmed[1:-1, :-2, 1:-1]
        + upper_y * rimmed[1:-1, 2:, 1:-1]
        + lower_x * rimmed[1:-1, 1:-1, :-2]
        + upper_x * rimmed[1:-1, 1:-1, 2:]
    )


def checker(shape):
    summed = (
        lax.broadcasted_iota(jnp.int32, shape, 0)
        + lax.broadcasted_iota(jnp.int32, shape, 1)
        + lax.broadcasted_iota(jnp.int32, shape, 2)
    )
    return summed % 2


def plain_rims(values):
    return jnp.pad(values, 1)


def with_rims(values):
    rimmed = padded(values, (("gz", 0), ("xy", 1)), 1)
    return jnp.pad(rimmed, ((0, 0), (0, 0), (1, 1)))


def smooth(pressure, source, faces, diagonal, factor, colours, rimmer):
    for colour in (0, 1):
        gathered = neighbours(faces, rimmer(pressure))
        updated = (factor * source + gathered) / diagonal
        pressure = jnp.where(colours == colour, updated, pressure)
    return pressure


def plain_sweep(pressure, source, faces, diagonal, factor, colours):
    return smooth(pressure, source, faces, diagonal, factor, colours, with_rims)


def residual_of(pressure, source, faces, diagonal, inverse, rimmer):
    return source - (diagonal * pressure - neighbours(faces, rimmer(pressure))) * inverse


def body(right_side, labels):
    densities = [density_of(labels)]
    for level_index in range(LEVELS):
        densities.append(coarsen(densities[-1]))
    saved = []
    source = right_side
    for level_index in range(LEVELS):
        density = densities[level_index]
        extent_z, extent_y, extent_x = density.shape
        colours = checker(density.shape)
        factor = 4.0**level_index
        rimmed = padded(density, (("gz", 0), ("xy", 1)), 1)
        rimmed = jnp.pad(rimmed, ((0, 0), (0, 0), (1, 1)))
        faces, diagonal = coefficients(density, rimmed)
        sweeper = partial(
            plain_sweep,
            source=source,
            faces=faces,
            diagonal=diagonal,
            factor=factor,
            colours=colours,
        )
        pressure = jnp.zeros_like(source)
        for repeat in range(SWEEPS):
            pressure = sweeper(pressure)
        saved.append((sweeper, pressure))
        leftover = residual_of(pressure, source, faces, diagonal, 1.0 / factor, with_rims)
        if level_index == 0:
            finest = (faces, diagonal)
        source = coarsen(leftover)
    coarse_density = densities[LEVELS]
    extent_z, extent_y, extent_x = source.shape
    part_density, part_source = (
        lax.all_gather(coarse_density, "xy", axis=1, tiled=True),
        lax.all_gather(source, "xy", axis=1, tiled=True),
    )
    whole_density, whole_source = (
        lax.all_gather(part_density, "gz", axis=0, tiled=True),
        lax.all_gather(part_source, "gz", axis=0, tiled=True),
    )
    faces, diagonal = coefficients(whole_density, jnp.pad(whole_density, 1))
    colours = checker(whole_density.shape)
    factor = 4.0**LEVELS

    def coarse_turn(counter, current):
        return smooth(current, whole_source, faces, diagonal, factor, colours, plain_rims)

    solved = lax.fori_loop(0, COARSE_SWEEPS, coarse_turn, jnp.zeros_like(whole_source))
    starts = (
        lax.axis_index("gz") * extent_z,
        lax.axis_index("xy") * extent_y,
        jnp.zeros((), jnp.int32),
    )
    pressure = lax.dynamic_slice(solved, starts, (extent_z, extent_y, extent_x))
    for level_index in reversed(range(LEVELS)):
        sweeper, below = saved[level_index]
        pressure = below + prolong(pressure)
        for repeat in range(SWEEPS):
            pressure = sweeper(pressure)
    faces, diagonal = finest
    remain = residual_of(pressure, right_side, faces, diagonal, 1.0, with_rims)
    return (pressure, remain)


def solution(mesh):
    return jax.shard_map(
        body,
        mesh=mesh,
        in_specs=(P("gz", "xy", None), P("gz", "xy", None)),
        out_specs=(P("gz", "xy", None), P("gz", "xy", None)),
        check_vma=False,
    )
```

profile of v0, /device:TPU:31, one launch (start us, length us, event | category | flops | bytes accessed | tf_op | source)
XLA Modules:
  0.0 780.5 jit_solution(7228150275108844389)
XLA Ops:
  6.9 4.6 collective-permute-start.1
  12.9 5.5 collective-permute-start.4
  20.3 7.0 collective-permute-start.5
  29.6 6.1 collective-permute-done.7
  37.3 4.6 collective-permute-start.8
  43.3 4.9 collective-permute-done.9
  53.3 5.0 collective-permute-start.25
  59.5 9.7 %reshape.58 = f32[16,2,4,2,64,2]{5,4,3,2,1,0:T(8,128)} reshape(f32[32,8,128]{2,1,0:T(8,128)S(1)} %get-tuple-element.256) | data formatting | bytes 262144 | tf_op jit(solution)/shard_map/reshape | solution.py:35
  73.9 5.5 collective-permute-start.12
  80.7 4.6 collective-permute-done.13
  85.4 8.3 %collective-permute-start.14 = (f32[34,1,128]{2,1,0:T(1,128)S(1)}, f32[34,1,128]{2,1,0:T(1,128)S(1)}, u32[]{:S(2)}, u32[]{:S(2)}) collective-permute-start(f32[34,1,128]{2,1,0:T(1,128)S(1)} %get-tuple-element.272), channel_id=1, source_target_pairs={{0,1},{1,2},{2,3},{3,4},{4,5},{5,6},{6,7},{7,8},{8,9},{9,10},{10,1... | collective-permute-start | bytes 52232 | tf_op jit(solution)/shard_map/ppermute | solution.py:23
  106.7 4.1 collective-permute-start.16
  115.2 8.9 %collective-permute-start.28 = (f32[18,1,64]{2,1,0:T(1,128)S(1)}, f32[18,1,64]{2,1,0:T(1,128)S(1)}, u32[]{:S(2)}, u32[]{:S(2)}) collective-permute-start(f32[18,1,64]{2,1,0:T(1,128)S(1)} %get-tuple-element.317), channel_id=1, source_target_pairs={{0,1},{1,2},{2,3},{3,4},{4,5},{5,6},{6,7},{7,8},{8,9},{9,10},{10,1... | collective-permute-start | bytes 13832 | tf_op jit(solution)/shard_map/ppermute | solution.py:23
  146.1 6.0 collective-permute-start.22
  154.2 6.3 collective-permute-done.23
  161.0 9.7 %reshape.57 = f32[16,2,4,2,64,2]{5,4,3,2,1,0:T(8,128)} reshape(f32[32,8,128]{2,1,0:T(8,128)S(1)} %fusion.121) | data formatting | bytes 262144 | tf_op jit(solution)/shard_map/reshape | solution.py:35
  199.7 4.6 collective-permute-done.37
  204.3 8.3 %collective-permute-start.38 = (f32[18,1,64]{2,1,0:T(1,128)S(1)}, f32[18,1,64]{2,1,0:T(1,128)S(1)}, u32[]{:S(2)}, u32[]{:S(2)}) collective-permute-start(f32[18,1,64]{2,1,0:T(1,128)S(1)} %get-tuple-element.312), channel_id=1, source_target_pairs={{0,1},{1,2},{2,3},{3,4},{4,5},{5,6},{6,7},{7,8},{8,9},{9,10},{10,1... | collective-permute-start | bytes 13832 | tf_op jit(solution)/shard_map/ppermute | solution.py:23
  214.5 7.0 collective-permute-start.52
  232.2 8.1 %collective-permute-start.42 = (f32[18,1,64]{2,1,0:T(1,128)S(1)}, f32[18,1,64]{2,1,0:T(1,128)S(1)}, u32[]{:S(2)}, u32[]{:S(2)}) collective-permute-start(f32[18,1,64]{2,1,0:T(1,128)S(1)} %get-tuple-element.310), channel_id=1, source_target_pairs={{0,1},{1,2},{2,3},{3,4},{4,5},{5,6},{6,7},{7,8},{8,9},{9,10},{10,1... | collective-permute-start | bytes 13832 | tf_op jit(solution)/shard_map/ppermute | solution.py:23
  242.3 7.0 collective-permute-start.53
  251.6 4.1 collective-permute-start.44
  260.3 8.1 %collective-permute-start.46 = (f32[18,1,64]{2,1,0:T(1,128)S(1)}, f32[18,1,64]{2,1,0:T(1,128)S(1)}, u32[]{:S(2)}, u32[]{:S(2)}) collective-permute-start(f32[18,1,64]{2,1,0:T(1,128)S(1)} %get-tuple-element.308), channel_id=1, source_target_pairs={{0,1},{1,2},{2,3},{3,4},{4,5},{5,6},{6,7},{7,8},{8,9},{9,10},{10,1... | collective-permute-start | bytes 13832 | tf_op jit(solution)/shard_map/ppermute | solution.py:23
  270.4 6.3 collective-permute-done.47
  291.7 6.4 collective-permute-done.59
  310.9 6.2 collective-permute-done.63
  329.8 49.0 %all-gather.3 = f32[64,16,4]{1,2,0:T(4,128)S(1)} all-gather(f32[1,16,4]{1,2,0:T(4,128)S(1)} %multiply_bitcast_fusion), channel_id=3, replica_groups=mesh['gz'=8,'xy'=64] {'xy'}, dimensions={0}, use_global_device_ids=true | all-gather | bytes 16640 | tf_op jit(solution)/shard_map/all_gather | solution.py:137
  383.5 19.3 %all_gather.15 = f32[32,64,16]{1,2,0:T(8,128)S(1)} all-gather(f32[4,64,16]{1,2,0:T(8,128)S(1)} %copy.20), channel_id=1, replica_groups=mesh['gz'=8,'xy'=64] {'gz'}, dimensions={0}, use_global_device_ids=true | all-gather | bytes 147456 | tf_op jit(solution)/shard_map/all_gather | solution.py:141
  402.9 10.7 %collective-permute-start.70 = (f32[10,1,32]{2,0,1:T(8,128)S(1)}, f32[10,1,32]{2,0,1:T(8,128)S(1)}, u32[]{:S(2)}, u32[]{:S(2)}) collective-permute-start(f32[10,1,32]{2,0,1:T(8,128)S(1)} %get-tuple-element.346), channel_id=1, source_target_pairs={{0,1},{1,2},{2,3},{3,4},{4,5},{5,6},{6,7},{7,8},{8,9},{9,10},{10,1... | collective-permute-start | bytes 3848 | tf_op jit(solution)/shard_map/ppermute | solution.py:23
  415.9 6.0 collective-permute-done.71
  422.3 46.7 %all-gather.2 = f32[64,16,4]{1,2,0:T(4,128)S(1)} all-gather(f32[1,16,4]{1,2,0:T(4,128)S(1)} %multiply_bitcast_fusion.1), channel_id=2, replica_groups=mesh['gz'=8,'xy'=64] {'xy'}, dimensions={0}, use_global_device_ids=true | all-gather | bytes 16640 | tf_op jit(solution)/shard_map/all_gather | solution.py:138
  471.6 18.8 %all_gather.13 = f32[32,64,16]{1,2,0:T(8,128)S(1)} all-gather(f32[4,64,16]{1,2,0:T(8,128)} %copy.18), channel_id=1, replica_groups=mesh['gz'=8,'xy'=64] {'gz'}, dimensions={0}, use_global_device_ids=true | all-gather | bytes 147456 | tf_op jit(solution)/shard_map/all_gather | solution.py:142
  490.3 8.6 %while.14 = (s32[]{:T(128)}, f32[32,64,16]{1,2,0:T(8,128)S(1)}, f32[32,64,16]{1,2,0:T(8,128)S(1)}, f32[32,64,16]{1,2,0:T(8,128)S(1)}, f32[32,64,16]{1,2,0:T(8,12...) while((s32[]{:T(128)}, f32[32,64,16]{1,2,0:T(8,128)S(1)}, ...), condition=%wide.region_9.10_spmd.clone.clone, body=%wide.region_8.9_spmd.clone.clone.sunk | while | flops 1933315 | bytes 2883711 | solution.py:151
  507.4 11.9 %collective-permute-start.74 = (f32[10,1,32]{2,0,1:T(8,128)S(1)}, f32[10,1,32]{2,0,1:T(8,128)S(1)}, u32[]{:S(2)}, u32[]{:S(2)}) collective-permute-start(f32[10,1,32]{2,0,1:T(8,128)S(1)} %get-tuple-element.344), channel_id=1, source_target_pairs={{0,1},{1,2},{2,3},{3,4},{4,5},{5,6},{6,7},{7,8},{8,9},{9,10},{10,1... | collective-permute-start | bytes 3848 | tf_op jit(solution)/shard_map/ppermute | solution.py:23
  521.2 6.4 collective-permute-done.75
  541.0 6.4 collective-permute-done.79
  561.9 6.4 collective-permute-done.83
  582.4 6.4 collective-permute-done.87
  603.9 6.4 collective-permute-done.91
  623.8 6.4 collective-permute-done.95
  643.7 6.4 collective-permute-done.99
  663.9 6.1 collective-permute-done.103
  675.1 6.9 reshape.61
  694.6 6.5 collective-permute-done.107
  714.1 6.5 collective-permute-done.111
  733.7 6.5 collective-permute-done.115
  753.2 6.5 collective-permute-done.119
  772.8 6.5 collective-permute-done.123
  (442 shorter events, 358.0 us)
Async XLA Ops:
  1.6 11.3 %collective-permute-start = (f32[1,8,128]{2,1,0:T(8,128)S(1)}, f32[1,8,128]{2,1,0:T(8,128)S(1)}, u32[]{:S(2)}, u32[]{:S(2)}) collective-permute-start(f32[1,8,128]{2,1,0:T(8,128)S(1)} %get-tuple-element.298), channel_id=1, source_target_pairs={{0,64},{64,128},{128,192},{192,256},{256,320},{320,384},{384,448},... | collective-permute-start | bytes 12296 | tf_op jit(solution)/shard_map/ppermute | solution.py:23
  6.9 13.4 %collective-permute-start.1 = (f32[1,8,128]{2,1,0:T(8,128)S(1)}, f32[1,8,128]{2,1,0:T(8,128)S(1)}, u32[]{:S(2)}, u32[]{:S(2)}) collective-permute-start(f32[1,8,128]{2,1,0:T(8,128)S(1)} %broadcast.197), channel_id=1, source_target_pairs={{0,64},{64,128},{128,192},{192,256},{256,320},{320,384},{384,448},... | collective-permute-start | bytes 12296 | tf_op jit(solution)/shard_map/ppermute | solution.py:23
  11.5 8.8 %collective-permute-start.3 = (f32[1,8,128]{2,1,0:T(8,128)S(1)}, f32[1,8,128]{2,1,0:T(8,128)S(1)}, u32[]{:S(2)}, u32[]{:S(2)}) collective-permute-start(f32[1,8,128]{2,1,0:T(8,128)S(1)} %broadcast.197), channel_id=1, source_target_pairs={{64,0},{128,64},{192,128},{256,192},{320,256},{384,320},{448,384},... | collective-permute-start | bytes 12296 | tf_op jit(solution)/shard_map/ppermute | solution.py:24
  12.9 16.4 %collective-permute-start.4 = (f32[34,1,128]{2,1,0:T(1,128)S(1)}, f32[34,1,128]{2,1,0:T(1,128)S(1)}, u32[]{:S(2)}, u32[]{:S(2)}) collective-permute-start(f32[34,1,128]{2,1,0:T(1,128)S(1)} %get-tuple-element.277), channel_id=1, source_target_pairs={{0,1},{1,2},{2,3},{3,4},{4,5},{5,6},{6,7},{7,8},{8,9},{9,10},{10,1... | collective-permute-start | bytes 52232 | tf_op jit(solution)/shard_map/ppermute | solution.py:23
  18.3 10.9 %collective-permute-start.6 = (f32[34,1,128]{2,1,0:T(1,128)S(1)}, f32[34,1,128]{2,1,0:T(1,128)S(1)}, u32[]{:S(2)}, u32[]{:S(2)}) collective-permute-start(f32[34,1,128]{2,1,0:T(1,128)S(1)} %get-tuple-element.276), channel_id=1, source_target_pairs={{1,0},{2,1},{3,2},{4,3},{5,4},{6,5},{7,6},{8,7},{9,8},{10,9},{11,1... | collective-permute-start | bytes 52232 | tf_op jit(solution)/shard_map/ppermute | solution.py:24
  20.3 9.3 %collective-permute-start.5 = (f32[34,1,128]{2,1,0:T(1,128)S(1)}, f32[34,1,128]{2,1,0:T(1,128)S(1)}, u32[]{:S(2)}, u32[]{:S(2)}) collective-permute-start(f32[34,1,128]{2,1,0:T(1,128)S(1)} %get-tuple-element.278), channel_id=1, source_target_pairs={{0,1},{1,2},{2,3},{3,4},{4,5},{5,6},{6,7},{7,8},{8,9},{9,10},{10,1... | collective-permute-start | bytes 52232 | tf_op jit(solution)/shard_map/ppermute | solution.py:23
  27.3 8.4 %collective-permute-start.7 = (f32[34,1,128]{2,1,0:T(1,128)S(1)}, f32[34,1,128]{2,1,0:T(1,128)S(1)}, u32[]{:S(2)}, u32[]{:S(2)}) collective-permute-start(f32[34,1,128]{2,1,0:T(1,128)S(1)} %get-tuple-element.279), channel_id=1, source_target_pairs={{1,0},{2,1},{3,2},{4,3},{5,4},{6,5},{7,6},{8,7},{9,8},{10,9},{11,1... | collective-permute-start | bytes 52232 | tf_op jit(solution)/shard_map/ppermute | solution.py:24
  48.2 25.1 %collective-permute-start.10 = (f32[34,1,128]{2,1,0:T(1,128)S(1)}, f32[34,1,128]{2,1,0:T(1,128)S(1)}, u32[]{:S(2)}, u32[]{:S(2)}) collective-permute-start(f32[34,1,128]{2,1,0:T(1,128)S(1)} %get-tuple-element.274), channel_id=1, source_target_pairs={{0,1},{1,2},{2,3},{3,4},{4,5},{5,6},{6,7},{7,8},{8,9},{9,10},{10,1... | collective-permute-start | bytes 52232 | tf_op jit(solution)/shard_map/ppermute | solution.py:23
  51.3 22.0 %collective-permute-start.11 = (f32[34,1,128]{2,1,0:T(1,128)S(1)}, f32[34,1,128]{2,1,0:T(1,128)S(1)}, u32[]{:S(2)}, u32[]{:S(2)}) collective-permute-start(f32[34,1,128]{2,1,0:T(1,128)S(1)} %get-tuple-element.275), channel_id=1, source_target_pairs={{1,0},{2,1},{3,2},{4,3},{5,4},{6,5},{7,6},{8,7},{9,8},{10,9},{11,1... | collective-permute-start | bytes 52232 | tf_op jit(solution)/shard_map/ppermute | solution.py:24
  53.3 70.9 %collective-permute-start.25 = (f32[1,4,64]{2,1,0:T(4,128)S(1)}, f32[1,4,64]{2,1,0:T(4,128)S(1)}, u32[]{:S(2)}, u32[]{:S(2)}) collective-permute-start(f32[1,4,64]{2,1,0:T(4,128)S(1)} %broadcast.201), channel_id=1, source_target_pairs={{0,64},{64,128},{128,192},{192,256},{256,320},{320,384},{384,448},... | collective-permute-start | bytes 3080 | tf_op jit(solution)/shard_map/ppermute | solution.py:23
  58.2 67.8 %collective-permute-start.27 = (f32[1,4,64]{2,1,0:T(4,128)S(1)}, f32[1,4,64]{2,1,0:T(4,128)S(1)}, u32[]{:S(2)}, u32[]{:S(2)}) collective-permute-start(f32[1,4,64]{2,1,0:T(4,128)S(1)} %broadcast.201), channel_id=1, source_target_pairs={{64,0},{128,64},{192,128},{256,192},{320,256},{384,320},{448,384},... | collective-permute-start | bytes 3080 | tf_op jit(solution)/shard_map/ppermute | solution.py:24
  85.4 15.1 %collective-permute-start.14 = (f32[34,1,128]{2,1,0:T(1,128)S(1)}, f32[34,1,128]{2,1,0:T(1,128)S(1)}, u32[]{:S(2)}, u32[]{:S(2)}) collective-permute-start(f32[34,1,128]{2,1,0:T(1,128)S(1)} %get-tuple-element.272), channel_id=1, source_target_pairs={{0,1},{1,2},{2,3},{3,4},{4,5},{5,6},{6,7},{7,8},{8,9},{9,10},{10,1... | collective-permute-start | bytes 52232 | tf_op jit(solution)/shard_map/ppermute | solution.py:23
  93.7 8.4 %collective-permute-start.15 = (f32[34,1,128]{2,1,0:T(1,128)S(1)}, f32[34,1,128]{2,1,0:T(1,128)S(1)}, u32[]{:S(2)}, u32[]{:S(2)}) collective-permute-start(f32[34,1,128]{2,1,0:T(1,128)S(1)} %get-tuple-element.273), channel_id=1, source_target_pairs={{1,0},{2,1},{3,2},{4,3},{5,4},{6,5},{7,6},{8,7},{9,8},{10,9},{11,1... | collective-permute-start | bytes 52232 | tf_op jit(solution)/shard_map/ppermute | solution.py:24
  95.6 11.1 %collective-permute-start.24 = (f32[1,4,64]{2,1,0:T(4,128)S(1)}, f32[1,4,64]{2,1,0:T(4,128)S(1)}, u32[]{:S(2)}, u32[]{:S(2)}) collective-permute-start(f32[1,4,64]{2,1,0:T(4,128)S(1)} %get-tuple-element.337), channel_id=1, source_target_pairs={{0,64},{64,128},{128,192},{192,256},{256,320},{320,384},{384,448},... | collective-permute-start | bytes 3080 | tf_op jit(solution)/shard_map/ppermute | solution.py:23
  100.5 10.3 %collective-permute-start.26 = (f32[1,4,64]{2,1,0:T(4,128)S(1)}, f32[1,4,64]{2,1,0:T(4,128)S(1)}, u32[]{:S(2)}, u32[]{:S(2)}) collective-permute-start(f32[1,4,64]{2,1,0:T(4,128)S(1)} %get-tuple-element.336), channel_id=1, source_target_pairs={{64,0},{128,64},{192,128},{256,192},{320,256},{384,320},{448,384},... | collective-permute-start | bytes 3080 | tf_op jit(solution)/shard_map/ppermute | solution.py:24
  102.1 125.5 %collective-permute-start.49 = (f32[1,2,32]{2,0,1:T(1,128)S(1)}, f32[1,2,32]{2,0,1:T(1,128)S(1)}, u32[]{:S(2)}, u32[]{:S(2)}) collective-permute-start(f32[1,2,32]{2,0,1:T(1,128)S(1)} %broadcast.204), channel_id=1, source_target_pairs={{0,64},{64,128},{128,192},{192,256},{256,320},{320,384},{384,448},... | collective-permute-start | bytes 776 | tf_op jit(solution)/shard_map/ppermute | solution.py:23
  112.1 116.8 %collective-permute-start.51 = (f32[1,2,32]{2,0,1:T(1,128)S(1)}, f32[1,2,32]{2,0,1:T(1,128)S(1)}, u32[]{:S(2)}, u32[]{:S(2)}) collective-permute-start(f32[1,2,32]{2,0,1:T(1,128)S(1)} %broadcast.204), channel_id=1, source_target_pairs={{64,0},{128,64},{192,128},{256,192},{320,256},{384,320},{448,384},... | collective-permute-start | bytes 776 | tf_op jit(solution)/shard_map/ppermute | solution.py:24
  115.2 22.9 %collective-permute-start.28 = (f32[18,1,64]{2,1,0:T(1,128)S(1)}, f32[18,1,64]{2,1,0:T(1,128)S(1)}, u32[]{:S(2)}, u32[]{:S(2)}) collective-permute-start(f32[18,1,64]{2,1,0:T(1,128)S(1)} %get-tuple-element.317), channel_id=1, source_target_pairs={{0,1},{1,2},{2,3},{3,4},{4,5},{5,6},{6,7},{7,8},{8,9},{9,10},{10,1... | collective-permute-start | bytes 13832 | tf_op jit(solution)/shard_map/ppermute | solution.py:23
  126.1 8.4 %collective-permute-start.19 = (f32[34,1,128]{2,1,0:T(1,128)S(1)}, f32[34,1,128]{2,1,0:T(1,128)S(1)}, u32[]{:S(2)}, u32[]{:S(2)}) collective-permute-start(f32[34,1,128]{2,1,0:T(1,128)S(1)} %get-tuple-element.271), channel_id=1, source_target_pairs={{1,0},{2,1},{3,2},{4,3},{5,4},{6,5},{7,6},{8,7},{9,8},{10,9},{11,1... | collective-permute-start | bytes 52232 | tf_op jit(solution)/shard_map/ppermute | solution.py:24
  128.6 13.1 %collective-permute-start.30 = (f32[18,1,64]{2,1,0:T(1,128)S(1)}, f32[18,1,64]{2,1,0:T(1,128)S(1)}, u32[]{:S(2)}, u32[]{:S(2)}) collective-permute-start(f32[18,1,64]{2,1,0:T(1,128)S(1)} %get-tuple-element.316), channel_id=1, source_target_pairs={{1,0},{2,1},{3,2},{4,3},{5,4},{6,5},{7,6},{8,7},{9,8},{10,9},{11,1... | collective-permute-start | bytes 13832 | tf_op jit(solution)/shard_map/ppermute | solution.py:24
  134.5 17.6 %collective-permute-start.29 = (f32[18,1,64]{2,1,0:T(1,128)S(1)}, f32[18,1,64]{2,1,0:T(1,128)S(1)}, u32[]{:S(2)}, u32[]{:S(2)}) collective-permute-start(f32[18,1,64]{2,1,0:T(1,128)S(1)} %get-tuple-element.318), channel_id=1, source_target_pairs={{0,1},{1,2},{2,3},{3,4},{4,5},{5,6},{6,7},{7,8},{8,9},{9,10},{10,1... | collective-permute-start | bytes 13832 | tf_op jit(solution)/shard_map/ppermute | solution.py:23
  143.2 10.9 %collective-permute-start.31 = (f32[18,1,64]{2,1,0:T(1,128)S(1)}, f32[18,1,64]{2,1,0:T(1,128)S(1)}, u32[]{:S(2)}, u32[]{:S(2)}) collective-permute-start(f32[18,1,64]{2,1,0:T(1,128)S(1)} %get-tuple-element.319), channel_id=1, source_target_pairs={{1,0},{2,1},{3,2},{4,3},{5,4},{6,5},{7,6},{8,7},{9,8},{10,9},{11,1... | collective-permute-start | bytes 13832 | tf_op jit(solution)/shard_map/ppermute | solution.py:24
  152.1 8.4 %collective-permute-start.23 = (f32[34,1,128]{2,1,0:T(1,128)S(1)}, f32[34,1,128]{2,1,0:T(1,128)S(1)}, u32[]{:S(2)}, u32[]{:S(2)}) collective-permute-start(f32[34,1,128]{2,1,0:T(1,128)S(1)} %get-tuple-element.269), channel_id=1, source_target_pairs={{1,0},{2,1},{3,2},{4,3},{5,4},{6,5},{7,6},{8,7},{9,8},{10,9},{11,1... | collective-permute-start | bytes 52232 | tf_op jit(solution)/shard_map/ppermute | solution.py:24
  186.8 8.3 %collective-permute-start.35 = (f32[18,1,64]{2,1,0:T(1,128)S(1)}, f32[18,1,64]{2,1,0:T(1,128)S(1)}, u32[]{:S(2)}, u32[]{:S(2)}) collective-permute-start(f32[18,1,64]{2,1,0:T(1,128)S(1)} %get-tuple-element.315), channel_id=1, source_target_pairs={{1,0},{2,1},{3,2},{4,3},{5,4},{6,5},{7,6},{8,7},{9,8},{10,9},{11,1... | collective-permute-start | bytes 13832 | tf_op jit(solution)/shard_map/ppermute | solution.py:24
  188.7 9.6 %collective-permute-start.48 = (f32[1,2,32]{2,0,1:T(1,128)S(1)}, f32[1,2,32]{2,0,1:T(1,128)S(1)}, u32[]{:S(2)}, u32[]{:S(2)}) collective-permute-start(f32[1,2,32]{2,0,1:T(1,128)S(1)} %get-tuple-element.377), channel_id=1, source_target_pairs={{0,64},{64,128},{128,192},{192,256},{256,320},{320,384},{384,448},... | collective-permute-start | bytes 776 | tf_op jit(solution)/shard_map/ppermute | solution.py:23
  204.3 17.2 %collective-permute-start.38 = (f32[18,1,64]{2,1,0:T(1,128)S(1)}, f32[18,1,64]{2,1,0:T(1,128)S(1)}, u32[]{:S(2)}, u32[]{:S(2)}) collective-permute-start(f32[18,1,64]{2,1,0:T(1,128)S(1)} %get-tuple-element.312), channel_id=1, source_target_pairs={{0,1},{1,2},{2,3},{3,4},{4,5},{5,6},{6,7},{7,8},{8,9},{9,10},{10,1... | collective-permute-start | bytes 13832 | tf_op jit(solution)/shard_map/ppermute | solution.py:23
  212.6 11.0 %collective-permute-start.39 = (f32[18,1,64]{2,1,0:T(1,128)S(1)}, f32[18,1,64]{2,1,0:T(1,128)S(1)}, u32[]{:S(2)}, u32[]{:S(2)}) collective-permute-start(f32[18,1,64]{2,1,0:T(1,128)S(1)} %get-tuple-element.313), channel_id=1, source_target_pairs={{1,0},{2,1},{3,2},{4,3},{5,4},{6,5},{7,6},{8,7},{9,8},{10,9},{11,1... | collective-permute-start | bytes 13832 | tf_op jit(solution)/shard_map/ppermute | solution.py:24
  214.5 41.1 %collective-permute-start.52 = (f32[10,1,32]{2,0,1:T(8,128)S(1)}, f32[10,1,32]{2,0,1:T(8,128)S(1)}, u32[]{:S(2)}, u32[]{:S(2)}) collective-permute-start(f32[10,1,32]{2,0,1:T(8,128)S(1)} %get-tuple-element.355), channel_id=1, source_target_pairs={{0,1},{1,2},{2,3},{3,4},{4,5},{5,6},{6,7},{7,8},{8,9},{9,10},{10,1... | collective-permute-start | bytes 3848 | tf_op jit(solution)/shard_map/ppermute | solution.py:23
  221.5 35.4 %collective-permute-start.54 = (f32[10,1,32]{2,0,1:T(8,128)S(1)}, f32[10,1,32]{2,0,1:T(8,128)S(1)}, u32[]{:S(2)}, u32[]{:S(2)}) collective-permute-start(f32[10,1,32]{2,0,1:T(8,128)S(1)} %get-tuple-element.354), channel_id=1, source_target_pairs={{1,0},{2,1},{3,2},{4,3},{5,4},{6,5},{7,6},{8,7},{9,8},{10,9},{11,1... | collective-permute-start | bytes 3848 | tf_op jit(solution)/shard_map/ppermute | solution.py:24
  232.2 17.0 %collective-permute-start.42 = (f32[18,1,64]{2,1,0:T(1,128)S(1)}, f32[18,1,64]{2,1,0:T(1,128)S(1)}, u32[]{:S(2)}, u32[]{:S(2)}) collective-permute-start(f32[18,1,64]{2,1,0:T(1,128)S(1)} %get-tuple-element.310), channel_id=1, source_target_pairs={{0,1},{1,2},{2,3},{3,4},{4,5},{5,6},{6,7},{7,8},{8,9},{9,10},{10,1... | collective-permute-start | bytes 13832 | tf_op jit(solution)/shard_map/ppermute | solution.py:23
  240.4 10.9 %collective-permute-start.43 = (f32[18,1,64]{2,1,0:T(1,128)S(1)}, f32[18,1,64]{2,1,0:T(1,128)S(1)}, u32[]{:S(2)}, u32[]{:S(2)}) collective-permute-start(f32[18,1,64]{2,1,0:T(1,128)S(1)} %get-tuple-element.311), channel_id=1, source_target_pairs={{1,0},{2,1},{3,2},{4,3},{5,4},{6,5},{7,6},{8,7},{9,8},{10,9},{11,1... | collective-permute-start | bytes 13832 | tf_op jit(solution)/shard_map/ppermute | solution.py:24
  242.3 28.0 %collective-permute-start.53 = (f32[10,1,32]{2,0,1:T(8,128)S(1)}, f32[10,1,32]{2,0,1:T(8,128)S(1)}, u32[]{:S(2)}, u32[]{:S(2)}) collective-permute-start(f32[10,1,32]{2,0,1:T(8,128)S(1)} %get-tuple-element.356), channel_id=1, source_target_pairs={{0,1},{1,2},{2,3},{3,4},{4,5},{5,6},{6,7},{7,8},{8,9},{9,10},{10,1... | collective-permute-start | bytes 3848 | tf_op jit(solution)/shard_map/ppermute | solution.py:23
  249.3 21.0 %collective-permute-start.55 = (f32[10,1,32]{2,0,1:T(8,128)S(1)}, f32[10,1,32]{2,0,1:T(8,128)S(1)}, u32[]{:S(2)}, u32[]{:S(2)}) collective-permute-start(f32[10,1,32]{2,0,1:T(8,128)S(1)} %get-tuple-element.357), channel_id=1, source_target_pairs={{1,0},{2,1},{3,2},{4,3},{5,4},{6,5},{7,6},{8,7},{9,8},{10,9},{11,1... | collective-permute-start | bytes 3848 | tf_op jit(solution)/shard_map/ppermute | solution.py:24
  260.3 10.2 %collective-permute-start.46 = (f32[18,1,64]{2,1,0:T(1,128)S(1)}, f32[18,1,64]{2,1,0:T(1,128)S(1)}, u32[]{:S(2)}, u32[]{:S(2)}) collective-permute-start(f32[18,1,64]{2,1,0:T(1,128)S(1)} %get-tuple-element.308), channel_id=1, source_target_pairs={{0,1},{1,2},{2,3},{3,4},{4,5},{5,6},{6,7},{7,8},{8,9},{9,10},{10,1... | collective-permute-start | bytes 13832 | tf_op jit(solution)/shard_map/ppermute | solution.py:23
  268.4 8.3 %collective-permute-start.47 = (f32[18,1,64]{2,1,0:T(1,128)S(1)}, f32[18,1,64]{2,1,0:T(1,128)S(1)}, u32[]{:S(2)}, u32[]{:S(2)}) collective-permute-start(f32[18,1,64]{2,1,0:T(1,128)S(1)} %get-tuple-element.309), channel_id=1, source_target_pairs={{1,0},{2,1},{3,2},{4,3},{5,4},{6,5},{7,6},{8,7},{9,8},{10,9},{11,1... | collective-permute-start | bytes 13832 | tf_op jit(solution)/shard_map/ppermute | solution.py:24
  324.5 54.7 %collective-permute-start.66 = (f32[10,1,32]{2,0,1:T(8,128)S(1)}, f32[10,1,32]{2,0,1:T(8,128)S(1)}, u32[]{:S(2)}, u32[]{:S(2)}) collective-permute-start(f32[10,1,32]{2,0,1:T(8,128)S(1)} %get-tuple-element.348), channel_id=1, source_target_pairs={{0,1},{1,2},{2,3},{3,4},{4,5},{5,6},{6,7},{7,8},{8,9},{9,10},{10,1... | collective-permute-start | bytes 3848 | tf_op jit(solution)/shard_map/ppermute | solution.py:23
  327.9 51.3 %collective-permute-start.67 = (f32[10,1,32]{2,0,1:T(8,128)S(1)}, f32[10,1,32]{2,0,1:T(8,128)S(1)}, u32[]{:S(2)}, u32[]{:S(2)}) collective-permute-start(f32[10,1,32]{2,0,1:T(8,128)S(1)} %get-tuple-element.349), channel_id=1, source_target_pairs={{1,0},{2,1},{3,2},{4,3},{5,4},{6,5},{7,6},{8,7},{9,8},{10,9},{11,1... | collective-permute-start | bytes 3848 | tf_op jit(solution)/shard_map/ppermute | solution.py:24
  379.4 23.5 %collective-permute-start.68 = (f32[1,2,32]{2,0,1:T(1,128)S(1)}, f32[1,2,32]{2,0,1:T(1,128)S(1)}, u32[]{:S(2)}, u32[]{:S(2)}) collective-permute-start(f32[1,2,32]{2,0,1:T(1,128)S(1)} %get-tuple-element.368), channel_id=1, source_target_pairs={{0,64},{64,128},{128,192},{192,256},{256,320},{320,384},{384,448},... | collective-permute-start | bytes 776 | tf_op jit(solution)/shard_map/ppermute | solution.py:23
  382.2 20.6 %collective-permute-start.69 = (f32[1,2,32]{2,0,1:T(1,128)S(1)}, f32[1,2,32]{2,0,1:T(1,128)S(1)}, u32[]{:S(2)}, u32[]{:S(2)}) collective-permute-start(f32[1,2,32]{2,0,1:T(1,128)S(1)} %get-tuple-element.369), channel_id=1, source_target_pairs={{64,0},{128,64},{192,128},{256,192},{320,256},{384,320},{448,384},... | collective-permute-start | bytes 776 | tf_op jit(solution)/shard_map/ppermute | solution.py:24
  402.9 13.0 %collective-permute-start.70 = (f32[10,1,32]{2,0,1:T(8,128)S(1)}, f32[10,1,32]{2,0,1:T(8,128)S(1)}, u32[]{:S(2)}, u32[]{:S(2)}) collective-permute-start(f32[10,1,32]{2,0,1:T(8,128)S(1)} %get-tuple-element.346), channel_id=1, source_target_pairs={{0,1},{1,2},{2,3},{3,4},{4,5},{5,6},{6,7},{7,8},{8,9},{9,10},{10,1... | collective-permute-start | bytes 3848 | tf_op jit(solution)/shard_map/ppermute | solution.py:23
  507.4 13.8 %collective-permute-start.74 = (f32[10,1,32]{2,0,1:T(8,128)S(1)}, f32[10,1,32]{2,0,1:T(8,128)S(1)}, u32[]{:S(2)}, u32[]{:S(2)}) collective-permute-start(f32[10,1,32]{2,0,1:T(8,128)S(1)} %get-tuple-element.344), channel_id=1, source_target_pairs={{0,1},{1,2},{2,3},{3,4},{4,5},{5,6},{6,7},{7,8},{8,9},{9,10},{10,1... | collective-permute-start | bytes 3848 | tf_op jit(solution)/shard_map/ppermute | solution.py:23
  601.9 8.3 %collective-permute-start.91 = (f32[18,1,64]{2,1,0:T(1,128)S(1)}, f32[18,1,64]{2,1,0:T(1,128)S(1)}, u32[]{:S(2)}, u32[]{:S(2)}) collective-permute-start(f32[18,1,64]{2,1,0:T(1,128)S(1)} %get-tuple-element.307), channel_id=1, source_target_pairs={{1,0},{2,1},{3,2},{4,3},{5,4},{6,5},{7,6},{8,7},{9,8},{10,9},{11,1... | collective-permute-start | bytes 13832 | tf_op jit(solution)/shard_map/ppermute | solution.py:24
  621.9 8.3 %collective-permute-start.95 = (f32[18,1,64]{2,1,0:T(1,128)S(1)}, f32[18,1,64]{2,1,0:T(1,128)S(1)}, u32[]{:S(2)}, u32[]{:S(2)}) collective-permute-start(f32[18,1,64]{2,1,0:T(1,128)S(1)} %get-tuple-element.305), channel_id=1, source_target_pairs={{1,0},{2,1},{3,2},{4,3},{5,4},{6,5},{7,6},{8,7},{9,8},{10,9},{11,1... | collective-permute-start | bytes 13832 | tf_op jit(solution)/shard_map/ppermute | solution.py:24
  692.6 8.4 %collective-permute-start.107 = (f32[34,1,128]{2,1,0:T(1,128)S(1)}, f32[34,1,128]{2,1,0:T(1,128)S(1)}, u32[]{:S(2)}, u32[]{:S(2)}) collective-permute-start(f32[34,1,128]{2,1,0:T(1,128)S(1)} %get-tuple-element.267), channel_id=1, source_target_pairs={{1,0},{2,1},{3,2},{4,3},{5,4},{6,5},{7,6},{8,7},{9,8},{10,9},{11,1... | collective-permute-start | bytes 52232 | tf_op jit(solution)/shard_map/ppermute | solution.py:24
  712.2 8.4 %collective-permute-start.111 = (f32[34,1,128]{2,1,0:T(1,128)S(1)}, f32[34,1,128]{2,1,0:T(1,128)S(1)}, u32[]{:S(2)}, u32[]{:S(2)}) collective-permute-start(f32[34,1,128]{2,1,0:T(1,128)S(1)} %get-tuple-element.265), channel_id=1, source_target_pairs={{1,0},{2,1},{3,2},{4,3},{5,4},{6,5},{7,6},{8,7},{9,8},{10,9},{11,1... | collective-permute-start | bytes 52232 | tf_op jit(solution)/shard_map/ppermute | solution.py:24
  731.7 8.4 %collective-permute-start.115 = (f32[34,1,128]{2,1,0:T(1,128)S(1)}, f32[34,1,128]{2,1,0:T(1,128)S(1)}, u32[]{:S(2)}, u32[]{:S(2)}) collective-permute-start(f32[34,1,128]{2,1,0:T(1,128)S(1)} %get-tuple-element.263), channel_id=1, source_target_pairs={{1,0},{2,1},{3,2},{4,3},{5,4},{6,5},{7,6},{8,7},{9,8},{10,9},{11,1... | collective-permute-start | bytes 52232 | tf_op jit(solution)/shard_map/ppermute | solution.py:24
  751.3 8.4 %collective-permute-start.119 = (f32[34,1,128]{2,1,0:T(1,128)S(1)}, f32[34,1,128]{2,1,0:T(1,128)S(1)}, u32[]{:S(2)}, u32[]{:S(2)}) collective-permute-start(f32[34,1,128]{2,1,0:T(1,128)S(1)} %get-tuple-element.261), channel_id=1, source_target_pairs={{1,0},{2,1},{3,2},{4,3},{5,4},{6,5},{7,6},{8,7},{9,8},{10,9},{11,1... | collective-permute-start | bytes 52232 | tf_op jit(solution)/shard_map/ppermute | solution.py:24
  770.9 8.4 %collective-permute-start.123 = (f32[34,1,128]{2,1,0:T(1,128)S(1)}, f32[34,1,128]{2,1,0:T(1,128)S(1)}, u32[]{:S(2)}, u32[]{:S(2)}) collective-permute-start(f32[34,1,128]{2,1,0:T(1,128)S(1)} %get-tuple-element.259), channel_id=1, source_target_pairs={{1,0},{2,1},{3,2},{4,3},{5,4},{6,5},{7,6},{8,7},{9,8},{10,9},{11,1... | collective-permute-start | bytes 52232 | tf_op jit(solution)/shard_map/ppermute | solution.py:24
  (90 other events, 2440.0 us)
where the time goes:
time: 785 us; the launch traced here: 780 us
  starting transfers between devices  366 us (47%)
  waiting for transfers between devices  202 us (26%)
  blocking collectives  134 us (17%)
  other arithmetic  37.9 us (5%)
  local copies, waits for them, and re-layouts  36.8 us (5%)
    ppermute x62, starting transfers between devices, padded(): before = lax.ppermute(last, axis, up)  266 us
    ppermute x62, waiting for transfers between devices, padded(): after = lax.ppermute(leading, axis, down)  202 us
    ppermute x62, starting transfers between devices, padded(): after = lax.ppermute(leading, axis, down)  100 us
    all_gather x1, blocking collectives, body(): lax.all_gather(coarse_density, 'xy', axis=1, tiled=True)  49 us
    all_gather x1, blocking collectives, body(): lax.all_gather(source, 'xy', axis=1, tiled=True)  46.7 us
    reshape x3, local copies, waits for them, and re-layouts, coarsen(): values.reshape(extent_z // 2, 2, extent_y // 2, 2, extent_x // 2, 2)  20.5 us
    all_gather x1, blocking collectives, body(): lax.all_gather(part_density, 'gz', axis=0, tiled=True)  19.3 us
    all_gather x1, blocking collectives, body(): lax.all_gather(part_source, 'gz', axis=0, tiled=True)  18.8 us
  transfers between devices with their start and end apart: 124, of which 46 were waited for; matrix products, arithmetic and copies ran while one was open for 4% of the time, Pallas kernels for 0%

commit v1 on v0

v1 whole, which is shorter than its diff:
```python
from functools import partial

import jax
import jax.numpy as jnp
from jax import lax
from jax.experimental import pallas as pl
from jax.experimental.pallas import tpu as pltpu
from jax.sharding import PartitionSpec as P

gas_density = 0.001
least = 1e-4
F32 = jnp.float32


def dot(a, b):
    return lax.dot_general(
        a, b, (((1,), (0,)), ((), ())), precision=lax.Precision.HIGHEST, preferred_element_type=F32
    )


def halving(offset, weight, width=128):
    row = lax.broadcasted_iota(jnp.int32, (128, 128), 0)
    column = lax.broadcasted_iota(jnp.int32, (128, 128), 1)
    return jnp.where((row // 2 + offset == column) & (row < width), weight, 0.0).astype(F32)


def doubling(width):
    row = lax.broadcasted_iota(jnp.int32, (128, 128), 0)
    column = lax.broadcasted_iota(jnp.int32, (128, 128), 1)
    return jnp.where((column // 2 == row) & (row < width), 1.0, 0.0).astype(F32)


def iota(shape, axis):
    return lax.broadcasted_iota(jnp.int32, shape, axis)


def low(a, axis):
    return pltpu.roll(a, 1, axis)


def high(a, axis):
    return pltpu.roll(a, a.shape[axis] - 1, axis)


class Level:
    def __init__(self, rows, shift, depth, full, by, bz, bx, inv, diag, source, value):
        self.rows, self.shift, self.depth, self.full = rows, shift, depth, full
        self.by, self.bz, self.bx, self.inv, self.diag = by, bz, bx, inv, diag
        self.source, self.value = source, value

    def coefficients(self, density, lo, hi, block):
        n = (hi - lo) // block
        assert n * block == hi - lo

        def step(i, _):
            y = lo + i * block
            d = density[pl.ds(y, block)]
            lower_y = 2.0 / jnp.maximum(d + density[pl.ds(y - 1, block)], least)
            upper_y = 2.0 / jnp.maximum(d + density[pl.ds(y + 1, block)], least)
            lower_z = 2.0 / jnp.maximum(d + low(d, 1), least)
            upper_z = high(lower_z, 1)
            side = low(d, 2)
            if self.full:
                lane = iota(d.shape, 2)
                side = jnp.where(lane == 0, 0.0, side)
            lower_x = 2.0 / jnp.maximum(d + side, least)
            upper_x = high(lower_x, 2)
            if self.full:
                upper_x = jnp.where(lane == 127, 2.0 / jnp.maximum(d, least), upper_x)
            total = lower_z + upper_z + lower_y + upper_y + lower_x + upper_x
            if self.full:
                lower_x = jnp.where(lane == 0, 0.0, lower_x)
            self.by[pl.ds(y, block)] = lower_y
            self.by[pl.ds(y + 1, block)] = upper_y
            self.bz[pl.ds(y, block)] = lower_z
            self.bx[pl.ds(y, block)] = lower_x
            self.inv[pl.ds(y, block)] = jnp.where(d > 0.0, 1.0 / total, 0.0)
            if self.diag is not None:
                self.diag[pl.ds(y, block)] = total
            return 0

        lax.fori_loop(0, n, step, 0)

    def gathered(self, y, block):
        v = self.value[pl.ds(y, block)]
        bz, bx = self.bz[pl.ds(y, block)], self.bx[pl.ds(y, block)]
        total = self.by[pl.ds(y, block)] * self.value[pl.ds(y - 1, block)]
        total += self.by[pl.ds(y + 1, block)] * self.value[pl.ds(y + 1, block)]
        total += bz * low(v, 1) + high(bz * v, 1)
        total += bx * low(v, 2) + high(bx * v, 2)
        return v, total

    def parity(self, block):
        shape = (block, self.depth, 128)
        return (iota(shape, 0) + iota(shape, 1) + iota(shape, 2) + self.shift) & 1

    def first(self, factor, lo, hi, block):
        parity = self.parity(block)
        n = (hi - lo) // block
        assert n * block == hi - lo

        def step(i, _):
            y = lo + i * block
            new = factor * self.source[pl.ds(y, block)] * self.inv[pl.ds(y, block)]
            self.value[pl.ds(y, block)] = jnp.where(parity == (y & 1), new, 0.0)
            return 0

        lax.fori_loop(0, n, step, 0)

    def half(self, colour, factor, lo, hi, block):
        parity = self.parity(block)
        n = (hi - lo) // block
        assert n * block == hi - lo

        def step(i, _):
            y = lo + i * block
            v, total = self.gathered(y, block)
            new = (factor * self.source[pl.ds(y, block)] + total) * self.inv[pl.ds(y, block)]
            self.value[pl.ds(y, block)] = jnp.where(parity == ((y + colour) & 1), new, v)
            return 0

        lax.fori_loop(0, n, step, 0)

    def residual(self, factor, y, block):
        v, total = self.gathered(y, block)
        return self.source[pl.ds(y, block)] - (self.diag[pl.ds(y, block)] * v - total) * (1.0 / factor)


def finest_down(s_ref, d_ref, before_ref, after_ref, message_ref, low_ref, high_ref,
                by, bz, bx, inv, diag, source, value, density, plane):
    zeros = jnp.zeros((5, 8, 128), F32)
    for ref in (source, density):
        for rows in (pl.ds(0, 5), pl.ds(13, 5)):
            ref[rows, 0:8] = zeros
            ref[rows, 56:64] = zeros
    source[0:5, 8:56] = before_ref[0:5]
    source[13:18, 8:56] = after_ref[0:5]
    density[0:5, 8:56] = before_ref[5:10]
    density[13:18, 8:56] = after_ref[5:10]
    source[5:13] = s_ref[...]
    density[5:13] = d_ref[...]
    value[0] = jnp.zeros((64, 128), F32)
    value[17] = jnp.zeros((64, 128), F32)
    level = Level(18, 5, 64, True, by, bz, bx, inv, diag, source, value)
    level.coefficients(density, 1, 17, 1)
    level.first(1.0, 1, 17, 1)
    level.half(1, 1.0, 2, 16, 1)
    level.half(0, 1.0, 3, 15, 1)
    level.half(1, 1.0, 4, 14, 1)
    to_low, to_high = halving(0, 0.125), halving(64, 0.125)
    for row in range(6):
        y = 3 + 2 * row
        plane[...] = density[y, 16:48] + density[y + 1, 16:48]
        pooled = plane[pl.ds(0, 16, stride=2)] + plane[pl.ds(1, 16, stride=2)]
        out = dot(pooled, to_high)
        if 0 < row < 5:
            left = level.residual(1.0, y, 2)
            plane[...] = left[0, 16:48] + left[1, 16:48]
            pooled = plane[pl.ds(0, 16, stride=2)] + plane[pl.ds(1, 16, stride=2)]
            out = out + dot(pooled, to_low)
        message_ref[row] = out
    low_ref[...] = value[5:10, 8:56]
    high_ref[...] = value[8:13, 8:56]


def middle_down(window_ref, far_before_ref, far_after_ref, coarse_ref, halo_ref,
                by, bz, bx, inv, source, value,
                diag, density, plane, by2, bz2, bx2, inv2, diag2, source2, value2, density2):
    lane = iota((1, 48, 128), 2)

    zeros = jnp.zeros((8, 128), F32)
    for i in range(9):
        for row, ref in ((i, far_before_ref), (21 + i, far_after_ref)):
            block = ref[i]
            source[row, 8:40] = block
            density[row, 8:40] = jnp.where(lane[0, :32] < 64, pltpu.roll(block, 64, 1), 0.0)
            for rows in (pl.ds(0, 8), pl.ds(40, 8)):
                source[row, rows] = zeros
                density[row, rows] = zeros
    for i in range(12):
        block = window_ref[i]
        source[9 + i] = block
        density[9 + i] = jnp.where(lane[0] < 64, pltpu.roll(block, 64, 1), 0.0)
    value[0] = jnp.zeros((48, 128), F32)
    value[29] = jnp.zeros((48, 128), F32)
    level = Level(30, 13, 48, False, by, bz, bx, inv, diag, source, value)
    level.coefficients(density, 1, 29, 1)
    level.first(4.0, 1, 29, 1)
    level.half(1, 4.0, 2, 28, 1)
    level.half(0, 4.0, 3, 27, 1)
    level.half(1, 4.0, 4, 26, 1)

    pool = halving(0, 0.125, 64)
    for row in range(12):
        y = 3 + 2 * row
        plane[...] = density[y] + density[y + 1]
        density2[row] = dot(plane[pl.ds(0, 24, stride=2)] + plane[pl.ds(1, 24, stride=2)], pool)
        if 0 < row < 11:
            left = level.residual(4.0, y, 2)
            plane[...] = left[0] + left[1]
            source2[row] = dot(plane[pl.ds(0, 24, stride=2)] + plane[pl.ds(1, 24, stride=2)], pool)
    value2[0] = jnp.zeros((24, 128), F32)
    value2[11] = jnp.zeros((24, 128), F32)
    below = Level(12, 5, 24, False, by2, bz2, bx2, inv2, diag2, source2, value2)
    below.coefficients(density2, 1, 11, 2)
    below.first(16.0, 1, 11, 2)
    below.half(1, 16.0, 2, 10, 2)
    below.half(0, 16.0, 3, 9, 2)
    below.half(1, 16.0, 4, 8, 2)
    left = below.residual(16.0, 5, 2)
    pool = halving(0, 0.125, 32)
    plane[0:24] = left[0] + left[1]
    upper = plane[pl.ds(8, 4, stride=2)] + plane[pl.ds(9, 4, stride=2)]
    plane[0:24] = density2[5] + density2[6]
    lower = plane[pl.ds(8, 4, stride=2)] + plane[pl.ds(9, 4, stride=2)]
    pooled = dot(jnp.concatenate([upper, lower], axis=0), pool)
    total = pooled[0:1]
    for i in range(1, 8):
        total = total + pltpu.roll(pooled[i : i + 1], 16 * i, 1)
    coarse_ref[...] = total
    for i in range(2):
        halo_ref[i] = (
            source2[5 + i, 8:16]
            + pltpu.roll(value2[5 + i, 8:16], 32, 1)
            + pltpu.roll(density2[5 + i, 8:16], 64, 1)
        )


def coarsest(planes, gathered_ref, density, source, by, bz, bx, inv, value):
    devices = gathered_ref.shape[0] // (planes // 4)
    shape = (8, 8, 128)
    row, lane = iota((8, 128), 0), iota((8, 128), 1)
    edge = jnp.zeros((8, 128), F32)
    for ref in (density, value):
        ref[0] = edge
        ref[planes + 1] = edge

    def spread(g, _):
        blocks = [gathered_ref[pl.ds(pl.multiple_of(g * devices + 8 * h, 8), 8)] for h in range(devices // 8)]
        for part, ref in enumerate((source, density)):
            for z in range(4):
                out = jnp.zeros((8, 128), F32)
                for h, block in enumerate(blocks):
                    moved = pltpu.roll(block, (16 * (h - z) - 64 * part) % 128, 1)
                    out = jnp.where(lane // 16 == h, moved, out)
                ref[1 + 4 * g + z] = out
        return 0

    lax.fori_loop(0, planes // 4, spread, 0)
    row, lane = iota(shape, 1), iota(shape, 2)
    first_y = (row == 0) & (lane < 16)
    last_y = (row == 7) & (lane >= 112)
    first_x = lane % 16 == 0
    last_x = lane % 16 == 15

    def low_y(a):
        turned = low(a, 1)
        return jnp.where(row == 0, pltpu.roll(turned, 16, 2), turned)

    def high_y(a):
        turned = high(a, 1)
        return jnp.where(row == 7, pltpu.roll(turned, 112, 2), turned)

    for start in range(1, planes + 1, 8):
        d = density[start : start + 8]
        lower_z = 2.0 / jnp.maximum(d + density[start - 1 : start + 7], least)
        upper_z = 2.0 / jnp.maximum(d + density[start + 1 : start + 9], least)
        lower_y = 2.0 / jnp.maximum(d + jnp.where(first_y, 0.0, low_y(d)), least)
        upper_y = 2.0 / jnp.maximum(d + jnp.where(last_y, 0.0, high_y(d)), least)
        lower_x = 2.0 / jnp.maximum(d + jnp.where(first_x, 0.0, low(d, 2)), least)
        upper_x = 2.0 / jnp.maximum(d + jnp.where(last_x, 0.0, high(d, 2)), least)
        total = lower_z + upper_z + lower_y + upper_y + lower_x + upper_x
        inverse = jnp.where(d > 0.0, 1.0 / total, 0.0)
        inv[start : start + 8] = inverse
        bz[start : start + 8] = lower_z
        bz[start + 1 : start + 9] = upper_z
        by[start : start + 8] = jnp.where(first_y, 0.0, lower_y)
        bx[start : start + 8] = jnp.where(first_x, 0.0, lower_x)
        source[start : start + 8] = 64.0 * source[start : start + 8]
        value[start : start + 8] = jnp.zeros(shape, F32)
    parity = (iota(shape, 0) + row + lane) & 1

    def sweep(_, carry):
        for colour in (0, 1):
            for start in range(1, planes + 1, 8):
                v = value[start : start + 8]
                cy, cx = by[start : start + 8], bx[start : start + 8]
                total = bz[start : start + 8] * value[start - 1 : start + 7]
                total += bz[start + 1 : start + 9] * value[start + 1 : start + 9]
                total += cy * low_y(v) + high_y(cy * v)
                total += cx * low(v, 2) + high(cx * v, 2)
                new = (source[start : start + 8] + total) * inv[start : start + 8]
                value[start : start + 8] = jnp.where(parity == colour, new, v)
        return carry

    lax.fori_loop(0, 12, sweep, 0)


def way_up(planes, place_ref, gathered_ref, halo_ref,
           by1, bz1, bx1, inv1, source1, below1,
           by0, bz0, bx0, inv0, diag0, source0, below0, before_ref, after_ref,
           pressure_ref, remain_ref,
           density3, source3, by3, bz3, bx3, inv3, value3,
           wide, density2, source2, by2, bz2, bx2, inv2, value2, value1, value0, plane):
    devices = gathered_ref.shape[0] // (planes // 4)
    coarsest(planes, gathered_ref, density3, source3, by3, bz3, bx3, inv3, value3)
    at_z, at_y = place_ref[0], place_ref[1]

    lane = iota((24, 128), 1)
    def halo(i):
        y = 2 * at_y + i - 8
        return jnp.where((y >= 0) & (y < 2 * devices), halo_ref[i], 0.0)

    for i in range(18):
        block = halo(i)
        source2[i] = jnp.where(lane < 32, block, 0.0)
        density2[i] = jnp.where(lane < 32, pltpu.roll(block, 64, 1), 0.0)
    level = Level(18, 8, 24, False, by2, bz2, bx2, inv2, None, source2, value2)
    level.coefficients(density2, 1, 17, 2)
    wide[0:4] = jnp.zeros((4, 8, 128), F32)
    wide[planes + 4 : planes + 8] = jnp.zeros((4, 8, 128), F32)
    wide[4 : planes + 4] = value3[1 : planes + 1]
    near = wide[pl.ds(4 * at_z, 12)]
    row, lane3 = iota((8, 128), 0), iota((8, 128), 1)
    double = doubling(16)
    for i in range(9):
        y = at_y + i - 4
        inside = (y >= 0) & (y < devices)
        y = jnp.clip(y, 0, devices - 1)
        picked = jnp.sum(jnp.where(row == y % 8, near, 0.0), axis=1)
        picked = pltpu.roll(picked, (128 - 16 * (y // 8)) % 128, 1)
        picked = jnp.where(inside & (iota((12, 128), 1) < 16), picked, 0.0)
        picked = dot(jnp.concatenate([picked, jnp.zeros((4, 128), F32)], axis=0), double)[0:12]
        plane[pl.ds(0, 12, stride=2)] = picked
        plane[pl.ds(1, 12, stride=2)] = picked
        for j in range(2):
            below = pltpu.roll(halo(2 * i + j), 96, 1)
            value2[2 * i + j] = jnp.where(lane < 32, below, 0.0) + plane[0:24]
    level.half(0, 16.0, 1, 17, 2)
    level.half(1, 16.0, 2, 16, 2)
    level.half(0, 16.0, 3, 15, 2)
    level.half(1, 16.0, 4, 14, 2)

    level = Level(30, 13, 48, False, by1, bz1, bx1, inv1, None, source1, value1)
    double = doubling(32)
    for i in range(10):
        picked = dot(value2[4 + i], double)
        plane[pl.ds(0, 24, stride=2)] = picked
        plane[pl.ds(1, 24, stride=2)] = picked
        for j in range(2):
            value1[5 + 2 * i + j] = below1[5 + 2 * i + j] + plane[0:48]
    level.half(0, 4.0, 7, 23, 2)
    level.half(1, 4.0, 8, 22, 2)
    level.half(0, 4.0, 9, 21, 2)
    level.half(1, 4.0, 10, 20, 2)

    level = Level(18, 5, 64, True, by0, bz0, bx0, inv0, diag0, source0, value0)
    double = doubling(64)
    for i in range(10):
        picked = dot(value1[10 + i, 8:40], double)
        plane[pl.ds(0, 32, stride=2)] = picked
        plane[pl.ds(1, 32, stride=2)] = picked
        for j in range(2):
            y = 2 * i + j - 1
            if 0 <= y < 5:
                value0[y] = plane[...]
                value0[y, 8:56] = value0[y, 8:56] + before_ref[y]
            elif 5 <= y < 13:
                value0[y] = below0[y] + plane[...]
            elif 13 <= y < 18:
                value0[y] = plane[...]
                value0[y, 8:56] = value0[y, 8:56] + after_ref[y - 13]
    level.half(0, 1.0, 1, 17, 1)
    level.half(1, 1.0, 2, 16, 1)
    level.half(0, 1.0, 3, 15, 1)
    level.half(1, 1.0, 4, 14, 1)
    for y in range(8):
        pressure_ref[y] = value0[5 + y, 16:48]
        remain_ref[y] = level.residual(1.0, 5 + y, 1)[0, 16:48]


def pair(array_up, array_down, axis, distance, ring=False):
    devices = lax.axis_size(axis)
    up = [(i, (i + distance) % devices) for i in range(devices if ring else devices - distance)]
    down = [(j, i) for i, j in up]
    return lax.ppermute(array_up, axis, up), lax.ppermute(array_down, axis, down)


def shape(*sizes):
    return jax.ShapeDtypeStruct(sizes, F32)


def vmem(*sizes):
    return pltpu.VMEM(sizes, F32)


def params():
    return pltpu.CompilerParams(vmem_limit_bytes=48 * 1024 * 1024)


def body(right_side, labels):
    gz, xy = lax.axis_size("gz"), lax.axis_size("xy")
    density = jnp.where(labels == 1, gas_density, 1.0).astype(F32)
    before, after = pair(
        jnp.concatenate([right_side[-8:], density[-9:]], axis=0),
        jnp.concatenate([right_side[:8], density[:9]], axis=0),
        "gz",
        1,
    )
    zeros = jnp.zeros((8, 8, 128), F32)
    wide_source = jnp.concatenate([zeros, before[:8], right_side, after[:8], zeros], axis=0)
    wide_density = jnp.concatenate([zeros[:7], before[8:], density, after[8:], zeros[:7]], axis=0)
    wide_source = jnp.swapaxes(wide_source, 0, 1)
    wide_density = jnp.swapaxes(wide_density, 0, 1)
    before, after = pair(
        jnp.concatenate([wide_source[3:, 8:56], wide_density[3:, 8:56]], axis=0),
        jnp.concatenate([wide_source[:5, 8:56], wide_density[:5, 8:56]], axis=0),
        "xy",
        1,
    )
    window0 = [shape(18, 64, 128)] * 7
    message, first_rows, last_rows, *level0 = pl.pallas_call(
        finest_down,
        out_shape=[shape(6, 16, 128), shape(5, 48, 128), shape(5, 48, 128)] + window0,
        scratch_shapes=[vmem(18, 64, 128), vmem(32, 128)],
        compiler_params=params(),
    )(wide_source, wide_density, before, after)

    before, after = pair(message, message, "gz", 1)
    window = jnp.concatenate([before, message, after], axis=1)
    before, after = pair(
        jnp.concatenate([window, last_rows], axis=0),
        jnp.concatenate([window, first_rows], axis=0),
        "xy",
        1,
    )
    value_before, value_after = before[6:], after[6:]
    before, after = before[:6], after[:6]
    near = jnp.concatenate([before[1:5], window[1:5], after[1:5]], axis=0)
    far_before, far_after = pair(
        jnp.concatenate([before[0:5], window[1:5]], axis=0)[:, 8:40],
        jnp.concatenate([window[1:5], after[1:6]], axis=0)[:, 8:40],
        "xy",
        2,
    )
    window1 = [shape(30, 48, 128)] * 6
    window2 = [vmem(12, 24, 128)] * 8
    coarse, halo, *level1 = pl.pallas_call(
        middle_down,
        out_shape=[shape(1, 128), shape(2, 8, 128)] + window1,
        scratch_shapes=[vmem(30, 48, 128), vmem(30, 48, 128), vmem(48, 128)] + window2,
        compiler_params=params(),
    )(near, far_before, far_after)

    everywhere = lax.all_to_all(
        jnp.broadcast_to(coarse[None], (gz * xy, 1, 128)), ("gz", "xy"), 0, 0, tiled=True
    ).reshape(gz * xy, 128)
    before, after = pair(halo, halo, "gz", 1)
    halo = jnp.concatenate([before, halo, after], axis=1)
    before, after = pair(halo, halo, "xy", 1, ring=True)
    halo = jnp.concatenate([before, halo, after], axis=0)
    before, after = pair(halo, halo, "xy", 3, ring=True)
    halo = jnp.concatenate([before, halo, after], axis=0)
    place = jnp.stack([lax.axis_index("gz"), lax.axis_index("xy")]).astype(jnp.int32)
    planes = 4 * gz
    pressure, remain = pl.pallas_call(
        partial(way_up, planes),
        out_shape=[shape(8, 32, 128)] * 2,
        in_specs=[pl.BlockSpec(memory_space=pltpu.SMEM)] + [pl.BlockSpec(memory_space=pltpu.VMEM)] * 17,
        scratch_shapes=[vmem(planes + 2, 8, 128)] * 7
        + [vmem(planes + 8, 8, 128)]
        + [vmem(18, 24, 128)] * 7
        + [vmem(30, 48, 128), vmem(18, 64, 128), vmem(64, 128)],
        compiler_params=params(),
    )(place, everywhere, halo, *level1, *level0, value_before, value_after)
    return jnp.swapaxes(pressure, 0, 1), jnp.swapaxes(remain, 0, 1)


def solution(mesh):
    return jax.shard_map(
        body,
        mesh=mesh,
        in_specs=(P("gz", "xy", None), P("gz", "xy", None)),
        out_specs=(P("gz", "xy", None), P("gz", "xy", None)),
        check_vma=False,
    )
```

time: 785 us -> 179 us (0.23)
  the two profiles are of different devices: /device:TPU:31 before, /device:TPU:1 now
where the time goes in v1:
time: 179 us; the launch traced here: 178 us
  starting transfers between devices  81.9 us (46%)
  Pallas kernels  40.5 us (23%)
  waiting for transfers between devices  33.9 us (19%)
  local copies, waits for them, and re-layouts  19.1 us (11%)
  other arithmetic  1.81 us (1%)
    ppermute x8, starting transfers between devices, pair(): lax.ppermute(array_up, axis, up)  39.4 us
    ppermute x8, waiting for transfers between devices, pair(): lax.ppermute(array_down, axis, down)  22.7 us
    ppermute x8, starting transfers between devices, pair(): lax.ppermute(array_down, axis, down)  22 us
    all_to_all x1, starting transfers between devices, body(): lax.all_to_all(jnp.broadcast_to(coarse[None], (gz * xy, 1, 128)), ('gz',...  20.5 us
    pallas_call x1, Pallas kernels, body(): pl.pallas_call(partial(way_up, planes), out_shape=[shape(8, 32, 128)] * 2...  20 us
    unnamed x56, local copies, waits for them, and re-layouts  15.6 us
    pallas_call x1, Pallas kernels, body(): pl.pallas_call(middle_down, out_shape=[shape(1, 128), shape(2, 8, 128)] +...  13.8 us
    all_to_all x1, waiting for transfers between devices, body(): lax.all_to_all(jnp.broadcast_to(coarse[None], (gz * xy, 1, 128)), ('gz',...  7.6 us
  transfers between devices with their start and end apart: 17, of which 12 were waited for; matrix products, arithmetic and copies ran while one was open for 1% of the time, Pallas kernels for 0%

profile of v1, /device:TPU:1, one launch (start us, length us, event | category | flops | bytes accessed | tf_op | source)
XLA Modules:
  0.0 178.3 jit_solution(8785339751735964082)
XLA Ops:
  0.6 0.9 fusion
  1.6 0.9 copy-done.15
  2.5 4.8 %collective-permute-start = (f32[17,8,128]{2,0,1:T(8,128)S(1)}, f32[17,8,128]{2,0,1:T(8,128)S(1)}, u32[]{:S(2)}, u32[]{:S(2)}) collective-permute-start(f32[17,8,128]{2,0,1:T(8,128)S(1)} %pad_maximum_fusion.7), channel_id=1, source_target_pairs={{0,64},{64,128},{128,192},{192,256},{256,320},{320,384},{384,448},... | collective-permute-start | bytes 208904 | tf_op jit(solution)/shard_map/ppermute | solution.py:386
  7.4 1.3 collective-permute-start.1
  9.0 4.4 %collective-permute-done.1 = f32[17,8,128]{2,0,1:T(8,128)S(1)} collective-permute-done((f32[17,8,128]{2,0,1:T(8,128)S(1)}, f32[17,8,128]{2,0,1:T(8,128)S(1)}, u32[]{:S(2)}, u32[]{:S(2)}) %collective-permute-start.1) | collective-permute-done | bytes 69664 | tf_op jit(solution)/shard_map/ppermute | solution.py:386
  13.4 0.8 slice-done.1
  14.5 5.8 %collective-permute-start.3 = (f32[10,48,128]{2,1,0:T(8,128)S(1)}, f32[10,48,128]{2,1,0:T(8,128)S(1)}, u32[]{:S(2)}, u32[]{:S(2)}) collective-permute-start(f32[10,48,128]{2,1,0:T(8,128)S(1)} %pad_maximum_fusion.4), channel_id=1, source_target_pairs={{1,0},{2,1},{3,2},{4,3},{5,4},{6,5},{7,6},{8,7},{9,8},{10,9},{11,1... | collective-permute-start | bytes 737288 | tf_op jit(solution)/shard_map/ppermute | solution.py:386
  20.3 1.9 %collective-permute-start.2 = (f32[10,48,128]{2,1,0:T(8,128)S(1)}, f32[10,48,128]{2,1,0:T(8,128)S(1)}, u32[]{:S(2)}, u32[]{:S(2)}) collective-permute-start(f32[10,48,128]{2,1,0:T(8,128)S(1)} %pad_maximum_fusion.3), channel_id=1, source_target_pairs={{0,1},{1,2},{2,3},{3,4},{4,5},{5,6},{6,7},{7,8},{8,9},{9,10},{10,1... | collective-permute-start | bytes 737288 | tf_op jit(solution)/shard_map/ppermute | solution.py:386
  22.2 1.0 collective-permute-done.3.after_ref
  23.2 2.1 %collective-permute-done.2.before_ref = f32[10,48,128]{2,1,0:T(8,128)S(1)} collective-permute-done((f32[10,48,128]{2,1,0:T(8,128)S(1)}, f32[10,48,128]{2,1,0:T(8,128)S(1)}, u32[]{:S(2)}, u32[]{:S(2)}) %collective-permute-start.2) | collective-permute-done | bytes 245792 | tf_op jit(solution)/shard_map/ppermute | solution.py:386
  25.3 6.8 %shard_map.41 = (f32[6,16,128]{2,1,0:T(8,128)S(1)}, f32[5,48,128]{2,1,0:T(8,128)S(1)}, f32[5,48,128]{2,1,0:T(8,128)S(1)}, f32[18,64,128]{2,1,0:T(8,128)S(1)}, f3...) custom-call(f32[8,64,128]{2,1,0:T(8,128)S(1)} %bitcast.11, ...), custom_call_target="tpu_custom_call" | custom-call | tf_op jit(solution)/shard_map/pallas_call | solution.py:422
  32.1 0.8 copy-done.9
  32.9 3.1 %collective-permute-start.4 = (f32[6,16,128]{2,1,0:T(8,128)S(1)}, f32[6,16,128]{2,1,0:T(8,128)S(1)}, u32[]{:S(2)}, u32[]{:S(2)}) collective-permute-start(f32[6,16,128]{2,1,0:T(8,128)S(1)} %get-tuple-element.22), channel_id=1, source_target_pairs={{0,64},{64,128},{128,192},{192,256},{256,320},{320,384},{384,448},... | collective-permute-start | bytes 147464 | tf_op jit(solution)/shard_map/ppermute | solution.py:386
  36.0 1.3 collective-permute-start.5
  37.3 5.3 %collective-permute-done.5 = f32[6,16,128]{2,1,0:T(8,128)S(1)} collective-permute-done((f32[6,16,128]{2,1,0:T(8,128)S(1)}, f32[6,16,128]{2,1,0:T(8,128)S(1)}, u32[]{:S(2)}, u32[]{:S(2)}) %collective-permute-start.5) | collective-permute-done | bytes 49184 | tf_op jit(solution)/shard_map/ppermute | solution.py:386
  42.8 1.9 %collective-permute-start.7 = (f32[11,48,128]{2,1,0:T(8,128)S(1)}, f32[11,48,128]{2,1,0:T(8,128)S(1)}, u32[]{:S(2)}, u32[]{:S(2)}) collective-permute-start(f32[11,48,128]{2,1,0:T(8,128)S(1)} %get-tuple-element.55), channel_id=1, source_target_pairs={{1,0},{2,1},{3,2},{4,3},{5,4},{6,5},{7,6},{8,7},{9,8},{10,9},{11,1... | collective-permute-start | bytes 811016 | tf_op jit(solution)/shard_map/ppermute | solution.py:386
  44.7 5.5 %collective-permute-start.6 = (f32[11,48,128]{2,1,0:T(8,128)S(1)}, f32[11,48,128]{2,1,0:T(8,128)S(1)}, u32[]{:S(2)}, u32[]{:S(2)}) collective-permute-start(f32[11,48,128]{2,1,0:T(8,128)S(1)} %get-tuple-element.54), channel_id=1, source_target_pairs={{0,1},{1,2},{2,3},{3,4},{4,5},{5,6},{6,7},{7,8},{8,9},{9,10},{10,1... | collective-permute-start | bytes 811016 | tf_op jit(solution)/shard_map/ppermute | solution.py:386
  50.2 2.2 %collective-permute-done.7 = f32[11,48,128]{2,1,0:T(8,128)S(1)} collective-permute-done((f32[11,48,128]{2,1,0:T(8,128)S(1)}, f32[11,48,128]{2,1,0:T(8,128)S(1)}, u32[]{:S(2)}, u32[]{:S(2)}) %collective-permute-start.7) | collective-permute-done | bytes 270368 | tf_op jit(solution)/shard_map/ppermute | solution.py:386
  52.5 1.2 collective-permute-done.6
  54.4 3.1 %collective-permute-start.8 = (f32[9,32,128]{2,1,0:T(8,128)S(1)}, f32[9,32,128]{2,1,0:T(8,128)S(1)}, u32[]{:S(2)}, u32[]{:S(2)}) collective-permute-start(f32[9,32,128]{2,1,0:T(8,128)S(1)} %get-tuple-element.61), channel_id=1, source_target_pairs={{0,2},{1,3},{2,4},{3,5},{4,6},{5,7},{6,8},{7,9},{8,10},{9,11},{10,... | collective-permute-start | bytes 442376 | tf_op jit(solution)/shard_map/ppermute | solution.py:386
  57.5 1.3 collective-permute-start.9
  58.8 0.9 slice-done
  59.7 3.6 %collective-permute-done.9.far_after_ref = f32[9,32,128]{2,1,0:T(8,128)S(1)} collective-permute-done((f32[9,32,128]{2,1,0:T(8,128)S(1)}, f32[9,32,128]{2,1,0:T(8,128)S(1)}, u32[]{:S(2)}, u32[]{:S(2)}) %collective-permute-start.9) | collective-permute-done | bytes 147488 | tf_op jit(solution)/shard_map/ppermute | solution.py:386
  63.4 13.8 %shard_map.42 = (f32[1,128]{1,0:T(1,128)S(1)}, f32[2,8,128]{2,1,0:T(8,128)S(1)}, f32[30,48,128]{2,1,0:T(8,128)S(1)}, f32[30,48,128]{2,1,0:T(8,128)S(1)}, f32[30,...) custom-call(f32[12,48,128]{2,1,0:T(8,128)S(1)} %pad_maximum_fusion.2., ...), custom_call_target="tpu_custom_call" | custom-call | tf_op jit(solution)/shard_map/pallas_call | solution.py:448
  77.2 0.9 copy-done
  78.1 0.9 copy-done.1
  79.0 0.9 copy-done.2
  79.9 0.9 copy-done.3
  80.7 0.9 copy-done.4
  81.6 4.8 %collective-permute-start.10 = (f32[2,8,128]{2,1,0:T(8,128)S(1)}, f32[2,8,128]{2,1,0:T(8,128)S(1)}, u32[]{:S(2)}, u32[]{:S(2)}) collective-permute-start(f32[2,8,128]{2,1,0:T(8,128)S(1)} %get-tuple-element.26), channel_id=1, source_target_pairs={{0,64},{64,128},{128,192},{192,256},{256,320},{320,384},{384,448},... | collective-permute-start | bytes 24584 | tf_op jit(solution)/shard_map/ppermute | solution.py:386
  86.4 1.3 collective-permute-start.11
  88.4 2.8 %collective-permute-done.11 = f32[2,8,128]{2,1,0:T(8,128)S(1)} collective-permute-done((f32[2,8,128]{2,1,0:T(8,128)S(1)}, f32[2,8,128]{2,1,0:T(8,128)S(1)}, u32[]{:S(2)}, u32[]{:S(2)}) %collective-permute-start.11) | collective-permute-done | bytes 8224 | tf_op jit(solution)/shard_map/ppermute | solution.py:386
  91.1 8.4 %collective-permute-start.12 = (f32[2,24,128]{2,1,0:T(8,128)S(1)}, f32[2,24,128]{2,1,0:T(8,128)S(1)}, u32[]{:S(2)}, u32[]{:S(2)}) collective-permute-start(f32[2,24,128]{2,1,0:T(8,128)S(1)} %constant_dynamic-update-slice_fusion.8), channel_id=1, source_target_pairs={{0,1},{1,2},{2,3},{3,4},{4,5},{5,6},{6,7},{7,8},{8,9},{9,10},{10,1... | collective-permute-start | bytes 73736 | tf_op jit(solution)/shard_map/ppermute | solution.py:386
  99.6 1.9 %collective-permute-start.13 = (f32[2,24,128]{2,1,0:T(8,128)S(1)}, f32[2,24,128]{2,1,0:T(8,128)S(1)}, u32[]{:S(2)}, u32[]{:S(2)}) collective-permute-start(f32[2,24,128]{2,1,0:T(8,128)S(1)} %constant_dynamic-update-slice_fusion.8), channel_id=1, source_target_pairs={{1,0},{2,1},{3,2},{4,3},{5,4},{6,5},{7,6},{8,7},{9,8},{10,9},{11,1... | collective-permute-start | bytes 73736 | tf_op jit(solution)/shard_map/ppermute | solution.py:386
  101.5 3.2 %collective-permute-done.13 = f32[2,24,128]{2,1,0:T(8,128)S(1)} collective-permute-done((f32[2,24,128]{2,1,0:T(8,128)S(1)}, f32[2,24,128]{2,1,0:T(8,128)S(1)}, u32[]{:S(2)}, u32[]{:S(2)}) %collective-permute-start.13) | collective-permute-done | bytes 24608 | tf_op jit(solution)/shard_map/ppermute | solution.py:386
  105.4 7.7 %collective-permute-start.14 = (f32[6,24,128]{2,1,0:T(8,128)}, f32[6,24,128]{2,1,0:T(8,128)}, u32[]{:S(2)}, u32[]{:S(2)}) collective-permute-start(f32[6,24,128]{2,1,0:T(8,128)} %pad_maximum_fusion.9), channel_id=1, source_target_pairs={{0,3},{1,4},{2,5},{3,6},{4,7},{5,8},{6,9},{7,10},{8,11},{9,12},{10... | collective-permute-start | bytes 221192 | tf_op jit(solution)/shard_map/ppermute | solution.py:386
  113.1 0.8 broadcast_in_dim.23
  114.0 20.5 %all-to-all-start = ((f32[512,1,128]{2,1,0:T(1,128)}), f32[512,1,128]{2,1,0:T(1,128)S(1)}, u32[]{:S(2)}, u32[]{:S(2)}) async-start(f32[512,1,128]{2,1,0:T(1,128)} %broadcast_in_dim.23), calls=%async_computation | async-start | bytes 524288 | tf_op jit(solution)/shard_map/all_to_all | solution.py:455
  134.4 7.2 %collective-permute-start.15 = (f32[6,24,128]{2,1,0:T(8,128)}, f32[6,24,128]{2,1,0:T(8,128)S(1)}, u32[]{:S(2)}, u32[]{:S(2)}) collective-permute-start(f32[6,24,128]{2,1,0:T(8,128)} %pad_maximum_fusion.9), channel_id=1, source_target_pairs={{3,0},{4,1},{5,2},{6,3},{7,4},{8,5},{9,6},{10,7},{11,8},{12,9},{13... | collective-permute-start | bytes 221192 | tf_op jit(solution)/shard_map/ppermute | solution.py:386
  141.7 0.9 constant_dynamic-update-slice_fusion.17
  144.2 7.6 %all-to-all-done = f32[512,1,128]{2,1,0:T(1,128)S(1)} async-done(((f32[512,1,128]{2,1,0:T(1,128)}), f32[512,1,128]{2,1,0:T(1,128)S(1)}, u32[]{:S(2)}, u32[]{:S(2)}) %all-to-all-start) | async-done | bytes 262176 | tf_op jit(solution)/shard_map/all_to_all | solution.py:455
  151.8 1.1 copy-done.6
  152.9 1.1 copy-done.8
  153.9 1.1 copy-done.10
  155.0 0.9 copy-done.11
  155.9 0.9 copy-done.13
  156.8 20.0 %shard_map.43 = (f32[8,32,128]{2,1,0:T(8,128)S(1)}, f32[8,32,128]{2,1,0:T(8,128)S(1)}) custom-call(s32[2]{0:T(128)S(1)} %pad_add_fusion.place_ref, f32[512,128]{1,0:T(8,128)S(1)} %bitcast.12, f32[18,24,128]{2,1,0:T(8,128)S(1)} %copy-done.13, f32[30,48,128]{2,1,0:T(8,128)S(1)} %get-tuple-element.27.by1, f32[30,48,128]{2,1,0:T(8,128)} %copy-done, ...), custom_call_target="tpu_custom_call" | custom-call | tf_op jit(solution)/shard_map/pallas_call | solution.py:466
  176.8 0.7 copy.14
  (74 shorter events, 5.2 us)
Async XLA Ops:
  1.6 0.9 copy-start.15
  2.5 6.5 %collective-permute-start = (f32[17,8,128]{2,0,1:T(8,128)S(1)}, f32[17,8,128]{2,0,1:T(8,128)S(1)}, u32[]{:S(2)}, u32[]{:S(2)}) collective-permute-start(f32[17,8,128]{2,0,1:T(8,128)S(1)} %pad_maximum_fusion.7), channel_id=1, source_target_pairs={{0,64},{64,128},{128,192},{192,256},{256,320},{320,384},{384,448},... | collective-permute-start | bytes 208904 | tf_op jit(solution)/shard_map/ppermute | solution.py:386
  7.4 6.0 %collective-permute-start.1 = (f32[17,8,128]{2,0,1:T(8,128)S(1)}, f32[17,8,128]{2,0,1:T(8,128)S(1)}, u32[]{:S(2)}, u32[]{:S(2)}) collective-permute-start(f32[17,8,128]{2,0,1:T(8,128)S(1)} %pad_maximum_fusion.8), channel_id=1, source_target_pairs={{64,0},{128,64},{192,128},{256,192},{320,256},{384,320},{448,384},... | collective-permute-start | bytes 208904 | tf_op jit(solution)/shard_map/ppermute | solution.py:386
  9.0 4.4 %copy-start.16 = (f32[17,8,128]{2,0,1:T(8,128)}, f32[17,8,128]{2,0,1:T(8,128)S(1)}, u32[]{:S(2)}) copy-start(f32[17,8,128]{2,0,1:T(8,128)S(1)} %collective-permute-done) | copy-start | bytes 208900
  13.4 0.8 slice-start.1
  14.5 8.7 %collective-permute-start.3 = (f32[10,48,128]{2,1,0:T(8,128)S(1)}, f32[10,48,128]{2,1,0:T(8,128)S(1)}, u32[]{:S(2)}, u32[]{:S(2)}) collective-permute-start(f32[10,48,128]{2,1,0:T(8,128)S(1)} %pad_maximum_fusion.4), channel_id=1, source_target_pairs={{1,0},{2,1},{3,2},{4,3},{5,4},{6,5},{7,6},{8,7},{9,8},{10,9},{11,1... | collective-permute-start | bytes 737288 | tf_op jit(solution)/shard_map/ppermute | solution.py:386
  20.3 5.0 %collective-permute-start.2 = (f32[10,48,128]{2,1,0:T(8,128)S(1)}, f32[10,48,128]{2,1,0:T(8,128)S(1)}, u32[]{:S(2)}, u32[]{:S(2)}) collective-permute-start(f32[10,48,128]{2,1,0:T(8,128)S(1)} %pad_maximum_fusion.3), channel_id=1, source_target_pairs={{0,1},{1,2},{2,3},{3,4},{4,5},{5,6},{6,7},{7,8},{8,9},{9,10},{10,1... | collective-permute-start | bytes 737288 | tf_op jit(solution)/shard_map/ppermute | solution.py:386
  32.1 0.8 copy-start.9
  32.9 9.8 %copy-start.5 = (f32[18,64,128]{2,1,0:T(8,128)}, f32[18,64,128]{2,1,0:T(8,128)S(1)}, u32[]{:S(2)}) copy-start(f32[18,64,128]{2,1,0:T(8,128)S(1)} %get-tuple-element.37.diag0) | copy-start | bytes 1769476
  32.9 9.8 %copy-start.7 = (f32[18,64,128]{2,1,0:T(8,128)}, f32[18,64,128]{2,1,0:T(8,128)S(1)}, u32[]{:S(2)}) copy-start(f32[18,64,128]{2,1,0:T(8,128)S(1)} %get-tuple-element.38.source0) | copy-start | bytes 1769476
  32.9 4.4 %collective-permute-start.4 = (f32[6,16,128]{2,1,0:T(8,128)S(1)}, f32[6,16,128]{2,1,0:T(8,128)S(1)}, u32[]{:S(2)}, u32[]{:S(2)}) collective-permute-start(f32[6,16,128]{2,1,0:T(8,128)S(1)} %get-tuple-element.22), channel_id=1, source_target_pairs={{0,64},{64,128},{128,192},{192,256},{256,320},{320,384},{384,448},... | collective-permute-start | bytes 147464 | tf_op jit(solution)/shard_map/ppermute | solution.py:386
  36.0 6.7 %collective-permute-start.5 = (f32[6,16,128]{2,1,0:T(8,128)S(1)}, f32[6,16,128]{2,1,0:T(8,128)S(1)}, u32[]{:S(2)}, u32[]{:S(2)}) collective-permute-start(f32[6,16,128]{2,1,0:T(8,128)S(1)} %get-tuple-element.22), channel_id=1, source_target_pairs={{64,0},{128,64},{192,128},{256,192},{320,256},{384,320},{448,384},... | collective-permute-start | bytes 147464 | tf_op jit(solution)/shard_map/ppermute | solution.py:386
  42.8 9.7 %collective-permute-start.7 = (f32[11,48,128]{2,1,0:T(8,128)S(1)}, f32[11,48,128]{2,1,0:T(8,128)S(1)}, u32[]{:S(2)}, u32[]{:S(2)}) collective-permute-start(f32[11,48,128]{2,1,0:T(8,128)S(1)} %get-tuple-element.55), channel_id=1, source_target_pairs={{1,0},{2,1},{3,2},{4,3},{5,4},{6,5},{7,6},{8,7},{9,8},{10,9},{11,1... | collective-permute-start | bytes 811016 | tf_op jit(solution)/shard_map/ppermute | solution.py:386
  44.7 8.9 %collective-permute-start.6 = (f32[11,48,128]{2,1,0:T(8,128)S(1)}, f32[11,48,128]{2,1,0:T(8,128)S(1)}, u32[]{:S(2)}, u32[]{:S(2)}) collective-permute-start(f32[11,48,128]{2,1,0:T(8,128)S(1)} %get-tuple-element.54), channel_id=1, source_target_pairs={{0,1},{1,2},{2,3},{3,4},{4,5},{5,6},{6,7},{7,8},{8,9},{9,10},{10,1... | collective-permute-start | bytes 811016 | tf_op jit(solution)/shard_map/ppermute | solution.py:386
  53.6 5.2 %copy-start.14 = (f32[11,48,128]{2,1,0:T(8,128)}, f32[11,48,128]{2,1,0:T(8,128)S(1)}, u32[]{:S(2)}) copy-start(f32[11,48,128]{2,1,0:T(8,128)S(1)} %collective-permute-done.6) | copy-start | bytes 811012
  54.4 5.4 %collective-permute-start.8 = (f32[9,32,128]{2,1,0:T(8,128)S(1)}, f32[9,32,128]{2,1,0:T(8,128)S(1)}, u32[]{:S(2)}, u32[]{:S(2)}) collective-permute-start(f32[9,32,128]{2,1,0:T(8,128)S(1)} %get-tuple-element.61), channel_id=1, source_target_pairs={{0,2},{1,3},{2,4},{3,5},{4,6},{5,7},{6,8},{7,9},{8,10},{9,11},{10,... | collective-permute-start | bytes 442376 | tf_op jit(solution)/shard_map/ppermute | solution.py:386
  57.5 5.9 %collective-permute-start.9 = (f32[9,32,128]{2,1,0:T(8,128)S(1)}, f32[9,32,128]{2,1,0:T(8,128)S(1)}, u32[]{:S(2)}, u32[]{:S(2)}) collective-permute-start(f32[9,32,128]{2,1,0:T(8,128)S(1)} %get-tuple-element.60), channel_id=1, source_target_pairs={{2,0},{3,1},{4,2},{5,3},{6,4},{7,5},{8,6},{9,7},{10,8},{11,9},{12,... | collective-permute-start | bytes 442376 | tf_op jit(solution)/shard_map/ppermute | solution.py:386
  58.8 0.9 slice-start
  77.2 1.0 copy-start
  78.1 0.9 copy-start.1
  79.0 0.9 copy-start.2
  79.9 0.9 copy-start.3
  80.7 0.9 copy-start.4
  81.6 6.1 %collective-permute-start.10 = (f32[2,8,128]{2,1,0:T(8,128)S(1)}, f32[2,8,128]{2,1,0:T(8,128)S(1)}, u32[]{:S(2)}, u32[]{:S(2)}) collective-permute-start(f32[2,8,128]{2,1,0:T(8,128)S(1)} %get-tuple-element.26), channel_id=1, source_target_pairs={{0,64},{64,128},{128,192},{192,256},{256,320},{320,384},{384,448},... | collective-permute-start | bytes 24584 | tf_op jit(solution)/shard_map/ppermute | solution.py:386
  86.4 4.7 %collective-permute-start.11 = (f32[2,8,128]{2,1,0:T(8,128)S(1)}, f32[2,8,128]{2,1,0:T(8,128)S(1)}, u32[]{:S(2)}, u32[]{:S(2)}) collective-permute-start(f32[2,8,128]{2,1,0:T(8,128)S(1)} %get-tuple-element.26), channel_id=1, source_target_pairs={{64,0},{128,64},{192,128},{256,192},{320,256},{384,320},{448,384},... | collective-permute-start | bytes 24584 | tf_op jit(solution)/shard_map/ppermute | solution.py:386
  87.7 0.6 copy-start.17
  91.1 10.4 %collective-permute-start.12 = (f32[2,24,128]{2,1,0:T(8,128)S(1)}, f32[2,24,128]{2,1,0:T(8,128)S(1)}, u32[]{:S(2)}, u32[]{:S(2)}) collective-permute-start(f32[2,24,128]{2,1,0:T(8,128)S(1)} %constant_dynamic-update-slice_fusion.8), channel_id=1, source_target_pairs={{0,1},{1,2},{2,3},{3,4},{4,5},{5,6},{6,7},{7,8},{8,9},{9,10},{10,1... | collective-permute-start | bytes 73736 | tf_op jit(solution)/shard_map/ppermute | solution.py:386
  99.6 5.1 %collective-permute-start.13 = (f32[2,24,128]{2,1,0:T(8,128)S(1)}, f32[2,24,128]{2,1,0:T(8,128)S(1)}, u32[]{:S(2)}, u32[]{:S(2)}) collective-permute-start(f32[2,24,128]{2,1,0:T(8,128)S(1)} %constant_dynamic-update-slice_fusion.8), channel_id=1, source_target_pairs={{1,0},{2,1},{3,2},{4,3},{5,4},{6,5},{7,6},{8,7},{9,8},{10,9},{11,1... | collective-permute-start | bytes 73736 | tf_op jit(solution)/shard_map/ppermute | solution.py:386
  105.4 36.3 %collective-permute-start.14 = (f32[6,24,128]{2,1,0:T(8,128)}, f32[6,24,128]{2,1,0:T(8,128)}, u32[]{:S(2)}, u32[]{:S(2)}) collective-permute-start(f32[6,24,128]{2,1,0:T(8,128)} %pad_maximum_fusion.9), channel_id=1, source_target_pairs={{0,3},{1,4},{2,5},{3,6},{4,7},{5,8},{6,9},{7,10},{8,11},{9,12},{10... | collective-permute-start | bytes 221192 | tf_op jit(solution)/shard_map/ppermute | solution.py:386
  114.0 37.8 %all-to-all-start = ((f32[512,1,128]{2,1,0:T(1,128)}), f32[512,1,128]{2,1,0:T(1,128)S(1)}, u32[]{:S(2)}, u32[]{:S(2)}) async-start(f32[512,1,128]{2,1,0:T(1,128)} %broadcast_in_dim.23), calls=%async_computation | async-start | bytes 524288 | tf_op jit(solution)/shard_map/all_to_all | solution.py:455
  134.4 9.1 %collective-permute-start.15 = (f32[6,24,128]{2,1,0:T(8,128)}, f32[6,24,128]{2,1,0:T(8,128)S(1)}, u32[]{:S(2)}, u32[]{:S(2)}) collective-permute-start(f32[6,24,128]{2,1,0:T(8,128)} %pad_maximum_fusion.9), channel_id=1, source_target_pairs={{3,0},{4,1},{5,2},{6,3},{7,4},{8,5},{9,6},{10,7},{11,8},{12,9},{13... | collective-permute-start | bytes 221192 | tf_op jit(solution)/shard_map/ppermute | solution.py:386
  142.6 0.7 copy-start.18
  143.5 0.7 copy-start.12
  151.8 1.1 copy-start.6
  152.9 1.1 copy-start.8
  153.9 1.1 copy-start.10
  155.0 0.9 copy-start.11
  155.9 0.9 copy-start.13

commit v2 on v1

--- a/solution.py
+++ b/solution.py
@@ -10,6 +10,7 @@
 gas_density = 0.001
 least = 1e-4
 F32 = jnp.float32
+GROUP = 4
 
 
 def dot(a, b):
@@ -126,8 +127,7 @@
         return self.source[pl.ds(y, block)] - (self.diag[pl.ds(y, block)] * v - total) * (1.0 / factor)
 
 
-def finest_down(s_ref, d_ref, before_ref, after_ref, message_ref, low_ref, high_ref,
-                by, bz, bx, inv, diag, source, value, density, plane):
+def finest_window(s_ref, d_ref, before_ref, after_ref, source, density):
     zeros = jnp.zeros((5, 8, 128), F32)
     for ref in (source, density):
         for rows in (pl.ds(0, 5), pl.ds(13, 5)):
@@ -139,91 +139,97 @@
     density[13:18, 8:56] = after_ref[5:10]
     source[5:13] = s_ref[...]
     density[5:13] = d_ref[...]
+
+
+def finest_down(s_ref, d_ref, before_ref, after_ref, message_ref, low_ref, high_ref, below_ref,
+                by, bz, bx, inv, diag, source, value, density, plane):
+    finest_window(s_ref, d_ref, before_ref, after_ref, source, density)
     value[0] = jnp.zeros((64, 128), F32)
     value[17] = jnp.zeros((64, 128), F32)
     level = Level(18, 5, 64, True, by, bz, bx, inv, diag, source, value)
-    level.coefficients(density, 1, 17, 1)
-    level.first(1.0, 1, 17, 1)
-    level.half(1, 1.0, 2, 16, 1)
-    level.half(0, 1.0, 3, 15, 1)
-    level.half(1, 1.0, 4, 14, 1)
+    level.coefficients(density, 1, 17, 2)
+    level.first(1.0, 1, 17, 2)
+    level.half(1, 1.0, 2, 16, 2)
+    level.half(0, 1.0, 3, 15, 2)
+    level.half(1, 1.0, 4, 14, 2)
     to_low, to_high = halving(0, 0.125), halving(64, 0.125)
-    for row in range(6):
-        y = 3 + 2 * row
-        plane[...] = density[y, 16:48] + density[y + 1, 16:48]
-        pooled = plane[pl.ds(0, 16, stride=2)] + plane[pl.ds(1, 16, stride=2)]
-        out = dot(pooled, to_high)
-        if 0 < row < 5:
-            left = level.residual(1.0, y, 2)
-            plane[...] = left[0, 16:48] + left[1, 16:48]
-            pooled = plane[pl.ds(0, 16, stride=2)] + plane[pl.ds(1, 16, stride=2)]
-            out = out + dot(pooled, to_low)
-        message_ref[row] = out
+    pooled = []
+    for row in range(4):
+        y = 5 + 2 * row
+        left = level.residual(1.0, y, 2)
+        plane[row] = left[0, 16:48] + left[1, 16:48]
+        plane[4 + row] = density[y, 16:48] + density[y + 1, 16:48]
+    for row in range(8):
+        pooled.append(plane[row, pl.ds(0, 16, stride=2)] + plane[row, pl.ds(1, 16, stride=2)])
+    out = dot(jnp.concatenate(pooled[:4], axis=0), to_low) + dot(jnp.concatenate(pooled[4:], axis=0), to_high)
+    message_ref[...] = out.reshape(4, 16, 128)
     low_ref[...] = value[5:10, 8:56]
     high_ref[...] = value[8:13, 8:56]
-
-
-def middle_down(window_ref, far_before_ref, far_after_ref, coarse_ref, halo_ref,
-                by, bz, bx, inv, source, value,
-                diag, density, plane, by2, bz2, bx2, inv2, diag2, source2, value2, density2):
-    lane = iota((1, 48, 128), 2)
-
-    zeros = jnp.zeros((8, 128), F32)
-    for i in range(9):
-        for row, ref in ((i, far_before_ref), (21 + i, far_after_ref)):
-            block = ref[i]
-            source[row, 8:40] = block
-            density[row, 8:40] = jnp.where(lane[0, :32] < 64, pltpu.roll(block, 64, 1), 0.0)
-            for rows in (pl.ds(0, 8), pl.ds(40, 8)):
-                source[row, rows] = zeros
-                density[row, rows] = zeros
-    for i in range(12):
-        block = window_ref[i]
-        source[9 + i] = block
-        density[9 + i] = jnp.where(lane[0] < 64, pltpu.roll(block, 64, 1), 0.0)
+    below_ref[...] = value[5:13]
+
+
+def middle_down(place_ref, window_ref, before_ref, after_ref, coarse_ref, halo_ref, kept_ref, below_ref,
+                by, bz, bx, inv, source, value, diag, density, plane,
+                by2, bz2, bx2, inv2, diag2, source2, value2, density2):
+    for start, rows, ref in ((0, 13, before_ref), (13, 16, window_ref), (29, 13, after_ref)):
+        block = ref[...]
+        source[start : start + rows] = block
+        density[start : start + rows] = jnp.where(iota(block.shape, 2) < 64, pltpu.roll(block, 64, 2), 0.0)
     value[0] = jnp.zeros((48, 128), F32)
-    value[29] = jnp.zeros((48, 128), F32)
-    level = Level(30, 13, 48, False, by, bz, bx, inv, diag, source, value)
-    level.coefficients(density, 1, 29, 1)
-    level.first(4.0, 1, 29, 1)
-    level.half(1, 4.0, 2, 28, 1)
-    level.half(0, 4.0, 3, 27, 1)
-    level.half(1, 4.0, 4, 26, 1)
+    value[41] = jnp.zeros((48, 128), F32)
+    level = Level(42, 13, 48, False, by, bz, bx, inv, diag, source, value)
+    level.coefficients(density, 1, 41, 2)
+    level.first(4.0, 1, 41, 2)
+    level.half(1, 4.0, 2, 40, 2)
+    level.half(0, 4.0, 3, 39, 2)
+    level.half(1, 4.0, 4, 38, 2)
+    mine = pl.ds(5 + 4 * place_ref[2], 20)
+    kept_ref[...] = source[mine]
+    below_ref[...] = value[mine]
 
     pool = halving(0, 0.125, 64)
-    for row in range(12):
+
+    def pooling(row, _):
         y = 3 + 2 * row
-        plane[...] = density[y] + density[y + 1]
-        density2[row] = dot(plane[pl.ds(0, 24, stride=2)] + plane[pl.ds(1, 24, stride=2)], pool)
-        if 0 < row < 11:
+        plane[0] = density[y] + density[y + 1]
+        density2[row] = dot(plane[0, pl.ds(0, 24, stride=2)] + plane[0, pl.ds(1, 24, stride=2)], pool)
+
+        @pl.when((row > 0) & (row < 17))
+        def _():
             left = level.residual(4.0, y, 2)
-            plane[...] = left[0] + left[1]
-            source2[row] = dot(plane[pl.ds(0, 24, stride=2)] + plane[pl.ds(1, 24, stride=2)], pool)
+            plane[1] = left[0] + left[1]
+            source2[row] = dot(plane[1, pl.ds(0, 24, stride=2)] + plane[1, pl.ds(1, 24, stride=2)], pool)
+
+        return 0
+
+    lax.fori_loop(0, 18, pooling, 0)
     value2[0] = jnp.zeros((24, 128), F32)
-    value2[11] = jnp.zeros((24, 128), F32)
-    below = Level(12, 5, 24, False, by2, bz2, bx2, inv2, diag2, source2, value2)
-    below.coefficients(density2, 1, 11, 2)
-    below.first(16.0, 1, 11, 2)
-    below.half(1, 16.0, 2, 10, 2)
-    below.half(0, 16.0, 3, 9, 2)
-    below.half(1, 16.0, 4, 8, 2)
-    left = below.residual(16.0, 5, 2)
+    value2[17] = jnp.zeros((24, 128), F32)
+    below = Level(18, 5, 24, False, by2, bz2, bx2, inv2, diag2, source2, value2)
+    below.coefficients(density2, 1, 17, 4)
+    below.first(16.0, 1, 17, 4)
+    below.half(1, 16.0, 2, 16, 7)
+    below.half(0, 16.0, 3, 15, 6)
+    below.half(1, 16.0, 4, 14, 5)
     pool = halving(0, 0.125, 32)
-    plane[0:24] = left[0] + left[1]
-    upper = plane[pl.ds(8, 4, stride=2)] + plane[pl.ds(9, 4, stride=2)]
-    plane[0:24] = density2[5] + density2[6]
-    lower = plane[pl.ds(8, 4, stride=2)] + plane[pl.ds(9, 4, stride=2)]
-    pooled = dot(jnp.concatenate([upper, lower], axis=0), pool)
-    total = pooled[0:1]
-    for i in range(1, 8):
-        total = total + pltpu.roll(pooled[i : i + 1], 16 * i, 1)
-    coarse_ref[...] = total
-    for i in range(2):
-        halo_ref[i] = (
-            source2[5 + i, 8:16]
-            + pltpu.roll(value2[5 + i, 8:16], 32, 1)
-            + pltpu.roll(density2[5 + i, 8:16], 64, 1)
-        )
+    rows = []
+    for row in range(4):
+        y = 5 + 2 * row
+        left = below.residual(16.0, y, 2)
+        plane[row, 0:24] = left[0] + left[1]
+        plane[4 + row, 0:24] = density2[y] + density2[y + 1]
+    for row in range(4):
+        for part in (row, 4 + row):
+            rows.append(plane[part, pl.ds(8, 4, stride=2)] + plane[part, pl.ds(9, 4, stride=2)])
+    pooled = dot(jnp.concatenate(rows, axis=0), pool)
+    for row in range(4):
+        total = pooled[8 * row : 8 * row + 1]
+        for i in range(1, 8):
+            total = total + pltpu.roll(pooled[8 * row + i : 8 * row + i + 1], 16 * i, 1)
+        coarse_ref[row : row + 1] = total
+    halo_ref[...] = (
+        source2[5:13, 8:16] + pltpu.roll(value2[5:13, 8:16], 32, 2) + pltpu.roll(density2[5:13, 8:16], 64, 2)
+    )
 
 
 def coarsest(planes, gathered_ref, density, source, by, bz, bx, inv, value):
@@ -296,87 +302,91 @@
     lax.fori_loop(0, 12, sweep, 0)
 
 
-def way_up(planes, place_ref, gathered_ref, halo_ref,
-           by1, bz1, bx1, inv1, source1, below1,
-           by0, bz0, bx0, inv0, diag0, source0, below0, before_ref, after_ref,
+def way_up(planes, place_ref, gathered_ref, halo_ref, kept_ref, below1,
+           s_ref, d_ref, rim_before_ref, rim_after_ref, below0, before_ref, after_ref,
            pressure_ref, remain_ref,
-           density3, source3, by3, bz3, bx3, inv3, value3,
-           wide, density2, source2, by2, bz2, bx2, inv2, value2, value1, value0, plane):
+           density3, source3, by3, bz3, bx3, inv3, value3, wide,
+           density2, source2, by2, bz2, bx2, inv2, value2,
+           density1, source1, by1, bz1, bx1, inv1, value1,
+           density0, source0, by0, bz0, bx0, inv0, diag0, value0, plane):
     devices = gathered_ref.shape[0] // (planes // 4)
+    at_z, at_y, at_group = place_ref[0], place_ref[1], place_ref[2]
     coarsest(planes, gathered_ref, density3, source3, by3, bz3, bx3, inv3, value3)
-    at_z, at_y = place_ref[0], place_ref[1]
-
-    lane = iota((24, 128), 1)
-    def halo(i):
-        y = 2 * at_y + i - 8
-        return jnp.where((y >= 0) & (y < 2 * devices), halo_ref[i], 0.0)
-
-    for i in range(18):
-        block = halo(i)
-        source2[i] = jnp.where(lane < 32, block, 0.0)
-        density2[i] = jnp.where(lane < 32, pltpu.roll(block, 64, 1), 0.0)
+
+    block = halo_ref[pl.ds(2 * at_group, 18)]
+    lane = iota(block.shape, 2)
+    source2[...] = jnp.where(lane < 32, block, 0.0)
+    density2[...] = jnp.where(lane < 32, pltpu.roll(block, 64, 2), 0.0)
+    value2[...] = jnp.where(lane < 32, pltpu.roll(block, 96, 2), 0.0)
     level = Level(18, 8, 24, False, by2, bz2, bx2, inv2, None, source2, value2)
-    level.coefficients(density2, 1, 17, 2)
+    level.coefficients(density2, 1, 17, 4)
     wide[0:4] = jnp.zeros((4, 8, 128), F32)
     wide[planes + 4 : planes + 8] = jnp.zeros((4, 8, 128), F32)
     wide[4 : planes + 4] = value3[1 : planes + 1]
     near = wide[pl.ds(4 * at_z, 12)]
-    row, lane3 = iota((8, 128), 0), iota((8, 128), 1)
-    double = doubling(16)
+    row = iota((8, 128), 0)
+    picked = []
     for i in range(9):
         y = at_y + i - 4
         inside = (y >= 0) & (y < devices)
         y = jnp.clip(y, 0, devices - 1)
-        picked = jnp.sum(jnp.where(row == y % 8, near, 0.0), axis=1)
-        picked = pltpu.roll(picked, (128 - 16 * (y // 8)) % 128, 1)
-        picked = jnp.where(inside & (iota((12, 128), 1) < 16), picked, 0.0)
-        picked = dot(jnp.concatenate([picked, jnp.zeros((4, 128), F32)], axis=0), double)[0:12]
-        plane[pl.ds(0, 12, stride=2)] = picked
-        plane[pl.ds(1, 12, stride=2)] = picked
+        rows = jnp.sum(jnp.where(row == y % 8, near, 0.0), axis=1)
+        rows = pltpu.roll(rows, (128 - 16 * (y // 8)) % 128, 1)
+        picked.append(jnp.where(inside & (iota((12, 128), 1) < 16), rows, 0.0))
+        picked.append(jnp.zeros((4, 128), F32))
+    spread = dot(jnp.concatenate(picked, axis=0), doubling(16))
+    for i in range(9):
+        plane[i, pl.ds(0, 12, stride=2)] = spread[16 * i : 16 * i + 12]
+        plane[i, pl.ds(1, 12, stride=2)] = spread[16 * i : 16 * i + 12]
+    for i in range(9):
         for j in range(2):
-            below = pltpu.roll(halo(2 * i + j), 96, 1)
-            value2[2 * i + j] = jnp.where(lane < 32, below, 0.0) + plane[0:24]
-    level.half(0, 16.0, 1, 17, 2)
-    level.half(1, 16.0, 2, 16, 2)
-    level.half(0, 16.0, 3, 15, 2)
-    level.half(1, 16.0, 4, 14, 2)
-
-    level = Level(30, 13, 48, False, by1, bz1, bx1, inv1, None, source1, value1)
-    double = doubling(32)
+            value2[2 * i + j] = value2[2 * i + j] + plane[i, 0:24]
+    level.half(0, 16.0, 1, 17, 4)
+    level.half(1, 16.0, 2, 16, 7)
+    level.half(0, 16.0, 3, 15, 6)
+    level.half(1, 16.0, 4, 14, 5)
+
+    source1[...] = kept_ref[...]
+    lane = iota((20, 48, 128), 2)
+    density1[...] = jnp.where(lane < 64, pltpu.roll(kept_ref[...], 64, 2), 0.0)
+    level = Level(20, 8, 48, False, by1, bz1, bx1, inv1, None, source1, value1)
+    level.coefficients(density1, 2, 18, 2)
+    spread = dot(value2[4:14].reshape(240, 128), doubling(32))
     for i in range(10):
-        picked = dot(value2[4 + i], double)
-        plane[pl.ds(0, 24, stride=2)] = picked
-        plane[pl.ds(1, 24, stride=2)] = picked
+        plane[i, pl.ds(0, 24, stride=2)] = spread[24 * i : 24 * i + 24]
+        plane[i, pl.ds(1, 24, stride=2)] = spread[24 * i : 24 * i + 24]
+    for i in range(10):
         for j in range(2):
-            value1[5 + 2 * i + j] = below1[5 + 2 * i + j] + plane[0:48]
-    level.half(0, 4.0, 7, 23, 2)
-    level.half(1, 4.0, 8, 22, 2)
-    level.half(0, 4.0, 9, 21, 2)
-    level.half(1, 4.0, 10, 20, 2)
-
+            value1[2 * i + j] = below1[2 * i + j] + plane[i, 0:48]
+    level.half(0, 4.0, 2, 18, 2)
+    level.half(1, 4.0, 3, 17, 2)
+    level.half(0, 4.0, 4, 16, 2)
+    level.half(1, 4.0, 5, 15, 2)
+
+    finest_window(s_ref, d_ref, rim_before_ref, rim_after_ref, source0, density0)
     level = Level(18, 5, 64, True, by0, bz0, bx0, inv0, diag0, source0, value0)
-    double = doubling(64)
+    level.coefficients(density0, 1, 17, 2)
+    spread = dot(value1[5:15, 8:40].reshape(320, 128), doubling(64))
     for i in range(10):
-        picked = dot(value1[10 + i, 8:40], double)
-        plane[pl.ds(0, 32, stride=2)] = picked
-        plane[pl.ds(1, 32, stride=2)] = picked
+        plane[i, pl.ds(0, 32, stride=2)] = spread[32 * i : 32 * i + 32]
+        plane[i, pl.ds(1, 32, stride=2)] = spread[32 * i : 32 * i + 32]
+    for i in range(10):
         for j in range(2):
             y = 2 * i + j - 1
-            if 0 <= y < 5:
-                value0[y] = plane[...]
-                value0[y, 8:56] = value0[y, 8:56] + before_ref[y]
-            elif 5 <= y < 13:
-                value0[y] = below0[y] + plane[...]
-            elif 13 <= y < 18:
-                value0[y] = plane[...]
-                value0[y, 8:56] = value0[y, 8:56] + after_ref[y - 13]
-    level.half(0, 1.0, 1, 17, 1)
-    level.half(1, 1.0, 2, 16, 1)
-    level.half(0, 1.0, 3, 15, 1)
-    level.half(1, 1.0, 4, 14, 1)
-    for y in range(8):
-        pressure_ref[y] = value0[5 + y, 16:48]
-        remain_ref[y] = level.residual(1.0, 5 + y, 1)[0, 16:48]
+            if 5 <= y < 13:
+                value0[y] = below0[y - 5] + plane[i]
+            elif 0 <= y < 18:
+                value0[y] = plane[i]
+    value0[0:5, 8:56] = value0[0:5, 8:56] + before_ref[...]
+    value0[13:18, 8:56] = value0[13:18, 8:56] + after_ref[...]
+    level.half(0, 1.0, 1, 17, 2)
+    level.half(1, 1.0, 2, 16, 2)
+    level.half(0, 1.0, 3, 15, 2)
+    level.half(1, 1.0, 4, 14, 2)
+    pressure_ref[...] = jnp.swapaxes(value0[5:13, 16:48], 0, 1)
+    for i in range(0, 8, 2):
+        plane[i : i + 2] = level.residual(1.0, 5 + i, 2)
+    remain_ref[...] = jnp.swapaxes(plane[0:8, 16:48], 0, 1)
 
 
 def pair(array_up, array_down, axis, distance, ring=False):
@@ -418,62 +428,54 @@
         "xy",
         1,
     )
-    window0 = [shape(18, 64, 128)] * 7
-    message, first_rows, last_rows, *level0 = pl.pallas_call(
+    finest = (wide_source, wide_density, before, after)
+    message, first_rows, last_rows, below0 = pl.pallas_call(
         finest_down,
-        out_shape=[shape(6, 16, 128), shape(5, 48, 128), shape(5, 48, 128)] + window0,
-        scratch_shapes=[vmem(18, 64, 128), vmem(32, 128)],
+        out_shape=[shape(4, 16, 128), shape(5, 48, 128), shape(5, 48, 128), shape(8, 64, 128)],
+        scratch_shapes=[vmem(18, 64, 128)] * 8 + [vmem(8, 32, 128)],
         compiler_params=params(),
-    )(wide_source, wide_density, before, after)
-
-    before, after = pair(message, message, "gz", 1)
-    window = jnp.concatenate([before, message, after], axis=1)
-    before, after = pair(
-        jnp.concatenate([window, last_rows], axis=0),
-        jnp.concatenate([window, first_rows], axis=0),
-        "xy",
-        1,
-    )
-    value_before, value_after = before[6:], after[6:]
-    before, after = before[:6], after[:6]
-    near = jnp.concatenate([before[1:5], window[1:5], after[1:5]], axis=0)
-    far_before, far_after = pair(
-        jnp.concatenate([before[0:5], window[1:5]], axis=0)[:, 8:40],
-        jnp.concatenate([window[1:5], after[1:6]], axis=0)[:, 8:40],
-        "xy",
-        2,
-    )
-    window1 = [shape(30, 48, 128)] * 6
-    window2 = [vmem(12, 24, 128)] * 8
-    coarse, halo, *level1 = pl.pallas_call(
+    )(*finest)
+
+    groups = [[GROUP * i + j for j in range(GROUP)] for i in range(xy // GROUP)]
+    window = lax.all_to_all(
+        jnp.broadcast_to(message[None], (GROUP, 4, 16, 128)), "xy", 0, 0, axis_index_groups=groups, tiled=True
+    ).reshape(4 * GROUP, 16, 128)
+    before, after = pair(window, window, "gz", 1)
+    window = jnp.concatenate([before, window, after], axis=1)
+    before, after = pair(window[-13:], window[:13], "xy", GROUP)
+    place = jnp.stack([lax.axis_index("gz"), lax.axis_index("xy"), lax.axis_index("xy") % GROUP]).astype(jnp.int32)
+    smem, block = pl.BlockSpec(memory_space=pltpu.SMEM), pl.BlockSpec(memory_space=pltpu.VMEM)
+    coarse, halo, kept, below1 = pl.pallas_call(
         middle_down,
-        out_shape=[shape(1, 128), shape(2, 8, 128)] + window1,
-        scratch_shapes=[vmem(30, 48, 128), vmem(30, 48, 128), vmem(48, 128)] + window2,
+        out_shape=[shape(4, 128), shape(8, 8, 128), shape(20, 48, 128), shape(20, 48, 128)],
+        in_specs=[smem] + [block] * 3,
+        scratch_shapes=[vmem(42, 48, 128)] * 8 + [vmem(8, 48, 128)] + [vmem(18, 24, 128)] * 8,
         compiler_params=params(),
-    )(near, far_before, far_after)
-
+    )(place, window, before, after)
+
+    peers = [[xy * z + GROUP * i + j for z in range(gz) for i in range(xy // GROUP)] for j in range(GROUP)]
     everywhere = lax.all_to_all(
-        jnp.broadcast_to(coarse[None], (gz * xy, 1, 128)), ("gz", "xy"), 0, 0, tiled=True
+        jnp.broadcast_to(coarse[None], (gz * xy // GROUP, 4, 128)),
+        ("gz", "xy"), 0, 0, axis_index_groups=peers, tiled=True,
     ).reshape(gz * xy, 128)
     before, after = pair(halo, halo, "gz", 1)
     halo = jnp.concatenate([before, halo, after], axis=1)
-    before, after = pair(halo, halo, "xy", 1, ring=True)
+    before, after = pair(halo, halo, "xy", GROUP)
     halo = jnp.concatenate([before, halo, after], axis=0)
-    before, after = pair(halo, halo, "xy", 3, ring=True)
-    halo = jnp.concatenate([before, halo, after], axis=0)
-    place = jnp.stack([lax.axis_index("gz"), lax.axis_index("xy")]).astype(jnp.int32)
+    value_before, value_after = pair(last_rows, first_rows, "xy", 1)
     planes = 4 * gz
-    pressure, remain = pl.pallas_call(
+    return pl.pallas_call(
         partial(way_up, planes),
-        out_shape=[shape(8, 32, 128)] * 2,
-        in_specs=[pl.BlockSpec(memory_space=pltpu.SMEM)] + [pl.BlockSpec(memory_space=pltpu.VMEM)] * 17,
+        out_shape=[shape(32, 8, 128)] * 2,
+        in_specs=[smem] + [block] * 11,
         scratch_shapes=[vmem(planes + 2, 8, 128)] * 7
         + [vmem(planes + 8, 8, 128)]
         + [vmem(18, 24, 128)] * 7
-        + [vmem(30, 48, 128), vmem(18, 64, 128), vmem(64, 128)],
+        + [vmem(20, 48, 128)] * 7
+        + [vmem(18, 64, 128)] * 8
+        + [vmem(10, 64, 128)],
         compiler_params=params(),
-    )(place, everywhere, halo, *level1, *level0, value_before, value_after)
-    return jnp.swapaxes(pressure, 0, 1), jnp.swapaxes(remain, 0, 1)
+    )(place, everywhere, halo, kept, below1, *finest, below0, value_before, value_after)
 
 
 def solution(mesh):

time: 179 us -> 158 us (0.88)
  the two profiles are of different devices: /device:TPU:1 before, /device:TPU:31 now
where the time goes in v2:
time: 158 us; the launch traced here: 157 us
  starting transfers between devices  69.2 us (44%)
  Pallas kernels  40.8 us (26%)
  waiting for transfers between devices  35.8 us (23%)
  blocking collectives  5.6 us (4%)
  local copies, waits for them, and re-layouts  4.29 us (3%)
    ppermute x7, starting transfers between devices, pair(): lax.ppermute(array_up, axis, up)  38 us
    ppermute x7, waiting for transfers between devices, pair(): lax.ppermute(array_down, axis, down)  26.6 us
    all_to_all x1, starting transfers between devices, body(): lax.all_to_all(jnp.broadcast_to(coarse[None], (gz * xy // GROUP, 4, 128))...  19.3 us
    pallas_call x1, Pallas kernels, body(): pl.pallas_call(middle_down, out_shape=[shape(4, 128), shape(8, 8, 128), s...  18.7 us
    pallas_call x1, Pallas kernels, body(): pl.pallas_call(partial(way_up, planes), out_shape=[shape(32, 8, 128)] * 2...  18.2 us
    ppermute x7, starting transfers between devices, pair(): lax.ppermute(array_down, axis, down)  11.9 us
    ppermute x7, waiting for transfers between devices, pair(): lax.ppermute(array_up, axis, up)  9.19 us
    all_to_all x1, blocking collectives, body(): lax.all_to_all(jnp.broadcast_to(message[None], (GROUP, 4, 16, 128)), 'xy'...  5.6 us
  transfers between devices with their start and end apart: 15, of which 9 were waited for; matrix products, arithmetic and copies ran while one was open for 1% of the time, Pallas kernels for 0%

profile of v2, /device:TPU:31, one launch (start us, length us, event | category | flops | bytes accessed | tf_op | source)
XLA Modules:
  0.0 156.9 jit_solution(8051508609346160088)
XLA Ops:
  0.6 0.8 fusion.4
  1.5 0.1 copy-done.8
  1.6 4.0 %collective-permute-start = (f32[17,8,128]{2,0,1:T(8,128)S(1)}, f32[17,8,128]{2,0,1:T(8,128)S(1)}, u32[]{:S(2)}, u32[]{:S(2)}) collective-permute-start(f32[17,8,128]{2,0,1:T(8,128)S(1)} %pad_maximum_fusion.4), channel_id=1, source_target_pairs={{0,64},{64,128},{128,192},{192,256},{256,320},{320,384},{384,448},... | collective-permute-start | bytes 208904 | tf_op jit(solution)/shard_map/ppermute | solution.py:396
  5.7 0.0 copy-start.6
  5.7 1.4 collective-permute-start.1
  7.1 0.1 collective-permute-done
  7.3 0.0 copy-done.6
  7.3 4.5 %collective-permute-done.1 = f32[17,8,128]{2,0,1:T(8,128)S(1)} collective-permute-done((f32[17,8,128]{2,0,1:T(8,128)S(1)}, f32[17,8,128]{2,0,1:T(8,128)S(1)}, u32[]{:S(2)}, u32[]{:S(2)}) %collective-permute-start.1) | collective-permute-done | bytes 69664 | tf_op jit(solution)/shard_map/ppermute | solution.py:396
  11.8 0.0 slice-start
  11.9 0.8 slice-done
  12.7 0.2 concatenate.30
  12.9 6.0 %collective-permute-start.2 = (f32[10,48,128]{2,1,0:T(8,128)S(1)}, f32[10,48,128]{2,1,0:T(8,128)S(1)}, u32[]{:S(2)}, u32[]{:S(2)}) collective-permute-start(f32[10,48,128]{2,1,0:T(8,128)S(1)} %pad_maximum_fusion.2), channel_id=1, source_target_pairs={{0,1},{1,2},{2,3},{3,4},{4,5},{5,6},{6,7},{7,8},{8,9},{9,10},{10,1... | collective-permute-start | bytes 737288 | tf_op jit(solution)/shard_map/ppermute | solution.py:396
  19.0 1.9 %collective-permute-start.3 = (f32[10,48,128]{2,1,0:T(8,128)S(1)}, f32[10,48,128]{2,1,0:T(8,128)S(1)}, u32[]{:S(2)}, u32[]{:S(2)}) collective-permute-start(f32[10,48,128]{2,1,0:T(8,128)S(1)} %pad_maximum_fusion.3), channel_id=1, source_target_pairs={{1,0},{2,1},{3,2},{4,3},{5,4},{6,5},{7,6},{8,7},{9,8},{10,9},{11,1... | collective-permute-start | bytes 737288 | tf_op jit(solution)/shard_map/ppermute | solution.py:396
  20.9 1.2 collective-permute-done.2.before_ref.rim_before_ref
  22.1 7.7 %collective-permute-done.3.after_ref.rim_after_ref = f32[10,48,128]{2,1,0:T(8,128)S(1)} collective-permute-done((f32[10,48,128]{2,1,0:T(8,128)S(1)}, f32[10,48,128]{2,1,0:T(8,128)S(1)}, u32[]{:S(2)}, u32[]{:S(2)}) %collective-permute-start.3) | collective-permute-done | bytes 245792 | tf_op jit(solution)/shard_map/ppermute | solution.py:396
  29.8 3.9 %shard_map.41 = (f32[4,16,128]{2,1,0:T(8,128)S(1)}, f32[5,48,128]{2,1,0:T(8,128)S(1)}, f32[5,48,128]{2,1,0:T(8,128)S(1)}, f32[8,64,128]{2,1,0:T(8,128)S(1)}) custom-call(f32[8,64,128]{2,1,0:T(8,128)S(1)} %bitcast.11, f32[8,64,128]{2,1,0:T(8,128)S(1)} %bitcast.8, f32[10,48,128]{2,1,0:T(8,128)S(1)} %collective-permute-done.2.before_ref.rim_before_ref, ...), custom_call_target="tpu_custom_call" | custom-call | tf_op jit(solution)/shard_map/pallas_call | solution.py:432
  33.7 0.0 copy-start.2
  33.7 0.0 copy-start.4
  33.7 5.6 %all_to_all.10 = f32[4,4,16,128]{3,2,1,0:T(8,128)S(1)} all-to-all(f32[4,4,16,128]{3,2,1,0:T(8,128)S(1)} %broadcast_in_dim.26), channel_id=1, replica_groups={{0,1,2,3},{4,5,6,7},{8,9,10,11},{12,13,14,15},{16,17,18,19},{20,21,22,2..., dimensions={0} | all-to-all | bytes 262144 | tf_op jit(solution)/shard_map/all_to_all | solution.py:440
  39.3 1.3 collective-permute-start.5
  40.6 4.6 %collective-permute-start.4 = (f32[16,16,128]{2,1,0:T(8,128)S(1)}, f32[16,16,128]{2,1,0:T(8,128)S(1)}, u32[]{:S(2)}, u32[]{:S(2)}) collective-permute-start(f32[16,16,128]{2,1,0:T(8,128)S(1)} %bitcast.15), channel_id=1, source_target_pairs={{0,64},{64,128},{128,192},{192,256},{256,320},{320,384},{384,448},... | collective-permute-start | bytes 393224 | tf_op jit(solution)/shard_map/ppermute | solution.py:396
  45.3 1.4 collective-permute-done.5
  46.6 0.9 collective-permute-done.4
  47.6 1.9 %collective-permute-start.7 = (f32[13,48,128]{2,1,0:T(8,128)S(1)}, f32[13,48,128]{2,1,0:T(8,128)S(1)}, u32[]{:S(2)}, u32[]{:S(2)}) collective-permute-start(f32[13,48,128]{2,1,0:T(8,128)S(1)} %get-tuple-element.18), channel_id=1, source_target_pairs={{4,0},{5,1},{6,2},{7,3},{8,4},{9,5},{10,6},{11,7},{12,8},{13,9},{1... | collective-permute-start | bytes 958472 | tf_op jit(solution)/shard_map/ppermute | solution.py:396
  49.5 7.0 %collective-permute-start.6 = (f32[13,48,128]{2,1,0:T(8,128)S(1)}, f32[13,48,128]{2,1,0:T(8,128)S(1)}, u32[]{:S(2)}, u32[]{:S(2)}) collective-permute-start(f32[13,48,128]{2,1,0:T(8,128)S(1)} %get-tuple-element.19), channel_id=1, source_target_pairs={{0,4},{1,5},{2,6},{3,7},{4,8},{5,9},{6,10},{7,11},{8,12},{9,13},{1... | collective-permute-start | bytes 958472 | tf_op jit(solution)/shard_map/ppermute | solution.py:396
  56.5 0.1 pad_add_fusion.place_ref
  56.6 5.4 %collective-permute-done.7.after_ref = f32[13,48,128]{2,1,0:T(8,128)S(1)} collective-permute-done((f32[13,48,128]{2,1,0:T(8,128)S(1)}, f32[13,48,128]{2,1,0:T(8,128)S(1)}, u32[]{:S(2)}, u32[]{:S(2)}) %collective-permute-start.7) | collective-permute-done | bytes 319520 | tf_op jit(solution)/shard_map/ppermute | solution.py:396
  62.0 7.0 %collective-permute-done.6.before_ref = f32[13,48,128]{2,1,0:T(8,128)S(1)} collective-permute-done((f32[13,48,128]{2,1,0:T(8,128)S(1)}, f32[13,48,128]{2,1,0:T(8,128)S(1)}, u32[]{:S(2)}, u32[]{:S(2)}) %collective-permute-start.6) | collective-permute-done | bytes 319520 | tf_op jit(solution)/shard_map/ppermute | solution.py:396
  69.0 18.7 %shard_map.42 = (f32[4,128]{1,0:T(4,128)S(1)}, f32[8,8,128]{2,1,0:T(8,128)}, f32[20,48,128]{2,1,0:T(8,128)S(1)}, f32[20,48,128]{2,1,0:T(8,128)S(1)}) custom-call(s32[3]{0:T(128)S(1)} %pad_add_fusion.place_ref, f32[16,48,128]{2,1,0:T(8,128)S(1)} %pad_maximum_fusion.window_ref, f32[13,48,128]{2,1,0:T(8,128)S(1)} %collective-permute-done.6.before_ref, ...), custom_call_target="tpu_custom_call" | custom-call | tf_op jit(solution)/shard_map/pallas_call | solution.py:448
  87.8 5.2 %collective-permute-start.8 = (f32[8,8,128]{2,1,0:T(8,128)}, f32[8,8,128]{2,1,0:T(8,128)S(1)}, u32[]{:S(2)}, u32[]{:S(2)}) collective-permute-start(f32[8,8,128]{2,1,0:T(8,128)} %get-tuple-element.12), channel_id=1, source_target_pairs={{0,64},{64,128},{128,192},{192,256},{256,320},{320,384},{384,448},... | collective-permute-start | bytes 98312 | tf_op jit(solution)/shard_map/ppermute | solution.py:396
  93.0 1.3 collective-permute-start.9
  94.3 0.7 broadcast_in_dim.27
  95.0 19.3 %all-to-all-start.1 = ((f32[128,4,128]{2,1,0:T(4,128)}), f32[128,4,128]{2,1,0:T(4,128)S(1)}, u32[]{:S(2)}, u32[]{:S(2)}) async-start(f32[128,4,128]{2,1,0:T(4,128)} %broadcast_in_dim.27), calls=%async_computation.1 | async-start | bytes 524288 | tf_op jit(solution)/shard_map/all_to_all | solution.py:457
  114.3 0.0 copy-start.3
  114.3 0.0 collective-permute-done.8
  114.3 0.8 constant_dynamic-update-slice_fusion.4
  115.1 0.0 collective-permute-done.9
  115.1 2.2 %collective-permute-start.11 = (f32[8,24,128]{2,1,0:T(8,128)S(1)}, f32[8,24,128]{2,1,0:T(8,128)S(1)}, u32[]{:S(2)}, u32[]{:S(2)}) collective-permute-start(f32[8,24,128]{2,1,0:T(8,128)S(1)} %constant_dynamic-update-slice_fusion.3), channel_id=1, source_target_pairs={{4,0},{5,1},{6,2},{7,3},{8,4},{9,5},{10,6},{11,7},{12,8},{13,9},{1... | collective-permute-start | bytes 294920 | tf_op jit(solution)/shard_map/ppermute | solution.py:396
  117.3 6.7 %collective-permute-start.10 = (f32[8,24,128]{2,1,0:T(8,128)S(1)}, f32[8,24,128]{2,1,0:T(8,128)S(1)}, u32[]{:S(2)}, u32[]{:S(2)}) collective-permute-start(f32[8,24,128]{2,1,0:T(8,128)S(1)} %constant_dynamic-update-slice_fusion.3), channel_id=1, source_target_pairs={{0,4},{1,5},{2,6},{3,7},{4,8},{5,9},{6,10},{7,11},{8,12},{9,13},{1... | collective-permute-start | bytes 294920 | tf_op jit(solution)/shard_map/ppermute | solution.py:396
  124.0 4.4 %collective-permute-start.12 = (f32[5,48,128]{2,1,0:T(8,128)S(1)}, f32[5,48,128]{2,1,0:T(8,128)S(1)}, u32[]{:S(2)}, u32[]{:S(2)}) collective-permute-start(f32[5,48,128]{2,1,0:T(8,128)S(1)} %copy-done.5), channel_id=1, source_target_pairs={{0,1},{1,2},{2,3},{3,4},{4,5},{5,6},{6,7},{7,8},{8,9},{9,10},{10,1... | collective-permute-start | bytes 368648 | tf_op jit(solution)/shard_map/ppermute | solution.py:396
  128.5 1.9 %collective-permute-start.13 = (f32[5,48,128]{2,1,0:T(8,128)S(1)}, f32[5,48,128]{2,1,0:T(8,128)S(1)}, u32[]{:S(2)}, u32[]{:S(2)}) collective-permute-start(f32[5,48,128]{2,1,0:T(8,128)S(1)} %copy-done.3), channel_id=1, source_target_pairs={{1,0},{2,1},{3,2},{4,3},{5,4},{6,5},{7,6},{8,7},{9,8},{10,9},{11,1... | collective-permute-start | bytes 368648 | tf_op jit(solution)/shard_map/ppermute | solution.py:396
  130.4 0.0 collective-permute-done.11
  130.4 0.0 collective-permute-done.10
  130.5 0.0 collective-permute-done.12.before_ref
  130.5 7.5 %collective-permute-done.13.after_ref = f32[5,48,128]{2,1,0:T(8,128)S(1)} collective-permute-done((f32[5,48,128]{2,1,0:T(8,128)S(1)}, f32[5,48,128]{2,1,0:T(8,128)S(1)}, u32[]{:S(2)}, u32[]{:S(2)}) %collective-permute-start.13) | collective-permute-done | bytes 122912 | tf_op jit(solution)/shard_map/ppermute | solution.py:396
  138.0 0.0 all-to-all-done.1
  138.0 0.7 copy-done.1
  138.7 18.2 %shard_map.43 = (f32[32,8,128]{2,1,0:T(8,128)}, f32[32,8,128]{2,1,0:T(8,128)}) custom-call(s32[3]{0:T(128)S(1)} %copy-done.1, f32[512,128]{1,0:T(8,128)S(1)} %bitcast.13, f32[24,24,128]{2,1,0:T(8,128)S(1)} %pad_maximum_fusion.1.halo_ref, f32[20,48,128]{2,1,0:T(8,128)S(1)} %get-tuple-element.13.kept_ref, f32[20,48,128]{2,1,0:T(8,128)S(1)} %get-tuple-element.14.below1, ...), custom_call_target="tpu_custom_call" | custom-call | tf_op jit(solution)/shard_map/pallas_call | solution.py:467
  (33 shorter events, 0.3 us)
Async XLA Ops:
  0.6 0.9 copy-start.8
  1.6 5.6 %collective-permute-start = (f32[17,8,128]{2,0,1:T(8,128)S(1)}, f32[17,8,128]{2,0,1:T(8,128)S(1)}, u32[]{:S(2)}, u32[]{:S(2)}) collective-permute-start(f32[17,8,128]{2,0,1:T(8,128)S(1)} %pad_maximum_fusion.4), channel_id=1, source_target_pairs={{0,64},{64,128},{128,192},{192,256},{256,320},{320,384},{384,448},... | collective-permute-start | bytes 208904 | tf_op jit(solution)/shard_map/ppermute | solution.py:396
  5.7 1.6 %copy-start.6 = (f32[32,8,128]{2,1,0:T(8,128)S(1)}, f32[32,8,128]{2,1,0:T(8,128)}, u32[]{:S(2)}) copy-start(f32[32,8,128]{2,1,0:T(8,128)} %param.2) | copy-start | bytes 393220
  5.7 6.1 %collective-permute-start.1 = (f32[17,8,128]{2,0,1:T(8,128)S(1)}, f32[17,8,128]{2,0,1:T(8,128)S(1)}, u32[]{:S(2)}, u32[]{:S(2)}) collective-permute-start(f32[17,8,128]{2,0,1:T(8,128)S(1)} %pad_maximum_fusion.5), channel_id=1, source_target_pairs={{64,0},{128,64},{192,128},{256,192},{320,256},{384,320},{448,384},... | collective-permute-start | bytes 208904 | tf_op jit(solution)/shard_map/ppermute | solution.py:396
  7.3 4.6 %copy-start.7 = (f32[17,8,128]{2,0,1:T(8,128)}, f32[17,8,128]{2,0,1:T(8,128)S(1)}, u32[]{:S(2)}) copy-start(f32[17,8,128]{2,0,1:T(8,128)S(1)} %collective-permute-done) | copy-start | bytes 208900
  11.8 0.8 slice-start
  12.9 9.2 %collective-permute-start.2 = (f32[10,48,128]{2,1,0:T(8,128)S(1)}, f32[10,48,128]{2,1,0:T(8,128)S(1)}, u32[]{:S(2)}, u32[]{:S(2)}) collective-permute-start(f32[10,48,128]{2,1,0:T(8,128)S(1)} %pad_maximum_fusion.2), channel_id=1, source_target_pairs={{0,1},{1,2},{2,3},{3,4},{4,5},{5,6},{6,7},{7,8},{8,9},{9,10},{10,1... | collective-permute-start | bytes 737288 | tf_op jit(solution)/shard_map/ppermute | solution.py:396
  19.0 10.8 %collective-permute-start.3 = (f32[10,48,128]{2,1,0:T(8,128)S(1)}, f32[10,48,128]{2,1,0:T(8,128)S(1)}, u32[]{:S(2)}, u32[]{:S(2)}) collective-permute-start(f32[10,48,128]{2,1,0:T(8,128)S(1)} %pad_maximum_fusion.3), channel_id=1, source_target_pairs={{1,0},{2,1},{3,2},{4,3},{5,4},{6,5},{7,6},{8,7},{9,8},{10,9},{11,1... | collective-permute-start | bytes 737288 | tf_op jit(solution)/shard_map/ppermute | solution.py:396
  33.7 5.6 %copy-start.2 = (f32[5,48,128]{2,1,0:T(8,128)}, f32[5,48,128]{2,1,0:T(8,128)S(1)}, u32[]{:S(2)}) copy-start(f32[5,48,128]{2,1,0:T(8,128)S(1)} %get-tuple-element.17) | copy-start | bytes 368644
  33.7 5.6 %copy-start.4 = (f32[5,48,128]{2,1,0:T(8,128)}, f32[5,48,128]{2,1,0:T(8,128)S(1)}, u32[]{:S(2)}) copy-start(f32[5,48,128]{2,1,0:T(8,128)S(1)} %get-tuple-element.16) | copy-start | bytes 368644
  39.3 7.3 %collective-permute-start.5 = (f32[16,16,128]{2,1,0:T(8,128)S(1)}, f32[16,16,128]{2,1,0:T(8,128)S(1)}, u32[]{:S(2)}, u32[]{:S(2)}) collective-permute-start(f32[16,16,128]{2,1,0:T(8,128)S(1)} %bitcast.14), channel_id=1, source_target_pairs={{64,0},{128,64},{192,128},{256,192},{320,256},{384,320},{448,384},... | collective-permute-start | bytes 393224 | tf_op jit(solution)/shard_map/ppermute | solution.py:396
  40.6 6.9 %collective-permute-start.4 = (f32[16,16,128]{2,1,0:T(8,128)S(1)}, f32[16,16,128]{2,1,0:T(8,128)S(1)}, u32[]{:S(2)}, u32[]{:S(2)}) collective-permute-start(f32[16,16,128]{2,1,0:T(8,128)S(1)} %bitcast.15), channel_id=1, source_target_pairs={{0,64},{64,128},{128,192},{192,256},{256,320},{320,384},{384,448},... | collective-permute-start | bytes 393224 | tf_op jit(solution)/shard_map/ppermute | solution.py:396
  47.6 14.4 %collective-permute-start.7 = (f32[13,48,128]{2,1,0:T(8,128)S(1)}, f32[13,48,128]{2,1,0:T(8,128)S(1)}, u32[]{:S(2)}, u32[]{:S(2)}) collective-permute-start(f32[13,48,128]{2,1,0:T(8,128)S(1)} %get-tuple-element.18), channel_id=1, source_target_pairs={{4,0},{5,1},{6,2},{7,3},{8,4},{9,5},{10,6},{11,7},{12,8},{13,9},{1... | collective-permute-start | bytes 958472 | tf_op jit(solution)/shard_map/ppermute | solution.py:396
  49.5 19.5 %collective-permute-start.6 = (f32[13,48,128]{2,1,0:T(8,128)S(1)}, f32[13,48,128]{2,1,0:T(8,128)S(1)}, u32[]{:S(2)}, u32[]{:S(2)}) collective-permute-start(f32[13,48,128]{2,1,0:T(8,128)S(1)} %get-tuple-element.19), channel_id=1, source_target_pairs={{0,4},{1,5},{2,6},{3,7},{4,8},{5,9},{6,10},{7,11},{8,12},{9,13},{1... | collective-permute-start | bytes 958472 | tf_op jit(solution)/shard_map/ppermute | solution.py:396
  56.6 31.2 %copy-start = (s32[3]{0:T(128)}, s32[3]{0:T(128)S(1)}, u32[]{:S(2)}) copy-start(s32[3]{0:T(128)S(1)} %pad_add_fusion.place_ref) | copy-start | bytes 40
  87.8 26.5 %collective-permute-start.8 = (f32[8,8,128]{2,1,0:T(8,128)}, f32[8,8,128]{2,1,0:T(8,128)S(1)}, u32[]{:S(2)}, u32[]{:S(2)}) collective-permute-start(f32[8,8,128]{2,1,0:T(8,128)} %get-tuple-element.12), channel_id=1, source_target_pairs={{0,64},{64,128},{128,192},{192,256},{256,320},{320,384},{384,448},... | collective-permute-start | bytes 98312 | tf_op jit(solution)/shard_map/ppermute | solution.py:396
  93.0 22.1 %collective-permute-start.9 = (f32[8,8,128]{2,1,0:T(8,128)}, f32[8,8,128]{2,1,0:T(8,128)S(1)}, u32[]{:S(2)}, u32[]{:S(2)}) collective-permute-start(f32[8,8,128]{2,1,0:T(8,128)} %get-tuple-element.12), channel_id=1, source_target_pairs={{64,0},{128,64},{192,128},{256,192},{320,256},{384,320},{448,384},... | collective-permute-start | bytes 98312 | tf_op jit(solution)/shard_map/ppermute | solution.py:396
  95.0 29.0 %copy-start.5 = (f32[5,48,128]{2,1,0:T(8,128)S(1)}, f32[5,48,128]{2,1,0:T(8,128)}, u32[]{:S(2)}) copy-start(f32[5,48,128]{2,1,0:T(8,128)} %copy-done.4) | copy-start | bytes 368644
  95.0 43.0 %all-to-all-start.1 = ((f32[128,4,128]{2,1,0:T(4,128)}), f32[128,4,128]{2,1,0:T(4,128)S(1)}, u32[]{:S(2)}, u32[]{:S(2)}) async-start(f32[128,4,128]{2,1,0:T(4,128)} %broadcast_in_dim.27), calls=%async_computation.1 | async-start | bytes 524288 | tf_op jit(solution)/shard_map/all_to_all | solution.py:457
  114.3 14.2 %copy-start.3 = (f32[5,48,128]{2,1,0:T(8,128)S(1)}, f32[5,48,128]{2,1,0:T(8,128)}, u32[]{:S(2)}) copy-start(f32[5,48,128]{2,1,0:T(8,128)} %copy-done.2) | copy-start | bytes 368644
  115.1 15.3 %collective-permute-start.11 = (f32[8,24,128]{2,1,0:T(8,128)S(1)}, f32[8,24,128]{2,1,0:T(8,128)S(1)}, u32[]{:S(2)}, u32[]{:S(2)}) collective-permute-start(f32[8,24,128]{2,1,0:T(8,128)S(1)} %constant_dynamic-update-slice_fusion.3), channel_id=1, source_target_pairs={{4,0},{5,1},{6,2},{7,3},{8,4},{9,5},{10,6},{11,7},{12,8},{13,9},{1... | collective-permute-start | bytes 294920 | tf_op jit(solution)/shard_map/ppermute | solution.py:396
  117.3 13.1 %collective-permute-start.10 = (f32[8,24,128]{2,1,0:T(8,128)S(1)}, f32[8,24,128]{2,1,0:T(8,128)S(1)}, u32[]{:S(2)}, u32[]{:S(2)}) collective-permute-start(f32[8,24,128]{2,1,0:T(8,128)S(1)} %constant_dynamic-update-slice_fusion.3), channel_id=1, source_target_pairs={{0,4},{1,5},{2,6},{3,7},{4,8},{5,9},{6,10},{7,11},{8,12},{9,13},{1... | collective-permute-start | bytes 294920 | tf_op jit(solution)/shard_map/ppermute | solution.py:396
  124.0 6.4 %collective-permute-start.12 = (f32[5,48,128]{2,1,0:T(8,128)S(1)}, f32[5,48,128]{2,1,0:T(8,128)S(1)}, u32[]{:S(2)}, u32[]{:S(2)}) collective-permute-start(f32[5,48,128]{2,1,0:T(8,128)S(1)} %copy-done.5), channel_id=1, source_target_pairs={{0,1},{1,2},{2,3},{3,4},{4,5},{5,6},{6,7},{7,8},{8,9},{9,10},{10,1... | collective-permute-start | bytes 368648 | tf_op jit(solution)/shard_map/ppermute | solution.py:396
  128.5 9.5 %collective-permute-start.13 = (f32[5,48,128]{2,1,0:T(8,128)S(1)}, f32[5,48,128]{2,1,0:T(8,128)S(1)}, u32[]{:S(2)}, u32[]{:S(2)}) collective-permute-start(f32[5,48,128]{2,1,0:T(8,128)S(1)} %copy-done.3), channel_id=1, source_target_pairs={{1,0},{2,1},{3,2},{4,3},{5,4},{6,5},{7,6},{8,7},{9,8},{10,9},{11,1... | collective-permute-start | bytes 368648 | tf_op jit(solution)/shard_map/ppermute | solution.py:396
  138.0 0.7 copy-start.1

commit v3 on v0

v3 whole, which is shorter than its diff:
```python
from functools import partial

import jax
import jax.numpy as jnp
from jax import lax
from jax.experimental import pallas as pl
from jax.experimental.pallas import tpu as pltpu
from jax.sharding import PartitionSpec as P

gas_density = 0.001
least = 1e-4
F32 = jnp.float32
GROUP = 4


def dot(a, b):
    return lax.dot_general(
        a, b, (((1,), (0,)), ((), ())), precision=lax.Precision.HIGHEST, preferred_element_type=F32
    )


def iota(shape, axis):
    return lax.broadcasted_iota(jnp.int32, shape, axis)


def halving(offset, weight, width=128):
    row, column = iota((128, 128), 0), iota((128, 128), 1)
    return jnp.where((row // 2 + offset == column) & (row < width), weight, 0.0).astype(F32)


def doubling(width, first=0, period=128):
    row, column = iota((128, 128), 0), iota((128, 128), 1)
    hit = ((column % period) // 2 + first == row) & (row < first + width)
    return jnp.where(hit, 1.0, 0.0).astype(F32)


def inverse(a):
    r = pl.reciprocal(a, approx=True)
    r = r * (2.0 - a * r)
    return r * (2.0 - a * r)


def blocks(lo, count, block, step):
    assert count % block == 0
    if count == block:
        step(lo)
    else:

        def turn(i, _):
            step(lo + i * block)
            return 0

        lax.fori_loop(0, count // block, turn, 0)


LOWER, UPPER, LEFT, RIGHT, OUT, INNER, INVERSE, DIAGONAL, SOURCE = 0, 2, 4, 6, 8, 10, 11, 13, 15
KEPT = 17


class Level:
    def __init__(self, density, keep, value, width, cross=0, ends=False):
        self.density, self.keep, self.value = density, keep, value
        self.depth, self.width, self.cross, self.ends = value.shape[2], width, cross, ends
        self.row, self.lane = iota((1, 8, 128), 1), iota((1, 8, 128), 2)
        self.odd = (self.row + self.lane) % 2 == 1

    def choose(self, mask, a, b):
        if not isinstance(a, float):
            shape, a = a.shape, a.reshape(-1, 8, 128)
        if not isinstance(b, float):
            shape, b = b.shape, b.reshape(-1, 8, 128)
        return jnp.where(mask, a, b).reshape(shape)

    def low(self, a):
        turned = pltpu.roll(a, 1, 1)
        if self.cross:
            head = turned[:, :8]
            head = jnp.where(self.row == 0, pltpu.roll(head, self.cross, 2), head)
            turned = head if self.depth == 8 else jnp.concatenate([head, turned[:, 8:]], axis=1)
        return turned

    def high(self, a):
        turned = pltpu.roll(a, self.depth - 1, 1)
        if self.cross:
            tail = turned[:, -8:]
            tail = jnp.where(self.row == 7, pltpu.roll(tail, 128 - self.cross, 2), tail)
            turned = tail if self.depth == 8 else jnp.concatenate([turned[:, :-8], tail], axis=1)
        return turned

    def coefficients(self, source, factor, lo, count, block):
        first_x, last_x = self.lane % max(self.width, 1) == 0, self.lane % max(self.width, 1) == self.width - 1
        if self.ends:
            first, last = (self.row == 0) & (self.lane < self.width), (self.row == 7) & (self.lane >= 128 - self.width)

        def coupling(a, b):
            return 2.0 * inverse(jnp.maximum(a + b, least))

        def both(place, at, even, odd):
            self.keep[place, at] = self.choose(self.odd, odd, even)
            self.keep[place + 1, at] = self.choose(self.odd, even, odd)

        def step(j):
            at = pl.ds(j, block)
            shape = (block, 2, self.depth, 128)
            rows = self.density[pl.ds(2 * j, 2 * block)].reshape(shape)
            before = self.density[pl.ds(2 * j - 1, 2 * block)].reshape(shape)[:, 0]
            after = self.density[pl.ds(2 * j + 1, 2 * block)].reshape(shape)[:, 1]
            inner = coupling(rows[:, 0], rows[:, 1])
            out = (coupling(rows[:, 0], before), coupling(rows[:, 1], after))
            parts = []
            for k in range(2):
                d = rows[:, k]
                if self.width or self.ends:
                    edge = 2.0 * inverse(jnp.maximum(d, least))
                lower = coupling(d, self.low(d))
                upper = self.high(lower)
                if self.ends:
                    lower, upper = self.choose(first, edge, lower), self.choose(last, edge, upper)
                left = coupling(d, pltpu.roll(d, 1, 2))
                right = pltpu.roll(left, 127, 2)
                if self.width:
                    left, right = self.choose(first_x, edge, left), self.choose(last_x, edge, right)
                total = lower + upper + (out[0] + inner if k == 0 else inner + out[1]) + left + right
                if self.ends:
                    lower, upper = self.choose(first, 0.0, lower), self.choose(last, 0.0, upper)
                if self.width:
                    left, right = self.choose(first_x, 0.0, left), self.choose(last_x, 0.0, right)
                parts.append((lower, upper, left, right, jnp.where(d > 0.0, inverse(total), 0.0), total))
            for place, even, odd in zip((LOWER, UPPER, LEFT, RIGHT, INVERSE, DIAGONAL), *parts):
                both(place, at, even, odd)
            both(OUT, at, out[0], out[1])
            self.keep[INNER, at] = inner
            if source is not None:
                rows = factor * source[pl.ds(2 * j, 2 * block)].reshape(shape)
                both(SOURCE, at, rows[:, 0], rows[:, 1])

        blocks(lo, count, block, step)

    def gathered(self, colour, j, block):
        at, keep = pl.ds(j, block), self.keep
        other = self.value.at[1 - colour]
        w = other[at]
        mask = self.odd if colour else jnp.logical_not(self.odd)
        side = self.choose(mask, other[pl.ds(j - 1, block)], other[pl.ds(j + 1, block)])
        total = keep[INNER, at] * w + keep[OUT + colour, at] * side
        total += keep[LOWER + colour, at] * self.low(w) + keep[UPPER + colour, at] * self.high(w)
        total += keep[LEFT + colour, at] * pltpu.roll(w, 1, 2) + keep[RIGHT + colour, at] * pltpu.roll(w, 127, 2)
        return total

    def first(self, lo, count, block):
        def step(j):
            at = pl.ds(j, block)
            self.value[0, at] = self.keep[SOURCE, at] * self.keep[INVERSE, at]

        blocks(lo, count, block, step)

    def half(self, colour, lo, count, block):
        def step(j):
            at = pl.ds(j, block)
            total = self.keep[SOURCE + colour, at] + self.gathered(colour, j, block)
            self.value[colour, at] = total * self.keep[INVERSE + colour, at]

        blocks(lo, count, block, step)

    def residual(self, factor, j, block):
        at, out = pl.ds(j, block), []
        for colour in (0, 1):
            total = self.keep[DIAGONAL + colour, at] * self.value[colour, at] - self.gathered(colour, j, block)
            out.append((self.keep[SOURCE + colour, at] - total) * (1.0 / factor))
        return out

    def rows(self, red, black):
        return self.choose(self.odd, black, red), self.choose(self.odd, red, black)

    def clear_red(self, pairs):
        for j in pairs:
            self.value[0, j] = jnp.zeros((self.depth, 128), F32)

    def clear(self, pairs):
        for j in pairs:
            self.value[:, j] = jnp.zeros((2, self.depth, 128), F32)


def finest_window(s_ref, d_ref, before_ref, after_ref, source, density):
    for ref in (source, density):
        for rows in (pl.ds(0, 6), pl.ds(14, 6)):
            ref[rows] = jnp.zeros((6, 64, 128), F32)
    source[1:6, 8:56] = before_ref[0:5]
    source[14:19, 8:56] = after_ref[0:5]
    density[1:6, 8:56] = before_ref[5:10]
    density[14:19, 8:56] = after_ref[5:10]
    source[6:14] = s_ref[...]
    density[6:14] = d_ref[...]


def finest_down(s_ref, d_ref, before_ref, after_ref, message_ref, low_ref, high_ref, below_ref,
                source, density, keep, value, plane):
    finest_window(s_ref, d_ref, before_ref, after_ref, source, density)
    level = Level(density, keep, value, 128)
    level.clear((0, 9))
    value[1, 1] = jnp.zeros((64, 128), F32)
    value[1, 8] = jnp.zeros((64, 128), F32)
    level.coefficients(source, 1.0, 1, 8, 1)
    level.first(1, 8, 2)
    level.half(1, 1, 8, 2)
    level.half(0, 2, 6, 2)
    level.half(1, 2, 6, 2)

    def pooling(j):
        red, black = level.residual(1.0, 3 + j, 1)
        plane[pl.ds(j, 1)] = (red + black)[:, 16:48]
        plane[pl.ds(4 + j, 1)] = (density[pl.ds(6 + 2 * j, 1)] + density[pl.ds(7 + 2 * j, 1)])[:, 16:48]

    blocks(0, 4, 1, pooling)
    pooled = plane[:, pl.ds(0, 16, stride=2)] + plane[:, pl.ds(1, 16, stride=2)]
    out = dot(pooled[:4].reshape(64, 128), halving(0, 0.125)) + dot(pooled[4:].reshape(64, 128), halving(64, 0.125))
    message_ref[...] = out.reshape(4, 16, 128)
    low_ref[...] = value[1, 3:6, 8:56]
    high_ref[...] = value[1, 4:7, 8:56]
    below_ref[...] = value[1, 3:7]


def folded(ref, rows, source, density, start):
    block = ref[rows]
    near, far = block[:, :24], block[:, 24:]
    left = iota(near.shape, 2) < 64
    source[start] = jnp.where(left, near, pltpu.roll(far, 64, 2))
    density[start] = jnp.where(left, pltpu.roll(near, 64, 2), far)


def middle_down(place_ref, window_ref, before_ref, after_ref, coarse_ref, halo_ref, kept_ref, below_ref,
                window, source, density, keep, value, plane, source2, density2, keep2, value2):
    window[1:43, 16:32] = window_ref[...]
    for ref, near, far in ((before_ref, 0, 8), (after_ref, 32, 32)):
        window[9:35, near : near + 16] = ref[0:416].reshape(26, 16, 128)
        for start, rows in ((1, 416), (35, 480)):
            window[start : start + 8, far : far + 8] = ref[rows : rows + 64].reshape(8, 8, 128)
            clear = 0 if near == 0 else 40
            window[start : start + 8, clear : clear + 8] = jnp.zeros((8, 8, 128), F32)
    for row in (0, 43):
        window[row] = jnp.zeros((48, 128), F32)
    blocks(0, 44, 4, lambda r: folded(window, pl.ds(r, 4), source, density, pl.ds(r, 4)))
    level = Level(density, keep, value, 64, 64)
    level.clear((0, 21))
    for j in (1, 20):
        value[1, j] = jnp.zeros((24, 128), F32)
    level.coefficients(source, 4.0, 1, 20, 2)
    level.first(1, 20, 5)
    level.half(1, 1, 20, 5)
    level.half(0, 2, 18, 6)
    level.half(1, 2, 18, 6)
    kept_ref[...] = window[pl.ds(6 + 4 * place_ref[2], 20)]
    below_ref[...] = value[1, pl.ds(3 + 2 * place_ref[2], 10)]

    def pooling(j):
        red, black = level.residual(4.0, 3 + j, 4)
        plane[pl.ds(j, 4), 0:24] = red + black

    blocks(0, 16, 4, pooling)
    rows = density[4:40].reshape(18, 2, 24, 128)
    plane[16:34, 0:24] = rows[:, 0] + rows[:, 1]
    pooled = plane[:, pl.ds(0, 16, stride=2)] + plane[:, pl.ds(1, 16, stride=2)]
    pooled = dot(pooled.reshape(34 * 16, 128), halving(0, 0.125)).reshape(34, 16, 128)
    lane = iota((34, 16, 128), 2)
    near, far = jnp.where(lane < 32, pooled, 0.0), jnp.where(lane < 32, pltpu.roll(pooled, 96, 2), 0.0)
    for ref, start, parts in ((source2, 2, slice(0, 16)), (density2, 1, slice(16, 34))):
        ref[start : start + parts.stop - parts.start, 0:12] = near[parts, 0:12]
        ref[start : start + parts.stop - parts.start, 12:24] = far[parts, 0:12]
    for row in (0, 19):
        density2[row] = jnp.zeros((24, 128), F32)
    below = Level(density2, keep2, value2, 0)
    below.clear((0, 9))
    for j in (1, 8):
        value2[1, j] = jnp.zeros((24, 128), F32)
    below.coefficients(source2, 16.0, 1, 8, 2)
    below.first(1, 8, 8)
    below.half(1, 1, 8, 4)
    below.half(0, 2, 6, 6)
    below.half(1, 2, 6, 6)
    red, black = below.residual(16.0, 3, 4)
    plane[0:4, 0:24] = red + black
    rows = density2[6:14].reshape(4, 2, 24, 128)
    plane[4:8, 0:24] = rows[:, 0] + rows[:, 1]
    rows = []
    for row in range(4):
        for part in (row, 4 + row):
            rows.append(plane[part, pl.ds(8, 4, stride=2)] + plane[part, pl.ds(9, 4, stride=2)])
    pooled = dot(jnp.concatenate(rows, axis=0), halving(0, 0.125, 32))
    for row in range(4):
        total = pooled[8 * row : 8 * row + 1]
        for i in range(1, 8):
            total = total + pltpu.roll(pooled[8 * row + i : 8 * row + i + 1], 16 * i, 1)
        coarse_ref[row : row + 1] = total
    for j in range(4):
        for k in range(2):
            row = 6 + 2 * j + k
            total = source2[row, 8:16] + pltpu.roll(density2[row, 8:16], 64, 1)
            if k == 0:
                total = total + pltpu.roll(value2[1, 3 + j, 8:16], 32, 1)
            halo_ref[2 * j + k] = total


def coarsest(planes, place_ref, gathered_ref, near_ref, source, density, keep, value, wide):
    groups = gathered_ref.shape[0]
    lane = iota((8, 128), 1)
    for row in (0, 1, planes + 2, planes + 3):
        density[row] = jnp.zeros((8, 128), F32)

    def spread(g, _):
        tiles = [
            jnp.concatenate([gathered_ref[2 * h, g], gathered_ref[2 * h + 1, g]], axis=0) for h in range(groups // 2)
        ]
        for part, ref in enumerate((source, density)):
            for z in range(4):
                out = jnp.zeros((8, 128), F32)
                for h, block in enumerate(tiles):
                    moved = pltpu.roll(block, (16 * (h - z) - 64 * part) % 128, 1)
                    out = jnp.where(lane // 16 == h, moved, out)
                ref[2 + 4 * g + z] = out
        return 0

    lax.fori_loop(0, planes // 4, spread, 0)
    level = Level(density, keep, value, 16, 16, ends=True)
    pairs = planes // 2
    value[...] = jnp.zeros(value.shape, F32)
    level.coefficients(source, 64.0, 1, pairs, 4)

    def sweep(_, carry):
        level.half(0, 1, pairs, pairs)
        level.half(1, 1, pairs, pairs)
        return carry

    lax.fori_loop(0, 12, sweep, 0)
    wide[0:4] = jnp.zeros((4, 8, 128), F32)
    wide[planes + 4 : planes + 8] = jnp.zeros((4, 8, 128), F32)
    even, odd = level.rows(value[0, 1 : pairs + 1], value[1, 1 : pairs + 1])
    for j in range(pairs):
        wide[4 + 2 * j] = even[j]
        wide[5 + 2 * j] = odd[j]
    near_ref[...] = wide[pl.ds(4 * place_ref[0], 12)]


def way_up(devices, place_ref, near_ref, halo_ref, kept_ref, below1_ref,
           s_ref, d_ref, rim_before_ref, rim_after_ref, below0_ref, before_ref, after_ref,
           pressure_ref, remain_ref,
           source2, density2, keep2, value2, source1, density1, keep1, value1,
           source0, density0, keep0, value0, plane):
    at_y, at_group = place_ref[1], place_ref[2]

    block = halo_ref[pl.ds(2 * at_group, 18)]
    lane = iota(block.shape, 2)
    source2[2:20] = block
    for rows in (slice(0, 2), slice(20, 22)):
        density2[rows] = jnp.zeros((2, 24, 128), F32)
    density2[2:20] = jnp.where(lane < 32, pltpu.roll(block, 64, 2), 0.0)
    level = Level(density2, keep2, value2, 0)
    level.clear((0, 10))
    level.coefficients(source2, 16.0, 1, 9, 3)
    row = iota((8, 128), 0)
    near = near_ref[...]
    picked = []
    for i in range(9):
        y = at_y + i - 4
        inside = (y >= 0) & (y < devices)
        y = jnp.clip(y, 0, devices - 1)
        rows = jnp.sum(jnp.where(row == y % 8, near, 0.0), axis=1)
        rows = pltpu.roll(rows, (128 - 16 * (y // 8)) % 128, 1)
        picked.append(jnp.where(inside & (iota((12, 128), 1) < 16), rows, 0.0))
        picked.append(jnp.zeros((4, 128), F32))
    spread = dot(jnp.concatenate(picked, axis=0), doubling(16)).reshape(9, 16, 128)
    plane[0:9, pl.ds(0, 12, stride=2)] = spread[:, 0:12]
    plane[0:9, pl.ds(1, 12, stride=2)] = spread[:, 0:12]
    below = jnp.where(lane < 32, pltpu.roll(block, 96, 2), 0.0).reshape(9, 2, 24, 128)[:, 0]
    value2[1, 1:10] = below + plane[0:9, 0:24]
    level.half(0, 1, 9, 3)
    level.half(1, 2, 7, 7)
    level.half(0, 2, 7, 7)
    level.half(1, 3, 5, 5)
    even, odd = level.rows(value2[0, 3:8], value2[1, 3:8])

    blocks(0, 20, 4, lambda r: folded(kept_ref, pl.ds(r, 4), source1, density1, pl.ds(r, 4)))
    level = Level(density1, keep1, value1, 64, 64)
    level.coefficients(source1, 4.0, 1, 8, 2)
    rows = jnp.stack([even, odd], axis=1).reshape(240, 128)
    spread = dot(rows, doubling(32, 0, 64)).reshape(10, 24, 128)
    plane[0:10, pl.ds(0, 24, stride=2)] = spread
    plane[0:10, pl.ds(1, 24, stride=2)] = spread
    left = iota((10, 24, 128), 2) < 64
    value1[1] = below1_ref[...] + jnp.where(left, plane[0:10, 0:24], plane[0:10, 24:48])
    level.clear_red((0, 9))
    level.half(0, 1, 8, 4)
    level.half(1, 1, 8, 4)
    level.half(0, 2, 6, 6)
    level.half(1, 2, 6, 6)
    even, odd = level.rows(value1[0, 2:8], value1[1, 2:8])
    rows = jnp.stack([even, odd], axis=1).reshape(12, 24, 128)[1:11]

    finest_window(s_ref, d_ref, rim_before_ref, rim_after_ref, source0, density0)
    level = Level(density0, keep0, value0, 128)
    level.coefficients(source0, 1.0, 1, 8, 1)
    near = dot(rows[:, 8:24].reshape(160, 128), doubling(64)).reshape(10, 16, 128)
    far = dot(rows[:, 0:16].reshape(160, 128), doubling(64, 64)).reshape(10, 16, 128)
    for start, part in ((0, near), (32, far)):
        plane[0:10, pl.ds(start, 16, stride=2)] = part
        plane[0:10, pl.ds(start + 1, 16, stride=2)] = part
    value0[1] = plane[...]
    value0[1, 0:3, 8:56] = value0[1, 0:3, 8:56] + before_ref[...]
    value0[1, 3:7] = value0[1, 3:7] + below0_ref[...]
    value0[1, 7:10, 8:56] = value0[1, 7:10, 8:56] + after_ref[...]
    level.clear_red((0, 9))
    level.half(0, 1, 8, 2)
    level.half(1, 1, 8, 2)
    level.half(0, 2, 6, 2)
    level.half(1, 2, 6, 2)
    even, odd = level.rows(value0[0, 3:7, 16:48], value0[1, 3:7, 16:48])
    pressure_ref[...] = jnp.swapaxes(jnp.stack([even, odd], axis=1).reshape(8, 32, 128), 0, 1)

    def remaining(j):
        red, black = level.residual(1.0, 3 + j, 1)
        even, odd = level.rows(red, black)
        plane[pl.ds(2 * j, 1)] = even
        plane[pl.ds(2 * j + 1, 1)] = odd

    blocks(0, 4, 1, remaining)
    remain_ref[...] = jnp.swapaxes(plane[0:8, 16:48], 0, 1)


def pair(array_up, array_down, axis, distance, ring=False):
    devices = lax.axis_size(axis)
    up = [(i, (i + distance) % devices) for i in range(devices if ring else devices - distance)]
    down = [(j, i) for i, j in up]
    return lax.ppermute(array_up, axis, up), lax.ppermute(array_down, axis, down)


def shape(*sizes):
    return jax.ShapeDtypeStruct(sizes, F32)


def vmem(*sizes):
    return pltpu.VMEM(sizes, F32)


def params():
    return pltpu.CompilerParams(vmem_limit_bytes=48 * 1024 * 1024)


def body(right_side, labels):
    gz, xy = lax.axis_size("gz"), lax.axis_size("xy")
    density = jnp.where(labels == 1, gas_density, 1.0).astype(F32)
    before, after = pair(
        jnp.concatenate([right_side[-8:], density[-9:]], axis=0),
        jnp.concatenate([right_side[:8], density[:9]], axis=0),
        "gz",
        1,
    )
    zeros = jnp.zeros((8, 8, 128), F32)
    wide_source = jnp.concatenate([zeros, before[:8], right_side, after[:8], zeros], axis=0)
    wide_density = jnp.concatenate([zeros[:7], before[8:], density, after[8:], zeros[:7]], axis=0)
    wide_source = jnp.swapaxes(wide_source, 0, 1)
    wide_density = jnp.swapaxes(wide_density, 0, 1)
    before, after = pair(
        jnp.concatenate([wide_source[3:, 8:56], wide_density[3:, 8:56]], axis=0),
        jnp.concatenate([wide_source[:5, 8:56], wide_density[:5, 8:56]], axis=0),
        "xy",
        1,
    )
    finest = (wide_source, wide_density, before, after)
    message, first_rows, last_rows, below0 = pl.pallas_call(
        finest_down,
        out_shape=[shape(4, 16, 128), shape(3, 48, 128), shape(3, 48, 128), shape(4, 64, 128)],
        scratch_shapes=[vmem(20, 64, 128)] * 2 + [vmem(KEPT, 10, 64, 128), vmem(2, 10, 64, 128), vmem(8, 32, 128)],
        compiler_params=params(),
    )(*finest)

    teams = [[GROUP * i + j for j in range(GROUP)] for i in range(xy // GROUP)]
    window = lax.all_to_all(
        jnp.broadcast_to(message[None], (GROUP, 4, 16, 128)), "xy", 0, 0, axis_index_groups=teams, tiled=True
    ).reshape(4 * GROUP, 16, 128)
    before, after = pair(window[-13:], window[:13], "xy", GROUP)
    window = jnp.concatenate([before, window, after], axis=0)

    def faces(near):
        parts = (window[8:34], window[:8, near], window[34:, near])
        return jnp.concatenate([part.reshape(-1, 128) for part in parts], axis=0)

    before, after = pair(faces(slice(8, 16)), faces(slice(0, 8)), "gz", 1)
    place = jnp.stack([lax.axis_index("gz"), lax.axis_index("xy"), lax.axis_index("xy") % GROUP]).astype(jnp.int32)
    smem, block = pl.BlockSpec(memory_space=pltpu.SMEM), pl.BlockSpec(memory_space=pltpu.VMEM)
    coarse, halo, kept, below1 = pl.pallas_call(
        middle_down,
        out_shape=[shape(4, 128), shape(8, 8, 128), shape(20, 48, 128), shape(10, 24, 128)],
        in_specs=[smem] + [block] * 3,
        scratch_shapes=[vmem(44, 48, 128)]
        + [vmem(44, 24, 128)] * 2
        + [vmem(KEPT, 22, 24, 128), vmem(2, 22, 24, 128), vmem(34, 32, 128)]
        + [vmem(20, 24, 128)] * 2
        + [vmem(KEPT, 10, 24, 128), vmem(2, 10, 24, 128)],
        compiler_params=params(),
    )(place, window, before, after)

    column = lax.all_to_all(
        jnp.broadcast_to(jnp.concatenate([coarse, halo.reshape(64, 128)], axis=0)[None], (gz, 68, 128)),
        "gz", 0, 0, tiled=True,
    )
    peers = [[GROUP * i + j for i in range(xy // GROUP)] for j in range(GROUP)]
    everywhere = lax.all_to_all(
        jnp.broadcast_to(column[None, :, :4], (xy // GROUP, gz, 4, 128)), "xy", 0, 0, axis_index_groups=peers, tiled=True
    )
    halo = jnp.pad(column[:, 4:], ((1, 1), (0, 0), (0, 0)))
    halo = lax.dynamic_slice(halo, (lax.axis_index("gz"), 0, 0), (3, 64, 128)).reshape(3, 8, 8, 128)
    halo = jnp.swapaxes(halo, 0, 1).reshape(8, 24, 128)
    before, after = pair(halo, halo, "xy", GROUP)
    halo = jnp.concatenate([before, halo, after], axis=0)
    value_before, value_after = pair(last_rows, first_rows, "xy", 1)
    planes = 4 * gz
    near = pl.pallas_call(
        partial(coarsest, planes),
        out_shape=shape(12, 8, 128),
        in_specs=[smem, block],
        scratch_shapes=[vmem(planes + 4, 8, 128)] * 2
        + [vmem(KEPT, planes // 2 + 2, 8, 128), vmem(2, planes // 2 + 2, 8, 128), vmem(planes + 8, 8, 128)],
        compiler_params=params(),
        cost_estimate=pl.CostEstimate(flops=100_000_000, bytes_accessed=16_000_000, transcendentals=0),
    )(place, everywhere)
    return pl.pallas_call(
        partial(way_up, xy),
        out_shape=[shape(32, 8, 128)] * 2,
        in_specs=[smem] + [block] * 11,
        scratch_shapes=[vmem(22, 24, 128)] * 2
        + [vmem(KEPT, 11, 24, 128), vmem(2, 11, 24, 128)]
        + [vmem(20, 24, 128)] * 2
        + [vmem(KEPT, 10, 24, 128), vmem(2, 10, 24, 128)]
        + [vmem(20, 64, 128)] * 2
        + [vmem(KEPT, 10, 64, 128), vmem(2, 10, 64, 128), vmem(10, 64, 128)],
        compiler_params=params(),
    )(place, near, halo, kept, below1, *finest, below0, value_before, value_after)


def solution(mesh):
    return jax.shard_map(
        body,
        mesh=mesh,
        in_specs=(P("gz", "xy", None), P("gz", "xy", None)),
        out_specs=(P("gz", "xy", None), P("gz", "xy", None)),
        check_vma=False,
    )
```

time: 785 us -> 134 us (0.17)
  the two profiles are of different devices: /device:TPU:31 before, /device:TPU:32 now
where the time goes in v3:
time: 134 us; the launch traced here: 133 us
  starting transfers between devices  55.4 us (41%)
  blocking collectives  30.7 us (23%)
  Pallas kernels  25.6 us (19%)
  waiting for transfers between devices  17.4 us (13%)
  local copies, waits for them, and re-layouts  2.88 us (2%)
    ppermute x6, starting transfers between devices, pair(): lax.ppermute(array_down, axis, down)  26.9 us
    all_to_all x1, blocking collectives, body(): lax.all_to_all(jnp.broadcast_to(jnp.concatenate([coarse, halo.reshape(64,...  23.7 us
    ppermute x6, starting transfers between devices, pair(): lax.ppermute(array_up, axis, up)  19.6 us
    ppermute x6, waiting for transfers between devices, pair(): lax.ppermute(array_down, axis, down)  12.8 us
    pallas_call x1, Pallas kernels, body(): pl.pallas_call(partial(way_up, xy), out_shape=[shape(32, 8, 128)] * 2, in...  9.11 us
    all_to_all x1, starting transfers between devices, body(): lax.all_to_all(jnp.broadcast_to(column[None, :, :4], (xy // GROUP, gz, 4,...  8.87 us
    pallas_call x1, Pallas kernels, body(): pl.pallas_call(middle_down, out_shape=[shape(4, 128), shape(8, 8, 128), s...  7.46 us
    all_to_all x1, blocking collectives, body(): lax.all_to_all(jnp.broadcast_to(message[None], (GROUP, 4, 16, 128)), 'xy'...  7.02 us
  transfers between devices with their start and end apart: 13, of which 8 were waited for; matrix products, arithmetic and copies ran while one was open for 0% of the time, Pallas kernels for 4%

profile of v3, /device:TPU:32, one launch (start us, length us, event | category | flops | bytes accessed | tf_op | source)
XLA Modules:
  0.0 133.3 jit_solution(16742709509806192496)
XLA Ops:
  0.6 0.0 copy-start.2
  0.6 0.8 fusion.7
  1.5 0.1 copy-done.2
  1.6 4.3 %collective-permute-start = (f32[17,8,128]{2,0,1:T(8,128)S(1)}, f32[17,8,128]{2,0,1:T(8,128)S(1)}, u32[]{:S(2)}, u32[]{:S(2)}) collective-permute-start(f32[17,8,128]{2,0,1:T(8,128)S(1)} %pad_maximum_fusion.6), channel_id=1, source_target_pairs={{0,64},{64,128},{128,192},{192,256},{256,320},{320,384},{384,448},... | collective-permute-start | bytes 208904 | tf_op jit(solution)/shard_map/ppermute | solution.py:432
  5.9 0.0 copy-start
  6.0 1.4 %collective-permute-start.1 = (f32[17,8,128]{2,0,1:T(8,128)S(1)}, f32[17,8,128]{2,0,1:T(8,128)S(1)}, u32[]{:S(2)}, u32[]{:S(2)}) collective-permute-start(f32[17,8,128]{2,0,1:T(8,128)S(1)} %pad_maximum_fusion.7), channel_id=1, source_target_pairs={{64,0},{128,64},{192,128},{256,192},{320,256},{384,320},{448,384},... | collective-permute-start | bytes 208904 | tf_op jit(solution)/shard_map/ppermute | solution.py:432
  7.4 0.7 collective-permute-done
  8.1 0.0 copy-start.1
  8.1 0.0 copy-done
  8.2 4.8 %collective-permute-done.1 = f32[17,8,128]{2,0,1:T(8,128)S(1)} collective-permute-done((f32[17,8,128]{2,0,1:T(8,128)S(1)}, f32[17,8,128]{2,0,1:T(8,128)S(1)}, u32[]{:S(2)}, u32[]{:S(2)}) %collective-permute-start.1) | collective-permute-done | bytes 69664 | tf_op jit(solution)/shard_map/ppermute | solution.py:432
  13.0 0.0 copy-done.1
  13.0 0.0 slice-start
  13.0 0.8 slice-done
  13.8 0.2 concatenate.36
  14.1 1.9 %collective-permute-start.2 = (f32[10,48,128]{2,1,0:T(8,128)S(1)}, f32[10,48,128]{2,1,0:T(8,128)S(1)}, u32[]{:S(2)}, u32[]{:S(2)}) collective-permute-start(f32[10,48,128]{2,1,0:T(8,128)S(1)} %pad_maximum_fusion.4), channel_id=1, source_target_pairs={{0,1},{1,2},{2,3},{3,4},{4,5},{5,6},{6,7},{7,8},{8,9},{9,10},{10,1... | collective-permute-start | bytes 737288 | tf_op jit(solution)/shard_map/ppermute | solution.py:432
  16.0 7.0 %collective-permute-start.3 = (f32[10,48,128]{2,1,0:T(8,128)S(1)}, f32[10,48,128]{2,1,0:T(8,128)S(1)}, u32[]{:S(2)}, u32[]{:S(2)}) collective-permute-start(f32[10,48,128]{2,1,0:T(8,128)S(1)} %pad_maximum_fusion.5), channel_id=1, source_target_pairs={{1,0},{2,1},{3,2},{4,3},{5,4},{6,5},{7,6},{8,7},{9,8},{10,9},{11,1... | collective-permute-start | bytes 737288 | tf_op jit(solution)/shard_map/ppermute | solution.py:432
  23.0 1.9 %collective-permute-done.2.before_ref.rim_before_ref = f32[10,48,128]{2,1,0:T(8,128)S(1)} collective-permute-done((f32[10,48,128]{2,1,0:T(8,128)S(1)}, f32[10,48,128]{2,1,0:T(8,128)S(1)}, u32[]{:S(2)}, u32[]{:S(2)}) %collective-permute-start.2) | collective-permute-done | bytes 245792 | tf_op jit(solution)/shard_map/ppermute | solution.py:432
  24.9 1.8 %collective-permute-done.3.after_ref.rim_after_ref = f32[10,48,128]{2,1,0:T(8,128)S(1)} collective-permute-done((f32[10,48,128]{2,1,0:T(8,128)S(1)}, f32[10,48,128]{2,1,0:T(8,128)S(1)}, u32[]{:S(2)}, u32[]{:S(2)}) %collective-permute-start.3) | collective-permute-done | bytes 245792 | tf_op jit(solution)/shard_map/ppermute | solution.py:432
  26.7 3.4 %shard_map.41 = (f32[4,16,128]{2,1,0:T(8,128)S(1)}, f32[3,48,128]{2,1,0:T(8,128)S(1)}, f32[3,48,128]{2,1,0:T(8,128)S(1)}, f32[4,64,128]{2,1,0:T(8,128)S(1)}) custom-call(f32[8,64,128]{2,1,0:T(8,128)S(1)} %bitcast.27, f32[8,64,128]{2,1,0:T(8,128)S(1)} %bitcast.24, f32[10,48,128]{2,1,0:T(8,128)S(1)} %collective-permute-done.2.before_ref.rim_before_ref, ...), custom_call_target="tpu_custom_call" | custom-call | tf_op jit(solution)/shard_map/pallas_call | solution.py:468
  30.2 7.0 %all_to_all.15 = f32[4,4,16,128]{3,2,1,0:T(8,128)S(1)} all-to-all(f32[4,4,16,128]{3,2,1,0:T(8,128)S(1)} %broadcast_in_dim.32), channel_id=1, replica_groups={{0,1,2,3},{4,5,6,7},{8,9,10,11},{12,13,14,15},{16,17,18,19},{20,21,22,2..., dimensions={0} | all-to-all | bytes 262144 | tf_op jit(solution)/shard_map/all_to_all | solution.py:476
  37.2 4.1 %collective-permute-start.4 = (f32[13,16,128]{2,1,0:T(8,128)S(1)}, f32[13,16,128]{2,1,0:T(8,128)S(1)}, u32[]{:S(2)}, u32[]{:S(2)}) collective-permute-start(f32[13,16,128]{2,1,0:T(8,128)S(1)} %get-tuple-element.24), channel_id=1, source_target_pairs={{0,4},{1,5},{2,6},{3,7},{4,8},{5,9},{6,10},{7,11},{8,12},{9,13},{1... | collective-permute-start | bytes 319496 | tf_op jit(solution)/shard_map/ppermute | solution.py:432
  41.3 5.4 %collective-permute-start.5 = (f32[13,16,128]{2,1,0:T(8,128)S(1)}, f32[13,16,128]{2,1,0:T(8,128)S(1)}, u32[]{:S(2)}, u32[]{:S(2)}) collective-permute-start(f32[13,16,128]{2,1,0:T(8,128)S(1)} %get-tuple-element.25), channel_id=1, source_target_pairs={{4,0},{5,1},{6,2},{7,3},{8,4},{9,5},{10,6},{11,7},{12,8},{13,9},{1... | collective-permute-start | bytes 319496 | tf_op jit(solution)/shard_map/ppermute | solution.py:432
  46.7 0.8 collective-permute-done.4
  47.5 2.2 %collective-permute-done.5 = f32[13,16,128]{2,1,0:T(8,128)S(1)} collective-permute-done((f32[13,16,128]{2,1,0:T(8,128)S(1)}, f32[13,16,128]{2,1,0:T(8,128)S(1)}, u32[]{:S(2)}, u32[]{:S(2)}) %collective-permute-start.5) | collective-permute-done | bytes 106528 | tf_op jit(solution)/shard_map/ppermute | solution.py:432
  49.8 1.3 collective-permute-start.7
  51.1 4.9 %collective-permute-start.6 = (f32[544,128]{1,0:T(8,128)S(1)}, f32[544,128]{1,0:T(8,128)S(1)}, u32[]{:S(2)}, u32[]{:S(2)}) collective-permute-start(f32[544,128]{1,0:T(8,128)S(1)} %get-tuple-element.23), channel_id=1, source_target_pairs={{0,64},{64,128},{128,192},{192,256},{256,320},{320,384},{384,448},... | collective-permute-start | bytes 835592 | tf_op jit(solution)/shard_map/ppermute | solution.py:432
  56.1 0.1 pad_add_fusion.place_ref
  56.1 4.0 %collective-permute-done.7.after_ref = f32[544,128]{1,0:T(8,128)S(1)} collective-permute-done((f32[544,128]{1,0:T(8,128)S(1)}, f32[544,128]{1,0:T(8,128)S(1)}, u32[]{:S(2)}, u32[]{:S(2)}) %collective-permute-start.7) | collective-permute-done | bytes 278560 | tf_op jit(solution)/shard_map/ppermute | solution.py:432
  60.1 1.2 collective-permute-done.6.before_ref
  61.3 7.5 %shard_map.42 = (f32[4,128]{1,0:T(4,128)S(1)}, f32[8,8,128]{2,1,0:T(8,128)S(1)}, f32[20,48,128]{2,1,0:T(8,128)S(1)}, f32[10,24,128]{2,1,0:T(8,128)S(1)}) custom-call(s32[3]{0:T(128)S(1)} %pad_add_fusion.place_ref, f32[42,16,128]{2,1,0:T(8,128)S(1)} %pad_maximum_fusion.window_ref, f32[544,128]{1,0:T(8,128)S(1)} %collective-permute-done.6.before_ref, ...), custom_call_target="tpu_custom_call" | custom-call | tf_op jit(solution)/shard_map/pallas_call | solution.py:489
  68.8 23.7 %all_to_all.16 = f32[8,68,128]{2,1,0:T(8,128)S(1)} all-to-all(f32[8,68,128]{2,1,0:T(8,128)S(1)} %broadcast_in_dim.33), channel_id=1, replica_groups=mesh['gz'=8,'xy'=64] {'gz'}, dimensions={0} | all-to-all | bytes 557056 | tf_op jit(solution)/shard_map/all_to_all | solution.py:501
  92.5 0.7 broadcast_in_dim.34
  93.2 8.9 %all-to-all-start.2 = ((f32[16,8,4,128]{3,2,1,0:T(4,128)}), f32[16,8,4,128]{3,2,1,0:T(4,128)S(1)}, u32[]{:S(2)}, u32[]{:S(2)}) async-start(f32[16,8,4,128]{3,2,1,0:T(4,128)} %broadcast_in_dim.34), calls=%async_computation.2 | async-start | bytes 524288 | tf_op jit(solution)/shard_map/all_to_all | solution.py:506
  102.2 4.9 %collective-permute-start.9 = (f32[8,24,128]{2,1,0:T(8,128)S(1)}, f32[8,24,128]{2,1,0:T(8,128)S(1)}, u32[]{:S(2)}, u32[]{:S(2)}) collective-permute-start(f32[8,24,128]{2,1,0:T(8,128)S(1)} %copy_bitcast_fusion), channel_id=1, source_target_pairs={{4,0},{5,1},{6,2},{7,3},{8,4},{9,5},{10,6},{11,7},{12,8},{13,9},{1... | collective-permute-start | bytes 294920 | tf_op jit(solution)/shard_map/ppermute | solution.py:432
  107.0 2.5 %collective-permute-start.8 = (f32[8,24,128]{2,1,0:T(8,128)S(1)}, f32[8,24,128]{2,1,0:T(8,128)S(1)}, u32[]{:S(2)}, u32[]{:S(2)}) collective-permute-start(f32[8,24,128]{2,1,0:T(8,128)S(1)} %copy_bitcast_fusion), channel_id=1, source_target_pairs={{0,4},{1,5},{2,6},{3,7},{4,8},{5,9},{6,10},{7,11},{8,12},{9,13},{1... | collective-permute-start | bytes 294920 | tf_op jit(solution)/shard_map/ppermute | solution.py:432
  109.5 1.9 %collective-permute-start.10 = (f32[3,48,128]{2,1,0:T(8,128)S(1)}, f32[3,48,128]{2,1,0:T(8,128)S(1)}, u32[]{:S(2)}, u32[]{:S(2)}) collective-permute-start(f32[3,48,128]{2,1,0:T(8,128)S(1)} %get-tuple-element.16), channel_id=1, source_target_pairs={{0,1},{1,2},{2,3},{3,4},{4,5},{5,6},{6,7},{7,8},{8,9},{9,10},{10,1... | collective-permute-start | bytes 221192 | tf_op jit(solution)/shard_map/ppermute | solution.py:432
  111.5 7.0 %collective-permute-start.11 = (f32[3,48,128]{2,1,0:T(8,128)S(1)}, f32[3,48,128]{2,1,0:T(8,128)S(1)}, u32[]{:S(2)}, u32[]{:S(2)}) collective-permute-start(f32[3,48,128]{2,1,0:T(8,128)S(1)} %get-tuple-element.17), channel_id=1, source_target_pairs={{1,0},{2,1},{3,2},{4,3},{5,4},{6,5},{7,6},{8,7},{9,8},{10,9},{11,1... | collective-permute-start | bytes 221192 | tf_op jit(solution)/shard_map/ppermute | solution.py:432
  118.4 0.0 collective-permute-done.9
  118.4 0.0 collective-permute-done.8
  118.5 0.0 all-to-all-done.2.gathered_ref
  118.5 5.6 %shard_map.43.near_ref = f32[12,8,128]{2,1,0:T(8,128)S(1)} custom-call(s32[3]{0:T(128)S(1)} %pad_add_fusion.place_ref, f32[16,8,4,128]{3,2,1,0:T(4,128)S(1)} %all-to-all-done.2.gathered_ref), custom_call_target="tpu_custom_call" | custom-call | flops 100000000 | bytes 16000000 | tf_op jit(solution)/shard_map/pallas_call | solution.py:516
  124.1 0.0 collective-permute-done.10.before_ref
  124.1 0.0 collective-permute-done.11.after_ref
  124.1 9.1 %shard_map.44 = (f32[32,8,128]{2,1,0:T(8,128)}, f32[32,8,128]{2,1,0:T(8,128)}) custom-call(s32[3]{0:T(128)S(1)} %pad_add_fusion.place_ref, f32[12,8,128]{2,1,0:T(8,128)S(1)} %shard_map.43.near_ref, f32[24,24,128]{2,1,0:T(8,128)S(1)} %pad_maximum_fusion.1.halo_ref, f32[20,48,128]{2,1,0:T(8,128)S(1)} %get-tuple-element.13.kept_ref, ...), custom_call_target="tpu_custom_call" | custom-call | tf_op jit(solution)/shard_map/pallas_call | solution.py:525
  (29 shorter events, 0.4 us)
Async XLA Ops:
  0.6 0.9 copy-start.2
  1.6 6.5 %collective-permute-start = (f32[17,8,128]{2,0,1:T(8,128)S(1)}, f32[17,8,128]{2,0,1:T(8,128)S(1)}, u32[]{:S(2)}, u32[]{:S(2)}) collective-permute-start(f32[17,8,128]{2,0,1:T(8,128)S(1)} %pad_maximum_fusion.6), channel_id=1, source_target_pairs={{0,64},{64,128},{128,192},{192,256},{256,320},{320,384},{384,448},... | collective-permute-start | bytes 208904 | tf_op jit(solution)/shard_map/ppermute | solution.py:432
  5.9 2.2 %copy-start = (f32[32,8,128]{2,1,0:T(8,128)S(1)}, f32[32,8,128]{2,1,0:T(8,128)}, u32[]{:S(2)}) copy-start(f32[32,8,128]{2,1,0:T(8,128)} %param.2) | copy-start | bytes 393220
  6.0 7.0 %collective-permute-start.1 = (f32[17,8,128]{2,0,1:T(8,128)S(1)}, f32[17,8,128]{2,0,1:T(8,128)S(1)}, u32[]{:S(2)}, u32[]{:S(2)}) collective-permute-start(f32[17,8,128]{2,0,1:T(8,128)S(1)} %pad_maximum_fusion.7), channel_id=1, source_target_pairs={{64,0},{128,64},{192,128},{256,192},{320,256},{384,320},{448,384},... | collective-permute-start | bytes 208904 | tf_op jit(solution)/shard_map/ppermute | solution.py:432
  8.1 4.9 %copy-start.1 = (f32[17,8,128]{2,0,1:T(8,128)}, f32[17,8,128]{2,0,1:T(8,128)S(1)}, u32[]{:S(2)}) copy-start(f32[17,8,128]{2,0,1:T(8,128)S(1)} %collective-permute-done) | copy-start | bytes 208900
  13.0 0.8 slice-start
  14.1 10.8 %collective-permute-start.2 = (f32[10,48,128]{2,1,0:T(8,128)S(1)}, f32[10,48,128]{2,1,0:T(8,128)S(1)}, u32[]{:S(2)}, u32[]{:S(2)}) collective-permute-start(f32[10,48,128]{2,1,0:T(8,128)S(1)} %pad_maximum_fusion.4), channel_id=1, source_target_pairs={{0,1},{1,2},{2,3},{3,4},{4,5},{5,6},{6,7},{7,8},{8,9},{9,10},{10,1... | collective-permute-start | bytes 737288 | tf_op jit(solution)/shard_map/ppermute | solution.py:432
  16.0 10.7 %collective-permute-start.3 = (f32[10,48,128]{2,1,0:T(8,128)S(1)}, f32[10,48,128]{2,1,0:T(8,128)S(1)}, u32[]{:S(2)}, u32[]{:S(2)}) collective-permute-start(f32[10,48,128]{2,1,0:T(8,128)S(1)} %pad_maximum_fusion.5), channel_id=1, source_target_pairs={{1,0},{2,1},{3,2},{4,3},{5,4},{6,5},{7,6},{8,7},{9,8},{10,9},{11,1... | collective-permute-start | bytes 737288 | tf_op jit(solution)/shard_map/ppermute | solution.py:432
  37.2 10.3 %collective-permute-start.4 = (f32[13,16,128]{2,1,0:T(8,128)S(1)}, f32[13,16,128]{2,1,0:T(8,128)S(1)}, u32[]{:S(2)}, u32[]{:S(2)}) collective-permute-start(f32[13,16,128]{2,1,0:T(8,128)S(1)} %get-tuple-element.24), channel_id=1, source_target_pairs={{0,4},{1,5},{2,6},{3,7},{4,8},{5,9},{6,10},{7,11},{8,12},{9,13},{1... | collective-permute-start | bytes 319496 | tf_op jit(solution)/shard_map/ppermute | solution.py:432
  41.3 8.4 %collective-permute-start.5 = (f32[13,16,128]{2,1,0:T(8,128)S(1)}, f32[13,16,128]{2,1,0:T(8,128)S(1)}, u32[]{:S(2)}, u32[]{:S(2)}) collective-permute-start(f32[13,16,128]{2,1,0:T(8,128)S(1)} %get-tuple-element.25), channel_id=1, source_target_pairs={{4,0},{5,1},{6,2},{7,3},{8,4},{9,5},{10,6},{11,7},{12,8},{13,9},{1... | collective-permute-start | bytes 319496 | tf_op jit(solution)/shard_map/ppermute | solution.py:432
  49.8 10.3 %collective-permute-start.7 = (f32[544,128]{1,0:T(8,128)S(1)}, f32[544,128]{1,0:T(8,128)S(1)}, u32[]{:S(2)}, u32[]{:S(2)}) collective-permute-start(f32[544,128]{1,0:T(8,128)S(1)} %get-tuple-element.22), channel_id=1, source_target_pairs={{64,0},{128,64},{192,128},{256,192},{320,256},{384,320},{448,384},... | collective-permute-start | bytes 835592 | tf_op jit(solution)/shard_map/ppermute | solution.py:432
  51.1 10.2 %collective-permute-start.6 = (f32[544,128]{1,0:T(8,128)S(1)}, f32[544,128]{1,0:T(8,128)S(1)}, u32[]{:S(2)}, u32[]{:S(2)}) collective-permute-start(f32[544,128]{1,0:T(8,128)S(1)} %get-tuple-element.23), channel_id=1, source_target_pairs={{0,64},{64,128},{128,192},{192,256},{256,320},{320,384},{384,448},... | collective-permute-start | bytes 835592 | tf_op jit(solution)/shard_map/ppermute | solution.py:432
  93.2 25.2 %all-to-all-start.2 = ((f32[16,8,4,128]{3,2,1,0:T(4,128)}), f32[16,8,4,128]{3,2,1,0:T(4,128)S(1)}, u32[]{:S(2)}, u32[]{:S(2)}) async-start(f32[16,8,4,128]{3,2,1,0:T(4,128)} %broadcast_in_dim.34), calls=%async_computation.2 | async-start | bytes 524288 | tf_op jit(solution)/shard_map/all_to_all | solution.py:506
  102.2 16.3 %collective-permute-start.9 = (f32[8,24,128]{2,1,0:T(8,128)S(1)}, f32[8,24,128]{2,1,0:T(8,128)S(1)}, u32[]{:S(2)}, u32[]{:S(2)}) collective-permute-start(f32[8,24,128]{2,1,0:T(8,128)S(1)} %copy_bitcast_fusion), channel_id=1, source_target_pairs={{4,0},{5,1},{6,2},{7,3},{8,4},{9,5},{10,6},{11,7},{12,8},{13,9},{1... | collective-permute-start | bytes 294920 | tf_op jit(solution)/shard_map/ppermute | solution.py:432
  107.0 11.4 %collective-permute-start.8 = (f32[8,24,128]{2,1,0:T(8,128)S(1)}, f32[8,24,128]{2,1,0:T(8,128)S(1)}, u32[]{:S(2)}, u32[]{:S(2)}) collective-permute-start(f32[8,24,128]{2,1,0:T(8,128)S(1)} %copy_bitcast_fusion), channel_id=1, source_target_pairs={{0,4},{1,5},{2,6},{3,7},{4,8},{5,9},{6,10},{7,11},{8,12},{9,13},{1... | collective-permute-start | bytes 294920 | tf_op jit(solution)/shard_map/ppermute | solution.py:432
  109.5 14.6 %collective-permute-start.10 = (f32[3,48,128]{2,1,0:T(8,128)S(1)}, f32[3,48,128]{2,1,0:T(8,128)S(1)}, u32[]{:S(2)}, u32[]{:S(2)}) collective-permute-start(f32[3,48,128]{2,1,0:T(8,128)S(1)} %get-tuple-element.16), channel_id=1, source_target_pairs={{0,1},{1,2},{2,3},{3,4},{4,5},{5,6},{6,7},{7,8},{8,9},{9,10},{10,1... | collective-permute-start | bytes 221192 | tf_op jit(solution)/shard_map/ppermute | solution.py:432
  111.5 12.7 %collective-permute-start.11 = (f32[3,48,128]{2,1,0:T(8,128)S(1)}, f32[3,48,128]{2,1,0:T(8,128)S(1)}, u32[]{:S(2)}, u32[]{:S(2)}) collective-permute-start(f32[3,48,128]{2,1,0:T(8,128)S(1)} %get-tuple-element.17), channel_id=1, source_target_pairs={{1,0},{2,1},{3,2},{4,3},{5,4},{6,5},{7,6},{8,7},{9,8},{10,9},{11,1... | collective-permute-start | bytes 221192 | tf_op jit(solution)/shard_map/ppermute | solution.py:432

commit v4 on v3

--- a/solution.py
+++ b/solution.py
@@ -193,7 +193,7 @@
     density[6:14] = d_ref[...]
 
 
-def finest_down(s_ref, d_ref, before_ref, after_ref, message_ref, low_ref, high_ref, below_ref,
+def finest_down(place_ref, s_ref, d_ref, before_ref, after_ref, chunk_ref, low_ref, high_ref, below_ref,
                 source, density, keep, value, plane):
     finest_window(s_ref, d_ref, before_ref, after_ref, source, density)
     level = Level(density, keep, value, 128)
@@ -214,9 +214,11 @@
     blocks(0, 4, 1, pooling)
     pooled = plane[:, pl.ds(0, 16, stride=2)] + plane[:, pl.ds(1, 16, stride=2)]
     out = dot(pooled[:4].reshape(64, 128), halving(0, 0.125)) + dot(pooled[4:].reshape(64, 128), halving(64, 0.125))
-    message_ref[...] = out.reshape(4, 16, 128)
-    low_ref[...] = value[1, 3:6, 8:56]
-    high_ref[...] = value[1, 4:7, 8:56]
+    low_ref[...] = value[1, 3:6, 8:56].reshape(144, 128)
+    high_ref[...] = value[1, 4:7, 8:56].reshape(144, 128)
+    for peer in range(GROUP):
+        chunk_ref[peer, 0:64] = out
+        chunk_ref[peer, 64:208] = jnp.where(peer > place_ref[2], high_ref[...], low_ref[...])
     below_ref[...] = value[1, 3:7]
 
 
@@ -228,7 +230,7 @@
     density[start] = jnp.where(left, pltpu.roll(near, 64, 2), far)
 
 
-def middle_down(place_ref, window_ref, before_ref, after_ref, coarse_ref, halo_ref, kept_ref, below_ref,
+def middle_down(place_ref, window_ref, before_ref, after_ref, chunk_ref, kept_ref, below_ref,
                 window, source, density, keep, value, plane, source2, density2, keep2, value2):
     window[1:43, 16:32] = window_ref[...]
     for ref, near, far in ((before_ref, 0, 8), (after_ref, 32, 32)):
@@ -290,14 +292,17 @@
         total = pooled[8 * row : 8 * row + 1]
         for i in range(1, 8):
             total = total + pltpu.roll(pooled[8 * row + i : 8 * row + i + 1], 16 * i, 1)
-        coarse_ref[row : row + 1] = total
+        chunk_ref[0, 64 + row : 65 + row] = total
     for j in range(4):
         for k in range(2):
             row = 6 + 2 * j + k
             total = source2[row, 8:16] + pltpu.roll(density2[row, 8:16], 64, 1)
             if k == 0:
                 total = total + pltpu.roll(value2[1, 3 + j, 8:16], 32, 1)
-            halo_ref[2 * j + k] = total
+            chunk_ref[0, 8 * (2 * j + k) : 8 * (2 * j + k) + 8] = total
+    chunk_ref[0, 68:72] = jnp.zeros((4, 128), F32)
+    for peer in range(1, chunk_ref.shape[0]):
+        chunk_ref[peer] = chunk_ref[0]
 
 
 def coarsest(planes, place_ref, gathered_ref, near_ref, source, density, keep, value, wide):
@@ -425,9 +430,9 @@
     remain_ref[...] = jnp.swapaxes(plane[0:8, 16:48], 0, 1)
 
 
-def pair(array_up, array_down, axis, distance, ring=False):
-    devices = lax.axis_size(axis)
-    up = [(i, (i + distance) % devices) for i in range(devices if ring else devices - distance)]
+def pair(array_up, array_down, axis, group=1):
+    groups = lax.axis_size(axis) // group
+    up = [(i * group + j, (i + 2) * group - 1 - j) for i in range(groups - 1) for j in range(group)]
     down = [(j, i) for i, j in up]
     return lax.ppermute(array_up, axis, up), lax.ppermute(array_down, axis, down)
 
@@ -441,7 +446,7 @@
 
 
 def params():
-    return pltpu.CompilerParams(vmem_limit_bytes=48 * 1024 * 1024)
+    return pltpu.CompilerParams(vmem_limit_bytes=24 * 1024 * 1024)
 
 
 def body(right_side, labels):
@@ -451,7 +456,6 @@
         jnp.concatenate([right_side[-8:], density[-9:]], axis=0),
         jnp.concatenate([right_side[:8], density[:9]], axis=0),
         "gz",
-        1,
     )
     zeros = jnp.zeros((8, 8, 128), F32)
     wide_source = jnp.concatenate([zeros, before[:8], right_side, after[:8], zeros], axis=0)
@@ -462,33 +466,41 @@
         jnp.concatenate([wide_source[3:, 8:56], wide_density[3:, 8:56]], axis=0),
         jnp.concatenate([wide_source[:5, 8:56], wide_density[:5, 8:56]], axis=0),
         "xy",
-        1,
     )
     finest = (wide_source, wide_density, before, after)
-    message, first_rows, last_rows, below0 = pl.pallas_call(
+    at_group = lax.axis_index("xy") % GROUP
+    place = jnp.stack([lax.axis_index("gz"), lax.axis_index("xy"), at_group]).astype(jnp.int32)
+    smem, block = pl.BlockSpec(memory_space=pltpu.SMEM), pl.BlockSpec(memory_space=pltpu.VMEM)
+    chunks, first_rows, last_rows, below0 = pl.pallas_call(
         finest_down,
-        out_shape=[shape(4, 16, 128), shape(3, 48, 128), shape(3, 48, 128), shape(4, 64, 128)],
+        out_shape=[shape(GROUP, 208, 128), shape(144, 128), shape(144, 128), shape(4, 64, 128)],
+        in_specs=[smem] + [block] * 4,
         scratch_shapes=[vmem(20, 64, 128)] * 2 + [vmem(KEPT, 10, 64, 128), vmem(2, 10, 64, 128), vmem(8, 32, 128)],
         compiler_params=params(),
-    )(*finest)
+    )(place, *finest)
 
     teams = [[GROUP * i + j for j in range(GROUP)] for i in range(xy // GROUP)]
-    window = lax.all_to_all(
-        jnp.broadcast_to(message[None], (GROUP, 4, 16, 128)), "xy", 0, 0, axis_index_groups=teams, tiled=True
-    ).reshape(4 * GROUP, 16, 128)
-    before, after = pair(window[-13:], window[:13], "xy", GROUP)
-    window = jnp.concatenate([before, window, after], axis=0)
+    chunks = lax.all_to_all(chunks, "xy", 0, 0, axis_index_groups=teams, tiled=True)
+    window = chunks[:, :64].reshape(4 * GROUP * 16, 128)
+    before, after = pair(
+        jnp.concatenate([window[-208:], last_rows], axis=0),
+        jnp.concatenate([window[:208], first_rows], axis=0),
+        "xy",
+        GROUP,
+    )
+    rims = jnp.concatenate([before[None, 208:], chunks[:, 64:], after[None, 208:]], axis=0)
+    value_before = lax.dynamic_index_in_dim(rims, at_group, 0, keepdims=False).reshape(3, 48, 128)
+    value_after = lax.dynamic_index_in_dim(rims, at_group + 2, 0, keepdims=False).reshape(3, 48, 128)
+    window = jnp.concatenate([before[:208], window, after[:208]], axis=0).reshape(-1, 16, 128)
 
     def faces(near):
         parts = (window[8:34], window[:8, near], window[34:, near])
         return jnp.concatenate([part.reshape(-1, 128) for part in parts], axis=0)
 
-    before, after = pair(faces(slice(8, 16)), faces(slice(0, 8)), "gz", 1)
-    place = jnp.stack([lax.axis_index("gz"), lax.axis_index("xy"), lax.axis_index("xy") % GROUP]).astype(jnp.int32)
-    smem, block = pl.BlockSpec(memory_space=pltpu.SMEM), pl.BlockSpec(memory_space=pltpu.VMEM)
-    coarse, halo, kept, below1 = pl.pallas_call(
+    before, after = pair(faces(slice(8, 16)), faces(slice(0, 8)), "gz")
+    chunks, kept, below1 = pl.pallas_call(
         middle_down,
-        out_shape=[shape(4, 128), shape(8, 8, 128), shape(20, 48, 128), shape(10, 24, 128)],
+        out_shape=[shape(gz, 72, 128), shape(20, 48, 128), shape(10, 24, 128)],
         in_specs=[smem] + [block] * 3,
         scratch_shapes=[vmem(44, 48, 128)]
         + [vmem(44, 24, 128)] * 2
@@ -498,20 +510,16 @@
         compiler_params=params(),
     )(place, window, before, after)
 
-    column = lax.all_to_all(
-        jnp.broadcast_to(jnp.concatenate([coarse, halo.reshape(64, 128)], axis=0)[None], (gz, 68, 128)),
-        "gz", 0, 0, tiled=True,
-    )
+    column = lax.all_to_all(chunks, "gz", 0, 0, tiled=True)
     peers = [[GROUP * i + j for i in range(xy // GROUP)] for j in range(GROUP)]
     everywhere = lax.all_to_all(
-        jnp.broadcast_to(column[None, :, :4], (xy // GROUP, gz, 4, 128)), "xy", 0, 0, axis_index_groups=peers, tiled=True
+        jnp.broadcast_to(column[None, :, 64:68], (xy // GROUP, gz, 4, 128)), "xy", 0, 0, axis_index_groups=peers, tiled=True
     )
-    halo = jnp.pad(column[:, 4:], ((1, 1), (0, 0), (0, 0)))
+    halo = jnp.pad(column[:, :64], ((1, 1), (0, 0), (0, 0)))
     halo = lax.dynamic_slice(halo, (lax.axis_index("gz"), 0, 0), (3, 64, 128)).reshape(3, 8, 8, 128)
     halo = jnp.swapaxes(halo, 0, 1).reshape(8, 24, 128)
     before, after = pair(halo, halo, "xy", GROUP)
     halo = jnp.concatenate([before, halo, after], axis=0)
-    value_before, value_after = pair(last_rows, first_rows, "xy", 1)
     planes = 4 * gz
     near = pl.pallas_call(
         partial(coarsest, planes),

time: 134 us -> 143 us (1.067)
  the two profiles are of different devices: /device:TPU:32 before, /device:TPU:33 now
where the time goes in v4:
time: 143 us; the launch traced here: 142 us
  starting transfers between devices  54.7 us (38%)
  waiting for transfers between devices  42 us (29%)
  Pallas kernels  26.9 us (19%)
  blocking collectives  11.7 us (8%)
  local copies, waits for them, and re-layouts  5.39 us (4%)
    ppermute x5, waiting for transfers between devices, pair(): lax.ppermute(array_down, axis, down)  19 us
    ppermute x5, starting transfers between devices, pair(): lax.ppermute(array_down, axis, down)  18.1 us
    ppermute x5, starting transfers between devices, pair(): lax.ppermute(array_up, axis, up)  17.3 us
    ppermute x5, waiting for transfers between devices, pair(): lax.ppermute(array_up, axis, up)  13.2 us
    all_to_all x1, starting transfers between devices, body(): column = lax.all_to_all(chunks, 'gz', 0, 0, tiled=True)  12.4 us
    all_to_all x1, blocking collectives, body(): lax.all_to_all(chunks, 'xy', 0, 0, axis_index_groups=teams, tiled=True)  11.7 us
    all_to_all x1, waiting for transfers between devices, body(): column = lax.all_to_all(chunks, 'gz', 0, 0, tiled=True)  9.75 us
    pallas_call x1, Pallas kernels, body(): pl.pallas_call(partial(way_up, xy), out_shape=[shape(32, 8, 128)] * 2, in...  9.11 us
  transfers between devices with their start and end apart: 12, of which 11 were waited for; matrix products, arithmetic and copies ran while one was open for 0% of the time, Pallas kernels for 0%

profile of v4, /device:TPU:33, one launch (start us, length us, event | category | flops | bytes accessed | tf_op | source)
XLA Modules:
  0.0 142.0 jit_solution(9135948445879392564)
XLA Ops:
  0.6 0.0 copy-start.5
  0.6 0.8 fusion.7
  1.5 0.1 copy-done.5
  1.6 4.0 %collective-permute-start = (f32[17,8,128]{2,0,1:T(8,128)S(1)}, f32[17,8,128]{2,0,1:T(8,128)S(1)}, u32[]{:S(2)}, u32[]{:S(2)}) collective-permute-start(f32[17,8,128]{2,0,1:T(8,128)S(1)} %pad_maximum_fusion.9), channel_id=1, source_target_pairs={{0,64},{64,128},{128,192},{192,256},{256,320},{320,384},{384,448},... | collective-permute-start | bytes 208904 | tf_op jit(solution)/shard_map/ppermute | solution.py:437
  5.7 0.0 copy-start.3
  5.7 1.4 %collective-permute-start.1 = (f32[17,8,128]{2,0,1:T(8,128)S(1)}, f32[17,8,128]{2,0,1:T(8,128)S(1)}, u32[]{:S(2)}, u32[]{:S(2)}) collective-permute-start(f32[17,8,128]{2,0,1:T(8,128)S(1)} %pad_maximum_fusion.10), channel_id=1, source_target_pairs={{64,0},{128,64},{192,128},{256,192},{320,256},{384,320},{448,384},... | collective-permute-start | bytes 208904 | tf_op jit(solution)/shard_map/ppermute | solution.py:437
  7.1 0.1 collective-permute-done
  7.3 0.0 copy-start.4
  7.3 0.0 copy-done.3
  7.3 4.5 %collective-permute-done.1 = f32[17,8,128]{2,0,1:T(8,128)S(1)} collective-permute-done((f32[17,8,128]{2,0,1:T(8,128)S(1)}, f32[17,8,128]{2,0,1:T(8,128)S(1)}, u32[]{:S(2)}, u32[]{:S(2)}) %collective-permute-start.1) | collective-permute-done | bytes 69664 | tf_op jit(solution)/shard_map/ppermute | solution.py:437
  11.8 0.0 copy-done.4
  11.8 0.0 slice-start.2
  11.9 0.8 slice-done.2
  12.7 0.2 concatenate.42
  12.9 4.8 %collective-permute-start.2 = (f32[10,48,128]{2,1,0:T(8,128)S(1)}, f32[10,48,128]{2,1,0:T(8,128)S(1)}, u32[]{:S(2)}, u32[]{:S(2)}) collective-permute-start(f32[10,48,128]{2,1,0:T(8,128)S(1)} %pad_maximum_fusion.5), channel_id=1, source_target_pairs={{0,1},{1,2},{2,3},{3,4},{4,5},{5,6},{6,7},{7,8},{8,9},{9,10},{10,1... | collective-permute-start | bytes 737288 | tf_op jit(solution)/shard_map/ppermute | solution.py:437
  17.8 1.9 %collective-permute-start.3 = (f32[10,48,128]{2,1,0:T(8,128)S(1)}, f32[10,48,128]{2,1,0:T(8,128)S(1)}, u32[]{:S(2)}, u32[]{:S(2)}) collective-permute-start(f32[10,48,128]{2,1,0:T(8,128)S(1)} %pad_maximum_fusion.6), channel_id=1, source_target_pairs={{1,0},{2,1},{3,2},{4,3},{5,4},{6,5},{7,6},{8,7},{9,8},{10,9},{11,1... | collective-permute-start | bytes 737288 | tf_op jit(solution)/shard_map/ppermute | solution.py:437
  19.7 0.1 pad_add_fusion.place_ref
  19.8 1.1 collective-permute-done.2.before_ref.rim_before_ref
  20.9 4.4 %collective-permute-done.3.after_ref.rim_after_ref = f32[10,48,128]{2,1,0:T(8,128)S(1)} collective-permute-done((f32[10,48,128]{2,1,0:T(8,128)S(1)}, f32[10,48,128]{2,1,0:T(8,128)S(1)}, u32[]{:S(2)}, u32[]{:S(2)}) %collective-permute-start.3) | collective-permute-done | bytes 245792 | tf_op jit(solution)/shard_map/ppermute | solution.py:437
  25.3 4.0 %shard_map.41 = (f32[4,208,128]{2,1,0:T(8,128)S(1)}, f32[144,128]{1,0:T(8,128)S(1)}, f32[144,128]{1,0:T(8,128)S(1)}, f32[4,64,128]{2,1,0:T(8,128)S(1)}) custom-call(s32[3]{0:T(128)S(1)} %pad_add_fusion.place_ref, f32[8,64,128]{2,1,0:T(8,128)S(1)} %bitcast.34, f32[8,64,128]{2,1,0:T(8,128)S(1)} %bitcast.29, ...), custom_call_target="tpu_custom_call" | custom-call | tf_op jit(solution)/shard_map/pallas_call | solution.py:474
  29.3 11.7 %all_to_all.15 = f32[4,208,128]{2,1,0:T(8,128)S(1)} all-to-all(f32[4,208,128]{2,1,0:T(8,128)S(1)} %get-tuple-element.9), channel_id=1, replica_groups={{0,1,2,3},{4,5,6,7},{8,9,10,11},{12,13,14,15},{16,17,18,19},{20,21,22,2..., dimensions={0} | all-to-all | bytes 851968 | tf_op jit(solution)/shard_map/all_to_all | solution.py:483
  40.9 0.0 copy-start
  41.0 6.4 %collective-permute-start.5 = (f32[352,128]{1,0:T(8,128)S(1)}, f32[352,128]{1,0:T(8,128)S(1)}, u32[]{:S(2)}, u32[]{:S(2)}) collective-permute-start(f32[352,128]{1,0:T(8,128)S(1)} %pad_maximum_fusion.8), channel_id=1, source_target_pairs={{7,0},{6,1},{5,2},{4,3},{11,4},{10,5},{9,6},{8,7},{15,8},{14,9},{1... | collective-permute-start | bytes 540680 | tf_op jit(solution)/shard_map/ppermute | solution.py:437
  47.4 1.9 %collective-permute-start.4 = (f32[352,128]{1,0:T(8,128)S(1)}, f32[352,128]{1,0:T(8,128)S(1)}, u32[]{:S(2)}, u32[]{:S(2)}) collective-permute-start(f32[352,128]{1,0:T(8,128)S(1)} %pad_maximum_fusion.7), channel_id=1, source_target_pairs={{0,7},{1,6},{2,5},{3,4},{4,11},{5,10},{6,9},{7,8},{8,15},{9,14},{1... | collective-permute-start | bytes 540680 | tf_op jit(solution)/shard_map/ppermute | solution.py:437
  49.3 2.3 %collective-permute-done.5 = f32[352,128]{1,0:T(8,128)S(1)} collective-permute-done((f32[352,128]{1,0:T(8,128)S(1)}, f32[352,128]{1,0:T(8,128)S(1)}, u32[]{:S(2)}, u32[]{:S(2)}) %collective-permute-start.5) | collective-permute-done | bytes 180256 | tf_op jit(solution)/shard_map/ppermute | solution.py:437
  51.7 0.7 copy-done.1
  52.3 6.4 %collective-permute-done.4 = f32[352,128]{1,0:T(8,128)S(1)} collective-permute-done((f32[352,128]{1,0:T(8,128)S(1)}, f32[352,128]{1,0:T(8,128)S(1)}, u32[]{:S(2)}, u32[]{:S(2)}) %collective-permute-start.4) | collective-permute-done | bytes 180256 | tf_op jit(solution)/shard_map/ppermute | solution.py:437
  58.7 0.9 slice-done.1
  59.7 1.3 collective-permute-start.7
  61.0 4.6 %collective-permute-start.6 = (f32[544,128]{1,0:T(8,128)S(1)}, f32[544,128]{1,0:T(8,128)S(1)}, u32[]{:S(2)}, u32[]{:S(2)}) collective-permute-start(f32[544,128]{1,0:T(8,128)S(1)} %get-tuple-element.27), channel_id=1, source_target_pairs={{0,64},{64,128},{128,192},{192,256},{256,320},{320,384},{384,448},... | collective-permute-start | bytes 835592 | tf_op jit(solution)/shard_map/ppermute | solution.py:437
  65.7 5.1 %collective-permute-done.7.after_ref = f32[544,128]{1,0:T(8,128)S(1)} collective-permute-done((f32[544,128]{1,0:T(8,128)S(1)}, f32[544,128]{1,0:T(8,128)S(1)}, u32[]{:S(2)}, u32[]{:S(2)}) %collective-permute-start.7) | collective-permute-done | bytes 278560 | tf_op jit(solution)/shard_map/ppermute | solution.py:437
  70.8 1.0 collective-permute-done.6.before_ref
  71.8 8.2 %shard_map.42 = (f32[8,72,128]{2,1,0:T(8,128)}, f32[20,48,128]{2,1,0:T(8,128)S(1)}, f32[10,24,128]{2,1,0:T(8,128)S(1)}) custom-call(s32[3]{0:T(128)S(1)} %pad_add_fusion.place_ref, f32[42,16,128]{2,1,0:T(8,128)S(1)} %bitcast.32, f32[544,128]{1,0:T(8,128)S(1)} %collective-permute-done.6.before_ref, f32[544,128]{1,0:T(8,128)S(1)} %collective-permute-done.7.after_ref), custom_call_target="tpu_custom_call" | custom-call | tf_op jit(solution)/shard_map/pallas_call | solution.py:501
  80.0 12.4 %all-to-all-start.1 = ((f32[8,72,128]{2,1,0:T(8,128)}), f32[8,72,128]{2,1,0:T(8,128)S(1)}, u32[]{:S(2)}, u32[]{:S(2)}) async-start(f32[8,72,128]{2,1,0:T(8,128)} %get-tuple-element.12), calls=%async_computation.1 | async-start | bytes 589824 | tf_op jit(solution)/shard_map/all_to_all | solution.py:513
  92.4 0.0 copy-done
  92.4 0.0 copy-start.2
  92.4 0.9 copy-done.2
  93.3 9.8 %all-to-all-done.1 = f32[8,72,128]{2,1,0:T(8,128)S(1)} async-done(((f32[8,72,128]{2,1,0:T(8,128)}), f32[8,72,128]{2,1,0:T(8,128)S(1)}, u32[]{:S(2)}, u32[]{:S(2)}) %all-to-all-start.1) | async-done | bytes 294944 | tf_op jit(solution)/shard_map/all_to_all | solution.py:513
  103.1 0.8 broadcast_in_dim.26
  103.9 6.8 %all-to-all-start.2 = ((f32[16,8,4,128]{3,2,1,0:T(4,128)}), f32[16,8,4,128]{3,2,1,0:T(4,128)S(1)}, u32[]{:S(2)}, u32[]{:S(2)}) async-start(f32[16,8,4,128]{3,2,1,0:T(4,128)} %broadcast_in_dim.26), calls=%async_computation.2 | async-start | bytes 524288 | tf_op jit(solution)/shard_map/all_to_all | solution.py:515
  110.7 0.0 slice-done
  110.8 7.1 %collective-permute-start.9 = (f32[8,24,128]{2,1,0:T(8,128)S(1)}, f32[8,24,128]{2,1,0:T(8,128)S(1)}, u32[]{:S(2)}, u32[]{:S(2)}) collective-permute-start(f32[8,24,128]{2,1,0:T(8,128)S(1)} %copy_bitcast_fusion), channel_id=1, source_target_pairs={{7,0},{6,1},{5,2},{4,3},{11,4},{10,5},{9,6},{8,7},{15,8},{14,9},{1... | collective-permute-start | bytes 294920 | tf_op jit(solution)/shard_map/ppermute | solution.py:437
  117.9 1.9 %collective-permute-start.8 = (f32[8,24,128]{2,1,0:T(8,128)S(1)}, f32[8,24,128]{2,1,0:T(8,128)S(1)}, u32[]{:S(2)}, u32[]{:S(2)}) collective-permute-start(f32[8,24,128]{2,1,0:T(8,128)S(1)} %copy_bitcast_fusion), channel_id=1, source_target_pairs={{0,7},{1,6},{2,5},{3,4},{4,11},{5,10},{6,9},{7,8},{8,15},{9,14},{1... | collective-permute-start | bytes 294920 | tf_op jit(solution)/shard_map/ppermute | solution.py:437
  119.9 2.7 %collective-permute-done.9 = f32[8,24,128]{2,1,0:T(8,128)S(1)} collective-permute-done((f32[8,24,128]{2,1,0:T(8,128)S(1)}, f32[8,24,128]{2,1,0:T(8,128)S(1)}, u32[]{:S(2)}, u32[]{:S(2)}) %collective-permute-start.9) | collective-permute-done | bytes 98336 | tf_op jit(solution)/shard_map/ppermute | solution.py:437
  122.6 4.6 %collective-permute-done.8 = f32[8,24,128]{2,1,0:T(8,128)S(1)} collective-permute-done((f32[8,24,128]{2,1,0:T(8,128)S(1)}, f32[8,24,128]{2,1,0:T(8,128)S(1)}, u32[]{:S(2)}, u32[]{:S(2)}) %collective-permute-start.8) | collective-permute-done | bytes 98336 | tf_op jit(solution)/shard_map/ppermute | solution.py:437
  127.2 0.0 all-to-all-done.2.gathered_ref
  127.2 5.6 %shard_map.43.near_ref = f32[12,8,128]{2,1,0:T(8,128)S(1)} custom-call(s32[3]{0:T(128)S(1)} %pad_add_fusion.place_ref, f32[16,8,4,128]{3,2,1,0:T(4,128)S(1)} %all-to-all-done.2.gathered_ref), custom_call_target="tpu_custom_call" | custom-call | flops 100000000 | bytes 16000000 | tf_op jit(solution)/shard_map/pallas_call | solution.py:524
  132.8 9.1 %shard_map.44 = (f32[32,8,128]{2,1,0:T(8,128)}, f32[32,8,128]{2,1,0:T(8,128)}) custom-call(s32[3]{0:T(128)S(1)} %pad_add_fusion.place_ref, f32[12,8,128]{2,1,0:T(8,128)S(1)} %shard_map.43.near_ref, f32[24,24,128]{2,1,0:T(8,128)S(1)} %pad_maximum_fusion.2.halo_ref, f32[20,48,128]{2,1,0:T(8,128)S(1)} %get-tuple-element.13.kept_ref, ...), custom_call_target="tpu_custom_call" | custom-call | tf_op jit(solution)/shard_map/pallas_call | solution.py:533
  (36 shorter events, 0.5 us)
Async XLA Ops:
  0.6 0.9 copy-start.5
  1.6 5.6 %collective-permute-start = (f32[17,8,128]{2,0,1:T(8,128)S(1)}, f32[17,8,128]{2,0,1:T(8,128)S(1)}, u32[]{:S(2)}, u32[]{:S(2)}) collective-permute-start(f32[17,8,128]{2,0,1:T(8,128)S(1)} %pad_maximum_fusion.9), channel_id=1, source_target_pairs={{0,64},{64,128},{128,192},{192,256},{256,320},{320,384},{384,448},... | collective-permute-start | bytes 208904 | tf_op jit(solution)/shard_map/ppermute | solution.py:437
  5.7 1.6 %copy-start.3 = (f32[32,8,128]{2,1,0:T(8,128)S(1)}, f32[32,8,128]{2,1,0:T(8,128)}, u32[]{:S(2)}) copy-start(f32[32,8,128]{2,1,0:T(8,128)} %param.2) | copy-start | bytes 393220
  5.7 6.1 %collective-permute-start.1 = (f32[17,8,128]{2,0,1:T(8,128)S(1)}, f32[17,8,128]{2,0,1:T(8,128)S(1)}, u32[]{:S(2)}, u32[]{:S(2)}) collective-permute-start(f32[17,8,128]{2,0,1:T(8,128)S(1)} %pad_maximum_fusion.10), channel_id=1, source_target_pairs={{64,0},{128,64},{192,128},{256,192},{320,256},{384,320},{448,384},... | collective-permute-start | bytes 208904 | tf_op jit(solution)/shard_map/ppermute | solution.py:437
  7.3 4.6 %copy-start.4 = (f32[17,8,128]{2,0,1:T(8,128)}, f32[17,8,128]{2,0,1:T(8,128)S(1)}, u32[]{:S(2)}) copy-start(f32[17,8,128]{2,0,1:T(8,128)S(1)} %collective-permute-done) | copy-start | bytes 208900
  11.8 0.8 slice-start.2
  12.9 8.0 %collective-permute-start.2 = (f32[10,48,128]{2,1,0:T(8,128)S(1)}, f32[10,48,128]{2,1,0:T(8,128)S(1)}, u32[]{:S(2)}, u32[]{:S(2)}) collective-permute-start(f32[10,48,128]{2,1,0:T(8,128)S(1)} %pad_maximum_fusion.5), channel_id=1, source_target_pairs={{0,1},{1,2},{2,3},{3,4},{4,5},{5,6},{6,7},{7,8},{8,9},{9,10},{10,1... | collective-permute-start | bytes 737288 | tf_op jit(solution)/shard_map/ppermute | solution.py:437
  17.8 7.5 %collective-permute-start.3 = (f32[10,48,128]{2,1,0:T(8,128)S(1)}, f32[10,48,128]{2,1,0:T(8,128)S(1)}, u32[]{:S(2)}, u32[]{:S(2)}) collective-permute-start(f32[10,48,128]{2,1,0:T(8,128)S(1)} %pad_maximum_fusion.6), channel_id=1, source_target_pairs={{1,0},{2,1},{3,2},{4,3},{5,4},{6,5},{7,6},{8,7},{9,8},{10,9},{11,1... | collective-permute-start | bytes 737288 | tf_op jit(solution)/shard_map/ppermute | solution.py:437
  40.9 51.5 %copy-start = (f32[4,208,128]{2,1,0:T(8,128)}, f32[4,208,128]{2,1,0:T(8,128)S(1)}, u32[]{:S(2)}) copy-start(f32[4,208,128]{2,1,0:T(8,128)S(1)} %all_to_all.15) | copy-start | bytes 1277956
  41.0 10.7 %collective-permute-start.5 = (f32[352,128]{1,0:T(8,128)S(1)}, f32[352,128]{1,0:T(8,128)S(1)}, u32[]{:S(2)}, u32[]{:S(2)}) collective-permute-start(f32[352,128]{1,0:T(8,128)S(1)} %pad_maximum_fusion.8), channel_id=1, source_target_pairs={{7,0},{6,1},{5,2},{4,3},{11,4},{10,5},{9,6},{8,7},{15,8},{14,9},{1... | collective-permute-start | bytes 540680 | tf_op jit(solution)/shard_map/ppermute | solution.py:437
  47.4 11.3 %collective-permute-start.4 = (f32[352,128]{1,0:T(8,128)S(1)}, f32[352,128]{1,0:T(8,128)S(1)}, u32[]{:S(2)}, u32[]{:S(2)}) collective-permute-start(f32[352,128]{1,0:T(8,128)S(1)} %pad_maximum_fusion.7), channel_id=1, source_target_pairs={{0,7},{1,6},{2,5},{3,4},{4,11},{5,10},{6,9},{7,8},{8,15},{9,14},{1... | collective-permute-start | bytes 540680 | tf_op jit(solution)/shard_map/ppermute | solution.py:437
  51.7 0.7 copy-start.1
  58.7 0.9 slice-start.1
  59.7 11.1 %collective-permute-start.7 = (f32[544,128]{1,0:T(8,128)S(1)}, f32[544,128]{1,0:T(8,128)S(1)}, u32[]{:S(2)}, u32[]{:S(2)}) collective-permute-start(f32[544,128]{1,0:T(8,128)S(1)} %get-tuple-element.26), channel_id=1, source_target_pairs={{64,0},{128,64},{192,128},{256,192},{320,256},{384,320},{448,384},... | collective-permute-start | bytes 835592 | tf_op jit(solution)/shard_map/ppermute | solution.py:437
  61.0 10.7 %collective-permute-start.6 = (f32[544,128]{1,0:T(8,128)S(1)}, f32[544,128]{1,0:T(8,128)S(1)}, u32[]{:S(2)}, u32[]{:S(2)}) collective-permute-start(f32[544,128]{1,0:T(8,128)S(1)} %get-tuple-element.27), channel_id=1, source_target_pairs={{0,64},{64,128},{128,192},{192,256},{256,320},{320,384},{384,448},... | collective-permute-start | bytes 835592 | tf_op jit(solution)/shard_map/ppermute | solution.py:437
  80.0 23.1 %all-to-all-start.1 = ((f32[8,72,128]{2,1,0:T(8,128)}), f32[8,72,128]{2,1,0:T(8,128)S(1)}, u32[]{:S(2)}, u32[]{:S(2)}) async-start(f32[8,72,128]{2,1,0:T(8,128)} %get-tuple-element.12), calls=%async_computation.1 | async-start | bytes 589824 | tf_op jit(solution)/shard_map/all_to_all | solution.py:513
  92.4 0.9 copy-start.2
  103.9 6.8 %slice-start = ((f32[4,208,128]{2,1,0:T(8,128)}), f32[4,144,128]{2,1,0:T(8,128)S(1)}, s32[]{:S(2)}) async-start(f32[4,208,128]{2,1,0:T(8,128)} %copy-done), calls=%async_computation.3 | async-start | bytes 589824 | tf_op jit(solution)/shard_map/slice | solution.py:491
  103.9 23.3 %all-to-all-start.2 = ((f32[16,8,4,128]{3,2,1,0:T(4,128)}), f32[16,8,4,128]{3,2,1,0:T(4,128)S(1)}, u32[]{:S(2)}, u32[]{:S(2)}) async-start(f32[16,8,4,128]{3,2,1,0:T(4,128)} %broadcast_in_dim.26), calls=%async_computation.2 | async-start | bytes 524288 | tf_op jit(solution)/shard_map/all_to_all | solution.py:515
  110.8 11.8 %collective-permute-start.9 = (f32[8,24,128]{2,1,0:T(8,128)S(1)}, f32[8,24,128]{2,1,0:T(8,128)S(1)}, u32[]{:S(2)}, u32[]{:S(2)}) collective-permute-start(f32[8,24,128]{2,1,0:T(8,128)S(1)} %copy_bitcast_fusion), channel_id=1, source_target_pairs={{7,0},{6,1},{5,2},{4,3},{11,4},{10,5},{9,6},{8,7},{15,8},{14,9},{1... | collective-permute-start | bytes 294920 | tf_op jit(solution)/shard_map/ppermute | solution.py:437
  117.9 9.3 %collective-permute-start.8 = (f32[8,24,128]{2,1,0:T(8,128)S(1)}, f32[8,24,128]{2,1,0:T(8,128)S(1)}, u32[]{:S(2)}, u32[]{:S(2)}) collective-permute-start(f32[8,24,128]{2,1,0:T(8,128)S(1)} %copy_bitcast_fusion), channel_id=1, source_target_pairs={{0,7},{1,6},{2,5},{3,4},{4,11},{5,10},{6,9},{7,8},{8,15},{9,14},{1... | collective-permute-start | bytes 294920 | tf_op jit(solution)/shard_map/ppermute | solution.py:437

commit v5 on v4

--- a/solution.py
+++ b/solution.py
@@ -35,9 +35,7 @@
 
 
 def inverse(a):
-    r = pl.reciprocal(a, approx=True)
-    r = r * (2.0 - a * r)
-    return r * (2.0 - a * r)
+    return pl.reciprocal(a, approx=True)
 
 
 def blocks(lo, count, block, step):
@@ -181,6 +179,23 @@
             self.value[:, j] = jnp.zeros((2, self.depth, 128), F32)
 
 
+def finest_rims(right_ref, labels_ref, before_ref, after_ref, s_ref, d_ref, low_ref, high_ref, source, density):
+    for ref, near in ((source, 8), (density, 7)):
+        ref[0:near] = jnp.zeros((near, 8, 128), F32)
+        ref[64 - near : 64] = jnp.zeros((near, 8, 128), F32)
+    source[8:16] = before_ref[0:8]
+    source[48:56] = after_ref[0:8]
+    source[16:48] = right_ref[...]
+    density[7:16] = before_ref[8:17]
+    density[48:57] = after_ref[8:17]
+    density[16:48] = jnp.where(labels_ref[...] == 1, gas_density, 1.0)
+    for start, wide, out in ((0, source, s_ref), (5, density, d_ref)):
+        rows = jnp.swapaxes(wide[...], 0, 1)
+        out[...] = rows
+        low_ref[start : start + 5] = rows[0:5, 8:56]
+        high_ref[start : start + 5] = rows[3:8, 8:56]
+
+
 def finest_window(s_ref, d_ref, before_ref, after_ref, source, density):
     for ref in (source, density):
         for rows in (pl.ds(0, 6), pl.ds(14, 6)):
@@ -193,7 +208,7 @@
     density[6:14] = d_ref[...]
 
 
-def finest_down(place_ref, s_ref, d_ref, before_ref, after_ref, chunk_ref, low_ref, high_ref, below_ref,
+def finest_down(s_ref, d_ref, before_ref, after_ref, chunk_ref, low_ref, high_ref, below_ref,
                 source, density, keep, value, plane):
     finest_window(s_ref, d_ref, before_ref, after_ref, source, density)
     level = Level(density, keep, value, 128)
@@ -214,11 +229,10 @@
     blocks(0, 4, 1, pooling)
     pooled = plane[:, pl.ds(0, 16, stride=2)] + plane[:, pl.ds(1, 16, stride=2)]
     out = dot(pooled[:4].reshape(64, 128), halving(0, 0.125)) + dot(pooled[4:].reshape(64, 128), halving(64, 0.125))
-    low_ref[...] = value[1, 3:6, 8:56].reshape(144, 128)
-    high_ref[...] = value[1, 4:7, 8:56].reshape(144, 128)
+    low_ref[...] = value[1, 3:6, 8:56]
+    high_ref[...] = value[1, 4:7, 8:56]
     for peer in range(GROUP):
-        chunk_ref[peer, 0:64] = out
-        chunk_ref[peer, 64:208] = jnp.where(peer > place_ref[2], high_ref[...], low_ref[...])
+        chunk_ref[peer] = out
     below_ref[...] = value[1, 3:7]
 
 
@@ -457,41 +471,29 @@
         jnp.concatenate([right_side[:8], density[:9]], axis=0),
         "gz",
     )
-    zeros = jnp.zeros((8, 8, 128), F32)
-    wide_source = jnp.concatenate([zeros, before[:8], right_side, after[:8], zeros], axis=0)
-    wide_density = jnp.concatenate([zeros[:7], before[8:], density, after[8:], zeros[:7]], axis=0)
-    wide_source = jnp.swapaxes(wide_source, 0, 1)
-    wide_density = jnp.swapaxes(wide_density, 0, 1)
-    before, after = pair(
-        jnp.concatenate([wide_source[3:, 8:56], wide_density[3:, 8:56]], axis=0),
-        jnp.concatenate([wide_source[:5, 8:56], wide_density[:5, 8:56]], axis=0),
-        "xy",
-    )
+    wide_source, wide_density, low_rim, high_rim = pl.pallas_call(
+        finest_rims,
+        out_shape=[shape(8, 64, 128)] * 2 + [shape(10, 48, 128)] * 2,
+        scratch_shapes=[vmem(64, 8, 128)] * 2,
+        compiler_params=params(),
+    )(right_side, labels, before, after)
+    before, after = pair(high_rim, low_rim, "xy")
     finest = (wide_source, wide_density, before, after)
     at_group = lax.axis_index("xy") % GROUP
     place = jnp.stack([lax.axis_index("gz"), lax.axis_index("xy"), at_group]).astype(jnp.int32)
     smem, block = pl.BlockSpec(memory_space=pltpu.SMEM), pl.BlockSpec(memory_space=pltpu.VMEM)
     chunks, first_rows, last_rows, below0 = pl.pallas_call(
         finest_down,
-        out_shape=[shape(GROUP, 208, 128), shape(144, 128), shape(144, 128), shape(4, 64, 128)],
-        in_specs=[smem] + [block] * 4,
+        out_shape=[shape(GROUP, 64, 128), shape(3, 48, 128), shape(3, 48, 128), shape(4, 64, 128)],
         scratch_shapes=[vmem(20, 64, 128)] * 2 + [vmem(KEPT, 10, 64, 128), vmem(2, 10, 64, 128), vmem(8, 32, 128)],
         compiler_params=params(),
-    )(place, *finest)
+    )(*finest)
 
     teams = [[GROUP * i + j for j in range(GROUP)] for i in range(xy // GROUP)]
     chunks = lax.all_to_all(chunks, "xy", 0, 0, axis_index_groups=teams, tiled=True)
-    window = chunks[:, :64].reshape(4 * GROUP * 16, 128)
-    before, after = pair(
-        jnp.concatenate([window[-208:], last_rows], axis=0),
-        jnp.concatenate([window[:208], first_rows], axis=0),
-        "xy",
-        GROUP,
-    )
-    rims = jnp.concatenate([before[None, 208:], chunks[:, 64:], after[None, 208:]], axis=0)
-    value_before = lax.dynamic_index_in_dim(rims, at_group, 0, keepdims=False).reshape(3, 48, 128)
-    value_after = lax.dynamic_index_in_dim(rims, at_group + 2, 0, keepdims=False).reshape(3, 48, 128)
-    window = jnp.concatenate([before[:208], window, after[:208]], axis=0).reshape(-1, 16, 128)
+    window = chunks.reshape(4 * GROUP, 16, 128)
+    before, after = pair(window[-13:], window[:13], "xy", GROUP)
+    window = jnp.concatenate([before, window, after], axis=0)
 
     def faces(near):
         parts = (window[8:34], window[:8, near], window[34:, near])
@@ -510,6 +512,7 @@
         compiler_params=params(),
     )(place, window, before, after)
 
+    value_before, value_after = pair(last_rows, first_rows, "xy")
     column = lax.all_to_all(chunks, "gz", 0, 0, tiled=True)
     peers = [[GROUP * i + j for i in range(xy // GROUP)] for j in range(GROUP)]
     everywhere = lax.all_to_all(

time: 143 us -> 133 us (0.930)
  waiting for transfers between devices: 42 us -> 23.1 us
  blocking collectives: 11.7 us -> 30.4 us
  starting transfers between devices: 54.7 us -> 50.9 us
  local copies, waits for them, and re-layouts: 5.39 us -> 1.79 us
  Pallas kernels: 26.9 us -> 25 us
    all_to_all x0 -> x1, blocking collectives: none -> 22.4 us  [body(): column = lax.all_to_all(chunks, 'gz', 0, 0, tiled=True)]
    all_to_all x1 -> x0, starting transfers between devices: 12.4 us -> none  [body(): column = lax.all_to_all(chunks, 'gz', 0, 0, tiled=True)]
    all_to_all x1 -> x0, waiting for transfers between devices: 9.75 us -> none  [body(): column = lax.all_to_all(chunks, 'gz', 0, 0, tiled=True)]
    ppermute x5 -> x6, waiting for transfers between devices: 13.2 us -> 7.22 us  [pair(): lax.ppermute(array_up, axis, up)]
    ppermute x5 -> x6, starting transfers between devices: 18.1 us -> 22.9 us  [pair(): lax.ppermute(array_down, axis, down)]
    ppermute x5 -> x6, starting transfers between devices: 17.3 us -> 21.1 us  [pair(): lax.ppermute(array_up, axis, up)]
    all_to_all x1, blocking collectives: 11.7 us -> 8.04 us  [body(): lax.all_to_all(chunks, 'xy', 0, 0, axis_index_groups=teams, tiled=True)]
    ppermute x5 -> x6, waiting for transfers between devices: 19 us -> 15.9 us  [pair(): lax.ppermute(array_down, axis, down)]
  transfers between devices with their start and end apart: 12 -> 13, of which waited for: 11 -> 8; matrix products, arithmetic and copies ran while one was open for 0% -> 0% of each run, Pallas kernels for 0% -> 4%
where the time goes in v5:
time: 133 us; the launch traced here: 132 us
  starting transfers between devices  50.9 us (38%)
  blocking collectives  30.4 us (23%)
  Pallas kernels  25 us (19%)
  waiting for transfers between devices  23.1 us (17%)
  local copies, waits for them, and re-layouts  1.79 us (1%)
    ppermute x6, starting transfers between devices, pair(): lax.ppermute(array_down, axis, down)  22.9 us
    all_to_all x1, blocking collectives, body(): column = lax.all_to_all(chunks, 'gz', 0, 0, tiled=True)  22.4 us
    ppermute x6, starting transfers between devices, pair(): lax.ppermute(array_up, axis, up)  21.1 us
    ppermute x6, waiting for transfers between devices, pair(): lax.ppermute(array_down, axis, down)  15.9 us
    pallas_call x1, Pallas kernels, body(): pl.pallas_call(partial(way_up, xy), out_shape=[shape(32, 8, 128)] * 2, in...  8.81 us
    all_to_all x1, blocking collectives, body(): lax.all_to_all(chunks, 'xy', 0, 0, axis_index_groups=teams, tiled=True)  8.04 us
    ppermute x6, waiting for transfers between devices, pair(): lax.ppermute(array_up, axis, up)  7.22 us
    pallas_call x1, Pallas kernels, body(): pl.pallas_call(middle_down, out_shape=[shape(gz, 72, 128), shape(20, 48,...  7.22 us
  transfers between devices with their start and end apart: 13, of which 8 were waited for; matrix products, arithmetic and copies ran while one was open for 0% of the time, Pallas kernels for 4%

profile of v5, /device:TPU:33, one launch (start us, length us, event | category | flops | bytes accessed | tf_op | source)
XLA Modules:
  0.0 132.2 jit_solution(2279192392953026626)
XLA Ops:
  0.6 0.0 copy-start
  0.6 0.8 fusion.4
  1.5 0.1 copy-done
  1.6 0.0 copy-start.1
  1.6 4.1 %collective-permute-start = (f32[17,8,128]{2,1,0:T(8,128)S(1)}, f32[17,8,128]{2,1,0:T(8,128)S(1)}, u32[]{:S(2)}, u32[]{:S(2)}) collective-permute-start(f32[17,8,128]{2,1,0:T(8,128)S(1)} %pad_maximum_fusion.4), channel_id=1, source_target_pairs={{0,64},{64,128},{128,192},{192,256},{256,320},{320,384},{384,448},... | collective-permute-start | bytes 208904 | tf_op jit(solution)/shard_map/ppermute | solution.py:451
  5.8 1.3 collective-permute-start.1
  7.1 0.0 collective-permute-done.before_ref
  7.1 4.4 %collective-permute-done.1.after_ref = f32[17,8,128]{2,1,0:T(8,128)S(1)} collective-permute-done((f32[17,8,128]{2,1,0:T(8,128)S(1)}, f32[17,8,128]{2,1,0:T(8,128)S(1)}, u32[]{:S(2)}, u32[]{:S(2)}) %collective-permute-start.1) | collective-permute-done | bytes 69664 | tf_op jit(solution)/shard_map/ppermute | solution.py:451
  11.5 0.0 copy-done.1
  11.5 0.1 shard_map.41
  11.6 4.8 %collective-permute-start.2 = (f32[10,48,128]{2,1,0:T(8,128)S(1)}, f32[10,48,128]{2,1,0:T(8,128)S(1)}, u32[]{:S(2)}, u32[]{:S(2)}) collective-permute-start(f32[10,48,128]{2,1,0:T(8,128)S(1)} %get-tuple-element.15), channel_id=1, source_target_pairs={{0,1},{1,2},{2,3},{3,4},{4,5},{5,6},{6,7},{7,8},{8,9},{9,10},{10,1... | collective-permute-start | bytes 737288 | tf_op jit(solution)/shard_map/ppermute | solution.py:451
  16.4 1.9 %collective-permute-start.3 = (f32[10,48,128]{2,1,0:T(8,128)S(1)}, f32[10,48,128]{2,1,0:T(8,128)S(1)}, u32[]{:S(2)}, u32[]{:S(2)}) collective-permute-start(f32[10,48,128]{2,1,0:T(8,128)S(1)} %get-tuple-element.16), channel_id=1, source_target_pairs={{1,0},{2,1},{3,2},{4,3},{5,4},{6,5},{7,6},{8,7},{9,8},{10,9},{11,1... | collective-permute-start | bytes 737288 | tf_op jit(solution)/shard_map/ppermute | solution.py:451
  18.3 1.2 collective-permute-done.2.before_ref.rim_before_ref
  19.5 4.4 %collective-permute-done.3.after_ref.rim_after_ref = f32[10,48,128]{2,1,0:T(8,128)S(1)} collective-permute-done((f32[10,48,128]{2,1,0:T(8,128)S(1)}, f32[10,48,128]{2,1,0:T(8,128)S(1)}, u32[]{:S(2)}, u32[]{:S(2)}) %collective-permute-start.3) | collective-permute-done | bytes 245792 | tf_op jit(solution)/shard_map/ppermute | solution.py:451
  23.9 3.3 %shard_map.42 = (f32[4,64,128]{2,1,0:T(8,128)S(1)}, f32[3,48,128]{2,1,0:T(8,128)S(1)}, f32[3,48,128]{2,1,0:T(8,128)S(1)}, f32[4,64,128]{2,1,0:T(8,128)S(1)}) custom-call(f32[8,64,128]{2,1,0:T(8,128)S(1)} %get-tuple-element.13.s_ref, f32[8,64,128]{2,1,0:T(8,128)S(1)} %get-tuple-element.14.d_ref, ...), custom_call_target="tpu_custom_call" | custom-call | tf_op jit(solution)/shard_map/pallas_call | solution.py:485
  27.2 8.0 %all_to_all.15 = f32[4,64,128]{2,1,0:T(8,128)S(1)} all-to-all(f32[4,64,128]{2,1,0:T(8,128)S(1)} %get-tuple-element.17), channel_id=1, replica_groups={{0,1,2,3},{4,5,6,7},{8,9,10,11},{12,13,14,15},{16,17,18,19},{20,21,22,2..., dimensions={0} | all-to-all | bytes 262144 | tf_op jit(solution)/shard_map/all_to_all | solution.py:493
  35.3 3.6 %collective-permute-start.4 = (f32[13,16,128]{2,1,0:T(8,128)S(1)}, f32[13,16,128]{2,1,0:T(8,128)S(1)}, u32[]{:S(2)}, u32[]{:S(2)}) collective-permute-start(f32[13,16,128]{2,1,0:T(8,128)S(1)} %get-tuple-element.26), channel_id=1, source_target_pairs={{0,7},{1,6},{2,5},{3,4},{4,11},{5,10},{6,9},{7,8},{8,15},{9,14},{1... | collective-permute-start | bytes 319496 | tf_op jit(solution)/shard_map/ppermute | solution.py:451
  38.9 5.3 %collective-permute-start.5 = (f32[13,16,128]{2,1,0:T(8,128)S(1)}, f32[13,16,128]{2,1,0:T(8,128)S(1)}, u32[]{:S(2)}, u32[]{:S(2)}) collective-permute-start(f32[13,16,128]{2,1,0:T(8,128)S(1)} %get-tuple-element.27), channel_id=1, source_target_pairs={{7,0},{6,1},{5,2},{4,3},{11,4},{10,5},{9,6},{8,7},{15,8},{14,9},{1... | collective-permute-start | bytes 319496 | tf_op jit(solution)/shard_map/ppermute | solution.py:451
  44.2 1.6 %collective-permute-done.4 = f32[13,16,128]{2,1,0:T(8,128)S(1)} collective-permute-done((f32[13,16,128]{2,1,0:T(8,128)S(1)}, f32[13,16,128]{2,1,0:T(8,128)S(1)}, u32[]{:S(2)}, u32[]{:S(2)}) %collective-permute-start.4) | collective-permute-done | bytes 106528 | tf_op jit(solution)/shard_map/ppermute | solution.py:451
  45.8 2.5 %collective-permute-done.5 = f32[13,16,128]{2,1,0:T(8,128)S(1)} collective-permute-done((f32[13,16,128]{2,1,0:T(8,128)S(1)}, f32[13,16,128]{2,1,0:T(8,128)S(1)}, u32[]{:S(2)}, u32[]{:S(2)}) %collective-permute-start.5) | collective-permute-done | bytes 106528 | tf_op jit(solution)/shard_map/ppermute | solution.py:451
  48.4 1.3 collective-permute-start.7
  49.7 4.6 %collective-permute-start.6 = (f32[544,128]{1,0:T(8,128)S(1)}, f32[544,128]{1,0:T(8,128)S(1)}, u32[]{:S(2)}, u32[]{:S(2)}) collective-permute-start(f32[544,128]{1,0:T(8,128)S(1)} %get-tuple-element.25), channel_id=1, source_target_pairs={{0,64},{64,128},{128,192},{192,256},{256,320},{320,384},{384,448},... | collective-permute-start | bytes 835592 | tf_op jit(solution)/shard_map/ppermute | solution.py:451
  54.3 0.1 pad_add_fusion.place_ref
  54.4 4.7 %collective-permute-done.7.after_ref = f32[544,128]{1,0:T(8,128)S(1)} collective-permute-done((f32[544,128]{1,0:T(8,128)S(1)}, f32[544,128]{1,0:T(8,128)S(1)}, u32[]{:S(2)}, u32[]{:S(2)}) %collective-permute-start.7) | collective-permute-done | bytes 278560 | tf_op jit(solution)/shard_map/ppermute | solution.py:451
  59.1 0.9 collective-permute-done.6.before_ref
  59.9 7.2 %shard_map.43 = (f32[8,72,128]{2,1,0:T(8,128)S(1)}, f32[20,48,128]{2,1,0:T(8,128)S(1)}, f32[10,24,128]{2,1,0:T(8,128)S(1)}) custom-call(s32[3]{0:T(128)S(1)} %pad_add_fusion.place_ref, f32[42,16,128]{2,1,0:T(8,128)S(1)} %pad_maximum_fusion.window_ref, f32[544,128]{1,0:T(8,128)S(1)} %collective-permute-done.6.before_ref, ...), custom_call_target="tpu_custom_call" | custom-call | tf_op jit(solution)/shard_map/pallas_call | solution.py:503
  67.2 22.4 %all_to_all.16 = f32[8,72,128]{2,1,0:T(8,128)S(1)} all-to-all(f32[8,72,128]{2,1,0:T(8,128)S(1)} %get-tuple-element.18), channel_id=1, replica_groups=mesh['gz'=8,'xy'=64] {'gz'}, dimensions={0} | all-to-all | bytes 589824 | tf_op jit(solution)/shard_map/all_to_all | solution.py:516
  89.5 0.8 broadcast_in_dim.16
  90.3 6.9 %all-to-all-start.2 = ((f32[16,8,4,128]{3,2,1,0:T(4,128)}), f32[16,8,4,128]{3,2,1,0:T(4,128)S(1)}, u32[]{:S(2)}, u32[]{:S(2)}) async-start(f32[16,8,4,128]{3,2,1,0:T(4,128)} %broadcast_in_dim.16), calls=%async_computation.2 | async-start | bytes 524288 | tf_op jit(solution)/shard_map/all_to_all | solution.py:518
  97.2 10.8 %collective-permute-start.9 = (f32[8,24,128]{2,1,0:T(8,128)S(1)}, f32[8,24,128]{2,1,0:T(8,128)S(1)}, u32[]{:S(2)}, u32[]{:S(2)}) collective-permute-start(f32[8,24,128]{2,1,0:T(8,128)S(1)} %copy_bitcast_fusion), channel_id=1, source_target_pairs={{7,0},{6,1},{5,2},{4,3},{11,4},{10,5},{9,6},{8,7},{15,8},{14,9},{1... | collective-permute-start | bytes 294920 | tf_op jit(solution)/shard_map/ppermute | solution.py:451
  108.0 1.9 %collective-permute-start.8 = (f32[8,24,128]{2,1,0:T(8,128)S(1)}, f32[8,24,128]{2,1,0:T(8,128)S(1)}, u32[]{:S(2)}, u32[]{:S(2)}) collective-permute-start(f32[8,24,128]{2,1,0:T(8,128)S(1)} %copy_bitcast_fusion), channel_id=1, source_target_pairs={{0,7},{1,6},{2,5},{3,4},{4,11},{5,10},{6,9},{7,8},{8,15},{9,14},{1... | collective-permute-start | bytes 294920 | tf_op jit(solution)/shard_map/ppermute | solution.py:451
  109.9 1.9 %collective-permute-start.10 = (f32[3,48,128]{2,1,0:T(8,128)S(1)}, f32[3,48,128]{2,1,0:T(8,128)S(1)}, u32[]{:S(2)}, u32[]{:S(2)}) collective-permute-start(f32[3,48,128]{2,1,0:T(8,128)S(1)} %get-tuple-element.22), channel_id=1, source_target_pairs={{0,1},{1,2},{2,3},{3,4},{4,5},{5,6},{6,7},{7,8},{8,9},{9,10},{10,1... | collective-permute-start | bytes 221192 | tf_op jit(solution)/shard_map/ppermute | solution.py:451
  111.8 2.4 %collective-permute-start.11 = (f32[3,48,128]{2,1,0:T(8,128)S(1)}, f32[3,48,128]{2,1,0:T(8,128)S(1)}, u32[]{:S(2)}, u32[]{:S(2)}) collective-permute-start(f32[3,48,128]{2,1,0:T(8,128)S(1)} %get-tuple-element.23), channel_id=1, source_target_pairs={{1,0},{2,1},{3,2},{4,3},{5,4},{6,5},{7,6},{8,7},{9,8},{10,9},{11,1... | collective-permute-start | bytes 221192 | tf_op jit(solution)/shard_map/ppermute | solution.py:451
  114.2 0.0 collective-permute-done.9
  114.3 3.5 %collective-permute-done.8 = f32[8,24,128]{2,1,0:T(8,128)S(1)} collective-permute-done((f32[8,24,128]{2,1,0:T(8,128)S(1)}, f32[8,24,128]{2,1,0:T(8,128)S(1)}, u32[]{:S(2)}, u32[]{:S(2)}) %collective-permute-start.8) | collective-permute-done | bytes 98336 | tf_op jit(solution)/shard_map/ppermute | solution.py:451
  117.8 0.0 all-to-all-done.2.gathered_ref
  117.8 5.6 %shard_map.44.near_ref = f32[12,8,128]{2,1,0:T(8,128)S(1)} custom-call(s32[3]{0:T(128)S(1)} %pad_add_fusion.place_ref, f32[16,8,4,128]{3,2,1,0:T(4,128)S(1)} %all-to-all-done.2.gathered_ref), custom_call_target="tpu_custom_call" | custom-call | flops 100000000 | bytes 16000000 | tf_op jit(solution)/shard_map/pallas_call | solution.py:527
  123.4 0.0 collective-permute-done.10.before_ref
  123.4 0.0 collective-permute-done.11.after_ref
  123.4 8.8 %shard_map.45 = (f32[32,8,128]{2,1,0:T(8,128)}, f32[32,8,128]{2,1,0:T(8,128)}) custom-call(s32[3]{0:T(128)S(1)} %pad_add_fusion.place_ref, f32[12,8,128]{2,1,0:T(8,128)S(1)} %shard_map.44.near_ref, f32[24,24,128]{2,1,0:T(8,128)S(1)} %pad_maximum_fusion.1.halo_ref, f32[20,48,128]{2,1,0:T(8,128)S(1)} %get-tuple-element.19.kept_ref, ...), custom_call_target="tpu_custom_call" | custom-call | tf_op jit(solution)/shard_map/pallas_call | solution.py:536
  (14 shorter events, 0.2 us)
Async XLA Ops:
  0.6 0.9 copy-start
  1.6 9.9 %copy-start.1 = (f32[32,8,128]{2,1,0:T(8,128)S(1)}, f32[32,8,128]{2,1,0:T(8,128)}, u32[]{:S(2)}) copy-start(f32[32,8,128]{2,1,0:T(8,128)} %right_ref.1) | copy-start | bytes 393220
  1.6 5.5 %collective-permute-start = (f32[17,8,128]{2,1,0:T(8,128)S(1)}, f32[17,8,128]{2,1,0:T(8,128)S(1)}, u32[]{:S(2)}, u32[]{:S(2)}) collective-permute-start(f32[17,8,128]{2,1,0:T(8,128)S(1)} %pad_maximum_fusion.4), channel_id=1, source_target_pairs={{0,64},{64,128},{128,192},{192,256},{256,320},{320,384},{384,448},... | collective-permute-start | bytes 208904 | tf_op jit(solution)/shard_map/ppermute | solution.py:451
  5.8 5.7 %collective-permute-start.1 = (f32[17,8,128]{2,1,0:T(8,128)S(1)}, f32[17,8,128]{2,1,0:T(8,128)S(1)}, u32[]{:S(2)}, u32[]{:S(2)}) collective-permute-start(f32[17,8,128]{2,1,0:T(8,128)S(1)} %pad_maximum_fusion.5), channel_id=1, source_target_pairs={{64,0},{128,64},{192,128},{256,192},{320,256},{384,320},{448,384},... | collective-permute-start | bytes 208904 | tf_op jit(solution)/shard_map/ppermute | solution.py:451
  11.6 8.0 %collective-permute-start.2 = (f32[10,48,128]{2,1,0:T(8,128)S(1)}, f32[10,48,128]{2,1,0:T(8,128)S(1)}, u32[]{:S(2)}, u32[]{:S(2)}) collective-permute-start(f32[10,48,128]{2,1,0:T(8,128)S(1)} %get-tuple-element.15), channel_id=1, source_target_pairs={{0,1},{1,2},{2,3},{3,4},{4,5},{5,6},{6,7},{7,8},{8,9},{9,10},{10,1... | collective-permute-start | bytes 737288 | tf_op jit(solution)/shard_map/ppermute | solution.py:451
  16.4 7.5 %collective-permute-start.3 = (f32[10,48,128]{2,1,0:T(8,128)S(1)}, f32[10,48,128]{2,1,0:T(8,128)S(1)}, u32[]{:S(2)}, u32[]{:S(2)}) collective-permute-start(f32[10,48,128]{2,1,0:T(8,128)S(1)} %get-tuple-element.16), channel_id=1, source_target_pairs={{1,0},{2,1},{3,2},{4,3},{5,4},{6,5},{7,6},{8,7},{9,8},{10,9},{11,1... | collective-permute-start | bytes 737288 | tf_op jit(solution)/shard_map/ppermute | solution.py:451
  35.3 10.5 %collective-permute-start.4 = (f32[13,16,128]{2,1,0:T(8,128)S(1)}, f32[13,16,128]{2,1,0:T(8,128)S(1)}, u32[]{:S(2)}, u32[]{:S(2)}) collective-permute-start(f32[13,16,128]{2,1,0:T(8,128)S(1)} %get-tuple-element.26), channel_id=1, source_target_pairs={{0,7},{1,6},{2,5},{3,4},{4,11},{5,10},{6,9},{7,8},{8,15},{9,14},{1... | collective-permute-start | bytes 319496 | tf_op jit(solution)/shard_map/ppermute | solution.py:451
  38.9 9.4 %collective-permute-start.5 = (f32[13,16,128]{2,1,0:T(8,128)S(1)}, f32[13,16,128]{2,1,0:T(8,128)S(1)}, u32[]{:S(2)}, u32[]{:S(2)}) collective-permute-start(f32[13,16,128]{2,1,0:T(8,128)S(1)} %get-tuple-element.27), channel_id=1, source_target_pairs={{7,0},{6,1},{5,2},{4,3},{11,4},{10,5},{9,6},{8,7},{15,8},{14,9},{1... | collective-permute-start | bytes 319496 | tf_op jit(solution)/shard_map/ppermute | solution.py:451
  48.4 10.7 %collective-permute-start.7 = (f32[544,128]{1,0:T(8,128)S(1)}, f32[544,128]{1,0:T(8,128)S(1)}, u32[]{:S(2)}, u32[]{:S(2)}) collective-permute-start(f32[544,128]{1,0:T(8,128)S(1)} %get-tuple-element.24), channel_id=1, source_target_pairs={{64,0},{128,64},{192,128},{256,192},{320,256},{384,320},{448,384},... | collective-permute-start | bytes 835592 | tf_op jit(solution)/shard_map/ppermute | solution.py:451
  49.7 10.3 %collective-permute-start.6 = (f32[544,128]{1,0:T(8,128)S(1)}, f32[544,128]{1,0:T(8,128)S(1)}, u32[]{:S(2)}, u32[]{:S(2)}) collective-permute-start(f32[544,128]{1,0:T(8,128)S(1)} %get-tuple-element.25), channel_id=1, source_target_pairs={{0,64},{64,128},{128,192},{192,256},{256,320},{320,384},{384,448},... | collective-permute-start | bytes 835592 | tf_op jit(solution)/shard_map/ppermute | solution.py:451
  90.3 27.5 %all-to-all-start.2 = ((f32[16,8,4,128]{3,2,1,0:T(4,128)}), f32[16,8,4,128]{3,2,1,0:T(4,128)S(1)}, u32[]{:S(2)}, u32[]{:S(2)}) async-start(f32[16,8,4,128]{3,2,1,0:T(4,128)} %broadcast_in_dim.16), calls=%async_computation.2 | async-start | bytes 524288 | tf_op jit(solution)/shard_map/all_to_all | solution.py:518
  97.2 17.0 %collective-permute-start.9 = (f32[8,24,128]{2,1,0:T(8,128)S(1)}, f32[8,24,128]{2,1,0:T(8,128)S(1)}, u32[]{:S(2)}, u32[]{:S(2)}) collective-permute-start(f32[8,24,128]{2,1,0:T(8,128)S(1)} %copy_bitcast_fusion), channel_id=1, source_target_pairs={{7,0},{6,1},{5,2},{4,3},{11,4},{10,5},{9,6},{8,7},{15,8},{14,9},{1... | collective-permute-start | bytes 294920 | tf_op jit(solution)/shard_map/ppermute | solution.py:451
  108.0 9.8 %collective-permute-start.8 = (f32[8,24,128]{2,1,0:T(8,128)S(1)}, f32[8,24,128]{2,1,0:T(8,128)S(1)}, u32[]{:S(2)}, u32[]{:S(2)}) collective-permute-start(f32[8,24,128]{2,1,0:T(8,128)S(1)} %copy_bitcast_fusion), channel_id=1, source_target_pairs={{0,7},{1,6},{2,5},{3,4},{4,11},{5,10},{6,9},{7,8},{8,15},{9,14},{1... | collective-permute-start | bytes 294920 | tf_op jit(solution)/shard_map/ppermute | solution.py:451
  109.9 13.5 %collective-permute-start.10 = (f32[3,48,128]{2,1,0:T(8,128)S(1)}, f32[3,48,128]{2,1,0:T(8,128)S(1)}, u32[]{:S(2)}, u32[]{:S(2)}) collective-permute-start(f32[3,48,128]{2,1,0:T(8,128)S(1)} %get-tuple-element.22), channel_id=1, source_target_pairs={{0,1},{1,2},{2,3},{3,4},{4,5},{5,6},{6,7},{7,8},{8,9},{9,10},{10,1... | collective-permute-start | bytes 221192 | tf_op jit(solution)/shard_map/ppermute | solution.py:451
  111.8 11.6 %collective-permute-start.11 = (f32[3,48,128]{2,1,0:T(8,128)S(1)}, f32[3,48,128]{2,1,0:T(8,128)S(1)}, u32[]{:S(2)}, u32[]{:S(2)}) collective-permute-start(f32[3,48,128]{2,1,0:T(8,128)S(1)} %get-tuple-element.23), channel_id=1, source_target_pairs={{1,0},{2,1},{3,2},{4,3},{5,4},{6,5},{7,6},{8,7},{9,8},{10,9},{11,1... | collective-permute-start | bytes 221192 | tf_op jit(solution)/shard_map/ppermute | solution.py:451

commit v6 on v5

--- a/solution.py
+++ b/solution.py
@@ -138,8 +138,8 @@
         at, keep = pl.ds(j, block), self.keep
         other = self.value.at[1 - colour]
         w = other[at]
-        mask = self.odd if colour else jnp.logical_not(self.odd)
-        side = self.choose(mask, other[pl.ds(j - 1, block)], other[pl.ds(j + 1, block)])
+        before, after = other[pl.ds(j - 1, block)], other[pl.ds(j + 1, block)]
+        side = self.choose(self.odd, before, after) if colour else self.choose(self.odd, after, before)
         total = keep[INNER, at] * w + keep[OUT + colour, at] * side
         total += keep[LOWER + colour, at] * self.low(w) + keep[UPPER + colour, at] * self.high(w)
         total += keep[LEFT + colour, at] * pltpu.roll(w, 1, 2) + keep[RIGHT + colour, at] * pltpu.roll(w, 127, 2)
@@ -208,8 +208,8 @@
     density[6:14] = d_ref[...]
 
 
-def finest_down(s_ref, d_ref, before_ref, after_ref, chunk_ref, low_ref, high_ref, below_ref,
-                source, density, keep, value, plane):
+def finest_down(s_ref, d_ref, before_ref, after_ref, chunk_ref, low_ref, high_ref, below_ref, keep,
+                source, density, value, plane):
     finest_window(s_ref, d_ref, before_ref, after_ref, source, density)
     level = Level(density, keep, value, 128)
     level.clear((0, 9))
@@ -244,8 +244,8 @@
     density[start] = jnp.where(left, pltpu.roll(near, 64, 2), far)
 
 
-def middle_down(place_ref, window_ref, before_ref, after_ref, chunk_ref, kept_ref, below_ref,
-                window, source, density, keep, value, plane, source2, density2, keep2, value2):
+def middle_down(place_ref, window_ref, before_ref, after_ref, chunk_ref, below_ref, keep,
+                window, source, density, value, plane, source2, density2, keep2, value2):
     window[1:43, 16:32] = window_ref[...]
     for ref, near, far in ((before_ref, 0, 8), (after_ref, 32, 32)):
         window[9:35, near : near + 16] = ref[0:416].reshape(26, 16, 128)
@@ -265,7 +265,6 @@
     level.half(1, 1, 20, 5)
     level.half(0, 2, 18, 6)
     level.half(1, 2, 18, 6)
-    kept_ref[...] = window[pl.ds(6 + 4 * place_ref[2], 20)]
     below_ref[...] = value[1, pl.ds(3 + 2 * place_ref[2], 10)]
 
     def pooling(j):
@@ -325,20 +324,24 @@
     for row in (0, 1, planes + 2, planes + 3):
         density[row] = jnp.zeros((8, 128), F32)
 
-    def spread(g, _):
+    def spread(g):
         tiles = [
             jnp.concatenate([gathered_ref[2 * h, g], gathered_ref[2 * h + 1, g]], axis=0) for h in range(groups // 2)
         ]
-        for part, ref in enumerate((source, density)):
-            for z in range(4):
-                out = jnp.zeros((8, 128), F32)
-                for h, block in enumerate(tiles):
-                    moved = pltpu.roll(block, (16 * (h - z) - 64 * part) % 128, 1)
-                    out = jnp.where(lane // 16 == h, moved, out)
-                ref[2 + 4 * g + z] = out
-        return 0
-
-    lax.fori_loop(0, planes // 4, spread, 0)
+        tiles += [jnp.zeros((8, 128), F32)] * (8 - len(tiles))
+        for step in (1, 2, 4):
+            upper = (lane // 16) % (2 * step) >= step
+            for i in range(8):
+                if i % (2 * step) < step:
+                    a, b = tiles[i], tiles[i + step]
+                    tiles[i] = jnp.where(upper, pltpu.roll(b, 16 * step, 1), a)
+                    tiles[i + step] = jnp.where(upper, b, pltpu.roll(a, 128 - 16 * step, 1))
+        for z in range(4):
+            source[2 + 4 * g + z] = tiles[z]
+            density[2 + 4 * g + z] = tiles[4 + z]
+
+    for g in range(planes // 4):
+        spread(g)
     level = Level(density, keep, value, 16, 16, ends=True)
     pairs = planes // 2
     value[...] = jnp.zeros(value.shape, F32)
@@ -359,11 +362,9 @@
     near_ref[...] = wide[pl.ds(4 * place_ref[0], 12)]
 
 
-def way_up(devices, place_ref, near_ref, halo_ref, kept_ref, below1_ref,
-           s_ref, d_ref, rim_before_ref, rim_after_ref, below0_ref, before_ref, after_ref,
+def way_up(devices, place_ref, near_ref, halo_ref, keep1, below1_ref, keep0, below0_ref, before_ref, after_ref,
            pressure_ref, remain_ref,
-           source2, density2, keep2, value2, source1, density1, keep1, value1,
-           source0, density0, keep0, value0, plane):
+           source2, density2, keep2, value2, value1, value0, plane):
     at_y, at_group = place_ref[1], place_ref[2]
 
     block = halo_ref[pl.ds(2 * at_group, 18)]
@@ -397,26 +398,24 @@
     level.half(1, 3, 5, 5)
     even, odd = level.rows(value2[0, 3:8], value2[1, 3:8])
 
-    blocks(0, 20, 4, lambda r: folded(kept_ref, pl.ds(r, 4), source1, density1, pl.ds(r, 4)))
-    level = Level(density1, keep1, value1, 64, 64)
-    level.coefficients(source1, 4.0, 1, 8, 2)
+    first = 3 + 2 * at_group
+    level = Level(None, keep1, value1, 64, 64)
     rows = jnp.stack([even, odd], axis=1).reshape(240, 128)
     spread = dot(rows, doubling(32, 0, 64)).reshape(10, 24, 128)
     plane[0:10, pl.ds(0, 24, stride=2)] = spread
     plane[0:10, pl.ds(1, 24, stride=2)] = spread
     left = iota((10, 24, 128), 2) < 64
-    value1[1] = below1_ref[...] + jnp.where(left, plane[0:10, 0:24], plane[0:10, 24:48])
-    level.clear_red((0, 9))
-    level.half(0, 1, 8, 4)
-    level.half(1, 1, 8, 4)
-    level.half(0, 2, 6, 6)
-    level.half(1, 2, 6, 6)
-    even, odd = level.rows(value1[0, 2:8], value1[1, 2:8])
+    value1[1, pl.ds(first, 10)] = below1_ref[...] + jnp.where(left, plane[0:10, 0:24], plane[0:10, 24:48])
+    level.clear_red((first, first + 9))
+    level.half(0, first + 1, 8, 4)
+    level.half(1, first + 1, 8, 4)
+    level.half(0, first + 2, 6, 6)
+    level.half(1, first + 2, 6, 6)
+    inside = pl.ds(first + 2, 6)
+    even, odd = level.rows(value1[0, inside], value1[1, inside])
     rows = jnp.stack([even, odd], axis=1).reshape(12, 24, 128)[1:11]
 
-    finest_window(s_ref, d_ref, rim_before_ref, rim_after_ref, source0, density0)
-    level = Level(density0, keep0, value0, 128)
-    level.coefficients(source0, 1.0, 1, 8, 1)
+    level = Level(None, keep0, value0, 128)
     near = dot(rows[:, 8:24].reshape(160, 128), doubling(64)).reshape(10, 16, 128)
     far = dot(rows[:, 0:16].reshape(160, 128), doubling(64, 64)).reshape(10, 16, 128)
     for start, part in ((0, near), (32, far)):
@@ -482,10 +481,10 @@
     at_group = lax.axis_index("xy") % GROUP
     place = jnp.stack([lax.axis_index("gz"), lax.axis_index("xy"), at_group]).astype(jnp.int32)
     smem, block = pl.BlockSpec(memory_space=pltpu.SMEM), pl.BlockSpec(memory_space=pltpu.VMEM)
-    chunks, first_rows, last_rows, below0 = pl.pallas_call(
+    chunks, first_rows, last_rows, below0, keep0 = pl.pallas_call(
         finest_down,
-        out_shape=[shape(GROUP, 64, 128), shape(3, 48, 128), shape(3, 48, 128), shape(4, 64, 128)],
-        scratch_shapes=[vmem(20, 64, 128)] * 2 + [vmem(KEPT, 10, 64, 128), vmem(2, 10, 64, 128), vmem(8, 32, 128)],
+        out_shape=[shape(GROUP, 64, 128), shape(3, 48, 128), shape(3, 48, 128), shape(4, 64, 128), shape(KEPT, 10, 64, 128)],
+        scratch_shapes=[vmem(20, 64, 128)] * 2 + [vmem(2, 10, 64, 128), vmem(8, 32, 128)],
         compiler_params=params(),
     )(*finest)
 
@@ -500,13 +499,13 @@
         return jnp.concatenate([part.reshape(-1, 128) for part in parts], axis=0)
 
     before, after = pair(faces(slice(8, 16)), faces(slice(0, 8)), "gz")
-    chunks, kept, below1 = pl.pallas_call(
+    chunks, below1, keep1 = pl.pallas_call(
         middle_down,
-        out_shape=[shape(gz, 72, 128), shape(20, 48, 128), shape(10, 24, 128)],
+        out_shape=[shape(gz, 72, 128), shape(10, 24, 128), shape(KEPT, 22, 24, 128)],
         in_specs=[smem] + [block] * 3,
         scratch_shapes=[vmem(44, 48, 128)]
         + [vmem(44, 24, 128)] * 2
-        + [vmem(KEPT, 22, 24, 128), vmem(2, 22, 24, 128), vmem(34, 32, 128)]
+        + [vmem(2, 22, 24, 128), vmem(34, 32, 128)]
         + [vmem(20, 24, 128)] * 2
         + [vmem(KEPT, 10, 24, 128), vmem(2, 10, 24, 128)],
         compiler_params=params(),
@@ -536,15 +535,12 @@
     return pl.pallas_call(
         partial(way_up, xy),
         out_shape=[shape(32, 8, 128)] * 2,
-        in_specs=[smem] + [block] * 11,
+        in_specs=[smem] + [block] * 8,
         scratch_shapes=[vmem(22, 24, 128)] * 2
         + [vmem(KEPT, 11, 24, 128), vmem(2, 11, 24, 128)]
-        + [vmem(20, 24, 128)] * 2
-        + [vmem(KEPT, 10, 24, 128), vmem(2, 10, 24, 128)]
-        + [vmem(20, 64, 128)] * 2
-        + [vmem(KEPT, 10, 64, 128), vmem(2, 10, 64, 128), vmem(10, 64, 128)],
+        + [vmem(2, 22, 24, 128), vmem(2, 10, 64, 128), vmem(10, 64, 128)],
         compiler_params=params(),
-    )(place, near, halo, kept, below1, *finest, below0, value_before, value_after)
+    )(place, near, halo, keep1, below1, keep0, below0, value_before, value_after)
 
 
 def solution(mesh):

time: 133 us -> 141 us (1.060)
  the two profiles are of different devices: /device:TPU:33 before, /device:TPU:31 now
where the time goes in v6:
time: 141 us; the launch traced here: 140 us
  starting transfers between devices  48.7 us (35%)
  blocking collectives  28.9 us (20%)
  waiting for transfers between devices  25.5 us (18%)
  Pallas kernels  21.5 us (15%)
  local copies, waits for them, and re-layouts  12.9 us (9%)
    ppermute x6, starting transfers between devices, pair(): lax.ppermute(array_up, axis, up)  26.7 us
    all_to_all x1, blocking collectives, body(): column = lax.all_to_all(chunks, 'gz', 0, 0, tiled=True)  23.3 us
    ppermute x6, waiting for transfers between devices, pair(): lax.ppermute(array_down, axis, down)  20.8 us
    ppermute x6, starting transfers between devices, pair(): lax.ppermute(array_down, axis, down)  15.1 us
    unnamed x12, local copies, waits for them, and re-layouts  11.2 us
    pallas_call x1, Pallas kernels, body(): pl.pallas_call(middle_down, out_shape=[shape(gz, 72, 128), shape(10, 24,...  7.22 us
    all_to_all x1, starting transfers between devices, body(): lax.all_to_all(jnp.broadcast_to(column[None, :, 64:68], (xy // GROUP, gz,...  6.96 us
    pallas_call x1, Pallas kernels, body(): pl.pallas_call(partial(way_up, xy), out_shape=[shape(32, 8, 128)] * 2, in...  6.05 us
  transfers between devices with their start and end apart: 13, of which 8 were waited for; matrix products, arithmetic and copies ran while one was open for 0% of the time, Pallas kernels for 4%

profile of v6, /device:TPU:31, one launch (start us, length us, event | category | flops | bytes accessed | tf_op | source)
XLA Modules:
  0.0 139.5 jit_solution(15304970696045007114)
XLA Ops:
  0.6 0.8 fusion.4
  1.4 0.9 compare_select_fusion
  2.4 4.0 %collective-permute-start = (f32[17,8,128]{2,1,0:T(8,128)S(1)}, f32[17,8,128]{2,1,0:T(8,128)S(1)}, u32[]{:S(2)}, u32[]{:S(2)}) collective-permute-start(f32[17,8,128]{2,1,0:T(8,128)S(1)} %pad_maximum_fusion.4), channel_id=1, source_target_pairs={{0,64},{64,128},{128,192},{192,256},{256,320},{320,384},{384,448},... | collective-permute-start | bytes 208904 | tf_op jit(solution)/shard_map/ppermute | solution.py:450
  6.4 1.3 collective-permute-start.1
  7.7 0.0 collective-permute-done.before_ref
  7.7 4.4 %collective-permute-done.1.after_ref = f32[17,8,128]{2,1,0:T(8,128)S(1)} collective-permute-done((f32[17,8,128]{2,1,0:T(8,128)S(1)}, f32[17,8,128]{2,1,0:T(8,128)S(1)}, u32[]{:S(2)}, u32[]{:S(2)}) %collective-permute-start.1) | collective-permute-done | bytes 69664 | tf_op jit(solution)/shard_map/ppermute | solution.py:450
  12.1 0.0 copy-start.4
  12.1 0.9 copy-done.4
  13.0 0.0 copy-start.5
  13.0 0.9 copy-done.5
  13.9 0.1 shard_map.41
  14.0 6.0 %collective-permute-start.2 = (f32[10,48,128]{2,1,0:T(8,128)S(1)}, f32[10,48,128]{2,1,0:T(8,128)S(1)}, u32[]{:S(2)}, u32[]{:S(2)}) collective-permute-start(f32[10,48,128]{2,1,0:T(8,128)S(1)} %get-tuple-element.16), channel_id=1, source_target_pairs={{0,1},{1,2},{2,3},{3,4},{4,5},{5,6},{6,7},{7,8},{8,9},{9,10},{10,1... | collective-permute-start | bytes 737288 | tf_op jit(solution)/shard_map/ppermute | solution.py:450
  20.0 1.9 %collective-permute-start.3 = (f32[10,48,128]{2,1,0:T(8,128)S(1)}, f32[10,48,128]{2,1,0:T(8,128)S(1)}, u32[]{:S(2)}, u32[]{:S(2)}) collective-permute-start(f32[10,48,128]{2,1,0:T(8,128)S(1)} %get-tuple-element.17), channel_id=1, source_target_pairs={{1,0},{2,1},{3,2},{4,3},{5,4},{6,5},{7,6},{8,7},{9,8},{10,9},{11,1... | collective-permute-start | bytes 737288 | tf_op jit(solution)/shard_map/ppermute | solution.py:450
  22.0 1.2 collective-permute-done.2.before_ref
  23.2 7.7 %collective-permute-done.3.after_ref = f32[10,48,128]{2,1,0:T(8,128)S(1)} collective-permute-done((f32[10,48,128]{2,1,0:T(8,128)S(1)}, f32[10,48,128]{2,1,0:T(8,128)S(1)}, u32[]{:S(2)}, u32[]{:S(2)}) %collective-permute-start.3) | collective-permute-done | bytes 245792 | tf_op jit(solution)/shard_map/ppermute | solution.py:450
  30.9 3.3 %shard_map.42 = (f32[4,64,128]{2,1,0:T(8,128)S(1)}, f32[3,48,128]{2,1,0:T(8,128)S(1)}, f32[3,48,128]{2,1,0:T(8,128)S(1)}, f32[4,64,128]{2,1,0:T(8,128)S(1)}, f32[17,10,64,128]{3,2,1,0:T(8,128)S(1)}) custom-call(f32[8,64,128]{2,1,0:T(8,128)S(1)} %get-tuple-element.14.s_ref, f32[8,64,128]{2,1,0:T(8,128)S(1)} %get-tuple-element.15.d_ref, ...), custom_call_target="tpu_custom_call" | custom-call | tf_op jit(solution)/shard_map/pallas_call | solution.py:484
  34.1 0.0 copy-start
  34.1 2.4 %copy-done = f32[17,10,64,128]{3,2,1,0:T(8,128)} copy-done((f32[17,10,64,128]{3,2,1,0:T(8,128)}, f32[17,10,64,128]{3,2,1,0:T(8,128)S(1)}, u32[]{:S(2)}) %copy-start) | copy-done | bytes 5570584
  36.6 5.6 %all_to_all.15 = f32[4,64,128]{2,1,0:T(8,128)S(1)} all-to-all(f32[4,64,128]{2,1,0:T(8,128)S(1)} %get-tuple-element.18), channel_id=1, replica_groups={{0,1,2,3},{4,5,6,7},{8,9,10,11},{12,13,14,15},{16,17,18,19},{20,21,22,2..., dimensions={0} | all-to-all | bytes 262144 | tf_op jit(solution)/shard_map/all_to_all | solution.py:492
  42.2 3.2 %collective-permute-start.4 = (f32[13,16,128]{2,1,0:T(8,128)S(1)}, f32[13,16,128]{2,1,0:T(8,128)S(1)}, u32[]{:S(2)}, u32[]{:S(2)}) collective-permute-start(f32[13,16,128]{2,1,0:T(8,128)S(1)} %get-tuple-element.28), channel_id=1, source_target_pairs={{0,7},{1,6},{2,5},{3,4},{4,11},{5,10},{6,9},{7,8},{8,15},{9,14},{1... | collective-permute-start | bytes 319496 | tf_op jit(solution)/shard_map/ppermute | solution.py:450
  45.3 3.6 %collective-permute-start.5 = (f32[13,16,128]{2,1,0:T(8,128)S(1)}, f32[13,16,128]{2,1,0:T(8,128)S(1)}, u32[]{:S(2)}, u32[]{:S(2)}) collective-permute-start(f32[13,16,128]{2,1,0:T(8,128)S(1)} %get-tuple-element.29), channel_id=1, source_target_pairs={{7,0},{6,1},{5,2},{4,3},{11,4},{10,5},{9,6},{8,7},{15,8},{14,9},{1... | collective-permute-start | bytes 319496 | tf_op jit(solution)/shard_map/ppermute | solution.py:450
  49.0 1.7 %collective-permute-done.4 = f32[13,16,128]{2,1,0:T(8,128)S(1)} collective-permute-done((f32[13,16,128]{2,1,0:T(8,128)S(1)}, f32[13,16,128]{2,1,0:T(8,128)S(1)}, u32[]{:S(2)}, u32[]{:S(2)}) %collective-permute-start.4) | collective-permute-done | bytes 106528 | tf_op jit(solution)/shard_map/ppermute | solution.py:450
  50.6 4.1 %collective-permute-done.5 = f32[13,16,128]{2,1,0:T(8,128)S(1)} collective-permute-done((f32[13,16,128]{2,1,0:T(8,128)S(1)}, f32[13,16,128]{2,1,0:T(8,128)S(1)}, u32[]{:S(2)}, u32[]{:S(2)}) %collective-permute-start.5) | collective-permute-done | bytes 106528 | tf_op jit(solution)/shard_map/ppermute | solution.py:450
  54.8 1.3 collective-permute-start.7
  56.1 4.6 %collective-permute-start.6 = (f32[544,128]{1,0:T(8,128)S(1)}, f32[544,128]{1,0:T(8,128)S(1)}, u32[]{:S(2)}, u32[]{:S(2)}) collective-permute-start(f32[544,128]{1,0:T(8,128)S(1)} %get-tuple-element.27), channel_id=1, source_target_pairs={{0,64},{64,128},{128,192},{192,256},{256,320},{320,384},{384,448},... | collective-permute-start | bytes 835592 | tf_op jit(solution)/shard_map/ppermute | solution.py:450
  60.8 0.1 pad_add_fusion.place_ref
  60.8 4.6 %collective-permute-done.7.after_ref = f32[544,128]{1,0:T(8,128)S(1)} collective-permute-done((f32[544,128]{1,0:T(8,128)S(1)}, f32[544,128]{1,0:T(8,128)S(1)}, u32[]{:S(2)}, u32[]{:S(2)}) %collective-permute-start.7) | collective-permute-done | bytes 278560 | tf_op jit(solution)/shard_map/ppermute | solution.py:450
  65.4 1.8 %collective-permute-done.6.before_ref = f32[544,128]{1,0:T(8,128)S(1)} collective-permute-done((f32[544,128]{1,0:T(8,128)S(1)}, f32[544,128]{1,0:T(8,128)S(1)}, u32[]{:S(2)}, u32[]{:S(2)}) %collective-permute-start.6) | collective-permute-done | bytes 278560 | tf_op jit(solution)/shard_map/ppermute | solution.py:450
  67.2 7.2 %shard_map.43 = (f32[8,72,128]{2,1,0:T(8,128)S(1)}, f32[10,24,128]{2,1,0:T(8,128)S(1)}, f32[17,22,24,128]{3,2,1,0:T(8,128)S(1)}) custom-call(s32[3]{0:T(128)S(1)} %pad_add_fusion.place_ref, f32[42,16,128]{2,1,0:T(8,128)S(1)} %pad_maximum_fusion.window_ref, f32[544,128]{1,0:T(8,128)S(1)} %collective-permute-done.6.before_ref, ...), custom_call_target="tpu_custom_call" | custom-call | tf_op jit(solution)/shard_map/pallas_call | solution.py:502
  74.4 0.0 copy-start.2
  74.4 2.1 %copy-done.2 = f32[17,22,24,128]{3,2,1,0:T(8,128)} copy-done((f32[17,22,24,128]{3,2,1,0:T(8,128)}, f32[17,22,24,128]{3,2,1,0:T(8,128)S(1)}, u32[]{:S(2)}) %copy-start.2) | copy-done | bytes 4595736
  76.6 23.3 %all_to_all.16 = f32[8,72,128]{2,1,0:T(8,128)S(1)} all-to-all(f32[8,72,128]{2,1,0:T(8,128)S(1)} %get-tuple-element.19), channel_id=1, replica_groups=mesh['gz'=8,'xy'=64] {'gz'}, dimensions={0} | all-to-all | bytes 589824 | tf_op jit(solution)/shard_map/all_to_all | solution.py:515
  99.9 0.8 broadcast_in_dim.16
  100.6 7.0 %all-to-all-start.2 = ((f32[16,8,4,128]{3,2,1,0:T(4,128)}), f32[16,8,4,128]{3,2,1,0:T(4,128)S(1)}, u32[]{:S(2)}, u32[]{:S(2)}) async-start(f32[16,8,4,128]{3,2,1,0:T(4,128)} %broadcast_in_dim.16), calls=%async_computation.2 | async-start | bytes 524288 | tf_op jit(solution)/shard_map/all_to_all | solution.py:517
  107.6 3.0 %collective-permute-start.9 = (f32[8,24,128]{2,1,0:T(8,128)S(1)}, f32[8,24,128]{2,1,0:T(8,128)S(1)}, u32[]{:S(2)}, u32[]{:S(2)}) collective-permute-start(f32[8,24,128]{2,1,0:T(8,128)S(1)} %copy_bitcast_fusion), channel_id=1, source_target_pairs={{7,0},{6,1},{5,2},{4,3},{11,4},{10,5},{9,6},{8,7},{15,8},{14,9},{1... | collective-permute-start | bytes 294920 | tf_op jit(solution)/shard_map/ppermute | solution.py:450
  110.7 5.9 %collective-permute-start.8 = (f32[8,24,128]{2,1,0:T(8,128)S(1)}, f32[8,24,128]{2,1,0:T(8,128)S(1)}, u32[]{:S(2)}, u32[]{:S(2)}) collective-permute-start(f32[8,24,128]{2,1,0:T(8,128)S(1)} %copy_bitcast_fusion), channel_id=1, source_target_pairs={{0,7},{1,6},{2,5},{3,4},{4,11},{5,10},{6,9},{7,8},{8,15},{9,14},{1... | collective-permute-start | bytes 294920 | tf_op jit(solution)/shard_map/ppermute | solution.py:450
  116.5 3.0 %collective-permute-start.10 = (f32[3,48,128]{2,1,0:T(8,128)S(1)}, f32[3,48,128]{2,1,0:T(8,128)S(1)}, u32[]{:S(2)}, u32[]{:S(2)}) collective-permute-start(f32[3,48,128]{2,1,0:T(8,128)S(1)} %get-tuple-element.24), channel_id=1, source_target_pairs={{0,1},{1,2},{2,3},{3,4},{4,5},{5,6},{6,7},{7,8},{8,9},{9,10},{10,1... | collective-permute-start | bytes 221192 | tf_op jit(solution)/shard_map/ppermute | solution.py:450
  119.6 3.9 %collective-permute-start.11 = (f32[3,48,128]{2,1,0:T(8,128)S(1)}, f32[3,48,128]{2,1,0:T(8,128)S(1)}, u32[]{:S(2)}, u32[]{:S(2)}) collective-permute-start(f32[3,48,128]{2,1,0:T(8,128)S(1)} %get-tuple-element.25), channel_id=1, source_target_pairs={{1,0},{2,1},{3,2},{4,3},{5,4},{6,5},{7,6},{8,7},{9,8},{10,9},{11,1... | collective-permute-start | bytes 221192 | tf_op jit(solution)/shard_map/ppermute | solution.py:450
  123.5 0.0 collective-permute-done.9
  123.5 0.0 collective-permute-done.8
  123.6 0.0 all-to-all-done.2.gathered_ref
  123.6 4.9 %shard_map.44.near_ref = f32[12,8,128]{2,1,0:T(8,128)S(1)} custom-call(s32[3]{0:T(128)S(1)} %pad_add_fusion.place_ref, f32[16,8,4,128]{3,2,1,0:T(4,128)S(1)} %all-to-all-done.2.gathered_ref), custom_call_target="tpu_custom_call" | custom-call | flops 100000000 | bytes 16000000 | tf_op jit(solution)/shard_map/pallas_call | solution.py:526
  128.5 0.0 collective-permute-done.10.before_ref
  128.5 0.1 collective-permute-done.11.after_ref
  128.6 0.0 copy-start.1
  128.6 2.6 %copy-done.1 = f32[17,10,64,128]{3,2,1,0:T(8,128)S(1)} copy-done((f32[17,10,64,128]{3,2,1,0:T(8,128)S(1)}, f32[17,10,64,128]{3,2,1,0:T(8,128)}, u32[]{:S(2)}) %copy-start.1) | copy-done | bytes 5570584
  131.2 2.3 %copy-done.3 = f32[17,22,24,128]{3,2,1,0:T(8,128)S(1)} copy-done((f32[17,22,24,128]{3,2,1,0:T(8,128)S(1)}, f32[17,22,24,128]{3,2,1,0:T(8,128)}, u32[]{:S(2)}) %copy-start.3) | copy-done | bytes 4595736
  133.5 6.0 %shard_map.45 = (f32[32,8,128]{2,1,0:T(8,128)}, f32[32,8,128]{2,1,0:T(8,128)}) custom-call(s32[3]{0:T(128)S(1)} %pad_add_fusion.place_ref, f32[12,8,128]{2,1,0:T(8,128)S(1)} %shard_map.44.near_ref, f32[24,24,128]{2,1,0:T(8,128)S(1)} %pad_maximum_fusion.1.halo_ref, f32[17,22,24,128]{3,2,1,0:T(8,128)S(1)} %copy-done.3, ...), custom_call_target="tpu_custom_call" | custom-call | tf_op jit(solution)/shard_map/pallas_call | solution.py:535
  (14 shorter events, 0.2 us)
Async XLA Ops:
  2.4 5.4 %collective-permute-start = (f32[17,8,128]{2,1,0:T(8,128)S(1)}, f32[17,8,128]{2,1,0:T(8,128)S(1)}, u32[]{:S(2)}, u32[]{:S(2)}) collective-permute-start(f32[17,8,128]{2,1,0:T(8,128)S(1)} %pad_maximum_fusion.4), channel_id=1, source_target_pairs={{0,64},{64,128},{128,192},{192,256},{256,320},{320,384},{384,448},... | collective-permute-start | bytes 208904 | tf_op jit(solution)/shard_map/ppermute | solution.py:450
  6.4 5.7 %collective-permute-start.1 = (f32[17,8,128]{2,1,0:T(8,128)S(1)}, f32[17,8,128]{2,1,0:T(8,128)S(1)}, u32[]{:S(2)}, u32[]{:S(2)}) collective-permute-start(f32[17,8,128]{2,1,0:T(8,128)S(1)} %pad_maximum_fusion.5), channel_id=1, source_target_pairs={{64,0},{128,64},{192,128},{256,192},{320,256},{384,320},{448,384},... | collective-permute-start | bytes 208904 | tf_op jit(solution)/shard_map/ppermute | solution.py:450
  12.1 0.9 copy-start.4
  13.0 0.9 copy-start.5
  14.0 9.2 %collective-permute-start.2 = (f32[10,48,128]{2,1,0:T(8,128)S(1)}, f32[10,48,128]{2,1,0:T(8,128)S(1)}, u32[]{:S(2)}, u32[]{:S(2)}) collective-permute-start(f32[10,48,128]{2,1,0:T(8,128)S(1)} %get-tuple-element.16), channel_id=1, source_target_pairs={{0,1},{1,2},{2,3},{3,4},{4,5},{5,6},{6,7},{7,8},{8,9},{9,10},{10,1... | collective-permute-start | bytes 737288 | tf_op jit(solution)/shard_map/ppermute | solution.py:450
  20.0 10.8 %collective-permute-start.3 = (f32[10,48,128]{2,1,0:T(8,128)S(1)}, f32[10,48,128]{2,1,0:T(8,128)S(1)}, u32[]{:S(2)}, u32[]{:S(2)}) collective-permute-start(f32[10,48,128]{2,1,0:T(8,128)S(1)} %get-tuple-element.17), channel_id=1, source_target_pairs={{1,0},{2,1},{3,2},{4,3},{5,4},{6,5},{7,6},{8,7},{9,8},{10,9},{11,1... | collective-permute-start | bytes 737288 | tf_op jit(solution)/shard_map/ppermute | solution.py:450
  34.1 2.4 %copy-start = (f32[17,10,64,128]{3,2,1,0:T(8,128)}, f32[17,10,64,128]{3,2,1,0:T(8,128)S(1)}, u32[]{:S(2)}) copy-start(f32[17,10,64,128]{3,2,1,0:T(8,128)S(1)} %get-tuple-element.22.keep0) | copy-start | bytes 16711684
  42.2 8.5 %collective-permute-start.4 = (f32[13,16,128]{2,1,0:T(8,128)S(1)}, f32[13,16,128]{2,1,0:T(8,128)S(1)}, u32[]{:S(2)}, u32[]{:S(2)}) collective-permute-start(f32[13,16,128]{2,1,0:T(8,128)S(1)} %get-tuple-element.28), channel_id=1, source_target_pairs={{0,7},{1,6},{2,5},{3,4},{4,11},{5,10},{6,9},{7,8},{8,15},{9,14},{1... | collective-permute-start | bytes 319496 | tf_op jit(solution)/shard_map/ppermute | solution.py:450
  45.3 9.3 %collective-permute-start.5 = (f32[13,16,128]{2,1,0:T(8,128)S(1)}, f32[13,16,128]{2,1,0:T(8,128)S(1)}, u32[]{:S(2)}, u32[]{:S(2)}) collective-permute-start(f32[13,16,128]{2,1,0:T(8,128)S(1)} %get-tuple-element.29), channel_id=1, source_target_pairs={{7,0},{6,1},{5,2},{4,3},{11,4},{10,5},{9,6},{8,7},{15,8},{14,9},{1... | collective-permute-start | bytes 319496 | tf_op jit(solution)/shard_map/ppermute | solution.py:450
  54.8 10.6 %collective-permute-start.7 = (f32[544,128]{1,0:T(8,128)S(1)}, f32[544,128]{1,0:T(8,128)S(1)}, u32[]{:S(2)}, u32[]{:S(2)}) collective-permute-start(f32[544,128]{1,0:T(8,128)S(1)} %get-tuple-element.26), channel_id=1, source_target_pairs={{64,0},{128,64},{192,128},{256,192},{320,256},{384,320},{448,384},... | collective-permute-start | bytes 835592 | tf_op jit(solution)/shard_map/ppermute | solution.py:450
  56.1 11.1 %collective-permute-start.6 = (f32[544,128]{1,0:T(8,128)S(1)}, f32[544,128]{1,0:T(8,128)S(1)}, u32[]{:S(2)}, u32[]{:S(2)}) collective-permute-start(f32[544,128]{1,0:T(8,128)S(1)} %get-tuple-element.27), channel_id=1, source_target_pairs={{0,64},{64,128},{128,192},{192,256},{256,320},{320,384},{384,448},... | collective-permute-start | bytes 835592 | tf_op jit(solution)/shard_map/ppermute | solution.py:450
  74.4 2.1 %copy-start.2 = (f32[17,22,24,128]{3,2,1,0:T(8,128)}, f32[17,22,24,128]{3,2,1,0:T(8,128)S(1)}, u32[]{:S(2)}) copy-start(f32[17,22,24,128]{3,2,1,0:T(8,128)S(1)} %get-tuple-element.20.keep1) | copy-start | bytes 13787140
  100.6 22.9 %all-to-all-start.2 = ((f32[16,8,4,128]{3,2,1,0:T(4,128)}), f32[16,8,4,128]{3,2,1,0:T(4,128)S(1)}, u32[]{:S(2)}, u32[]{:S(2)}) async-start(f32[16,8,4,128]{3,2,1,0:T(4,128)} %broadcast_in_dim.16), calls=%async_computation.2 | async-start | bytes 524288 | tf_op jit(solution)/shard_map/all_to_all | solution.py:517
  107.6 15.9 %collective-permute-start.9 = (f32[8,24,128]{2,1,0:T(8,128)S(1)}, f32[8,24,128]{2,1,0:T(8,128)S(1)}, u32[]{:S(2)}, u32[]{:S(2)}) collective-permute-start(f32[8,24,128]{2,1,0:T(8,128)S(1)} %copy_bitcast_fusion), channel_id=1, source_target_pairs={{7,0},{6,1},{5,2},{4,3},{11,4},{10,5},{9,6},{8,7},{15,8},{14,9},{1... | collective-permute-start | bytes 294920 | tf_op jit(solution)/shard_map/ppermute | solution.py:450
  110.7 12.8 %collective-permute-start.8 = (f32[8,24,128]{2,1,0:T(8,128)S(1)}, f32[8,24,128]{2,1,0:T(8,128)S(1)}, u32[]{:S(2)}, u32[]{:S(2)}) collective-permute-start(f32[8,24,128]{2,1,0:T(8,128)S(1)} %copy_bitcast_fusion), channel_id=1, source_target_pairs={{0,7},{1,6},{2,5},{3,4},{4,11},{5,10},{6,9},{7,8},{8,15},{9,14},{1... | collective-permute-start | bytes 294920 | tf_op jit(solution)/shard_map/ppermute | solution.py:450
  116.5 11.9 %collective-permute-start.10 = (f32[3,48,128]{2,1,0:T(8,128)S(1)}, f32[3,48,128]{2,1,0:T(8,128)S(1)}, u32[]{:S(2)}, u32[]{:S(2)}) collective-permute-start(f32[3,48,128]{2,1,0:T(8,128)S(1)} %get-tuple-element.24), channel_id=1, source_target_pairs={{0,1},{1,2},{2,3},{3,4},{4,5},{5,6},{6,7},{7,8},{8,9},{9,10},{10,1... | collective-permute-start | bytes 221192 | tf_op jit(solution)/shard_map/ppermute | solution.py:450
  119.6 9.0 %collective-permute-start.11 = (f32[3,48,128]{2,1,0:T(8,128)S(1)}, f32[3,48,128]{2,1,0:T(8,128)S(1)}, u32[]{:S(2)}, u32[]{:S(2)}) collective-permute-start(f32[3,48,128]{2,1,0:T(8,128)S(1)} %get-tuple-element.25), channel_id=1, source_target_pairs={{1,0},{2,1},{3,2},{4,3},{5,4},{6,5},{7,6},{8,7},{9,8},{10,9},{11,1... | collective-permute-start | bytes 221192 | tf_op jit(solution)/shard_map/ppermute | solution.py:450
  128.6 2.6 %copy-start.1 = (f32[17,10,64,128]{3,2,1,0:T(8,128)S(1)}, f32[17,10,64,128]{3,2,1,0:T(8,128)}, u32[]{:S(2)}) copy-start(f32[17,10,64,128]{3,2,1,0:T(8,128)} %copy-done) | copy-start | bytes 16711684
  131.2 2.3 %copy-start.3 = (f32[17,22,24,128]{3,2,1,0:T(8,128)S(1)}, f32[17,22,24,128]{3,2,1,0:T(8,128)}, u32[]{:S(2)}) copy-start(f32[17,22,24,128]{3,2,1,0:T(8,128)} %copy-done.2) | copy-start | bytes 13787140

commit v7 on v5

--- a/solution.py
+++ b/solution.py
@@ -11,6 +11,15 @@
 least = 1e-4
 F32 = jnp.float32
 GROUP = 4
+FACES = (
+    (range(13, 29), 13),
+    (range(9, 13), 12),
+    (range(29, 33), 12),
+    (range(5, 9), 8),
+    (range(33, 37), 8),
+    (range(1, 5), 4),
+    (range(37, 41), 4),
+)
 
 
 def dot(a, b):
@@ -51,8 +60,8 @@
         lax.fori_loop(0, count // block, turn, 0)
 
 
-LOWER, UPPER, LEFT, RIGHT, OUT, INNER, INVERSE, DIAGONAL, SOURCE = 0, 2, 4, 6, 8, 10, 11, 13, 15
-KEPT = 17
+LOWER, LEFT, OUT, INNER, INVERSE, DIAGONAL, SOURCE = 0, 2, 4, 6, 7, 9, 11
+KEPT = 13
 
 
 class Level:
@@ -120,11 +129,11 @@
                     left, right = self.choose(first_x, edge, left), self.choose(last_x, edge, right)
                 total = lower + upper + (out[0] + inner if k == 0 else inner + out[1]) + left + right
                 if self.ends:
-                    lower, upper = self.choose(first, 0.0, lower), self.choose(last, 0.0, upper)
+                    lower = self.choose(first, 0.0, lower)
                 if self.width:
-                    left, right = self.choose(first_x, 0.0, left), self.choose(last_x, 0.0, right)
-                parts.append((lower, upper, left, right, jnp.where(d > 0.0, inverse(total), 0.0), total))
-            for place, even, odd in zip((LOWER, UPPER, LEFT, RIGHT, INVERSE, DIAGONAL), *parts):
+                    left = self.choose(first_x, 0.0, left)
+                parts.append((lower, left, jnp.where(d > 0.0, inverse(total), 0.0), total))
+            for place, even, odd in zip((LOWER, LEFT, INVERSE, DIAGONAL), *parts):
                 both(place, at, even, odd)
             both(OUT, at, out[0], out[1])
             self.keep[INNER, at] = inner
@@ -138,11 +147,11 @@
         at, keep = pl.ds(j, block), self.keep
         other = self.value.at[1 - colour]
         w = other[at]
-        mask = self.odd if colour else jnp.logical_not(self.odd)
-        side = self.choose(mask, other[pl.ds(j - 1, block)], other[pl.ds(j + 1, block)])
+        before, after = other[pl.ds(j - 1, block)], other[pl.ds(j + 1, block)]
+        side = self.choose(self.odd, before, after) if colour else self.choose(self.odd, after, before)
         total = keep[INNER, at] * w + keep[OUT + colour, at] * side
-        total += keep[LOWER + colour, at] * self.low(w) + keep[UPPER + colour, at] * self.high(w)
-        total += keep[LEFT + colour, at] * pltpu.roll(w, 1, 2) + keep[RIGHT + colour, at] * pltpu.roll(w, 127, 2)
+        total += keep[LOWER + colour, at] * self.low(w) + self.high(keep[LOWER + 1 - colour, at] * w)
+        total += keep[LEFT + colour, at] * pltpu.roll(w, 1, 2) + pltpu.roll(keep[LEFT + 1 - colour, at] * w, 127, 2)
         return total
 
     def first(self, lo, count, block):
@@ -246,13 +255,15 @@
 
 def middle_down(place_ref, window_ref, before_ref, after_ref, chunk_ref, kept_ref, below_ref,
                 window, source, density, keep, value, plane, source2, density2, keep2, value2):
+    for near, ref in ((0, before_ref), (32, after_ref)):
+        window[0:44, near : near + 16] = jnp.zeros((44, 16, 128), F32)
+        start = 0
+        for rows, planes in FACES:
+            low = 16 - planes if near == 0 else 32
+            for row in rows:
+                window[row + 1, low : low + planes] = ref[start : start + planes]
+                start += planes
     window[1:43, 16:32] = window_ref[...]
-    for ref, near, far in ((before_ref, 0, 8), (after_ref, 32, 32)):
-        window[9:35, near : near + 16] = ref[0:416].reshape(26, 16, 128)
-        for start, rows in ((1, 416), (35, 480)):
-            window[start : start + 8, far : far + 8] = ref[rows : rows + 64].reshape(8, 8, 128)
-            clear = 0 if near == 0 else 40
-            window[start : start + 8, clear : clear + 8] = jnp.zeros((8, 8, 128), F32)
     for row in (0, 43):
         window[row] = jnp.zeros((48, 128), F32)
     blocks(0, 44, 4, lambda r: folded(window, pl.ds(r, 4), source, density, pl.ds(r, 4)))
@@ -306,15 +317,17 @@
         total = pooled[8 * row : 8 * row + 1]
         for i in range(1, 8):
             total = total + pltpu.roll(pooled[8 * row + i : 8 * row + i + 1], 16 * i, 1)
-        chunk_ref[0, 64 + row : 65 + row] = total
+        chunk_ref[0, 40 + row : 41 + row] = total
+    black = jnp.zeros((8, 128), F32)
     for j in range(4):
-        for k in range(2):
-            row = 6 + 2 * j + k
-            total = source2[row, 8:16] + pltpu.roll(density2[row, 8:16], 64, 1)
-            if k == 0:
-                total = total + pltpu.roll(value2[1, 3 + j, 8:16], 32, 1)
-            chunk_ref[0, 8 * (2 * j + k) : 8 * (2 * j + k) + 8] = total
-    chunk_ref[0, 68:72] = jnp.zeros((4, 128), F32)
+        total = black
+        for k, ref in enumerate((source2, density2, source2, density2)):
+            total = total + pltpu.roll(ref[6 + 2 * j + k // 2, 8:16], 32 * k, 1)
+        chunk_ref[0, 8 * j : 8 * j + 8] = total
+    for j in range(4):
+        black = black + pltpu.roll(value2[1, 3 + j, 8:16], 32 * j, 1)
+    chunk_ref[0, 32:40] = black
+    chunk_ref[0, 44:48] = jnp.zeros((4, 128), F32)
     for peer in range(1, chunk_ref.shape[0]):
         chunk_ref[peer] = chunk_ref[0]
 
@@ -325,20 +338,25 @@
     for row in (0, 1, planes + 2, planes + 3):
         density[row] = jnp.zeros((8, 128), F32)
 
-    def spread(g, _):
+    def spread(g):
         tiles = [
-            jnp.concatenate([gathered_ref[2 * h, g], gathered_ref[2 * h + 1, g]], axis=0) for h in range(groups // 2)
+            jnp.concatenate([gathered_ref[2 * h + k, 4 * g : 4 * g + 4] for k in range(2)], axis=0)
+            for h in range(groups // 2)
         ]
-        for part, ref in enumerate((source, density)):
-            for z in range(4):
-                out = jnp.zeros((8, 128), F32)
-                for h, block in enumerate(tiles):
-                    moved = pltpu.roll(block, (16 * (h - z) - 64 * part) % 128, 1)
-                    out = jnp.where(lane // 16 == h, moved, out)
-                ref[2 + 4 * g + z] = out
-        return 0
-
-    lax.fori_loop(0, planes // 4, spread, 0)
+        tiles += [jnp.zeros((8, 128), F32)] * (8 - len(tiles))
+        for step in (1, 2, 4):
+            upper = (lane // 16) % (2 * step) >= step
+            for i in range(8):
+                if i % (2 * step) < step:
+                    a, b = tiles[i], tiles[i + step]
+                    tiles[i] = jnp.where(upper, pltpu.roll(b, 16 * step, 1), a)
+                    tiles[i + step] = jnp.where(upper, b, pltpu.roll(a, 128 - 16 * step, 1))
+        for z in range(4):
+            source[2 + 4 * g + z] = tiles[z]
+            density[2 + 4 * g + z] = tiles[4 + z]
+
+    for g in range(planes // 4):
+        spread(g)
     level = Level(density, keep, value, 16, 16, ends=True)
     pairs = planes // 2
     value[...] = jnp.zeros(value.shape, F32)
@@ -366,12 +384,18 @@
            source0, density0, keep0, value0, plane):
     at_y, at_group = place_ref[1], place_ref[2]
 
-    block = halo_ref[pl.ds(2 * at_group, 18)]
-    lane = iota(block.shape, 2)
-    source2[2:20] = block
+    lane = iota((24, 128), 1)
     for rows in (slice(0, 2), slice(20, 22)):
         density2[rows] = jnp.zeros((2, 24, 128), F32)
-    density2[2:20] = jnp.where(lane < 32, pltpu.roll(block, 64, 2), 0.0)
+    for i in range(9):
+        group, part = (at_group + i) // 4, (at_group + i) % 4
+        block = halo_ref[5 * group + part]
+        for k in range(2):
+            row = 2 + 2 * i + k
+            source2[row] = pltpu.roll(block, 64, 1) if k else block
+            density2[row] = jnp.where(lane < 32, pltpu.roll(block, 96 - 64 * k, 1), 0.0)
+        black = pltpu.roll(halo_ref[5 * group + 4], (128 - 32 * part) % 128, 1)
+        value2[1, 1 + i] = jnp.where(lane < 32, black, 0.0)
     level = Level(density2, keep2, value2, 0)
     level.clear((0, 10))
     level.coefficients(source2, 16.0, 1, 9, 3)
@@ -389,8 +413,7 @@
     spread = dot(jnp.concatenate(picked, axis=0), doubling(16)).reshape(9, 16, 128)
     plane[0:9, pl.ds(0, 12, stride=2)] = spread[:, 0:12]
     plane[0:9, pl.ds(1, 12, stride=2)] = spread[:, 0:12]
-    below = jnp.where(lane < 32, pltpu.roll(block, 96, 2), 0.0).reshape(9, 2, 24, 128)[:, 0]
-    value2[1, 1:10] = below + plane[0:9, 0:24]
+    value2[1, 1:10] = value2[1, 1:10] + plane[0:9, 0:24]
     level.half(0, 1, 9, 3)
     level.half(1, 2, 7, 7)
     level.half(0, 2, 7, 7)
@@ -495,14 +518,17 @@
     before, after = pair(window[-13:], window[:13], "xy", GROUP)
     window = jnp.concatenate([before, window, after], axis=0)
 
-    def faces(near):
-        parts = (window[8:34], window[:8, near], window[34:, near])
-        return jnp.concatenate([part.reshape(-1, 128) for part in parts], axis=0)
-
-    before, after = pair(faces(slice(8, 16)), faces(slice(0, 8)), "gz")
+    def faces(up):
+        parts = []
+        for rows, planes in FACES:
+            part = window[rows.start : rows.stop, 16 - planes :] if up else window[rows.start : rows.stop, :planes]
+            parts.append(part.reshape(-1, 128))
+        return jnp.concatenate(parts, axis=0)
+
+    before, after = pair(faces(True), faces(False), "gz")
     chunks, kept, below1 = pl.pallas_call(
         middle_down,
-        out_shape=[shape(gz, 72, 128), shape(20, 48, 128), shape(10, 24, 128)],
+        out_shape=[shape(gz, 48, 128), shape(20, 48, 128), shape(10, 24, 128)],
         in_specs=[smem] + [block] * 3,
         scratch_shapes=[vmem(44, 48, 128)]
         + [vmem(44, 24, 128)] * 2
@@ -516,11 +542,12 @@
     column = lax.all_to_all(chunks, "gz", 0, 0, tiled=True)
     peers = [[GROUP * i + j for i in range(xy // GROUP)] for j in range(GROUP)]
     everywhere = lax.all_to_all(
-        jnp.broadcast_to(column[None, :, 64:68], (xy // GROUP, gz, 4, 128)), "xy", 0, 0, axis_index_groups=peers, tiled=True
+        jnp.broadcast_to(column[:, 40:44].reshape(1, 4 * gz, 128), (xy // GROUP, 4 * gz, 128)),
+        "xy", 0, 0, axis_index_groups=peers, tiled=True,
     )
-    halo = jnp.pad(column[:, :64], ((1, 1), (0, 0), (0, 0)))
-    halo = lax.dynamic_slice(halo, (lax.axis_index("gz"), 0, 0), (3, 64, 128)).reshape(3, 8, 8, 128)
-    halo = jnp.swapaxes(halo, 0, 1).reshape(8, 24, 128)
+    halo = jnp.pad(column[:, :40], ((1, 1), (0, 0), (0, 0)))
+    halo = lax.dynamic_slice(halo, (lax.axis_index("gz"), 0, 0), (3, 40, 128)).reshape(3, 5, 8, 128)
+    halo = jnp.swapaxes(halo, 0, 1).reshape(5, 24, 128)
     before, after = pair(halo, halo, "xy", GROUP)
     halo = jnp.concatenate([before, halo, after], axis=0)
     planes = 4 * gz

time: 133 us -> 128 us (0.962)
  the two profiles are of different devices: /device:TPU:33 before, /device:TPU:31 now
where the time goes in v7:
time: 128 us; the launch traced here: 127 us
  starting transfers between devices  51.8 us (40%)
  waiting for transfers between devices  32.1 us (25%)
  Pallas kernels  24.9 us (19%)
  blocking collectives  14.7 us (11%)
  local copies, waits for them, and re-layouts  1.86 us (1%)
    ppermute x6, starting transfers between devices, pair(): lax.ppermute(array_up, axis, up)  26.9 us
    ppermute x6, waiting for transfers between devices, pair(): lax.ppermute(array_down, axis, down)  23.4 us
    all_to_all x1, blocking collectives, body(): column = lax.all_to_all(chunks, 'gz', 0, 0, tiled=True)  14.7 us
    ppermute x6, starting transfers between devices, pair(): lax.ppermute(array_down, axis, down)  14.6 us
    pallas_call x1, Pallas kernels, body(): pl.pallas_call(partial(way_up, xy), out_shape=[shape(32, 8, 128)] * 2, in...  8.81 us
    pallas_call x1, Pallas kernels, body(): pl.pallas_call(middle_down, out_shape=[shape(gz, 48, 128), shape(20, 48,...  7.22 us
    all_to_all x1, starting transfers between devices, body(): lax.all_to_all(jnp.broadcast_to(column[:, 40:44].reshape(1, 4 * gz, 128),...  6.96 us
    ppermute x6, waiting for transfers between devices, pair(): lax.ppermute(array_up, axis, up)  6.25 us
  transfers between devices with their start and end apart: 14, of which 9 were waited for; matrix products, arithmetic and copies ran while one was open for 0% of the time, Pallas kernels for 4%

profile of v7, /device:TPU:31, one launch (start us, length us, event | category | flops | bytes accessed | tf_op | source)
XLA Modules:
  0.0 126.5 jit_solution(12411056070898647451)
XLA Ops:
  0.6 0.0 copy-start
  0.6 0.8 fusion.3
  1.5 0.1 copy-done
  1.6 0.0 copy-start.1
  1.6 4.1 %collective-permute-start = (f32[17,8,128]{2,1,0:T(8,128)S(1)}, f32[17,8,128]{2,1,0:T(8,128)S(1)}, u32[]{:S(2)}, u32[]{:S(2)}) collective-permute-start(f32[17,8,128]{2,1,0:T(8,128)S(1)} %pad_maximum_fusion.2), channel_id=1, source_target_pairs={{0,64},{64,128},{128,192},{192,256},{256,320},{320,384},{384,448},... | collective-permute-start | bytes 208904 | tf_op jit(solution)/shard_map/ppermute | solution.py:474
  5.8 1.3 %collective-permute-start.1 = (f32[17,8,128]{2,1,0:T(8,128)S(1)}, f32[17,8,128]{2,1,0:T(8,128)S(1)}, u32[]{:S(2)}, u32[]{:S(2)}) collective-permute-start(f32[17,8,128]{2,1,0:T(8,128)S(1)} %pad_maximum_fusion.3), channel_id=1, source_target_pairs={{64,0},{128,64},{192,128},{256,192},{320,256},{384,320},{448,384},... | collective-permute-start | bytes 208904 | tf_op jit(solution)/shard_map/ppermute | solution.py:474
  7.1 0.0 collective-permute-done.before_ref
  7.1 4.4 %collective-permute-done.1.after_ref = f32[17,8,128]{2,1,0:T(8,128)S(1)} collective-permute-done((f32[17,8,128]{2,1,0:T(8,128)S(1)}, f32[17,8,128]{2,1,0:T(8,128)S(1)}, u32[]{:S(2)}, u32[]{:S(2)}) %collective-permute-start.1) | collective-permute-done | bytes 69664 | tf_op jit(solution)/shard_map/ppermute | solution.py:474
  11.5 0.0 copy-done.1
  11.5 0.1 shard_map.41
  11.6 6.0 %collective-permute-start.2 = (f32[10,48,128]{2,1,0:T(8,128)S(1)}, f32[10,48,128]{2,1,0:T(8,128)S(1)}, u32[]{:S(2)}, u32[]{:S(2)}) collective-permute-start(f32[10,48,128]{2,1,0:T(8,128)S(1)} %get-tuple-element.15), channel_id=1, source_target_pairs={{0,1},{1,2},{2,3},{3,4},{4,5},{5,6},{6,7},{7,8},{8,9},{9,10},{10,1... | collective-permute-start | bytes 737288 | tf_op jit(solution)/shard_map/ppermute | solution.py:474
  17.6 1.9 %collective-permute-start.3 = (f32[10,48,128]{2,1,0:T(8,128)S(1)}, f32[10,48,128]{2,1,0:T(8,128)S(1)}, u32[]{:S(2)}, u32[]{:S(2)}) collective-permute-start(f32[10,48,128]{2,1,0:T(8,128)S(1)} %get-tuple-element.16), channel_id=1, source_target_pairs={{1,0},{2,1},{3,2},{4,3},{5,4},{6,5},{7,6},{8,7},{9,8},{10,9},{11,1... | collective-permute-start | bytes 737288 | tf_op jit(solution)/shard_map/ppermute | solution.py:474
  19.6 1.2 collective-permute-done.2.before_ref.rim_before_ref
  20.7 7.7 %collective-permute-done.3.after_ref.rim_after_ref = f32[10,48,128]{2,1,0:T(8,128)S(1)} collective-permute-done((f32[10,48,128]{2,1,0:T(8,128)S(1)}, f32[10,48,128]{2,1,0:T(8,128)S(1)}, u32[]{:S(2)}, u32[]{:S(2)}) %collective-permute-start.3) | collective-permute-done | bytes 245792 | tf_op jit(solution)/shard_map/ppermute | solution.py:474
  28.5 3.9 %shard_map.42 = (f32[4,64,128]{2,1,0:T(8,128)}, f32[3,48,128]{2,1,0:T(8,128)S(1)}, f32[3,48,128]{2,1,0:T(8,128)S(1)}, f32[4,64,128]{2,1,0:T(8,128)S(1)}) custom-call(f32[8,64,128]{2,1,0:T(8,128)S(1)} %get-tuple-element.13.s_ref, f32[8,64,128]{2,1,0:T(8,128)S(1)} %get-tuple-element.14.d_ref, ...), custom_call_target="tpu_custom_call" | custom-call | tf_op jit(solution)/shard_map/pallas_call | solution.py:508
  32.3 3.3 %all-to-all-start = ((f32[4,64,128]{2,1,0:T(8,128)}), f32[4,64,128]{2,1,0:T(8,128)S(1)}, u32[]{:S(2)}, u32[]{:S(2)}) async-start(f32[4,64,128]{2,1,0:T(8,128)} %get-tuple-element.17), calls=%async_computation | async-start | bytes 262144 | tf_op jit(solution)/shard_map/all_to_all | solution.py:516
  35.7 2.5 %all-to-all-done = f32[4,64,128]{2,1,0:T(8,128)S(1)} async-done(((f32[4,64,128]{2,1,0:T(8,128)}), f32[4,64,128]{2,1,0:T(8,128)S(1)}, u32[]{:S(2)}, u32[]{:S(2)}) %all-to-all-start) | async-done | bytes 131104 | tf_op jit(solution)/shard_map/all_to_all | solution.py:516
  38.2 3.9 %collective-permute-start.4 = (f32[13,16,128]{2,1,0:T(8,128)S(1)}, f32[13,16,128]{2,1,0:T(8,128)S(1)}, u32[]{:S(2)}, u32[]{:S(2)}) collective-permute-start(f32[13,16,128]{2,1,0:T(8,128)S(1)} %get-tuple-element.26), channel_id=1, source_target_pairs={{0,7},{1,6},{2,5},{3,4},{4,11},{5,10},{6,9},{7,8},{8,15},{9,14},{1... | collective-permute-start | bytes 319496 | tf_op jit(solution)/shard_map/ppermute | solution.py:474
  42.1 2.9 %collective-permute-start.5 = (f32[13,16,128]{2,1,0:T(8,128)S(1)}, f32[13,16,128]{2,1,0:T(8,128)S(1)}, u32[]{:S(2)}, u32[]{:S(2)}) collective-permute-start(f32[13,16,128]{2,1,0:T(8,128)S(1)} %get-tuple-element.27), channel_id=1, source_target_pairs={{7,0},{6,1},{5,2},{4,3},{11,4},{10,5},{9,6},{8,7},{15,8},{14,9},{1... | collective-permute-start | bytes 319496 | tf_op jit(solution)/shard_map/ppermute | solution.py:474
  45.1 1.6 %collective-permute-done.4 = f32[13,16,128]{2,1,0:T(8,128)S(1)} collective-permute-done((f32[13,16,128]{2,1,0:T(8,128)S(1)}, f32[13,16,128]{2,1,0:T(8,128)S(1)}, u32[]{:S(2)}, u32[]{:S(2)}) %collective-permute-start.4) | collective-permute-done | bytes 106528 | tf_op jit(solution)/shard_map/ppermute | solution.py:474
  46.7 4.8 %collective-permute-done.5 = f32[13,16,128]{2,1,0:T(8,128)S(1)} collective-permute-done((f32[13,16,128]{2,1,0:T(8,128)S(1)}, f32[13,16,128]{2,1,0:T(8,128)S(1)}, u32[]{:S(2)}, u32[]{:S(2)}) %collective-permute-start.5) | collective-permute-done | bytes 106528 | tf_op jit(solution)/shard_map/ppermute | solution.py:474
  51.6 4.0 %collective-permute-start.6 = (f32[400,128]{1,0:T(8,128)S(1)}, f32[400,128]{1,0:T(8,128)S(1)}, u32[]{:S(2)}, u32[]{:S(2)}) collective-permute-start(f32[400,128]{1,0:T(8,128)S(1)} %constant_dynamic-update-slice_fusion), channel_id=1, source_target_pairs={{0,64},{64,128},{128,192},{192,256},{256,320},{320,384},{384,448},... | collective-permute-start | bytes 614408 | tf_op jit(solution)/shard_map/ppermute | solution.py:474
  55.6 1.3 %collective-permute-start.7 = (f32[400,128]{1,0:T(8,128)S(1)}, f32[400,128]{1,0:T(8,128)S(1)}, u32[]{:S(2)}, u32[]{:S(2)}) collective-permute-start(f32[400,128]{1,0:T(8,128)S(1)} %constant_dynamic-update-slice_fusion.7), channel_id=1, source_target_pairs={{64,0},{128,64},{192,128},{256,192},{320,256},{384,320},{448,384},... | collective-permute-start | bytes 614408 | tf_op jit(solution)/shard_map/ppermute | solution.py:474
  56.9 0.1 pad_add_fusion.place_ref
  57.0 3.4 %collective-permute-done.6.before_ref = f32[400,128]{1,0:T(8,128)S(1)} collective-permute-done((f32[400,128]{1,0:T(8,128)S(1)}, f32[400,128]{1,0:T(8,128)S(1)}, u32[]{:S(2)}, u32[]{:S(2)}) %collective-permute-start.6) | collective-permute-done | bytes 204832 | tf_op jit(solution)/shard_map/ppermute | solution.py:474
  60.4 5.8 %collective-permute-done.7.after_ref = f32[400,128]{1,0:T(8,128)S(1)} collective-permute-done((f32[400,128]{1,0:T(8,128)S(1)}, f32[400,128]{1,0:T(8,128)S(1)}, u32[]{:S(2)}, u32[]{:S(2)}) %collective-permute-start.7) | collective-permute-done | bytes 204832 | tf_op jit(solution)/shard_map/ppermute | solution.py:474
  66.3 7.2 %shard_map.43 = (f32[8,48,128]{2,1,0:T(8,128)S(1)}, f32[20,48,128]{2,1,0:T(8,128)S(1)}, f32[10,24,128]{2,1,0:T(8,128)S(1)}) custom-call(s32[3]{0:T(128)S(1)} %pad_add_fusion.place_ref, f32[42,16,128]{2,1,0:T(8,128)S(1)} %pad_maximum_fusion.window_ref, f32[400,128]{1,0:T(8,128)S(1)} %collective-permute-done.6.before_ref, ...), custom_call_target="tpu_custom_call" | custom-call | tf_op jit(solution)/shard_map/pallas_call | solution.py:529
  73.5 14.7 %all_to_all.15 = f32[8,48,128]{2,1,0:T(8,128)S(1)} all-to-all(f32[8,48,128]{2,1,0:T(8,128)S(1)} %get-tuple-element.18), channel_id=1, replica_groups=mesh['gz'=8,'xy'=64] {'gz'}, dimensions={0} | all-to-all | bytes 393216 | tf_op jit(solution)/shard_map/all_to_all | solution.py:542
  88.2 0.7 broadcast_in_dim.18
  88.9 7.0 %all-to-all-start.2 = ((f32[16,32,128]{2,1,0:T(8,128)}), f32[16,32,128]{2,1,0:T(8,128)S(1)}, u32[]{:S(2)}, u32[]{:S(2)}) async-start(f32[16,32,128]{2,1,0:T(8,128)} %broadcast_in_dim.18), calls=%async_computation.2 | async-start | bytes 524288 | tf_op jit(solution)/shard_map/all_to_all | solution.py:544
  95.9 3.9 %collective-permute-start.9 = (f32[5,24,128]{2,1,0:T(8,128)S(1)}, f32[5,24,128]{2,1,0:T(8,128)S(1)}, u32[]{:S(2)}, u32[]{:S(2)}) collective-permute-start(f32[5,24,128]{2,1,0:T(8,128)S(1)} %copy_bitcast_fusion), channel_id=1, source_target_pairs={{7,0},{6,1},{5,2},{4,3},{11,4},{10,5},{9,6},{8,7},{15,8},{14,9},{1... | collective-permute-start | bytes 184328 | tf_op jit(solution)/shard_map/ppermute | solution.py:474
  99.8 5.0 %collective-permute-start.8 = (f32[5,24,128]{2,1,0:T(8,128)S(1)}, f32[5,24,128]{2,1,0:T(8,128)S(1)}, u32[]{:S(2)}, u32[]{:S(2)}) collective-permute-start(f32[5,24,128]{2,1,0:T(8,128)S(1)} %copy_bitcast_fusion), channel_id=1, source_target_pairs={{0,7},{1,6},{2,5},{3,4},{4,11},{5,10},{6,9},{7,8},{8,15},{9,14},{1... | collective-permute-start | bytes 184328 | tf_op jit(solution)/shard_map/ppermute | solution.py:474
  104.8 3.9 %collective-permute-start.10 = (f32[3,48,128]{2,1,0:T(8,128)S(1)}, f32[3,48,128]{2,1,0:T(8,128)S(1)}, u32[]{:S(2)}, u32[]{:S(2)}) collective-permute-start(f32[3,48,128]{2,1,0:T(8,128)S(1)} %get-tuple-element.22), channel_id=1, source_target_pairs={{0,1},{1,2},{2,3},{3,4},{4,5},{5,6},{6,7},{7,8},{8,9},{9,10},{10,1... | collective-permute-start | bytes 221192 | tf_op jit(solution)/shard_map/ppermute | solution.py:474
  108.7 3.3 %collective-permute-start.11 = (f32[3,48,128]{2,1,0:T(8,128)S(1)}, f32[3,48,128]{2,1,0:T(8,128)S(1)}, u32[]{:S(2)}, u32[]{:S(2)}) collective-permute-start(f32[3,48,128]{2,1,0:T(8,128)S(1)} %get-tuple-element.23), channel_id=1, source_target_pairs={{1,0},{2,1},{3,2},{4,3},{5,4},{6,5},{7,6},{8,7},{9,8},{10,9},{11,1... | collective-permute-start | bytes 221192 | tf_op jit(solution)/shard_map/ppermute | solution.py:474
  112.1 0.0 collective-permute-done.9
  112.1 0.0 collective-permute-done.8
  112.1 0.0 all-to-all-done.2.gathered_ref
  112.1 4.9 %shard_map.44.near_ref = f32[12,8,128]{2,1,0:T(8,128)S(1)} custom-call(s32[3]{0:T(128)S(1)} %pad_add_fusion.place_ref, f32[16,32,128]{2,1,0:T(8,128)S(1)} %all-to-all-done.2.gathered_ref), custom_call_target="tpu_custom_call" | custom-call | flops 100000000 | bytes 16000000 | tf_op jit(solution)/shard_map/pallas_call | solution.py:554
  117.0 0.0 collective-permute-done.10.before_ref
  117.0 0.7 collective-permute-done.11.after_ref
  117.7 8.8 %shard_map.45 = (f32[32,8,128]{2,1,0:T(8,128)}, f32[32,8,128]{2,1,0:T(8,128)}) custom-call(s32[3]{0:T(128)S(1)} %pad_add_fusion.place_ref, f32[12,8,128]{2,1,0:T(8,128)S(1)} %shard_map.44.near_ref, f32[15,24,128]{2,1,0:T(8,128)S(1)} %pad_maximum_fusion.1.halo_ref, f32[20,48,128]{2,1,0:T(8,128)S(1)} %get-tuple-element.19.kept_ref, ...), custom_call_target="tpu_custom_call" | custom-call | tf_op jit(solution)/shard_map/pallas_call | solution.py:563
  (32 shorter events, 0.3 us)
Async XLA Ops:
  0.6 0.9 copy-start
  1.6 9.9 %copy-start.1 = (f32[32,8,128]{2,1,0:T(8,128)S(1)}, f32[32,8,128]{2,1,0:T(8,128)}, u32[]{:S(2)}) copy-start(f32[32,8,128]{2,1,0:T(8,128)} %right_ref.1) | copy-start | bytes 393220
  1.6 5.5 %collective-permute-start = (f32[17,8,128]{2,1,0:T(8,128)S(1)}, f32[17,8,128]{2,1,0:T(8,128)S(1)}, u32[]{:S(2)}, u32[]{:S(2)}) collective-permute-start(f32[17,8,128]{2,1,0:T(8,128)S(1)} %pad_maximum_fusion.2), channel_id=1, source_target_pairs={{0,64},{64,128},{128,192},{192,256},{256,320},{320,384},{384,448},... | collective-permute-start | bytes 208904 | tf_op jit(solution)/shard_map/ppermute | solution.py:474
  5.8 5.7 %collective-permute-start.1 = (f32[17,8,128]{2,1,0:T(8,128)S(1)}, f32[17,8,128]{2,1,0:T(8,128)S(1)}, u32[]{:S(2)}, u32[]{:S(2)}) collective-permute-start(f32[17,8,128]{2,1,0:T(8,128)S(1)} %pad_maximum_fusion.3), channel_id=1, source_target_pairs={{64,0},{128,64},{192,128},{256,192},{320,256},{384,320},{448,384},... | collective-permute-start | bytes 208904 | tf_op jit(solution)/shard_map/ppermute | solution.py:474
  11.6 9.2 %collective-permute-start.2 = (f32[10,48,128]{2,1,0:T(8,128)S(1)}, f32[10,48,128]{2,1,0:T(8,128)S(1)}, u32[]{:S(2)}, u32[]{:S(2)}) collective-permute-start(f32[10,48,128]{2,1,0:T(8,128)S(1)} %get-tuple-element.15), channel_id=1, source_target_pairs={{0,1},{1,2},{2,3},{3,4},{4,5},{5,6},{6,7},{7,8},{8,9},{9,10},{10,1... | collective-permute-start | bytes 737288 | tf_op jit(solution)/shard_map/ppermute | solution.py:474
  17.6 10.8 %collective-permute-start.3 = (f32[10,48,128]{2,1,0:T(8,128)S(1)}, f32[10,48,128]{2,1,0:T(8,128)S(1)}, u32[]{:S(2)}, u32[]{:S(2)}) collective-permute-start(f32[10,48,128]{2,1,0:T(8,128)S(1)} %get-tuple-element.16), channel_id=1, source_target_pairs={{1,0},{2,1},{3,2},{4,3},{5,4},{6,5},{7,6},{8,7},{9,8},{10,9},{11,1... | collective-permute-start | bytes 737288 | tf_op jit(solution)/shard_map/ppermute | solution.py:474
  32.3 5.8 %all-to-all-start = ((f32[4,64,128]{2,1,0:T(8,128)}), f32[4,64,128]{2,1,0:T(8,128)S(1)}, u32[]{:S(2)}, u32[]{:S(2)}) async-start(f32[4,64,128]{2,1,0:T(8,128)} %get-tuple-element.17), calls=%async_computation | async-start | bytes 262144 | tf_op jit(solution)/shard_map/all_to_all | solution.py:516
  38.2 8.5 %collective-permute-start.4 = (f32[13,16,128]{2,1,0:T(8,128)S(1)}, f32[13,16,128]{2,1,0:T(8,128)S(1)}, u32[]{:S(2)}, u32[]{:S(2)}) collective-permute-start(f32[13,16,128]{2,1,0:T(8,128)S(1)} %get-tuple-element.26), channel_id=1, source_target_pairs={{0,7},{1,6},{2,5},{3,4},{4,11},{5,10},{6,9},{7,8},{8,15},{9,14},{1... | collective-permute-start | bytes 319496 | tf_op jit(solution)/shard_map/ppermute | solution.py:474
  42.1 9.3 %collective-permute-start.5 = (f32[13,16,128]{2,1,0:T(8,128)S(1)}, f32[13,16,128]{2,1,0:T(8,128)S(1)}, u32[]{:S(2)}, u32[]{:S(2)}) collective-permute-start(f32[13,16,128]{2,1,0:T(8,128)S(1)} %get-tuple-element.27), channel_id=1, source_target_pairs={{7,0},{6,1},{5,2},{4,3},{11,4},{10,5},{9,6},{8,7},{15,8},{14,9},{1... | collective-permute-start | bytes 319496 | tf_op jit(solution)/shard_map/ppermute | solution.py:474
  51.6 8.9 %collective-permute-start.6 = (f32[400,128]{1,0:T(8,128)S(1)}, f32[400,128]{1,0:T(8,128)S(1)}, u32[]{:S(2)}, u32[]{:S(2)}) collective-permute-start(f32[400,128]{1,0:T(8,128)S(1)} %constant_dynamic-update-slice_fusion), channel_id=1, source_target_pairs={{0,64},{64,128},{128,192},{192,256},{256,320},{320,384},{384,448},... | collective-permute-start | bytes 614408 | tf_op jit(solution)/shard_map/ppermute | solution.py:474
  55.6 10.7 %collective-permute-start.7 = (f32[400,128]{1,0:T(8,128)S(1)}, f32[400,128]{1,0:T(8,128)S(1)}, u32[]{:S(2)}, u32[]{:S(2)}) collective-permute-start(f32[400,128]{1,0:T(8,128)S(1)} %constant_dynamic-update-slice_fusion.7), channel_id=1, source_target_pairs={{64,0},{128,64},{192,128},{256,192},{320,256},{384,320},{448,384},... | collective-permute-start | bytes 614408 | tf_op jit(solution)/shard_map/ppermute | solution.py:474
  88.9 23.2 %all-to-all-start.2 = ((f32[16,32,128]{2,1,0:T(8,128)}), f32[16,32,128]{2,1,0:T(8,128)S(1)}, u32[]{:S(2)}, u32[]{:S(2)}) async-start(f32[16,32,128]{2,1,0:T(8,128)} %broadcast_in_dim.18), calls=%async_computation.2 | async-start | bytes 524288 | tf_op jit(solution)/shard_map/all_to_all | solution.py:544
  95.9 16.1 %collective-permute-start.9 = (f32[5,24,128]{2,1,0:T(8,128)S(1)}, f32[5,24,128]{2,1,0:T(8,128)S(1)}, u32[]{:S(2)}, u32[]{:S(2)}) collective-permute-start(f32[5,24,128]{2,1,0:T(8,128)S(1)} %copy_bitcast_fusion), channel_id=1, source_target_pairs={{7,0},{6,1},{5,2},{4,3},{11,4},{10,5},{9,6},{8,7},{15,8},{14,9},{1... | collective-permute-start | bytes 184328 | tf_op jit(solution)/shard_map/ppermute | solution.py:474
  99.8 12.3 %collective-permute-start.8 = (f32[5,24,128]{2,1,0:T(8,128)S(1)}, f32[5,24,128]{2,1,0:T(8,128)S(1)}, u32[]{:S(2)}, u32[]{:S(2)}) collective-permute-start(f32[5,24,128]{2,1,0:T(8,128)S(1)} %copy_bitcast_fusion), channel_id=1, source_target_pairs={{0,7},{1,6},{2,5},{3,4},{4,11},{5,10},{6,9},{7,8},{8,15},{9,14},{1... | collective-permute-start | bytes 184328 | tf_op jit(solution)/shard_map/ppermute | solution.py:474
  104.8 12.2 %collective-permute-start.10 = (f32[3,48,128]{2,1,0:T(8,128)S(1)}, f32[3,48,128]{2,1,0:T(8,128)S(1)}, u32[]{:S(2)}, u32[]{:S(2)}) collective-permute-start(f32[3,48,128]{2,1,0:T(8,128)S(1)} %get-tuple-element.22), channel_id=1, source_target_pairs={{0,1},{1,2},{2,3},{3,4},{4,5},{5,6},{6,7},{7,8},{8,9},{9,10},{10,1... | collective-permute-start | bytes 221192 | tf_op jit(solution)/shard_map/ppermute | solution.py:474
  108.7 9.0 %collective-permute-start.11 = (f32[3,48,128]{2,1,0:T(8,128)S(1)}, f32[3,48,128]{2,1,0:T(8,128)S(1)}, u32[]{:S(2)}, u32[]{:S(2)}) collective-permute-start(f32[3,48,128]{2,1,0:T(8,128)S(1)} %get-tuple-element.23), channel_id=1, source_target_pairs={{1,0},{2,1},{3,2},{4,3},{5,4},{6,5},{7,6},{8,7},{9,8},{10,9},{11,1... | collective-permute-start | bytes 221192 | tf_op jit(solution)/shard_map/ppermute | solution.py:474

commit v8 on v7

--- a/solution.py
+++ b/solution.py
@@ -224,18 +224,19 @@
     level.clear((0, 9))
     value[1, 1] = jnp.zeros((64, 128), F32)
     value[1, 8] = jnp.zeros((64, 128), F32)
-    level.coefficients(source, 1.0, 1, 8, 1)
-    level.first(1, 8, 2)
-    level.half(1, 1, 8, 2)
-    level.half(0, 2, 6, 2)
-    level.half(1, 2, 6, 2)
+    level.coefficients(source, 1.0, 1, 8, 2)
+    level.first(1, 8, 4)
+    level.half(1, 1, 8, 4)
+    level.half(0, 2, 6, 3)
+    level.half(1, 2, 6, 3)
 
     def pooling(j):
-        red, black = level.residual(1.0, 3 + j, 1)
-        plane[pl.ds(j, 1)] = (red + black)[:, 16:48]
-        plane[pl.ds(4 + j, 1)] = (density[pl.ds(6 + 2 * j, 1)] + density[pl.ds(7 + 2 * j, 1)])[:, 16:48]
-
-    blocks(0, 4, 1, pooling)
+        red, black = level.residual(1.0, 3 + j, 2)
+        plane[pl.ds(j, 2)] = (red + black)[:, 16:48]
+        rows = density[pl.ds(6 + 2 * j, 4), 16:48].reshape(2, 2, 32, 128)
+        plane[pl.ds(4 + j, 2)] = rows[:, 0] + rows[:, 1]
+
+    blocks(0, 4, 2, pooling)
     pooled = plane[:, pl.ds(0, 16, stride=2)] + plane[:, pl.ds(1, 16, stride=2)]
     out = dot(pooled[:4].reshape(64, 128), halving(0, 0.125)) + dot(pooled[4:].reshape(64, 128), halving(64, 0.125))
     low_ref[...] = value[1, 3:6, 8:56]
@@ -266,24 +267,24 @@
     window[1:43, 16:32] = window_ref[...]
     for row in (0, 43):
         window[row] = jnp.zeros((48, 128), F32)
-    blocks(0, 44, 4, lambda r: folded(window, pl.ds(r, 4), source, density, pl.ds(r, 4)))
+    blocks(0, 44, 11, lambda r: folded(window, pl.ds(r, 11), source, density, pl.ds(r, 11)))
     level = Level(density, keep, value, 64, 64)
     level.clear((0, 21))
     for j in (1, 20):
         value[1, j] = jnp.zeros((24, 128), F32)
-    level.coefficients(source, 4.0, 1, 20, 2)
-    level.first(1, 20, 5)
-    level.half(1, 1, 20, 5)
-    level.half(0, 2, 18, 6)
-    level.half(1, 2, 18, 6)
+    level.coefficients(source, 4.0, 1, 20, 5)
+    level.first(1, 20, 10)
+    level.half(1, 1, 20, 10)
+    level.half(0, 2, 18, 9)
+    level.half(1, 2, 18, 9)
     kept_ref[...] = window[pl.ds(6 + 4 * place_ref[2], 20)]
     below_ref[...] = value[1, pl.ds(3 + 2 * place_ref[2], 10)]
 
     def pooling(j):
-        red, black = level.residual(4.0, 3 + j, 4)
-        plane[pl.ds(j, 4), 0:24] = red + black
-
-    blocks(0, 16, 4, pooling)
+        red, black = level.residual(4.0, 3 + j, 8)
+        plane[pl.ds(j, 8), 0:24] = red + black
+
+    blocks(0, 16, 8, pooling)
     rows = density[4:40].reshape(18, 2, 24, 128)
     plane[16:34, 0:24] = rows[:, 0] + rows[:, 1]
     pooled = plane[:, pl.ds(0, 16, stride=2)] + plane[:, pl.ds(1, 16, stride=2)]
@@ -299,9 +300,9 @@
     below.clear((0, 9))
     for j in (1, 8):
         value2[1, j] = jnp.zeros((24, 128), F32)
-    below.coefficients(source2, 16.0, 1, 8, 2)
+    below.coefficients(source2, 16.0, 1, 8, 4)
     below.first(1, 8, 8)
-    below.half(1, 1, 8, 4)
+    below.half(1, 1, 8, 8)
     below.half(0, 2, 6, 6)
     below.half(1, 2, 6, 6)
     red, black = below.residual(16.0, 3, 4)
@@ -332,7 +333,8 @@
         chunk_ref[peer] = chunk_ref[0]
 
 
-def coarsest(planes, place_ref, gathered_ref, near_ref, source, density, keep, value, wide):
+def coarsest(place_ref, gathered_ref, source, density, keep, value, wide, besides):
+    planes = wide.shape[0] - 8
     groups = gathered_ref.shape[0]
     lane = iota((8, 128), 1)
     for row in (0, 1, planes + 2, planes + 3):
@@ -362,28 +364,34 @@
     value[...] = jnp.zeros(value.shape, F32)
     level.coefficients(source, 64.0, 1, pairs, 4)
 
-    def sweep(_, carry):
-        level.half(0, 1, pairs, pairs)
-        level.half(1, 1, pairs, pairs)
-        return carry
-
-    lax.fori_loop(0, 12, sweep, 0)
+    for turns, beside in besides:
+
+        def sweep(i, carry):
+            beside(i)
+            level.half(0, 1, pairs, pairs)
+            level.half(1, 1, pairs, pairs)
+            return carry
+
+        lax.fori_loop(0, turns, sweep, 0)
     wide[0:4] = jnp.zeros((4, 8, 128), F32)
     wide[planes + 4 : planes + 8] = jnp.zeros((4, 8, 128), F32)
     even, odd = level.rows(value[0, 1 : pairs + 1], value[1, 1 : pairs + 1])
     for j in range(pairs):
         wide[4 + 2 * j] = even[j]
         wide[5 + 2 * j] = odd[j]
-    near_ref[...] = wide[pl.ds(4 * place_ref[0], 12)]
-
-
-def way_up(devices, place_ref, near_ref, halo_ref, kept_ref, below1_ref,
+    return wide[pl.ds(4 * place_ref[0], 12)]
+
+
+def way_up(devices, place_ref, gathered_ref, halo_ref, kept_ref, below1_ref,
            s_ref, d_ref, rim_before_ref, rim_after_ref, below0_ref, before_ref, after_ref,
            pressure_ref, remain_ref,
+           source3, density3, keep3, value3, wide,
            source2, density2, keep2, value2, source1, density1, keep1, value1,
            source0, density0, keep0, value0, plane):
     at_y, at_group = place_ref[1], place_ref[2]
-
+    level1 = Level(density1, keep1, value1, 64, 64)
+    finest_window(s_ref, d_ref, rim_before_ref, rim_after_ref, source0, density0)
+    level0 = Level(density0, keep0, value0, 128)
     lane = iota((24, 128), 1)
     for rows in (slice(0, 2), slice(20, 22)):
         density2[rows] = jnp.zeros((2, 24, 128), F32)
@@ -398,9 +406,25 @@
         value2[1, 1 + i] = jnp.where(lane < 32, black, 0.0)
     level = Level(density2, keep2, value2, 0)
     level.clear((0, 10))
-    level.coefficients(source2, 16.0, 1, 9, 3)
+
+    def finest(i):
+        level0.coefficients(source0, 1.0, 1 + 2 * i, 2, 2)
+
+    def folding(i):
+        rows = pl.ds(5 * i, 5)
+        folded(kept_ref, rows, source1, density1, rows)
+        finest(i)
+
+    near = coarsest(
+        place_ref, gathered_ref, source3, density3, keep3, value3, wide,
+        (
+            (4, folding),
+            (3, lambda i: level.coefficients(source2, 16.0, 1 + 3 * i, 3, 3)),
+            (4, lambda i: level1.coefficients(source1, 4.0, 1 + 2 * i, 2, 2)),
+            (1, lambda i: None),
+        ),
+    )
     row = iota((8, 128), 0)
-    near = near_ref[...]
     picked = []
     for i in range(9):
         y = at_y + i - 4
@@ -414,15 +438,13 @@
     plane[0:9, pl.ds(0, 12, stride=2)] = spread[:, 0:12]
     plane[0:9, pl.ds(1, 12, stride=2)] = spread[:, 0:12]
     value2[1, 1:10] = value2[1, 1:10] + plane[0:9, 0:24]
-    level.half(0, 1, 9, 3)
+    level.half(0, 1, 9, 9)
     level.half(1, 2, 7, 7)
     level.half(0, 2, 7, 7)
     level.half(1, 3, 5, 5)
     even, odd = level.rows(value2[0, 3:8], value2[1, 3:8])
 
-    blocks(0, 20, 4, lambda r: folded(kept_ref, pl.ds(r, 4), source1, density1, pl.ds(r, 4)))
-    level = Level(density1, keep1, value1, 64, 64)
-    level.coefficients(source1, 4.0, 1, 8, 2)
+    level = level1
     rows = jnp.stack([even, odd], axis=1).reshape(240, 128)
     spread = dot(rows, doubling(32, 0, 64)).reshape(10, 24, 128)
     plane[0:10, pl.ds(0, 24, stride=2)] = spread
@@ -437,9 +459,7 @@
     even, odd = level.rows(value1[0, 2:8], value1[1, 2:8])
     rows = jnp.stack([even, odd], axis=1).reshape(12, 24, 128)[1:11]
 
-    finest_window(s_ref, d_ref, rim_before_ref, rim_after_ref, source0, density0)
-    level = Level(density0, keep0, value0, 128)
-    level.coefficients(source0, 1.0, 1, 8, 1)
+    level = level0
     near = dot(rows[:, 8:24].reshape(160, 128), doubling(64)).reshape(10, 16, 128)
     far = dot(rows[:, 0:16].reshape(160, 128), doubling(64, 64)).reshape(10, 16, 128)
     for start, part in ((0, near), (32, far)):
@@ -450,20 +470,19 @@
     value0[1, 3:7] = value0[1, 3:7] + below0_ref[...]
     value0[1, 7:10, 8:56] = value0[1, 7:10, 8:56] + after_ref[...]
     level.clear_red((0, 9))
-    level.half(0, 1, 8, 2)
-    level.half(1, 1, 8, 2)
-    level.half(0, 2, 6, 2)
-    level.half(1, 2, 6, 2)
+    level.half(0, 1, 8, 4)
+    level.half(1, 1, 8, 4)
+    level.half(0, 2, 6, 3)
+    level.half(1, 2, 6, 3)
     even, odd = level.rows(value0[0, 3:7, 16:48], value0[1, 3:7, 16:48])
     pressure_ref[...] = jnp.swapaxes(jnp.stack([even, odd], axis=1).reshape(8, 32, 128), 0, 1)
 
     def remaining(j):
-        red, black = level.residual(1.0, 3 + j, 1)
+        red, black = level.residual(1.0, 3 + j, 2)
         even, odd = level.rows(red, black)
-        plane[pl.ds(2 * j, 1)] = even
-        plane[pl.ds(2 * j + 1, 1)] = odd
-
-    blocks(0, 4, 1, remaining)
+        plane[pl.ds(2 * j, 4)] = jnp.stack([even, odd], axis=1).reshape(4, 64, 128)
+
+    blocks(0, 4, 2, remaining)
     remain_ref[...] = jnp.swapaxes(plane[0:8, 16:48], 0, 1)
 
 
@@ -551,27 +570,20 @@
     before, after = pair(halo, halo, "xy", GROUP)
     halo = jnp.concatenate([before, halo, after], axis=0)
     planes = 4 * gz
-    near = pl.pallas_call(
-        partial(coarsest, planes),
-        out_shape=shape(12, 8, 128),
-        in_specs=[smem, block],
-        scratch_shapes=[vmem(planes + 4, 8, 128)] * 2
-        + [vmem(KEPT, planes // 2 + 2, 8, 128), vmem(2, planes // 2 + 2, 8, 128), vmem(planes + 8, 8, 128)],
-        compiler_params=params(),
-        cost_estimate=pl.CostEstimate(flops=100_000_000, bytes_accessed=16_000_000, transcendentals=0),
-    )(place, everywhere)
     return pl.pallas_call(
         partial(way_up, xy),
         out_shape=[shape(32, 8, 128)] * 2,
         in_specs=[smem] + [block] * 11,
-        scratch_shapes=[vmem(22, 24, 128)] * 2
+        scratch_shapes=[vmem(planes + 4, 8, 128)] * 2
+        + [vmem(KEPT, planes // 2 + 2, 8, 128), vmem(2, planes // 2 + 2, 8, 128), vmem(planes + 8, 8, 128)]
+        + [vmem(22, 24, 128)] * 2
         + [vmem(KEPT, 11, 24, 128), vmem(2, 11, 24, 128)]
         + [vmem(20, 24, 128)] * 2
         + [vmem(KEPT, 10, 24, 128), vmem(2, 10, 24, 128)]
         + [vmem(20, 64, 128)] * 2
         + [vmem(KEPT, 10, 64, 128), vmem(2, 10, 64, 128), vmem(10, 64, 128)],
         compiler_params=params(),
-    )(place, near, halo, kept, below1, *finest, below0, value_before, value_after)
+    )(place, everywhere, halo, kept, below1, *finest, below0, value_before, value_after)
 
 
 def solution(mesh):

time: 128 us -> 126 us (0.984)
  Pallas kernels: 24.9 us -> 19.2 us
  waiting for transfers between devices: 32.1 us -> 37 us
    ppermute x6, waiting for transfers between devices: 23.4 us -> 28.3 us  [pair(): lax.ppermute(array_down, axis, down)]
    pallas_call x1 -> x0, Pallas kernels: 4.86 us -> none  [body(): pl.pallas_call(partial(coarsest, planes), out_shape=shape(12, 8, 128), in...]
    pallas_call x1, Pallas kernels: 8.81 us -> 10.9 us  [body(): pl.pallas_call(partial(way_up, xy), out_shape=[shape(32, 8, 128)] * 2, in...]
    pallas_call x1, Pallas kernels: 7.22 us -> 5.23 us  [body(): pl.pallas_call(middle_down, out_shape=[shape(gz, 48, 128), shape(20, 48,...]
  transfers between devices with their start and end apart: 14 -> 14, of which waited for: 9 -> 9; matrix products, arithmetic and copies ran while one was open for 0% -> 0% of each run, Pallas kernels for 4% -> 0%
where the time goes in v8:
time: 126 us
  starting transfers between devices  51.8 us (41%)
  waiting for transfers between devices  37 us (29%)
  Pallas kernels  19.2 us (15%)
  blocking collectives  14.7 us (12%)
  local copies, waits for them, and re-layouts  1.86 us (1%)
    ppermute x6, waiting for transfers between devices, pair(): lax.ppermute(array_down, axis, down)  28.3 us
    ppermute x6, starting transfers between devices, pair(): lax.ppermute(array_up, axis, up)  26.9 us
    all_to_all x1, blocking collectives, body(): column = lax.all_to_all(chunks, 'gz', 0, 0, tiled=True)  14.7 us
    ppermute x6, starting transfers between devices, pair(): lax.ppermute(array_down, axis, down)  14.6 us
    pallas_call x1, Pallas kernels, body(): pl.pallas_call(partial(way_up, xy), out_shape=[shape(32, 8, 128)] * 2, in...  10.9 us
    all_to_all x1, starting transfers between devices, body(): lax.all_to_all(jnp.broadcast_to(column[:, 40:44].reshape(1, 4 * gz, 128),...  6.96 us
    ppermute x6, waiting for transfers between devices, pair(): lax.ppermute(array_up, axis, up)  6.25 us
    pallas_call x1, Pallas kernels, body(): pl.pallas_call(middle_down, out_shape=[shape(gz, 48, 128), shape(20, 48,...  5.23 us
  transfers between devices with their start and end apart: 14, of which 9 were waited for; matrix products, arithmetic and copies ran while one was open for 0% of the time, Pallas kernels for 0%

profile of v8, /device:TPU:31, one launch (start us, length us, event | category | flops | bytes accessed | tf_op | source)
XLA Modules:
  0.0 125.7 jit_solution(18013095181284353563)
XLA Ops:
  0.6 0.0 copy-start
  0.6 0.8 fusion.3
  1.5 0.1 copy-done
  1.6 0.0 copy-start.1
  1.6 4.1 %collective-permute-start = (f32[17,8,128]{2,1,0:T(8,128)S(1)}, f32[17,8,128]{2,1,0:T(8,128)S(1)}, u32[]{:S(2)}, u32[]{:S(2)}) collective-permute-start(f32[17,8,128]{2,1,0:T(8,128)S(1)} %pad_maximum_fusion.2), channel_id=1, source_target_pairs={{0,64},{64,128},{128,192},{192,256},{256,320},{320,384},{384,448},... | collective-permute-start | bytes 208904 | tf_op jit(solution)/shard_map/ppermute | solution.py:493
  5.8 1.3 %collective-permute-start.1 = (f32[17,8,128]{2,1,0:T(8,128)S(1)}, f32[17,8,128]{2,1,0:T(8,128)S(1)}, u32[]{:S(2)}, u32[]{:S(2)}) collective-permute-start(f32[17,8,128]{2,1,0:T(8,128)S(1)} %pad_maximum_fusion.3), channel_id=1, source_target_pairs={{64,0},{128,64},{192,128},{256,192},{320,256},{384,320},{448,384},... | collective-permute-start | bytes 208904 | tf_op jit(solution)/shard_map/ppermute | solution.py:493
  7.1 0.0 collective-permute-done.before_ref
  7.1 4.4 %collective-permute-done.1.after_ref = f32[17,8,128]{2,1,0:T(8,128)S(1)} collective-permute-done((f32[17,8,128]{2,1,0:T(8,128)S(1)}, f32[17,8,128]{2,1,0:T(8,128)S(1)}, u32[]{:S(2)}, u32[]{:S(2)}) %collective-permute-start.1) | collective-permute-done | bytes 69664 | tf_op jit(solution)/shard_map/ppermute | solution.py:493
  11.5 0.0 copy-done.1
  11.5 0.1 shard_map.41
  11.6 6.0 %collective-permute-start.2 = (f32[10,48,128]{2,1,0:T(8,128)S(1)}, f32[10,48,128]{2,1,0:T(8,128)S(1)}, u32[]{:S(2)}, u32[]{:S(2)}) collective-permute-start(f32[10,48,128]{2,1,0:T(8,128)S(1)} %get-tuple-element.15), channel_id=1, source_target_pairs={{0,1},{1,2},{2,3},{3,4},{4,5},{5,6},{6,7},{7,8},{8,9},{9,10},{10,1... | collective-permute-start | bytes 737288 | tf_op jit(solution)/shard_map/ppermute | solution.py:493
  17.6 1.9 %collective-permute-start.3 = (f32[10,48,128]{2,1,0:T(8,128)S(1)}, f32[10,48,128]{2,1,0:T(8,128)S(1)}, u32[]{:S(2)}, u32[]{:S(2)}) collective-permute-start(f32[10,48,128]{2,1,0:T(8,128)S(1)} %get-tuple-element.16), channel_id=1, source_target_pairs={{1,0},{2,1},{3,2},{4,3},{5,4},{6,5},{7,6},{8,7},{9,8},{10,9},{11,1... | collective-permute-start | bytes 737288 | tf_op jit(solution)/shard_map/ppermute | solution.py:493
  19.6 1.2 collective-permute-done.2.before_ref.rim_before_ref
  20.7 7.7 %collective-permute-done.3.after_ref.rim_after_ref = f32[10,48,128]{2,1,0:T(8,128)S(1)} collective-permute-done((f32[10,48,128]{2,1,0:T(8,128)S(1)}, f32[10,48,128]{2,1,0:T(8,128)S(1)}, u32[]{:S(2)}, u32[]{:S(2)}) %collective-permute-start.3) | collective-permute-done | bytes 245792 | tf_op jit(solution)/shard_map/ppermute | solution.py:493
  28.5 3.0 %shard_map.42 = (f32[4,64,128]{2,1,0:T(8,128)}, f32[3,48,128]{2,1,0:T(8,128)S(1)}, f32[3,48,128]{2,1,0:T(8,128)S(1)}, f32[4,64,128]{2,1,0:T(8,128)S(1)}) custom-call(f32[8,64,128]{2,1,0:T(8,128)S(1)} %get-tuple-element.13.s_ref, f32[8,64,128]{2,1,0:T(8,128)S(1)} %get-tuple-element.14.d_ref, ...), custom_call_target="tpu_custom_call" | custom-call | tf_op jit(solution)/shard_map/pallas_call | solution.py:527
  31.4 3.3 %all-to-all-start = ((f32[4,64,128]{2,1,0:T(8,128)}), f32[4,64,128]{2,1,0:T(8,128)S(1)}, u32[]{:S(2)}, u32[]{:S(2)}) async-start(f32[4,64,128]{2,1,0:T(8,128)} %get-tuple-element.17), calls=%async_computation | async-start | bytes 262144 | tf_op jit(solution)/shard_map/all_to_all | solution.py:535
  34.8 2.5 %all-to-all-done = f32[4,64,128]{2,1,0:T(8,128)S(1)} async-done(((f32[4,64,128]{2,1,0:T(8,128)}), f32[4,64,128]{2,1,0:T(8,128)S(1)}, u32[]{:S(2)}, u32[]{:S(2)}) %all-to-all-start) | async-done | bytes 131104 | tf_op jit(solution)/shard_map/all_to_all | solution.py:535
  37.3 3.9 %collective-permute-start.4 = (f32[13,16,128]{2,1,0:T(8,128)S(1)}, f32[13,16,128]{2,1,0:T(8,128)S(1)}, u32[]{:S(2)}, u32[]{:S(2)}) collective-permute-start(f32[13,16,128]{2,1,0:T(8,128)S(1)} %get-tuple-element.26), channel_id=1, source_target_pairs={{0,7},{1,6},{2,5},{3,4},{4,11},{5,10},{6,9},{7,8},{8,15},{9,14},{1... | collective-permute-start | bytes 319496 | tf_op jit(solution)/shard_map/ppermute | solution.py:493
  41.2 2.9 %collective-permute-start.5 = (f32[13,16,128]{2,1,0:T(8,128)S(1)}, f32[13,16,128]{2,1,0:T(8,128)S(1)}, u32[]{:S(2)}, u32[]{:S(2)}) collective-permute-start(f32[13,16,128]{2,1,0:T(8,128)S(1)} %get-tuple-element.27), channel_id=1, source_target_pairs={{7,0},{6,1},{5,2},{4,3},{11,4},{10,5},{9,6},{8,7},{15,8},{14,9},{1... | collective-permute-start | bytes 319496 | tf_op jit(solution)/shard_map/ppermute | solution.py:493
  44.1 1.6 %collective-permute-done.4 = f32[13,16,128]{2,1,0:T(8,128)S(1)} collective-permute-done((f32[13,16,128]{2,1,0:T(8,128)S(1)}, f32[13,16,128]{2,1,0:T(8,128)S(1)}, u32[]{:S(2)}, u32[]{:S(2)}) %collective-permute-start.4) | collective-permute-done | bytes 106528 | tf_op jit(solution)/shard_map/ppermute | solution.py:493
  45.7 4.8 %collective-permute-done.5 = f32[13,16,128]{2,1,0:T(8,128)S(1)} collective-permute-done((f32[13,16,128]{2,1,0:T(8,128)S(1)}, f32[13,16,128]{2,1,0:T(8,128)S(1)}, u32[]{:S(2)}, u32[]{:S(2)}) %collective-permute-start.5) | collective-permute-done | bytes 106528 | tf_op jit(solution)/shard_map/ppermute | solution.py:493
  50.6 4.0 %collective-permute-start.6 = (f32[400,128]{1,0:T(8,128)S(1)}, f32[400,128]{1,0:T(8,128)S(1)}, u32[]{:S(2)}, u32[]{:S(2)}) collective-permute-start(f32[400,128]{1,0:T(8,128)S(1)} %constant_dynamic-update-slice_fusion), channel_id=1, source_target_pairs={{0,64},{64,128},{128,192},{192,256},{256,320},{320,384},{384,448},... | collective-permute-start | bytes 614408 | tf_op jit(solution)/shard_map/ppermute | solution.py:493
  54.7 1.3 %collective-permute-start.7 = (f32[400,128]{1,0:T(8,128)S(1)}, f32[400,128]{1,0:T(8,128)S(1)}, u32[]{:S(2)}, u32[]{:S(2)}) collective-permute-start(f32[400,128]{1,0:T(8,128)S(1)} %constant_dynamic-update-slice_fusion.7), channel_id=1, source_target_pairs={{64,0},{128,64},{192,128},{256,192},{320,256},{384,320},{448,384},... | collective-permute-start | bytes 614408 | tf_op jit(solution)/shard_map/ppermute | solution.py:493
  56.0 0.1 pad_add_fusion.place_ref
  56.1 3.4 %collective-permute-done.6.before_ref = f32[400,128]{1,0:T(8,128)S(1)} collective-permute-done((f32[400,128]{1,0:T(8,128)S(1)}, f32[400,128]{1,0:T(8,128)S(1)}, u32[]{:S(2)}, u32[]{:S(2)}) %collective-permute-start.6) | collective-permute-done | bytes 204832 | tf_op jit(solution)/shard_map/ppermute | solution.py:493
  59.5 5.8 %collective-permute-done.7.after_ref = f32[400,128]{1,0:T(8,128)S(1)} collective-permute-done((f32[400,128]{1,0:T(8,128)S(1)}, f32[400,128]{1,0:T(8,128)S(1)}, u32[]{:S(2)}, u32[]{:S(2)}) %collective-permute-start.7) | collective-permute-done | bytes 204832 | tf_op jit(solution)/shard_map/ppermute | solution.py:493
  65.4 5.2 %shard_map.43 = (f32[8,48,128]{2,1,0:T(8,128)S(1)}, f32[20,48,128]{2,1,0:T(8,128)S(1)}, f32[10,24,128]{2,1,0:T(8,128)S(1)}) custom-call(s32[3]{0:T(128)S(1)} %pad_add_fusion.place_ref, f32[42,16,128]{2,1,0:T(8,128)S(1)} %pad_maximum_fusion.window_ref, f32[400,128]{1,0:T(8,128)S(1)} %collective-permute-done.6.before_ref, ...), custom_call_target="tpu_custom_call" | custom-call | tf_op jit(solution)/shard_map/pallas_call | solution.py:548
  70.6 14.7 %all_to_all.15 = f32[8,48,128]{2,1,0:T(8,128)S(1)} all-to-all(f32[8,48,128]{2,1,0:T(8,128)S(1)} %get-tuple-element.18), channel_id=1, replica_groups=mesh['gz'=8,'xy'=64] {'gz'}, dimensions={0} | all-to-all | bytes 393216 | tf_op jit(solution)/shard_map/all_to_all | solution.py:561
  85.3 0.7 broadcast_in_dim.18
  86.0 7.0 %all-to-all-start.2 = ((f32[16,32,128]{2,1,0:T(8,128)}), f32[16,32,128]{2,1,0:T(8,128)S(1)}, u32[]{:S(2)}, u32[]{:S(2)}) async-start(f32[16,32,128]{2,1,0:T(8,128)} %broadcast_in_dim.18), calls=%async_computation.2 | async-start | bytes 524288 | tf_op jit(solution)/shard_map/all_to_all | solution.py:563
  93.0 3.9 %collective-permute-start.9 = (f32[5,24,128]{2,1,0:T(8,128)S(1)}, f32[5,24,128]{2,1,0:T(8,128)S(1)}, u32[]{:S(2)}, u32[]{:S(2)}) collective-permute-start(f32[5,24,128]{2,1,0:T(8,128)S(1)} %copy_bitcast_fusion), channel_id=1, source_target_pairs={{7,0},{6,1},{5,2},{4,3},{11,4},{10,5},{9,6},{8,7},{15,8},{14,9},{1... | collective-permute-start | bytes 184328 | tf_op jit(solution)/shard_map/ppermute | solution.py:493
  96.9 5.0 %collective-permute-start.8 = (f32[5,24,128]{2,1,0:T(8,128)S(1)}, f32[5,24,128]{2,1,0:T(8,128)S(1)}, u32[]{:S(2)}, u32[]{:S(2)}) collective-permute-start(f32[5,24,128]{2,1,0:T(8,128)S(1)} %copy_bitcast_fusion), channel_id=1, source_target_pairs={{0,7},{1,6},{2,5},{3,4},{4,11},{5,10},{6,9},{7,8},{8,15},{9,14},{1... | collective-permute-start | bytes 184328 | tf_op jit(solution)/shard_map/ppermute | solution.py:493
  101.9 3.9 %collective-permute-start.10 = (f32[3,48,128]{2,1,0:T(8,128)S(1)}, f32[3,48,128]{2,1,0:T(8,128)S(1)}, u32[]{:S(2)}, u32[]{:S(2)}) collective-permute-start(f32[3,48,128]{2,1,0:T(8,128)S(1)} %get-tuple-element.22), channel_id=1, source_target_pairs={{0,1},{1,2},{2,3},{3,4},{4,5},{5,6},{6,7},{7,8},{8,9},{9,10},{10,1... | collective-permute-start | bytes 221192 | tf_op jit(solution)/shard_map/ppermute | solution.py:493
  105.8 3.3 %collective-permute-start.11 = (f32[3,48,128]{2,1,0:T(8,128)S(1)}, f32[3,48,128]{2,1,0:T(8,128)S(1)}, u32[]{:S(2)}, u32[]{:S(2)}) collective-permute-start(f32[3,48,128]{2,1,0:T(8,128)S(1)} %get-tuple-element.23), channel_id=1, source_target_pairs={{1,0},{2,1},{3,2},{4,3},{5,4},{6,5},{7,6},{8,7},{9,8},{10,9},{11,1... | collective-permute-start | bytes 221192 | tf_op jit(solution)/shard_map/ppermute | solution.py:493
  109.2 0.0 collective-permute-done.9
  109.2 0.0 collective-permute-done.8
  109.2 0.0 collective-permute-done.10.before_ref
  109.2 5.6 %collective-permute-done.11.after_ref = f32[3,48,128]{2,1,0:T(8,128)S(1)} collective-permute-done((f32[3,48,128]{2,1,0:T(8,128)S(1)}, f32[3,48,128]{2,1,0:T(8,128)S(1)}, u32[]{:S(2)}, u32[]{:S(2)}) %collective-permute-start.11) | collective-permute-done | bytes 73760 | tf_op jit(solution)/shard_map/ppermute | solution.py:493
  114.8 0.0 all-to-all-done.2.gathered_ref
  114.8 10.9 %shard_map.44 = (f32[32,8,128]{2,1,0:T(8,128)}, f32[32,8,128]{2,1,0:T(8,128)}) custom-call(s32[3]{0:T(128)S(1)} %pad_add_fusion.place_ref, f32[16,32,128]{2,1,0:T(8,128)S(1)} %all-to-all-done.2.gathered_ref, f32[15,24,128]{2,1,0:T(8,128)S(1)} %pad_maximum_fusion.1.halo_ref, f32[20,48,128]{2,1,0:T(8,128)S(1)} %get-tuple-element.19.kept_ref, ...), custom_call_target="tpu_custom_call" | custom-call | tf_op jit(solution)/shard_map/pallas_call | solution.py:573
  (32 shorter events, 0.3 us)
Async XLA Ops:
  0.6 0.9 copy-start
  1.6 9.9 %copy-start.1 = (f32[32,8,128]{2,1,0:T(8,128)S(1)}, f32[32,8,128]{2,1,0:T(8,128)}, u32[]{:S(2)}) copy-start(f32[32,8,128]{2,1,0:T(8,128)} %right_ref.1) | copy-start | bytes 393220
  1.6 5.5 %collective-permute-start = (f32[17,8,128]{2,1,0:T(8,128)S(1)}, f32[17,8,128]{2,1,0:T(8,128)S(1)}, u32[]{:S(2)}, u32[]{:S(2)}) collective-permute-start(f32[17,8,128]{2,1,0:T(8,128)S(1)} %pad_maximum_fusion.2), channel_id=1, source_target_pairs={{0,64},{64,128},{128,192},{192,256},{256,320},{320,384},{384,448},... | collective-permute-start | bytes 208904 | tf_op jit(solution)/shard_map/ppermute | solution.py:493
  5.8 5.7 %collective-permute-start.1 = (f32[17,8,128]{2,1,0:T(8,128)S(1)}, f32[17,8,128]{2,1,0:T(8,128)S(1)}, u32[]{:S(2)}, u32[]{:S(2)}) collective-permute-start(f32[17,8,128]{2,1,0:T(8,128)S(1)} %pad_maximum_fusion.3), channel_id=1, source_target_pairs={{64,0},{128,64},{192,128},{256,192},{320,256},{384,320},{448,384},... | collective-permute-start | bytes 208904 | tf_op jit(solution)/shard_map/ppermute | solution.py:493
  11.6 9.2 %collective-permute-start.2 = (f32[10,48,128]{2,1,0:T(8,128)S(1)}, f32[10,48,128]{2,1,0:T(8,128)S(1)}, u32[]{:S(2)}, u32[]{:S(2)}) collective-permute-start(f32[10,48,128]{2,1,0:T(8,128)S(1)} %get-tuple-element.15), channel_id=1, source_target_pairs={{0,1},{1,2},{2,3},{3,4},{4,5},{5,6},{6,7},{7,8},{8,9},{9,10},{10,1... | collective-permute-start | bytes 737288 | tf_op jit(solution)/shard_map/ppermute | solution.py:493
  17.6 10.8 %collective-permute-start.3 = (f32[10,48,128]{2,1,0:T(8,128)S(1)}, f32[10,48,128]{2,1,0:T(8,128)S(1)}, u32[]{:S(2)}, u32[]{:S(2)}) collective-permute-start(f32[10,48,128]{2,1,0:T(8,128)S(1)} %get-tuple-element.16), channel_id=1, source_target_pairs={{1,0},{2,1},{3,2},{4,3},{5,4},{6,5},{7,6},{8,7},{9,8},{10,9},{11,1... | collective-permute-start | bytes 737288 | tf_op jit(solution)/shard_map/ppermute | solution.py:493
  31.4 5.8 %all-to-all-start = ((f32[4,64,128]{2,1,0:T(8,128)}), f32[4,64,128]{2,1,0:T(8,128)S(1)}, u32[]{:S(2)}, u32[]{:S(2)}) async-start(f32[4,64,128]{2,1,0:T(8,128)} %get-tuple-element.17), calls=%async_computation | async-start | bytes 262144 | tf_op jit(solution)/shard_map/all_to_all | solution.py:535
  37.3 8.5 %collective-permute-start.4 = (f32[13,16,128]{2,1,0:T(8,128)S(1)}, f32[13,16,128]{2,1,0:T(8,128)S(1)}, u32[]{:S(2)}, u32[]{:S(2)}) collective-permute-start(f32[13,16,128]{2,1,0:T(8,128)S(1)} %get-tuple-element.26), channel_id=1, source_target_pairs={{0,7},{1,6},{2,5},{3,4},{4,11},{5,10},{6,9},{7,8},{8,15},{9,14},{1... | collective-permute-start | bytes 319496 | tf_op jit(solution)/shard_map/ppermute | solution.py:493
  41.2 9.3 %collective-permute-start.5 = (f32[13,16,128]{2,1,0:T(8,128)S(1)}, f32[13,16,128]{2,1,0:T(8,128)S(1)}, u32[]{:S(2)}, u32[]{:S(2)}) collective-permute-start(f32[13,16,128]{2,1,0:T(8,128)S(1)} %get-tuple-element.27), channel_id=1, source_target_pairs={{7,0},{6,1},{5,2},{4,3},{11,4},{10,5},{9,6},{8,7},{15,8},{14,9},{1... | collective-permute-start | bytes 319496 | tf_op jit(solution)/shard_map/ppermute | solution.py:493
  50.6 8.9 %collective-permute-start.6 = (f32[400,128]{1,0:T(8,128)S(1)}, f32[400,128]{1,0:T(8,128)S(1)}, u32[]{:S(2)}, u32[]{:S(2)}) collective-permute-start(f32[400,128]{1,0:T(8,128)S(1)} %constant_dynamic-update-slice_fusion), channel_id=1, source_target_pairs={{0,64},{64,128},{128,192},{192,256},{256,320},{320,384},{384,448},... | collective-permute-start | bytes 614408 | tf_op jit(solution)/shard_map/ppermute | solution.py:493
  54.7 10.7 %collective-permute-start.7 = (f32[400,128]{1,0:T(8,128)S(1)}, f32[400,128]{1,0:T(8,128)S(1)}, u32[]{:S(2)}, u32[]{:S(2)}) collective-permute-start(f32[400,128]{1,0:T(8,128)S(1)} %constant_dynamic-update-slice_fusion.7), channel_id=1, source_target_pairs={{64,0},{128,64},{192,128},{256,192},{320,256},{384,320},{448,384},... | collective-permute-start | bytes 614408 | tf_op jit(solution)/shard_map/ppermute | solution.py:493
  86.0 28.8 %all-to-all-start.2 = ((f32[16,32,128]{2,1,0:T(8,128)}), f32[16,32,128]{2,1,0:T(8,128)S(1)}, u32[]{:S(2)}, u32[]{:S(2)}) async-start(f32[16,32,128]{2,1,0:T(8,128)} %broadcast_in_dim.18), calls=%async_computation.2 | async-start | bytes 524288 | tf_op jit(solution)/shard_map/all_to_all | solution.py:563
  93.0 16.1 %collective-permute-start.9 = (f32[5,24,128]{2,1,0:T(8,128)S(1)}, f32[5,24,128]{2,1,0:T(8,128)S(1)}, u32[]{:S(2)}, u32[]{:S(2)}) collective-permute-start(f32[5,24,128]{2,1,0:T(8,128)S(1)} %copy_bitcast_fusion), channel_id=1, source_target_pairs={{7,0},{6,1},{5,2},{4,3},{11,4},{10,5},{9,6},{8,7},{15,8},{14,9},{1... | collective-permute-start | bytes 184328 | tf_op jit(solution)/shard_map/ppermute | solution.py:493
  96.9 12.2 %collective-permute-start.8 = (f32[5,24,128]{2,1,0:T(8,128)S(1)}, f32[5,24,128]{2,1,0:T(8,128)S(1)}, u32[]{:S(2)}, u32[]{:S(2)}) collective-permute-start(f32[5,24,128]{2,1,0:T(8,128)S(1)} %copy_bitcast_fusion), channel_id=1, source_target_pairs={{0,7},{1,6},{2,5},{3,4},{4,11},{5,10},{6,9},{7,8},{8,15},{9,14},{1... | collective-permute-start | bytes 184328 | tf_op jit(solution)/shard_map/ppermute | solution.py:493
  101.9 7.3 %collective-permute-start.10 = (f32[3,48,128]{2,1,0:T(8,128)S(1)}, f32[3,48,128]{2,1,0:T(8,128)S(1)}, u32[]{:S(2)}, u32[]{:S(2)}) collective-permute-start(f32[3,48,128]{2,1,0:T(8,128)S(1)} %get-tuple-element.22), channel_id=1, source_target_pairs={{0,1},{1,2},{2,3},{3,4},{4,5},{5,6},{6,7},{7,8},{8,9},{9,10},{10,1... | collective-permute-start | bytes 221192 | tf_op jit(solution)/shard_map/ppermute | solution.py:493
  105.8 9.0 %collective-permute-start.11 = (f32[3,48,128]{2,1,0:T(8,128)S(1)}, f32[3,48,128]{2,1,0:T(8,128)S(1)}, u32[]{:S(2)}, u32[]{:S(2)}) collective-permute-start(f32[3,48,128]{2,1,0:T(8,128)S(1)} %get-tuple-element.23), channel_id=1, source_target_pairs={{1,0},{2,1},{3,2},{4,3},{5,4},{6,5},{7,6},{8,7},{9,8},{10,9},{11,1... | collective-permute-start | bytes 221192 | tf_op jit(solution)/shard_map/ppermute | solution.py:493

commit v9 on v8

--- a/solution.py
+++ b/solution.py
@@ -545,6 +545,8 @@
         return jnp.concatenate(parts, axis=0)
 
     before, after = pair(faces(True), faces(False), "gz")
+    rims = pair(last_rows, first_rows, "xy")
+    before, after, value_before, value_after = lax.optimization_barrier((before, after, *rims))
     chunks, kept, below1 = pl.pallas_call(
         middle_down,
         out_shape=[shape(gz, 48, 128), shape(20, 48, 128), shape(10, 24, 128)],
@@ -557,7 +559,6 @@
         compiler_params=params(),
     )(place, window, before, after)
 
-    value_before, value_after = pair(last_rows, first_rows, "xy")
     column = lax.all_to_all(chunks, "gz", 0, 0, tiled=True)
     peers = [[GROUP * i + j for i in range(xy // GROUP)] for j in range(GROUP)]
     everywhere = lax.all_to_all(

time: 126 us -> 124 us (0.984)
  the two profiles are of different devices: /device:TPU:31 before, /device:TPU:32 now
where the time goes in v9:
time: 124 us
  starting transfers between devices  55.7 us (45%)
  waiting for transfers between devices  25.8 us (21%)
  blocking collectives  20.1 us (16%)
  Pallas kernels  19.2 us (15%)
  local copies, waits for them, and re-layouts  1.86 us (2%)
    ppermute x6, starting transfers between devices, pair(): lax.ppermute(array_down, axis, down)  28.8 us
    all_to_all x1, blocking collectives, body(): column = lax.all_to_all(chunks, 'gz', 0, 0, tiled=True)  20.1 us
    ppermute x6, starting transfers between devices, pair(): lax.ppermute(array_up, axis, up)  16.4 us
    ppermute x6, waiting for transfers between devices, pair(): lax.ppermute(array_down, axis, down)  12.2 us
    pallas_call x1, Pallas kernels, body(): pl.pallas_call(partial(way_up, xy), out_shape=[shape(32, 8, 128)] * 2, in...  10.9 us
    ppermute x6, waiting for transfers between devices, pair(): lax.ppermute(array_up, axis, up)  9.01 us
    all_to_all x1, starting transfers between devices, body(): lax.all_to_all(jnp.broadcast_to(column[:, 40:44].reshape(1, 4 * gz, 128),...  7.22 us
    pallas_call x1, Pallas kernels, body(): pl.pallas_call(middle_down, out_shape=[shape(gz, 48, 128), shape(20, 48,...  5.23 us
  transfers between devices with their start and end apart: 14, of which 11 were waited for; matrix products, arithmetic and copies ran while one was open for 0% of the time, Pallas kernels for 0%

profile of v9, /device:TPU:32, one launch (start us, length us, event | category | flops | bytes accessed | tf_op | source)
XLA Modules:
  0.0 123.8 jit_solution(2820041010109652663)
XLA Ops:
  0.6 0.0 copy-start
  0.6 0.8 fusion.3
  1.5 0.1 copy-done
  1.6 0.0 copy-start.1
  1.6 4.4 %collective-permute-start = (f32[17,8,128]{2,1,0:T(8,128)S(1)}, f32[17,8,128]{2,1,0:T(8,128)S(1)}, u32[]{:S(2)}, u32[]{:S(2)}) collective-permute-start(f32[17,8,128]{2,1,0:T(8,128)S(1)} %pad_maximum_fusion.2), channel_id=1, source_target_pairs={{0,64},{64,128},{128,192},{192,256},{256,320},{320,384},{384,448},... | collective-permute-start | bytes 208904 | tf_op jit(solution)/shard_map/ppermute | solution.py:493
  6.1 1.3 %collective-permute-start.1 = (f32[17,8,128]{2,1,0:T(8,128)S(1)}, f32[17,8,128]{2,1,0:T(8,128)S(1)}, u32[]{:S(2)}, u32[]{:S(2)}) collective-permute-start(f32[17,8,128]{2,1,0:T(8,128)S(1)} %pad_maximum_fusion.3), channel_id=1, source_target_pairs={{64,0},{128,64},{192,128},{256,192},{320,256},{384,320},{448,384},... | collective-permute-start | bytes 208904 | tf_op jit(solution)/shard_map/ppermute | solution.py:493
  7.4 0.6 collective-permute-done.before_ref
  8.0 4.7 %collective-permute-done.1.after_ref = f32[17,8,128]{2,1,0:T(8,128)S(1)} collective-permute-done((f32[17,8,128]{2,1,0:T(8,128)S(1)}, f32[17,8,128]{2,1,0:T(8,128)S(1)}, u32[]{:S(2)}, u32[]{:S(2)}) %collective-permute-start.1) | collective-permute-done | bytes 69664 | tf_op jit(solution)/shard_map/ppermute | solution.py:493
  12.6 0.0 copy-done.1
  12.6 0.1 shard_map.41
  12.7 1.9 %collective-permute-start.2 = (f32[10,48,128]{2,1,0:T(8,128)S(1)}, f32[10,48,128]{2,1,0:T(8,128)S(1)}, u32[]{:S(2)}, u32[]{:S(2)}) collective-permute-start(f32[10,48,128]{2,1,0:T(8,128)S(1)} %get-tuple-element.19), channel_id=1, source_target_pairs={{0,1},{1,2},{2,3},{3,4},{4,5},{5,6},{6,7},{7,8},{8,9},{9,10},{10,1... | collective-permute-start | bytes 737288 | tf_op jit(solution)/shard_map/ppermute | solution.py:493
  14.7 7.0 %collective-permute-start.3 = (f32[10,48,128]{2,1,0:T(8,128)S(1)}, f32[10,48,128]{2,1,0:T(8,128)S(1)}, u32[]{:S(2)}, u32[]{:S(2)}) collective-permute-start(f32[10,48,128]{2,1,0:T(8,128)S(1)} %get-tuple-element.20), channel_id=1, source_target_pairs={{1,0},{2,1},{3,2},{4,3},{5,4},{6,5},{7,6},{8,7},{9,8},{10,9},{11,1... | collective-permute-start | bytes 737288 | tf_op jit(solution)/shard_map/ppermute | solution.py:493
  21.6 1.9 %collective-permute-done.2.before_ref.rim_before_ref = f32[10,48,128]{2,1,0:T(8,128)S(1)} collective-permute-done((f32[10,48,128]{2,1,0:T(8,128)S(1)}, f32[10,48,128]{2,1,0:T(8,128)S(1)}, u32[]{:S(2)}, u32[]{:S(2)}) %collective-permute-start.2) | collective-permute-done | bytes 245792 | tf_op jit(solution)/shard_map/ppermute | solution.py:493
  23.6 1.8 %collective-permute-done.3.after_ref.rim_after_ref = f32[10,48,128]{2,1,0:T(8,128)S(1)} collective-permute-done((f32[10,48,128]{2,1,0:T(8,128)S(1)}, f32[10,48,128]{2,1,0:T(8,128)S(1)}, u32[]{:S(2)}, u32[]{:S(2)}) %collective-permute-start.3) | collective-permute-done | bytes 245792 | tf_op jit(solution)/shard_map/ppermute | solution.py:493
  25.3 3.0 %shard_map.42 = (f32[4,64,128]{2,1,0:T(8,128)}, f32[3,48,128]{2,1,0:T(8,128)S(1)}, f32[3,48,128]{2,1,0:T(8,128)S(1)}, f32[4,64,128]{2,1,0:T(8,128)S(1)}) custom-call(f32[8,64,128]{2,1,0:T(8,128)S(1)} %get-tuple-element.17.s_ref, f32[8,64,128]{2,1,0:T(8,128)S(1)} %get-tuple-element.18.d_ref, ...), custom_call_target="tpu_custom_call" | custom-call | tf_op jit(solution)/shard_map/pallas_call | solution.py:527
  28.3 3.3 %all-to-all-start = ((f32[4,64,128]{2,1,0:T(8,128)}), f32[4,64,128]{2,1,0:T(8,128)S(1)}, u32[]{:S(2)}, u32[]{:S(2)}) async-start(f32[4,64,128]{2,1,0:T(8,128)} %get-tuple-element.21), calls=%async_computation | async-start | bytes 262144 | tf_op jit(solution)/shard_map/all_to_all | solution.py:535
  31.6 4.6 %all-to-all-done = f32[4,64,128]{2,1,0:T(8,128)S(1)} async-done(((f32[4,64,128]{2,1,0:T(8,128)}), f32[4,64,128]{2,1,0:T(8,128)S(1)}, u32[]{:S(2)}, u32[]{:S(2)}) %all-to-all-start) | async-done | bytes 131104 | tf_op jit(solution)/shard_map/all_to_all | solution.py:535
  36.3 1.9 %collective-permute-start.4 = (f32[13,16,128]{2,1,0:T(8,128)S(1)}, f32[13,16,128]{2,1,0:T(8,128)S(1)}, u32[]{:S(2)}, u32[]{:S(2)}) collective-permute-start(f32[13,16,128]{2,1,0:T(8,128)S(1)} %get-tuple-element.34), channel_id=1, source_target_pairs={{0,7},{1,6},{2,5},{3,4},{4,11},{5,10},{6,9},{7,8},{8,15},{9,14},{1... | collective-permute-start | bytes 319496 | tf_op jit(solution)/shard_map/ppermute | solution.py:493
  38.2 7.0 %collective-permute-start.5 = (f32[13,16,128]{2,1,0:T(8,128)S(1)}, f32[13,16,128]{2,1,0:T(8,128)S(1)}, u32[]{:S(2)}, u32[]{:S(2)}) collective-permute-start(f32[13,16,128]{2,1,0:T(8,128)S(1)} %get-tuple-element.35), channel_id=1, source_target_pairs={{7,0},{6,1},{5,2},{4,3},{11,4},{10,5},{9,6},{8,7},{15,8},{14,9},{1... | collective-permute-start | bytes 319496 | tf_op jit(solution)/shard_map/ppermute | solution.py:493
  45.2 1.3 %collective-permute-done.4 = f32[13,16,128]{2,1,0:T(8,128)S(1)} collective-permute-done((f32[13,16,128]{2,1,0:T(8,128)S(1)}, f32[13,16,128]{2,1,0:T(8,128)S(1)}, u32[]{:S(2)}, u32[]{:S(2)}) %collective-permute-start.4) | collective-permute-done | bytes 106528 | tf_op jit(solution)/shard_map/ppermute | solution.py:493
  46.5 2.1 %collective-permute-done.5 = f32[13,16,128]{2,1,0:T(8,128)S(1)} collective-permute-done((f32[13,16,128]{2,1,0:T(8,128)S(1)}, f32[13,16,128]{2,1,0:T(8,128)S(1)}, u32[]{:S(2)}, u32[]{:S(2)}) %collective-permute-start.5) | collective-permute-done | bytes 106528 | tf_op jit(solution)/shard_map/ppermute | solution.py:493
  48.8 4.3 %collective-permute-start.6 = (f32[400,128]{1,0:T(8,128)S(1)}, f32[400,128]{1,0:T(8,128)S(1)}, u32[]{:S(2)}, u32[]{:S(2)}) collective-permute-start(f32[400,128]{1,0:T(8,128)S(1)} %constant_dynamic-update-slice_fusion), channel_id=1, source_target_pairs={{0,64},{64,128},{128,192},{192,256},{256,320},{320,384},{384,448},... | collective-permute-start | bytes 614408 | tf_op jit(solution)/shard_map/ppermute | solution.py:493
  53.1 1.3 %collective-permute-start.7 = (f32[400,128]{1,0:T(8,128)S(1)}, f32[400,128]{1,0:T(8,128)S(1)}, u32[]{:S(2)}, u32[]{:S(2)}) collective-permute-start(f32[400,128]{1,0:T(8,128)S(1)} %constant_dynamic-update-slice_fusion.7), channel_id=1, source_target_pairs={{64,0},{128,64},{192,128},{256,192},{320,256},{384,320},{448,384},... | collective-permute-start | bytes 614408 | tf_op jit(solution)/shard_map/ppermute | solution.py:493
  54.4 0.1 pad_add_fusion.place_ref
  54.5 1.9 %collective-permute-start.8 = (f32[3,48,128]{2,1,0:T(8,128)S(1)}, f32[3,48,128]{2,1,0:T(8,128)S(1)}, u32[]{:S(2)}, u32[]{:S(2)}) collective-permute-start(f32[3,48,128]{2,1,0:T(8,128)S(1)} %get-tuple-element.22), channel_id=1, source_target_pairs={{0,1},{1,2},{2,3},{3,4},{4,5},{5,6},{6,7},{7,8},{8,9},{9,10},{10,1... | collective-permute-start | bytes 221192 | tf_op jit(solution)/shard_map/ppermute | solution.py:493
  56.4 7.0 %collective-permute-start.9 = (f32[3,48,128]{2,1,0:T(8,128)S(1)}, f32[3,48,128]{2,1,0:T(8,128)S(1)}, u32[]{:S(2)}, u32[]{:S(2)}) collective-permute-start(f32[3,48,128]{2,1,0:T(8,128)S(1)} %get-tuple-element.23), channel_id=1, source_target_pairs={{1,0},{2,1},{3,2},{4,3},{5,4},{6,5},{7,6},{8,7},{9,8},{10,9},{11,1... | collective-permute-start | bytes 221192 | tf_op jit(solution)/shard_map/ppermute | solution.py:493
  63.4 0.1 collective-permute-done.8.before_ref
  63.4 1.9 %collective-permute-done.9.after_ref = f32[3,48,128]{2,1,0:T(8,128)S(1)} collective-permute-done((f32[3,48,128]{2,1,0:T(8,128)S(1)}, f32[3,48,128]{2,1,0:T(8,128)S(1)}, u32[]{:S(2)}, u32[]{:S(2)}) %collective-permute-start.9) | collective-permute-done | bytes 73760 | tf_op jit(solution)/shard_map/ppermute | solution.py:493
  65.3 0.0 collective-permute-done.6.before_ref
  65.3 0.0 collective-permute-done.7.after_ref
  65.3 5.2 %shard_map.43 = (f32[8,48,128]{2,1,0:T(8,128)S(1)}, f32[20,48,128]{2,1,0:T(8,128)S(1)}, f32[10,24,128]{2,1,0:T(8,128)S(1)}) custom-call(s32[3]{0:T(128)S(1)} %pad_add_fusion.place_ref, f32[42,16,128]{2,1,0:T(8,128)S(1)} %pad_maximum_fusion.window_ref, f32[400,128]{1,0:T(8,128)S(1)} %collective-permute-done.6.before_ref, ...), custom_call_target="tpu_custom_call" | custom-call | tf_op jit(solution)/shard_map/pallas_call | solution.py:550
  70.5 20.1 %all_to_all.15 = f32[8,48,128]{2,1,0:T(8,128)S(1)} all-to-all(f32[8,48,128]{2,1,0:T(8,128)S(1)} %get-tuple-element.26), channel_id=1, replica_groups=mesh['gz'=8,'xy'=64] {'gz'}, dimensions={0} | all-to-all | bytes 393216 | tf_op jit(solution)/shard_map/all_to_all | solution.py:562
  90.6 0.7 broadcast_in_dim.18
  91.4 7.2 %all-to-all-start.2 = ((f32[16,32,128]{2,1,0:T(8,128)}), f32[16,32,128]{2,1,0:T(8,128)S(1)}, u32[]{:S(2)}, u32[]{:S(2)}) async-start(f32[16,32,128]{2,1,0:T(8,128)} %broadcast_in_dim.18), calls=%async_computation.2 | async-start | bytes 524288 | tf_op jit(solution)/shard_map/all_to_all | solution.py:564
  98.6 5.3 %collective-permute-start.11 = (f32[5,24,128]{2,1,0:T(8,128)S(1)}, f32[5,24,128]{2,1,0:T(8,128)S(1)}, u32[]{:S(2)}, u32[]{:S(2)}) collective-permute-start(f32[5,24,128]{2,1,0:T(8,128)S(1)} %copy_bitcast_fusion), channel_id=1, source_target_pairs={{7,0},{6,1},{5,2},{4,3},{11,4},{10,5},{9,6},{8,7},{15,8},{14,9},{1... | collective-permute-start | bytes 184328 | tf_op jit(solution)/shard_map/ppermute | solution.py:493
  104.0 1.9 %collective-permute-start.10 = (f32[5,24,128]{2,1,0:T(8,128)S(1)}, f32[5,24,128]{2,1,0:T(8,128)S(1)}, u32[]{:S(2)}, u32[]{:S(2)}) collective-permute-start(f32[5,24,128]{2,1,0:T(8,128)S(1)} %copy_bitcast_fusion), channel_id=1, source_target_pairs={{0,7},{1,6},{2,5},{3,4},{4,11},{5,10},{6,9},{7,8},{8,15},{9,14},{1... | collective-permute-start | bytes 184328 | tf_op jit(solution)/shard_map/ppermute | solution.py:493
  105.9 1.8 %collective-permute-done.11 = f32[5,24,128]{2,1,0:T(8,128)S(1)} collective-permute-done((f32[5,24,128]{2,1,0:T(8,128)S(1)}, f32[5,24,128]{2,1,0:T(8,128)S(1)}, u32[]{:S(2)}, u32[]{:S(2)}) %collective-permute-start.11) | collective-permute-done | bytes 61472 | tf_op jit(solution)/shard_map/ppermute | solution.py:493
  107.7 5.1 %collective-permute-done.10 = f32[5,24,128]{2,1,0:T(8,128)S(1)} collective-permute-done((f32[5,24,128]{2,1,0:T(8,128)S(1)}, f32[5,24,128]{2,1,0:T(8,128)S(1)}, u32[]{:S(2)}, u32[]{:S(2)}) %collective-permute-start.10) | collective-permute-done | bytes 61472 | tf_op jit(solution)/shard_map/ppermute | solution.py:493
  112.8 0.0 all-to-all-done.2.gathered_ref
  112.8 10.9 %shard_map.44 = (f32[32,8,128]{2,1,0:T(8,128)}, f32[32,8,128]{2,1,0:T(8,128)}) custom-call(s32[3]{0:T(128)S(1)} %pad_add_fusion.place_ref, f32[16,32,128]{2,1,0:T(8,128)S(1)} %all-to-all-done.2.gathered_ref, f32[15,24,128]{2,1,0:T(8,128)S(1)} %pad_maximum_fusion.1.halo_ref, f32[20,48,128]{2,1,0:T(8,128)S(1)} %get-tuple-element.27.kept_ref, ...), custom_call_target="tpu_custom_call" | custom-call | tf_op jit(solution)/shard_map/pallas_call | solution.py:574
  (32 shorter events, 0.3 us)
Async XLA Ops:
  0.6 0.9 copy-start
  1.6 11.0 %copy-start.1 = (f32[32,8,128]{2,1,0:T(8,128)S(1)}, f32[32,8,128]{2,1,0:T(8,128)}, u32[]{:S(2)}) copy-start(f32[32,8,128]{2,1,0:T(8,128)} %right_ref.1) | copy-start | bytes 393220
  1.6 6.3 %collective-permute-start = (f32[17,8,128]{2,1,0:T(8,128)S(1)}, f32[17,8,128]{2,1,0:T(8,128)S(1)}, u32[]{:S(2)}, u32[]{:S(2)}) collective-permute-start(f32[17,8,128]{2,1,0:T(8,128)S(1)} %pad_maximum_fusion.2), channel_id=1, source_target_pairs={{0,64},{64,128},{128,192},{192,256},{256,320},{320,384},{384,448},... | collective-permute-start | bytes 208904 | tf_op jit(solution)/shard_map/ppermute | solution.py:493
  6.1 6.6 %collective-permute-start.1 = (f32[17,8,128]{2,1,0:T(8,128)S(1)}, f32[17,8,128]{2,1,0:T(8,128)S(1)}, u32[]{:S(2)}, u32[]{:S(2)}) collective-permute-start(f32[17,8,128]{2,1,0:T(8,128)S(1)} %pad_maximum_fusion.3), channel_id=1, source_target_pairs={{64,0},{128,64},{192,128},{256,192},{320,256},{384,320},{448,384},... | collective-permute-start | bytes 208904 | tf_op jit(solution)/shard_map/ppermute | solution.py:493
  12.7 10.8 %collective-permute-start.2 = (f32[10,48,128]{2,1,0:T(8,128)S(1)}, f32[10,48,128]{2,1,0:T(8,128)S(1)}, u32[]{:S(2)}, u32[]{:S(2)}) collective-permute-start(f32[10,48,128]{2,1,0:T(8,128)S(1)} %get-tuple-element.19), channel_id=1, source_target_pairs={{0,1},{1,2},{2,3},{3,4},{4,5},{5,6},{6,7},{7,8},{8,9},{9,10},{10,1... | collective-permute-start | bytes 737288 | tf_op jit(solution)/shard_map/ppermute | solution.py:493
  14.7 10.7 %collective-permute-start.3 = (f32[10,48,128]{2,1,0:T(8,128)S(1)}, f32[10,48,128]{2,1,0:T(8,128)S(1)}, u32[]{:S(2)}, u32[]{:S(2)}) collective-permute-start(f32[10,48,128]{2,1,0:T(8,128)S(1)} %get-tuple-element.20), channel_id=1, source_target_pairs={{1,0},{2,1},{3,2},{4,3},{5,4},{6,5},{7,6},{8,7},{9,8},{10,9},{11,1... | collective-permute-start | bytes 737288 | tf_op jit(solution)/shard_map/ppermute | solution.py:493
  28.3 7.9 %all-to-all-start = ((f32[4,64,128]{2,1,0:T(8,128)}), f32[4,64,128]{2,1,0:T(8,128)S(1)}, u32[]{:S(2)}, u32[]{:S(2)}) async-start(f32[4,64,128]{2,1,0:T(8,128)} %get-tuple-element.21), calls=%async_computation | async-start | bytes 262144 | tf_op jit(solution)/shard_map/all_to_all | solution.py:535
  36.3 10.2 %collective-permute-start.4 = (f32[13,16,128]{2,1,0:T(8,128)S(1)}, f32[13,16,128]{2,1,0:T(8,128)S(1)}, u32[]{:S(2)}, u32[]{:S(2)}) collective-permute-start(f32[13,16,128]{2,1,0:T(8,128)S(1)} %get-tuple-element.34), channel_id=1, source_target_pairs={{0,7},{1,6},{2,5},{3,4},{4,11},{5,10},{6,9},{7,8},{8,15},{9,14},{1... | collective-permute-start | bytes 319496 | tf_op jit(solution)/shard_map/ppermute | solution.py:493
  38.2 10.4 %collective-permute-start.5 = (f32[13,16,128]{2,1,0:T(8,128)S(1)}, f32[13,16,128]{2,1,0:T(8,128)S(1)}, u32[]{:S(2)}, u32[]{:S(2)}) collective-permute-start(f32[13,16,128]{2,1,0:T(8,128)S(1)} %get-tuple-element.35), channel_id=1, source_target_pairs={{7,0},{6,1},{5,2},{4,3},{11,4},{10,5},{9,6},{8,7},{15,8},{14,9},{1... | collective-permute-start | bytes 319496 | tf_op jit(solution)/shard_map/ppermute | solution.py:493
  48.8 16.6 %collective-permute-start.6 = (f32[400,128]{1,0:T(8,128)S(1)}, f32[400,128]{1,0:T(8,128)S(1)}, u32[]{:S(2)}, u32[]{:S(2)}) collective-permute-start(f32[400,128]{1,0:T(8,128)S(1)} %constant_dynamic-update-slice_fusion), channel_id=1, source_target_pairs={{0,64},{64,128},{128,192},{192,256},{256,320},{320,384},{384,448},... | collective-permute-start | bytes 614408 | tf_op jit(solution)/shard_map/ppermute | solution.py:493
  53.1 12.2 %collective-permute-start.7 = (f32[400,128]{1,0:T(8,128)S(1)}, f32[400,128]{1,0:T(8,128)S(1)}, u32[]{:S(2)}, u32[]{:S(2)}) collective-permute-start(f32[400,128]{1,0:T(8,128)S(1)} %constant_dynamic-update-slice_fusion.7), channel_id=1, source_target_pairs={{64,0},{128,64},{192,128},{256,192},{320,256},{384,320},{448,384},... | collective-permute-start | bytes 614408 | tf_op jit(solution)/shard_map/ppermute | solution.py:493
  54.5 9.0 %collective-permute-start.8 = (f32[3,48,128]{2,1,0:T(8,128)S(1)}, f32[3,48,128]{2,1,0:T(8,128)S(1)}, u32[]{:S(2)}, u32[]{:S(2)}) collective-permute-start(f32[3,48,128]{2,1,0:T(8,128)S(1)} %get-tuple-element.22), channel_id=1, source_target_pairs={{0,1},{1,2},{2,3},{3,4},{4,5},{5,6},{6,7},{7,8},{8,9},{9,10},{10,1... | collective-permute-start | bytes 221192 | tf_op jit(solution)/shard_map/ppermute | solution.py:493
  56.4 8.9 %collective-permute-start.9 = (f32[3,48,128]{2,1,0:T(8,128)S(1)}, f32[3,48,128]{2,1,0:T(8,128)S(1)}, u32[]{:S(2)}, u32[]{:S(2)}) collective-permute-start(f32[3,48,128]{2,1,0:T(8,128)S(1)} %get-tuple-element.23), channel_id=1, source_target_pairs={{1,0},{2,1},{3,2},{4,3},{5,4},{6,5},{7,6},{8,7},{9,8},{10,9},{11,1... | collective-permute-start | bytes 221192 | tf_op jit(solution)/shard_map/ppermute | solution.py:493
  91.4 21.5 %all-to-all-start.2 = ((f32[16,32,128]{2,1,0:T(8,128)}), f32[16,32,128]{2,1,0:T(8,128)S(1)}, u32[]{:S(2)}, u32[]{:S(2)}) async-start(f32[16,32,128]{2,1,0:T(8,128)} %broadcast_in_dim.18), calls=%async_computation.2 | async-start | bytes 524288 | tf_op jit(solution)/shard_map/all_to_all | solution.py:564
  98.6 9.1 %collective-permute-start.11 = (f32[5,24,128]{2,1,0:T(8,128)S(1)}, f32[5,24,128]{2,1,0:T(8,128)S(1)}, u32[]{:S(2)}, u32[]{:S(2)}) collective-permute-start(f32[5,24,128]{2,1,0:T(8,128)S(1)} %copy_bitcast_fusion), channel_id=1, source_target_pairs={{7,0},{6,1},{5,2},{4,3},{11,4},{10,5},{9,6},{8,7},{15,8},{14,9},{1... | collective-permute-start | bytes 184328 | tf_op jit(solution)/shard_map/ppermute | solution.py:493
  104.0 8.9 %collective-permute-start.10 = (f32[5,24,128]{2,1,0:T(8,128)S(1)}, f32[5,24,128]{2,1,0:T(8,128)S(1)}, u32[]{:S(2)}, u32[]{:S(2)}) collective-permute-start(f32[5,24,128]{2,1,0:T(8,128)S(1)} %copy_bitcast_fusion), channel_id=1, source_target_pairs={{0,7},{1,6},{2,5},{3,4},{4,11},{5,10},{6,9},{7,8},{8,15},{9,14},{1... | collective-permute-start | bytes 184328 | tf_op jit(solution)/shard_map/ppermute | solution.py:493

commit v10 on v9

--- a/solution.py
+++ b/solution.py
@@ -382,16 +382,34 @@
     return wide[pl.ds(4 * place_ref[0], 12)]
 
 
-def way_up(devices, place_ref, gathered_ref, halo_ref, kept_ref, below1_ref,
-           s_ref, d_ref, rim_before_ref, rim_after_ref, below0_ref, before_ref, after_ref,
-           pressure_ref, remain_ref,
-           source3, density3, keep3, value3, wide,
-           source2, density2, keep2, value2, source1, density1, keep1, value1,
-           source0, density0, keep0, value0, plane):
-    at_y, at_group = place_ref[1], place_ref[2]
+def solve(place_ref, gathered_ref, kept_ref, s_ref, d_ref, rim_before_ref, rim_after_ref,
+          near_ref, keep1, keep0,
+          source3, density3, keep3, value3, wide, source1, density1, value1, source0, density0, value0):
     level1 = Level(density1, keep1, value1, 64, 64)
     finest_window(s_ref, d_ref, rim_before_ref, rim_after_ref, source0, density0)
     level0 = Level(density0, keep0, value0, 128)
+
+    def finest(i):
+        rows = pl.ds(5 * i, 5)
+        folded(kept_ref, rows, source1, density1, rows)
+        level0.coefficients(source0, 1.0, 1 + 2 * i, 2, 2)
+
+    near_ref[...] = coarsest(
+        place_ref, gathered_ref, source3, density3, keep3, value3, wide,
+        (
+            (4, finest),
+            (4, lambda i: level1.coefficients(source1, 4.0, 1 + 2 * i, 2, 2)),
+            (4, lambda i: None),
+        ),
+    )
+
+
+def way_up(devices, place_ref, near_ref, halo_ref, keep1, keep0, below1_ref, below0_ref, before_ref, after_ref,
+           pressure_ref, remain_ref,
+           source2, density2, keep2, value2, value1, value0, plane):
+    at_y, at_group = place_ref[1], place_ref[2]
+    level1 = Level(None, keep1, value1, 64, 64)
+    level0 = Level(None, keep0, value0, 128)
     lane = iota((24, 128), 1)
     for rows in (slice(0, 2), slice(20, 22)):
         density2[rows] = jnp.zeros((2, 24, 128), F32)
@@ -406,24 +424,8 @@
         value2[1, 1 + i] = jnp.where(lane < 32, black, 0.0)
     level = Level(density2, keep2, value2, 0)
     level.clear((0, 10))
-
-    def finest(i):
-        level0.coefficients(source0, 1.0, 1 + 2 * i, 2, 2)
-
-    def folding(i):
-        rows = pl.ds(5 * i, 5)
-        folded(kept_ref, rows, source1, density1, rows)
-        finest(i)
-
-    near = coarsest(
-        place_ref, gathered_ref, source3, density3, keep3, value3, wide,
-        (
-            (4, folding),
-            (3, lambda i: level.coefficients(source2, 16.0, 1 + 3 * i, 3, 3)),
-            (4, lambda i: level1.coefficients(source1, 4.0, 1 + 2 * i, 2, 2)),
-            (1, lambda i: None),
-        ),
-    )
+    level.coefficients(source2, 16.0, 1, 9, 3)
+    near = near_ref[...]
     row = iota((8, 128), 0)
     picked = []
     for i in range(9):
@@ -571,20 +573,28 @@
     before, after = pair(halo, halo, "xy", GROUP)
     halo = jnp.concatenate([before, halo, after], axis=0)
     planes = 4 * gz
+    near, keep1, keep0 = pl.pallas_call(
+        solve,
+        out_shape=[shape(12, 8, 128), shape(KEPT, 10, 24, 128), shape(KEPT, 10, 64, 128)],
+        in_specs=[smem] + [block] * 6,
+        scratch_shapes=[vmem(planes + 4, 8, 128)] * 2
+        + [vmem(KEPT, planes // 2 + 2, 8, 128), vmem(2, planes // 2 + 2, 8, 128), vmem(planes + 8, 8, 128)]
+        + [vmem(20, 24, 128)] * 2
+        + [vmem(2, 10, 24, 128)]
+        + [vmem(20, 64, 128)] * 2
+        + [vmem(2, 10, 64, 128)],
+        compiler_params=params(),
+        cost_estimate=pl.CostEstimate(flops=100_000_000, bytes_accessed=16_000_000, transcendentals=0),
+    )(place, everywhere, kept, *finest)
     return pl.pallas_call(
         partial(way_up, xy),
         out_shape=[shape(32, 8, 128)] * 2,
-        in_specs=[smem] + [block] * 11,
-        scratch_shapes=[vmem(planes + 4, 8, 128)] * 2
-        + [vmem(KEPT, planes // 2 + 2, 8, 128), vmem(2, planes // 2 + 2, 8, 128), vmem(planes + 8, 8, 128)]
-        + [vmem(22, 24, 128)] * 2
+        in_specs=[smem] + [block] * 8,
+        scratch_shapes=[vmem(22, 24, 128)] * 2
         + [vmem(KEPT, 11, 24, 128), vmem(2, 11, 24, 128)]
-        + [vmem(20, 24, 128)] * 2
-        + [vmem(KEPT, 10, 24, 128), vmem(2, 10, 24, 128)]
-        + [vmem(20, 64, 128)] * 2
-        + [vmem(KEPT, 10, 64, 128), vmem(2, 10, 64, 128), vmem(10, 64, 128)],
+        + [vmem(2, 10, 24, 128), vmem(2, 10, 64, 128), vmem(10, 64, 128)],
         compiler_params=params(),
-    )(place, everywhere, halo, kept, below1, *finest, below0, value_before, value_after)
+    )(place, near, halo, keep1, keep0, below1, below0, value_before, value_after)
 
 
 def solution(mesh):

time: 124 us -> 128 us (1.032)
  local copies, waits for them, and re-layouts: 1.86 us -> 3.51 us
    pallas_call x0 -> x1, Pallas kernels: none -> 6.08 us  [body(): pl.pallas_call(solve, out_shape=[shape(12, 8, 128), shape(KEPT, 10, 24, 1...]
    pallas_call x1, Pallas kernels: 10.9 us -> 5.5 us  [body(): pl.pallas_call(partial(way_up, xy), out_shape=[shape(32, 8, 128)] * 2, in...]
    unnamed x13, local copies, waits for them, and re-layouts: 0.17 us -> 1.86 us
where the time goes in v10:
time: 128 us; the launch traced here: 127 us
  starting transfers between devices  55.6 us (43%)
  waiting for transfers between devices  25.8 us (20%)
  blocking collectives  20.1 us (16%)
  Pallas kernels  19.9 us (16%)
  local copies, waits for them, and re-layouts  3.51 us (3%)
    ppermute x6, starting transfers between devices, pair(): lax.ppermute(array_down, axis, down)  28.8 us
    all_to_all x1, blocking collectives, body(): column = lax.all_to_all(chunks, 'gz', 0, 0, tiled=True)  20.1 us
    ppermute x6, starting transfers between devices, pair(): lax.ppermute(array_up, axis, up)  16.2 us
    ppermute x6, waiting for transfers between devices, pair(): lax.ppermute(array_down, axis, down)  12.2 us
    ppermute x6, waiting for transfers between devices, pair(): lax.ppermute(array_up, axis, up)  9.01 us
    all_to_all x1, starting transfers between devices, body(): lax.all_to_all(jnp.broadcast_to(column[:, 40:44].reshape(1, 4 * gz, 128),...  7.22 us
    pallas_call x1, Pallas kernels, body(): pl.pallas_call(solve, out_shape=[shape(12, 8, 128), shape(KEPT, 10, 24, 1...  6.08 us
    pallas_call x1, Pallas kernels, body(): pl.pallas_call(partial(way_up, xy), out_shape=[shape(32, 8, 128)] * 2, in...  5.5 us
  transfers between devices with their start and end apart: 14, of which 11 were waited for; matrix products, arithmetic and copies ran while one was open for 0% of the time, Pallas kernels for 0%

profile of v10, /device:TPU:32, one launch (start us, length us, event | category | flops | bytes accessed | tf_op | source)
XLA Modules:
  0.0 126.8 jit_solution(7946122290262705696)
XLA Ops:
  0.6 0.8 fusion.3
  1.4 0.9 compare_select_fusion
  2.4 4.3 %collective-permute-start = (f32[17,8,128]{2,1,0:T(8,128)S(1)}, f32[17,8,128]{2,1,0:T(8,128)S(1)}, u32[]{:S(2)}, u32[]{:S(2)}) collective-permute-start(f32[17,8,128]{2,1,0:T(8,128)S(1)} %pad_maximum_fusion.2), channel_id=1, source_target_pairs={{0,64},{64,128},{128,192},{192,256},{256,320},{320,384},{384,448},... | collective-permute-start | bytes 208904 | tf_op jit(solution)/shard_map/ppermute | solution.py:495
  6.7 1.3 %collective-permute-start.1 = (f32[17,8,128]{2,1,0:T(8,128)S(1)}, f32[17,8,128]{2,1,0:T(8,128)S(1)}, u32[]{:S(2)}, u32[]{:S(2)}) collective-permute-start(f32[17,8,128]{2,1,0:T(8,128)S(1)} %pad_maximum_fusion.3), channel_id=1, source_target_pairs={{64,0},{128,64},{192,128},{256,192},{320,256},{384,320},{448,384},... | collective-permute-start | bytes 208904 | tf_op jit(solution)/shard_map/ppermute | solution.py:495
  8.0 0.6 collective-permute-done.before_ref
  8.6 4.7 %collective-permute-done.1.after_ref = f32[17,8,128]{2,1,0:T(8,128)S(1)} collective-permute-done((f32[17,8,128]{2,1,0:T(8,128)S(1)}, f32[17,8,128]{2,1,0:T(8,128)S(1)}, u32[]{:S(2)}, u32[]{:S(2)}) %collective-permute-start.1) | collective-permute-done | bytes 69664 | tf_op jit(solution)/shard_map/ppermute | solution.py:495
  13.2 0.0 copy-start
  13.2 0.9 copy-done
  14.1 0.0 copy-start.1
  14.1 0.9 copy-done.1
  15.0 0.1 shard_map.41
  15.1 1.9 %collective-permute-start.2 = (f32[10,48,128]{2,1,0:T(8,128)S(1)}, f32[10,48,128]{2,1,0:T(8,128)S(1)}, u32[]{:S(2)}, u32[]{:S(2)}) collective-permute-start(f32[10,48,128]{2,1,0:T(8,128)S(1)} %get-tuple-element.22), channel_id=1, source_target_pairs={{0,1},{1,2},{2,3},{3,4},{4,5},{5,6},{6,7},{7,8},{8,9},{9,10},{10,1... | collective-permute-start | bytes 737288 | tf_op jit(solution)/shard_map/ppermute | solution.py:495
  17.1 7.0 %collective-permute-start.3 = (f32[10,48,128]{2,1,0:T(8,128)S(1)}, f32[10,48,128]{2,1,0:T(8,128)S(1)}, u32[]{:S(2)}, u32[]{:S(2)}) collective-permute-start(f32[10,48,128]{2,1,0:T(8,128)S(1)} %get-tuple-element.23), channel_id=1, source_target_pairs={{1,0},{2,1},{3,2},{4,3},{5,4},{6,5},{7,6},{8,7},{9,8},{10,9},{11,1... | collective-permute-start | bytes 737288 | tf_op jit(solution)/shard_map/ppermute | solution.py:495
  24.0 1.9 %collective-permute-done.2.before_ref.rim_before_ref = f32[10,48,128]{2,1,0:T(8,128)S(1)} collective-permute-done((f32[10,48,128]{2,1,0:T(8,128)S(1)}, f32[10,48,128]{2,1,0:T(8,128)S(1)}, u32[]{:S(2)}, u32[]{:S(2)}) %collective-permute-start.2) | collective-permute-done | bytes 245792 | tf_op jit(solution)/shard_map/ppermute | solution.py:495
  26.0 1.8 %collective-permute-done.3.after_ref.rim_after_ref = f32[10,48,128]{2,1,0:T(8,128)S(1)} collective-permute-done((f32[10,48,128]{2,1,0:T(8,128)S(1)}, f32[10,48,128]{2,1,0:T(8,128)S(1)}, u32[]{:S(2)}, u32[]{:S(2)}) %collective-permute-start.3) | collective-permute-done | bytes 245792 | tf_op jit(solution)/shard_map/ppermute | solution.py:495
  27.7 3.0 %shard_map.42 = (f32[4,64,128]{2,1,0:T(8,128)}, f32[3,48,128]{2,1,0:T(8,128)S(1)}, f32[3,48,128]{2,1,0:T(8,128)S(1)}, f32[4,64,128]{2,1,0:T(8,128)S(1)}) custom-call(f32[8,64,128]{2,1,0:T(8,128)S(1)} %get-tuple-element.20.s_ref, f32[8,64,128]{2,1,0:T(8,128)S(1)} %get-tuple-element.21.d_ref, ...), custom_call_target="tpu_custom_call" | custom-call | tf_op jit(solution)/shard_map/pallas_call | solution.py:529
  30.7 3.3 %all-to-all-start = ((f32[4,64,128]{2,1,0:T(8,128)}), f32[4,64,128]{2,1,0:T(8,128)S(1)}, u32[]{:S(2)}, u32[]{:S(2)}) async-start(f32[4,64,128]{2,1,0:T(8,128)} %get-tuple-element.24), calls=%async_computation | async-start | bytes 262144 | tf_op jit(solution)/shard_map/all_to_all | solution.py:537
  34.0 4.6 %all-to-all-done = f32[4,64,128]{2,1,0:T(8,128)S(1)} async-done(((f32[4,64,128]{2,1,0:T(8,128)}), f32[4,64,128]{2,1,0:T(8,128)S(1)}, u32[]{:S(2)}, u32[]{:S(2)}) %all-to-all-start) | async-done | bytes 131104 | tf_op jit(solution)/shard_map/all_to_all | solution.py:537
  38.7 1.9 %collective-permute-start.4 = (f32[13,16,128]{2,1,0:T(8,128)S(1)}, f32[13,16,128]{2,1,0:T(8,128)S(1)}, u32[]{:S(2)}, u32[]{:S(2)}) collective-permute-start(f32[13,16,128]{2,1,0:T(8,128)S(1)} %get-tuple-element.40), channel_id=1, source_target_pairs={{0,7},{1,6},{2,5},{3,4},{4,11},{5,10},{6,9},{7,8},{8,15},{9,14},{1... | collective-permute-start | bytes 319496 | tf_op jit(solution)/shard_map/ppermute | solution.py:495
  40.6 7.0 %collective-permute-start.5 = (f32[13,16,128]{2,1,0:T(8,128)S(1)}, f32[13,16,128]{2,1,0:T(8,128)S(1)}, u32[]{:S(2)}, u32[]{:S(2)}) collective-permute-start(f32[13,16,128]{2,1,0:T(8,128)S(1)} %get-tuple-element.41), channel_id=1, source_target_pairs={{7,0},{6,1},{5,2},{4,3},{11,4},{10,5},{9,6},{8,7},{15,8},{14,9},{1... | collective-permute-start | bytes 319496 | tf_op jit(solution)/shard_map/ppermute | solution.py:495
  47.6 1.3 %collective-permute-done.4 = f32[13,16,128]{2,1,0:T(8,128)S(1)} collective-permute-done((f32[13,16,128]{2,1,0:T(8,128)S(1)}, f32[13,16,128]{2,1,0:T(8,128)S(1)}, u32[]{:S(2)}, u32[]{:S(2)}) %collective-permute-start.4) | collective-permute-done | bytes 106528 | tf_op jit(solution)/shard_map/ppermute | solution.py:495
  48.9 2.1 %collective-permute-done.5 = f32[13,16,128]{2,1,0:T(8,128)S(1)} collective-permute-done((f32[13,16,128]{2,1,0:T(8,128)S(1)}, f32[13,16,128]{2,1,0:T(8,128)S(1)}, u32[]{:S(2)}, u32[]{:S(2)}) %collective-permute-start.5) | collective-permute-done | bytes 106528 | tf_op jit(solution)/shard_map/ppermute | solution.py:495
  51.2 4.3 %collective-permute-start.6 = (f32[400,128]{1,0:T(8,128)S(1)}, f32[400,128]{1,0:T(8,128)S(1)}, u32[]{:S(2)}, u32[]{:S(2)}) collective-permute-start(f32[400,128]{1,0:T(8,128)S(1)} %constant_dynamic-update-slice_fusion), channel_id=1, source_target_pairs={{0,64},{64,128},{128,192},{192,256},{256,320},{320,384},{384,448},... | collective-permute-start | bytes 614408 | tf_op jit(solution)/shard_map/ppermute | solution.py:495
  55.5 1.3 %collective-permute-start.7 = (f32[400,128]{1,0:T(8,128)S(1)}, f32[400,128]{1,0:T(8,128)S(1)}, u32[]{:S(2)}, u32[]{:S(2)}) collective-permute-start(f32[400,128]{1,0:T(8,128)S(1)} %constant_dynamic-update-slice_fusion.7), channel_id=1, source_target_pairs={{64,0},{128,64},{192,128},{256,192},{320,256},{384,320},{448,384},... | collective-permute-start | bytes 614408 | tf_op jit(solution)/shard_map/ppermute | solution.py:495
  56.8 0.1 pad_add_fusion.place_ref
  56.9 1.9 %collective-permute-start.8 = (f32[3,48,128]{2,1,0:T(8,128)S(1)}, f32[3,48,128]{2,1,0:T(8,128)S(1)}, u32[]{:S(2)}, u32[]{:S(2)}) collective-permute-start(f32[3,48,128]{2,1,0:T(8,128)S(1)} %get-tuple-element.25), channel_id=1, source_target_pairs={{0,1},{1,2},{2,3},{3,4},{4,5},{5,6},{6,7},{7,8},{8,9},{9,10},{10,1... | collective-permute-start | bytes 221192 | tf_op jit(solution)/shard_map/ppermute | solution.py:495
  58.8 7.0 %collective-permute-start.9 = (f32[3,48,128]{2,1,0:T(8,128)S(1)}, f32[3,48,128]{2,1,0:T(8,128)S(1)}, u32[]{:S(2)}, u32[]{:S(2)}) collective-permute-start(f32[3,48,128]{2,1,0:T(8,128)S(1)} %get-tuple-element.26), channel_id=1, source_target_pairs={{1,0},{2,1},{3,2},{4,3},{5,4},{6,5},{7,6},{8,7},{9,8},{10,9},{11,1... | collective-permute-start | bytes 221192 | tf_op jit(solution)/shard_map/ppermute | solution.py:495
  65.8 0.1 collective-permute-done.8.before_ref
  65.8 1.9 %collective-permute-done.9.after_ref = f32[3,48,128]{2,1,0:T(8,128)S(1)} collective-permute-done((f32[3,48,128]{2,1,0:T(8,128)S(1)}, f32[3,48,128]{2,1,0:T(8,128)S(1)}, u32[]{:S(2)}, u32[]{:S(2)}) %collective-permute-start.9) | collective-permute-done | bytes 73760 | tf_op jit(solution)/shard_map/ppermute | solution.py:495
  67.7 0.0 collective-permute-done.6.before_ref
  67.7 0.0 collective-permute-done.7.after_ref
  67.7 5.2 %shard_map.43 = (f32[8,48,128]{2,1,0:T(8,128)S(1)}, f32[20,48,128]{2,1,0:T(8,128)S(1)}, f32[10,24,128]{2,1,0:T(8,128)S(1)}) custom-call(s32[3]{0:T(128)S(1)} %pad_add_fusion.place_ref, f32[42,16,128]{2,1,0:T(8,128)S(1)} %pad_maximum_fusion.window_ref, f32[400,128]{1,0:T(8,128)S(1)} %collective-permute-done.6.before_ref, ...), custom_call_target="tpu_custom_call" | custom-call | tf_op jit(solution)/shard_map/pallas_call | solution.py:552
  73.0 20.1 %all_to_all.15 = f32[8,48,128]{2,1,0:T(8,128)S(1)} all-to-all(f32[8,48,128]{2,1,0:T(8,128)S(1)} %get-tuple-element.29), channel_id=1, replica_groups=mesh['gz'=8,'xy'=64] {'gz'}, dimensions={0} | all-to-all | bytes 393216 | tf_op jit(solution)/shard_map/all_to_all | solution.py:564
  93.0 0.7 broadcast_in_dim.18
  93.8 7.2 %all-to-all-start.2 = ((f32[16,32,128]{2,1,0:T(8,128)}), f32[16,32,128]{2,1,0:T(8,128)S(1)}, u32[]{:S(2)}, u32[]{:S(2)}) async-start(f32[16,32,128]{2,1,0:T(8,128)} %broadcast_in_dim.18), calls=%async_computation.2 | async-start | bytes 524288 | tf_op jit(solution)/shard_map/all_to_all | solution.py:566
  101.0 5.3 %collective-permute-start.11 = (f32[5,24,128]{2,1,0:T(8,128)S(1)}, f32[5,24,128]{2,1,0:T(8,128)S(1)}, u32[]{:S(2)}, u32[]{:S(2)}) collective-permute-start(f32[5,24,128]{2,1,0:T(8,128)S(1)} %copy_bitcast_fusion), channel_id=1, source_target_pairs={{7,0},{6,1},{5,2},{4,3},{11,4},{10,5},{9,6},{8,7},{15,8},{14,9},{1... | collective-permute-start | bytes 184328 | tf_op jit(solution)/shard_map/ppermute | solution.py:495
  106.4 1.9 %collective-permute-start.10 = (f32[5,24,128]{2,1,0:T(8,128)S(1)}, f32[5,24,128]{2,1,0:T(8,128)S(1)}, u32[]{:S(2)}, u32[]{:S(2)}) collective-permute-start(f32[5,24,128]{2,1,0:T(8,128)S(1)} %copy_bitcast_fusion), channel_id=1, source_target_pairs={{0,7},{1,6},{2,5},{3,4},{4,11},{5,10},{6,9},{7,8},{8,15},{9,14},{1... | collective-permute-start | bytes 184328 | tf_op jit(solution)/shard_map/ppermute | solution.py:495
  108.3 1.8 %collective-permute-done.11 = f32[5,24,128]{2,1,0:T(8,128)S(1)} collective-permute-done((f32[5,24,128]{2,1,0:T(8,128)S(1)}, f32[5,24,128]{2,1,0:T(8,128)S(1)}, u32[]{:S(2)}, u32[]{:S(2)}) %collective-permute-start.11) | collective-permute-done | bytes 61472 | tf_op jit(solution)/shard_map/ppermute | solution.py:495
  110.1 5.1 %collective-permute-done.10 = f32[5,24,128]{2,1,0:T(8,128)S(1)} collective-permute-done((f32[5,24,128]{2,1,0:T(8,128)S(1)}, f32[5,24,128]{2,1,0:T(8,128)S(1)}, u32[]{:S(2)}, u32[]{:S(2)}) %collective-permute-start.10) | collective-permute-done | bytes 61472 | tf_op jit(solution)/shard_map/ppermute | solution.py:495
  115.2 0.0 all-to-all-done.2.gathered_ref
  115.3 6.1 %shard_map.44 = (f32[12,8,128]{2,1,0:T(8,128)S(1)}, f32[13,10,24,128]{3,2,1,0:T(8,128)S(1)}, f32[13,10,64,128]{3,2,1,0:T(8,128)S(1)}) custom-call(s32[3]{0:T(128)S(1)} %pad_add_fusion.place_ref, f32[16,32,128]{2,1,0:T(8,128)S(1)} %all-to-all-done.2.gathered_ref, f32[20,48,128]{2,1,0:T(8,128)S(1)} %get-tuple-element.30.kept_ref, ...), custom_call_target="tpu_custom_call" | custom-call | flops 100000000 | bytes 16000000 | tf_op jit(solution)/shard_map/pallas_call | solution.py:576
  121.3 5.5 %shard_map.45 = (f32[32,8,128]{2,1,0:T(8,128)}, f32[32,8,128]{2,1,0:T(8,128)}) custom-call(s32[3]{0:T(128)S(1)} %pad_add_fusion.place_ref, f32[12,8,128]{2,1,0:T(8,128)S(1)} %get-tuple-element.31.near_ref, f32[15,24,128]{2,1,0:T(8,128)S(1)} %pad_maximum_fusion.1.halo_ref, f32[13,10,24,128]{3,2,1,0:T(8,128)S(1)} %get-tuple-element.32.keep1, ...), custom_call_target="tpu_custom_call" | custom-call | tf_op jit(solution)/shard_map/pallas_call | solution.py:589
  (31 shorter events, 0.2 us)
Async XLA Ops:
  2.4 6.2 %collective-permute-start = (f32[17,8,128]{2,1,0:T(8,128)S(1)}, f32[17,8,128]{2,1,0:T(8,128)S(1)}, u32[]{:S(2)}, u32[]{:S(2)}) collective-permute-start(f32[17,8,128]{2,1,0:T(8,128)S(1)} %pad_maximum_fusion.2), channel_id=1, source_target_pairs={{0,64},{64,128},{128,192},{192,256},{256,320},{320,384},{384,448},... | collective-permute-start | bytes 208904 | tf_op jit(solution)/shard_map/ppermute | solution.py:495
  6.7 6.6 %collective-permute-start.1 = (f32[17,8,128]{2,1,0:T(8,128)S(1)}, f32[17,8,128]{2,1,0:T(8,128)S(1)}, u32[]{:S(2)}, u32[]{:S(2)}) collective-permute-start(f32[17,8,128]{2,1,0:T(8,128)S(1)} %pad_maximum_fusion.3), channel_id=1, source_target_pairs={{64,0},{128,64},{192,128},{256,192},{320,256},{384,320},{448,384},... | collective-permute-start | bytes 208904 | tf_op jit(solution)/shard_map/ppermute | solution.py:495
  13.2 0.9 copy-start
  14.1 0.9 copy-start.1
  15.1 10.8 %collective-permute-start.2 = (f32[10,48,128]{2,1,0:T(8,128)S(1)}, f32[10,48,128]{2,1,0:T(8,128)S(1)}, u32[]{:S(2)}, u32[]{:S(2)}) collective-permute-start(f32[10,48,128]{2,1,0:T(8,128)S(1)} %get-tuple-element.22), channel_id=1, source_target_pairs={{0,1},{1,2},{2,3},{3,4},{4,5},{5,6},{6,7},{7,8},{8,9},{9,10},{10,1... | collective-permute-start | bytes 737288 | tf_op jit(solution)/shard_map/ppermute | solution.py:495
  17.1 10.7 %collective-permute-start.3 = (f32[10,48,128]{2,1,0:T(8,128)S(1)}, f32[10,48,128]{2,1,0:T(8,128)S(1)}, u32[]{:S(2)}, u32[]{:S(2)}) collective-permute-start(f32[10,48,128]{2,1,0:T(8,128)S(1)} %get-tuple-element.23), channel_id=1, source_target_pairs={{1,0},{2,1},{3,2},{4,3},{5,4},{6,5},{7,6},{8,7},{9,8},{10,9},{11,1... | collective-permute-start | bytes 737288 | tf_op jit(solution)/shard_map/ppermute | solution.py:495
  30.7 7.9 %all-to-all-start = ((f32[4,64,128]{2,1,0:T(8,128)}), f32[4,64,128]{2,1,0:T(8,128)S(1)}, u32[]{:S(2)}, u32[]{:S(2)}) async-start(f32[4,64,128]{2,1,0:T(8,128)} %get-tuple-element.24), calls=%async_computation | async-start | bytes 262144 | tf_op jit(solution)/shard_map/all_to_all | solution.py:537
  38.7 10.2 %collective-permute-start.4 = (f32[13,16,128]{2,1,0:T(8,128)S(1)}, f32[13,16,128]{2,1,0:T(8,128)S(1)}, u32[]{:S(2)}, u32[]{:S(2)}) collective-permute-start(f32[13,16,128]{2,1,0:T(8,128)S(1)} %get-tuple-element.40), channel_id=1, source_target_pairs={{0,7},{1,6},{2,5},{3,4},{4,11},{5,10},{6,9},{7,8},{8,15},{9,14},{1... | collective-permute-start | bytes 319496 | tf_op jit(solution)/shard_map/ppermute | solution.py:495
  40.6 10.4 %collective-permute-start.5 = (f32[13,16,128]{2,1,0:T(8,128)S(1)}, f32[13,16,128]{2,1,0:T(8,128)S(1)}, u32[]{:S(2)}, u32[]{:S(2)}) collective-permute-start(f32[13,16,128]{2,1,0:T(8,128)S(1)} %get-tuple-element.41), channel_id=1, source_target_pairs={{7,0},{6,1},{5,2},{4,3},{11,4},{10,5},{9,6},{8,7},{15,8},{14,9},{1... | collective-permute-start | bytes 319496 | tf_op jit(solution)/shard_map/ppermute | solution.py:495
  51.2 16.6 %collective-permute-start.6 = (f32[400,128]{1,0:T(8,128)S(1)}, f32[400,128]{1,0:T(8,128)S(1)}, u32[]{:S(2)}, u32[]{:S(2)}) collective-permute-start(f32[400,128]{1,0:T(8,128)S(1)} %constant_dynamic-update-slice_fusion), channel_id=1, source_target_pairs={{0,64},{64,128},{128,192},{192,256},{256,320},{320,384},{384,448},... | collective-permute-start | bytes 614408 | tf_op jit(solution)/shard_map/ppermute | solution.py:495
  55.5 12.2 %collective-permute-start.7 = (f32[400,128]{1,0:T(8,128)S(1)}, f32[400,128]{1,0:T(8,128)S(1)}, u32[]{:S(2)}, u32[]{:S(2)}) collective-permute-start(f32[400,128]{1,0:T(8,128)S(1)} %constant_dynamic-update-slice_fusion.7), channel_id=1, source_target_pairs={{64,0},{128,64},{192,128},{256,192},{320,256},{384,320},{448,384},... | collective-permute-start | bytes 614408 | tf_op jit(solution)/shard_map/ppermute | solution.py:495
  56.9 9.0 %collective-permute-start.8 = (f32[3,48,128]{2,1,0:T(8,128)S(1)}, f32[3,48,128]{2,1,0:T(8,128)S(1)}, u32[]{:S(2)}, u32[]{:S(2)}) collective-permute-start(f32[3,48,128]{2,1,0:T(8,128)S(1)} %get-tuple-element.25), channel_id=1, source_target_pairs={{0,1},{1,2},{2,3},{3,4},{4,5},{5,6},{6,7},{7,8},{8,9},{9,10},{10,1... | collective-permute-start | bytes 221192 | tf_op jit(solution)/shard_map/ppermute | solution.py:495
  58.8 8.9 %collective-permute-start.9 = (f32[3,48,128]{2,1,0:T(8,128)S(1)}, f32[3,48,128]{2,1,0:T(8,128)S(1)}, u32[]{:S(2)}, u32[]{:S(2)}) collective-permute-start(f32[3,48,128]{2,1,0:T(8,128)S(1)} %get-tuple-element.26), channel_id=1, source_target_pairs={{1,0},{2,1},{3,2},{4,3},{5,4},{6,5},{7,6},{8,7},{9,8},{10,9},{11,1... | collective-permute-start | bytes 221192 | tf_op jit(solution)/shard_map/ppermute | solution.py:495
  93.8 21.5 %all-to-all-start.2 = ((f32[16,32,128]{2,1,0:T(8,128)}), f32[16,32,128]{2,1,0:T(8,128)S(1)}, u32[]{:S(2)}, u32[]{:S(2)}) async-start(f32[16,32,128]{2,1,0:T(8,128)} %broadcast_in_dim.18), calls=%async_computation.2 | async-start | bytes 524288 | tf_op jit(solution)/shard_map/all_to_all | solution.py:566
  101.0 9.1 %collective-permute-start.11 = (f32[5,24,128]{2,1,0:T(8,128)S(1)}, f32[5,24,128]{2,1,0:T(8,128)S(1)}, u32[]{:S(2)}, u32[]{:S(2)}) collective-permute-start(f32[5,24,128]{2,1,0:T(8,128)S(1)} %copy_bitcast_fusion), channel_id=1, source_target_pairs={{7,0},{6,1},{5,2},{4,3},{11,4},{10,5},{9,6},{8,7},{15,8},{14,9},{1... | collective-permute-start | bytes 184328 | tf_op jit(solution)/shard_map/ppermute | solution.py:495
  106.4 8.9 %collective-permute-start.10 = (f32[5,24,128]{2,1,0:T(8,128)S(1)}, f32[5,24,128]{2,1,0:T(8,128)S(1)}, u32[]{:S(2)}, u32[]{:S(2)}) collective-permute-start(f32[5,24,128]{2,1,0:T(8,128)S(1)} %copy_bitcast_fusion), channel_id=1, source_target_pairs={{0,7},{1,6},{2,5},{3,4},{4,11},{5,10},{6,9},{7,8},{8,15},{9,14},{1... | collective-permute-start | bytes 184328 | tf_op jit(solution)/shard_map/ppermute | solution.py:495

commit v11 on v9

--- a/solution.py
+++ b/solution.py
@@ -254,7 +254,7 @@
     density[start] = jnp.where(left, pltpu.roll(near, 64, 2), far)
 
 
-def middle_down(place_ref, window_ref, before_ref, after_ref, chunk_ref, kept_ref, below_ref,
+def middle_down(place_ref, window_ref, before_ref, after_ref, chunk_ref, halo_ref, kept_ref, below_ref,
                 window, source, density, keep, value, plane, source2, density2, keep2, value2):
     for near, ref in ((0, before_ref), (32, after_ref)):
         window[0:44, near : near + 16] = jnp.zeros((44, 16, 128), F32)
@@ -318,33 +318,29 @@
         total = pooled[8 * row : 8 * row + 1]
         for i in range(1, 8):
             total = total + pltpu.roll(pooled[8 * row + i : 8 * row + i + 1], 16 * i, 1)
-        chunk_ref[0, 40 + row : 41 + row] = total
+        chunk_ref[0, row : row + 1] = total
     black = jnp.zeros((8, 128), F32)
     for j in range(4):
         total = black
         for k, ref in enumerate((source2, density2, source2, density2)):
             total = total + pltpu.roll(ref[6 + 2 * j + k // 2, 8:16], 32 * k, 1)
-        chunk_ref[0, 8 * j : 8 * j + 8] = total
+        halo_ref[8 * j : 8 * j + 8] = total
     for j in range(4):
         black = black + pltpu.roll(value2[1, 3 + j, 8:16], 32 * j, 1)
-    chunk_ref[0, 32:40] = black
-    chunk_ref[0, 44:48] = jnp.zeros((4, 128), F32)
+    halo_ref[32:40] = black
+    chunk_ref[0, 4:8] = jnp.zeros((4, 128), F32)
     for peer in range(1, chunk_ref.shape[0]):
         chunk_ref[peer] = chunk_ref[0]
 
 
 def coarsest(place_ref, gathered_ref, source, density, keep, value, wide, besides):
     planes = wide.shape[0] - 8
-    groups = gathered_ref.shape[0]
     lane = iota((8, 128), 1)
     for row in (0, 1, planes + 2, planes + 3):
         density[row] = jnp.zeros((8, 128), F32)
 
     def spread(g):
-        tiles = [
-            jnp.concatenate([gathered_ref[2 * h + k, 4 * g : 4 * g + 4] for k in range(2)], axis=0)
-            for h in range(groups // 2)
-        ]
+        tiles = [gathered_ref[g, 8 * h : 8 * h + 8] for h in range(gathered_ref.shape[1] // 8)]
         tiles += [jnp.zeros((8, 128), F32)] * (8 - len(tiles))
         for step in (1, 2, 4):
             upper = (lane // 16) % (2 * step) >= step
@@ -547,9 +543,9 @@
     before, after = pair(faces(True), faces(False), "gz")
     rims = pair(last_rows, first_rows, "xy")
     before, after, value_before, value_after = lax.optimization_barrier((before, after, *rims))
-    chunks, kept, below1 = pl.pallas_call(
+    chunks, halo, kept, below1 = pl.pallas_call(
         middle_down,
-        out_shape=[shape(gz, 48, 128), shape(20, 48, 128), shape(10, 24, 128)],
+        out_shape=[shape(xy // GROUP, 8, 128), shape(40, 128), shape(20, 48, 128), shape(10, 24, 128)],
         in_specs=[smem] + [block] * 3,
         scratch_shapes=[vmem(44, 48, 128)]
         + [vmem(44, 24, 128)] * 2
@@ -559,17 +555,14 @@
         compiler_params=params(),
     )(place, window, before, after)
 
-    column = lax.all_to_all(chunks, "gz", 0, 0, tiled=True)
     peers = [[GROUP * i + j for i in range(xy // GROUP)] for j in range(GROUP)]
-    everywhere = lax.all_to_all(
-        jnp.broadcast_to(column[:, 40:44].reshape(1, 4 * gz, 128), (xy // GROUP, 4 * gz, 128)),
-        "xy", 0, 0, axis_index_groups=peers, tiled=True,
-    )
-    halo = jnp.pad(column[:, :40], ((1, 1), (0, 0), (0, 0)))
-    halo = lax.dynamic_slice(halo, (lax.axis_index("gz"), 0, 0), (3, 40, 128)).reshape(3, 5, 8, 128)
-    halo = jnp.swapaxes(halo, 0, 1).reshape(5, 24, 128)
+    chunks = lax.all_to_all(chunks, "xy", 0, 0, axis_index_groups=peers, tiled=True)
     before, after = pair(halo, halo, "xy", GROUP)
     halo = jnp.concatenate([before, halo, after], axis=0)
+    layer = chunks[:, :4].reshape(1, xy, 128)
+    everywhere = lax.all_to_all(jnp.broadcast_to(layer, (gz, xy, 128)), "gz", 0, 0, tiled=True)
+    before, after = pair(halo, halo, "gz")
+    halo = jnp.concatenate([part.reshape(15, 8, 128) for part in (before, halo, after)], axis=1)
     planes = 4 * gz
     return pl.pallas_call(
         partial(way_up, xy),

time: 124 us -> 122 us (0.984)
  the two profiles are of different devices: /device:TPU:32 before, /device:TPU:40 now
where the time goes in v11:
time: 122 us; the launch traced here: 121 us
  starting transfers between devices  74.7 us (61%)
  waiting for transfers between devices  23.6 us (19%)
  Pallas kernels  19.8 us (16%)
  local copies, waits for them, and re-layouts  1.82 us (1%)
    ppermute x7, starting transfers between devices, pair(): lax.ppermute(array_up, axis, up)  27.1 us
    ppermute x7, starting transfers between devices, pair(): lax.ppermute(array_down, axis, down)  22.6 us
    ppermute x7, waiting for transfers between devices, pair(): lax.ppermute(array_down, axis, down)  11.5 us
    all_to_all x1, starting transfers between devices, body(): lax.all_to_all(chunks, 'xy', 0, 0, axis_index_groups=peers, tiled=True)  11.2 us
    pallas_call x1, Pallas kernels, body(): pl.pallas_call(partial(way_up, xy), out_shape=[shape(32, 8, 128)] * 2, in...  10.9 us
    all_to_all x1, starting transfers between devices, body(): lax.all_to_all(jnp.broadcast_to(layer, (gz, xy, 128)), 'gz', 0, 0, tiled=...  10.5 us
    pallas_call x1, Pallas kernels, body(): pl.pallas_call(middle_down, out_shape=[shape(xy // GROUP, 8, 128), shape(...  5.85 us
    all_to_all x1, waiting for transfers between devices, body(): lax.all_to_all(chunks, 'xy', 0, 0, axis_index_groups=teams, tiled=True)  4.58 us
  transfers between devices with their start and end apart: 17, of which 12 were waited for; matrix products, arithmetic and copies ran while one was open for 1% of the time, Pallas kernels for 0%

profile of v11, /device:TPU:40, one launch (start us, length us, event | category | flops | bytes accessed | tf_op | source)
XLA Modules:
  0.0 121.2 jit_solution(16059351388467146622)
XLA Ops:
  0.6 0.0 copy-start
  0.6 0.8 fusion.2
  1.5 0.1 copy-done
  1.6 0.0 copy-start.1
  1.6 4.4 %collective-permute-start = (f32[17,8,128]{2,1,0:T(8,128)S(1)}, f32[17,8,128]{2,1,0:T(8,128)S(1)}, u32[]{:S(2)}, u32[]{:S(2)}) collective-permute-start(f32[17,8,128]{2,1,0:T(8,128)S(1)} %pad_maximum_fusion.2), channel_id=1, source_target_pairs={{0,64},{64,128},{128,192},{192,256},{256,320},{320,384},{384,448},... | collective-permute-start | bytes 208904 | tf_op jit(solution)/shard_map/ppermute | solution.py:489
  6.1 1.3 %collective-permute-start.1 = (f32[17,8,128]{2,1,0:T(8,128)S(1)}, f32[17,8,128]{2,1,0:T(8,128)S(1)}, u32[]{:S(2)}, u32[]{:S(2)}) collective-permute-start(f32[17,8,128]{2,1,0:T(8,128)S(1)} %pad_maximum_fusion.3), channel_id=1, source_target_pairs={{64,0},{128,64},{192,128},{256,192},{320,256},{384,320},{448,384},... | collective-permute-start | bytes 208904 | tf_op jit(solution)/shard_map/ppermute | solution.py:489
  7.4 0.6 collective-permute-done.before_ref
  8.0 4.7 %collective-permute-done.1.after_ref = f32[17,8,128]{2,1,0:T(8,128)S(1)} collective-permute-done((f32[17,8,128]{2,1,0:T(8,128)S(1)}, f32[17,8,128]{2,1,0:T(8,128)S(1)}, u32[]{:S(2)}, u32[]{:S(2)}) %collective-permute-start.1) | collective-permute-done | bytes 69664 | tf_op jit(solution)/shard_map/ppermute | solution.py:489
  12.6 0.0 copy-done.1
  12.6 0.1 shard_map.41
  12.7 1.9 %collective-permute-start.2 = (f32[10,48,128]{2,1,0:T(8,128)S(1)}, f32[10,48,128]{2,1,0:T(8,128)S(1)}, u32[]{:S(2)}, u32[]{:S(2)}) collective-permute-start(f32[10,48,128]{2,1,0:T(8,128)S(1)} %get-tuple-element.20), channel_id=1, source_target_pairs={{0,1},{1,2},{2,3},{3,4},{4,5},{5,6},{6,7},{7,8},{8,9},{9,10},{10,1... | collective-permute-start | bytes 737288 | tf_op jit(solution)/shard_map/ppermute | solution.py:489
  14.7 5.8 %collective-permute-start.3 = (f32[10,48,128]{2,1,0:T(8,128)S(1)}, f32[10,48,128]{2,1,0:T(8,128)S(1)}, u32[]{:S(2)}, u32[]{:S(2)}) collective-permute-start(f32[10,48,128]{2,1,0:T(8,128)S(1)} %get-tuple-element.21), channel_id=1, source_target_pairs={{1,0},{2,1},{3,2},{4,3},{5,4},{6,5},{7,6},{8,7},{9,8},{10,9},{11,1... | collective-permute-start | bytes 737288 | tf_op jit(solution)/shard_map/ppermute | solution.py:489
  20.4 1.9 %collective-permute-done.2.before_ref.rim_before_ref = f32[10,48,128]{2,1,0:T(8,128)S(1)} collective-permute-done((f32[10,48,128]{2,1,0:T(8,128)S(1)}, f32[10,48,128]{2,1,0:T(8,128)S(1)}, u32[]{:S(2)}, u32[]{:S(2)}) %collective-permute-start.2) | collective-permute-done | bytes 245792 | tf_op jit(solution)/shard_map/ppermute | solution.py:489
  22.4 1.8 %collective-permute-done.3.after_ref.rim_after_ref = f32[10,48,128]{2,1,0:T(8,128)S(1)} collective-permute-done((f32[10,48,128]{2,1,0:T(8,128)S(1)}, f32[10,48,128]{2,1,0:T(8,128)S(1)}, u32[]{:S(2)}, u32[]{:S(2)}) %collective-permute-start.3) | collective-permute-done | bytes 245792 | tf_op jit(solution)/shard_map/ppermute | solution.py:489
  24.1 3.0 %shard_map.42 = (f32[4,64,128]{2,1,0:T(8,128)}, f32[3,48,128]{2,1,0:T(8,128)S(1)}, f32[3,48,128]{2,1,0:T(8,128)S(1)}, f32[4,64,128]{2,1,0:T(8,128)S(1)}) custom-call(f32[8,64,128]{2,1,0:T(8,128)S(1)} %get-tuple-element.18.s_ref, f32[8,64,128]{2,1,0:T(8,128)S(1)} %get-tuple-element.19.d_ref, ...), custom_call_target="tpu_custom_call" | custom-call | tf_op jit(solution)/shard_map/pallas_call | solution.py:523
  27.1 3.3 %all-to-all-start = ((f32[4,64,128]{2,1,0:T(8,128)}), f32[4,64,128]{2,1,0:T(8,128)S(1)}, u32[]{:S(2)}, u32[]{:S(2)}) async-start(f32[4,64,128]{2,1,0:T(8,128)} %get-tuple-element.22), calls=%async_computation | async-start | bytes 262144 | tf_op jit(solution)/shard_map/all_to_all | solution.py:531
  30.4 4.6 %all-to-all-done = f32[4,64,128]{2,1,0:T(8,128)S(1)} async-done(((f32[4,64,128]{2,1,0:T(8,128)}), f32[4,64,128]{2,1,0:T(8,128)S(1)}, u32[]{:S(2)}, u32[]{:S(2)}) %all-to-all-start) | async-done | bytes 131104 | tf_op jit(solution)/shard_map/all_to_all | solution.py:531
  35.0 3.0 %collective-permute-start.4 = (f32[13,16,128]{2,1,0:T(8,128)S(1)}, f32[13,16,128]{2,1,0:T(8,128)S(1)}, u32[]{:S(2)}, u32[]{:S(2)}) collective-permute-start(f32[13,16,128]{2,1,0:T(8,128)S(1)} %get-tuple-element.36), channel_id=1, source_target_pairs={{0,7},{1,6},{2,5},{3,4},{4,11},{5,10},{6,9},{7,8},{8,15},{9,14},{1... | collective-permute-start | bytes 319496 | tf_op jit(solution)/shard_map/ppermute | solution.py:489
  38.1 4.7 %collective-permute-start.5 = (f32[13,16,128]{2,1,0:T(8,128)S(1)}, f32[13,16,128]{2,1,0:T(8,128)S(1)}, u32[]{:S(2)}, u32[]{:S(2)}) collective-permute-start(f32[13,16,128]{2,1,0:T(8,128)S(1)} %get-tuple-element.37), channel_id=1, source_target_pairs={{7,0},{6,1},{5,2},{4,3},{11,4},{10,5},{9,6},{8,7},{15,8},{14,9},{1... | collective-permute-start | bytes 319496 | tf_op jit(solution)/shard_map/ppermute | solution.py:489
  42.8 1.2 collective-permute-done.4
  44.0 1.7 %collective-permute-done.5 = f32[13,16,128]{2,1,0:T(8,128)S(1)} collective-permute-done((f32[13,16,128]{2,1,0:T(8,128)S(1)}, f32[13,16,128]{2,1,0:T(8,128)S(1)}, u32[]{:S(2)}, u32[]{:S(2)}) %collective-permute-start.5) | collective-permute-done | bytes 106528 | tf_op jit(solution)/shard_map/ppermute | solution.py:489
  45.9 4.3 %collective-permute-start.6 = (f32[400,128]{1,0:T(8,128)S(1)}, f32[400,128]{1,0:T(8,128)S(1)}, u32[]{:S(2)}, u32[]{:S(2)}) collective-permute-start(f32[400,128]{1,0:T(8,128)S(1)} %constant_dynamic-update-slice_fusion), channel_id=1, source_target_pairs={{0,64},{64,128},{128,192},{192,256},{256,320},{320,384},{384,448},... | collective-permute-start | bytes 614408 | tf_op jit(solution)/shard_map/ppermute | solution.py:489
  50.2 1.3 %collective-permute-start.7 = (f32[400,128]{1,0:T(8,128)S(1)}, f32[400,128]{1,0:T(8,128)S(1)}, u32[]{:S(2)}, u32[]{:S(2)}) collective-permute-start(f32[400,128]{1,0:T(8,128)S(1)} %constant_dynamic-update-slice_fusion.7), channel_id=1, source_target_pairs={{64,0},{128,64},{192,128},{256,192},{320,256},{384,320},{448,384},... | collective-permute-start | bytes 614408 | tf_op jit(solution)/shard_map/ppermute | solution.py:489
  51.5 0.1 pad_add_fusion.place_ref
  51.6 2.2 %collective-permute-start.8 = (f32[3,48,128]{2,1,0:T(8,128)S(1)}, f32[3,48,128]{2,1,0:T(8,128)S(1)}, u32[]{:S(2)}, u32[]{:S(2)}) collective-permute-start(f32[3,48,128]{2,1,0:T(8,128)S(1)} %get-tuple-element.23), channel_id=1, source_target_pairs={{0,1},{1,2},{2,3},{3,4},{4,5},{5,6},{6,7},{7,8},{8,9},{9,10},{10,1... | collective-permute-start | bytes 221192 | tf_op jit(solution)/shard_map/ppermute | solution.py:489
  53.7 5.5 %collective-permute-start.9 = (f32[3,48,128]{2,1,0:T(8,128)S(1)}, f32[3,48,128]{2,1,0:T(8,128)S(1)}, u32[]{:S(2)}, u32[]{:S(2)}) collective-permute-start(f32[3,48,128]{2,1,0:T(8,128)S(1)} %get-tuple-element.24), channel_id=1, source_target_pairs={{1,0},{2,1},{3,2},{4,3},{5,4},{6,5},{7,6},{8,7},{9,8},{10,9},{11,1... | collective-permute-start | bytes 221192 | tf_op jit(solution)/shard_map/ppermute | solution.py:489
  59.3 0.1 collective-permute-done.8.before_ref
  59.3 1.9 %collective-permute-done.9.after_ref = f32[3,48,128]{2,1,0:T(8,128)S(1)} collective-permute-done((f32[3,48,128]{2,1,0:T(8,128)S(1)}, f32[3,48,128]{2,1,0:T(8,128)S(1)}, u32[]{:S(2)}, u32[]{:S(2)}) %collective-permute-start.9) | collective-permute-done | bytes 73760 | tf_op jit(solution)/shard_map/ppermute | solution.py:489
  61.2 0.0 collective-permute-done.6.before_ref
  61.2 0.0 collective-permute-done.7.after_ref
  61.2 5.9 %shard_map.43 = (f32[16,8,128]{2,1,0:T(8,128)}, f32[40,128]{1,0:T(8,128)S(1)}, f32[20,48,128]{2,1,0:T(8,128)S(1)}, f32[10,24,128]{2,1,0:T(8,128)S(1)}) custom-call(s32[3]{0:T(128)S(1)} %pad_add_fusion.place_ref, f32[42,16,128]{2,1,0:T(8,128)S(1)} %pad_maximum_fusion.window_ref, f32[400,128]{1,0:T(8,128)S(1)} %collective-permute-done.6.before_ref, ...), custom_call_target="tpu_custom_call" | custom-call | tf_op jit(solution)/shard_map/pallas_call | solution.py:546
  67.1 11.2 %all-to-all-start.1 = ((f32[16,8,128]{2,1,0:T(8,128)}), f32[16,8,128]{2,1,0:T(8,128)S(1)}, u32[]{:S(2)}, u32[]{:S(2)}) async-start(f32[16,8,128]{2,1,0:T(8,128)} %get-tuple-element.27), calls=%async_computation.1 | async-start | bytes 131072 | tf_op jit(solution)/shard_map/all_to_all | solution.py:559
  78.3 6.7 %collective-permute-start.10 = (f32[40,128]{1,0:T(8,128)S(1)}, f32[40,128]{1,0:T(8,128)S(1)}, u32[]{:S(2)}, u32[]{:S(2)}) collective-permute-start(f32[40,128]{1,0:T(8,128)S(1)} %get-tuple-element.28), channel_id=1, source_target_pairs={{0,7},{1,6},{2,5},{3,4},{4,11},{5,10},{6,9},{7,8},{8,15},{9,14},{1... | collective-permute-start | bytes 61448 | tf_op jit(solution)/shard_map/ppermute | solution.py:489
  85.0 2.8 %collective-permute-start.11 = (f32[40,128]{1,0:T(8,128)S(1)}, f32[40,128]{1,0:T(8,128)S(1)}, u32[]{:S(2)}, u32[]{:S(2)}) collective-permute-start(f32[40,128]{1,0:T(8,128)S(1)} %get-tuple-element.28), channel_id=1, source_target_pairs={{7,0},{6,1},{5,2},{4,3},{11,4},{10,5},{9,6},{8,7},{15,8},{14,9},{1... | collective-permute-start | bytes 61448 | tf_op jit(solution)/shard_map/ppermute | solution.py:489
  87.9 0.0 all-to-all-done.1
  87.9 0.7 broadcast_in_dim.18
  88.6 10.5 %all-to-all-start.2 = ((f32[8,64,128]{2,1,0:T(8,128)}), f32[8,64,128]{2,1,0:T(8,128)S(1)}, u32[]{:S(2)}, u32[]{:S(2)}) async-start(f32[8,64,128]{2,1,0:T(8,128)} %broadcast_in_dim.18), calls=%async_computation.2 | async-start | bytes 524288 | tf_op jit(solution)/shard_map/all_to_all | solution.py:563
  99.1 0.0 collective-permute-done.10
  99.1 0.0 collective-permute-done.11
  99.1 1.3 %collective-permute-start.13 = (f32[120,128]{1,0:T(8,128)S(1)}, f32[120,128]{1,0:T(8,128)S(1)}, u32[]{:S(2)}, u32[]{:S(2)}) collective-permute-start(f32[120,128]{1,0:T(8,128)S(1)} %constant_dynamic-update-slice_fusion.14), channel_id=1, source_target_pairs={{64,0},{128,64},{192,128},{256,192},{320,256},{384,320},{448,384},... | collective-permute-start | bytes 184328 | tf_op jit(solution)/shard_map/ppermute | solution.py:489
  100.4 4.5 %collective-permute-start.12 = (f32[120,128]{1,0:T(8,128)S(1)}, f32[120,128]{1,0:T(8,128)S(1)}, u32[]{:S(2)}, u32[]{:S(2)}) collective-permute-start(f32[120,128]{1,0:T(8,128)S(1)} %constant_dynamic-update-slice_fusion.14), channel_id=1, source_target_pairs={{0,64},{64,128},{128,192},{192,256},{256,320},{320,384},{384,448},... | collective-permute-start | bytes 184328 | tf_op jit(solution)/shard_map/ppermute | solution.py:489
  105.0 1.5 %collective-permute-done.13 = f32[120,128]{1,0:T(8,128)S(1)} collective-permute-done((f32[120,128]{1,0:T(8,128)S(1)}, f32[120,128]{1,0:T(8,128)S(1)}, u32[]{:S(2)}, u32[]{:S(2)}) %collective-permute-start.13) | collective-permute-done | bytes 61472 | tf_op jit(solution)/shard_map/ppermute | solution.py:489
  106.5 0.3 collective-permute-done.12
  106.9 3.4 %all-to-all-done.2.gathered_ref = f32[8,64,128]{2,1,0:T(8,128)S(1)} async-done(((f32[8,64,128]{2,1,0:T(8,128)}), f32[8,64,128]{2,1,0:T(8,128)S(1)}, u32[]{:S(2)}, u32[]{:S(2)}) %all-to-all-start.2) | async-done | bytes 262176 | tf_op jit(solution)/shard_map/all_to_all | solution.py:563
  110.2 10.9 %shard_map.44 = (f32[32,8,128]{2,1,0:T(8,128)}, f32[32,8,128]{2,1,0:T(8,128)}) custom-call(s32[3]{0:T(128)S(1)} %pad_add_fusion.place_ref, f32[8,64,128]{2,1,0:T(8,128)S(1)} %all-to-all-done.2.gathered_ref, f32[15,24,128]{2,1,0:T(8,128)S(1)} %pad_maximum_fusion.1.halo_ref, f32[20,48,128]{2,1,0:T(8,128)S(1)} %get-tuple-element.29.kept_ref, ...), custom_call_target="tpu_custom_call" | custom-call | tf_op jit(solution)/shard_map/pallas_call | solution.py:567
  (33 shorter events, 0.3 us)
Async XLA Ops:
  0.6 0.9 copy-start
  1.6 11.0 %copy-start.1 = (f32[32,8,128]{2,1,0:T(8,128)S(1)}, f32[32,8,128]{2,1,0:T(8,128)}, u32[]{:S(2)}) copy-start(f32[32,8,128]{2,1,0:T(8,128)} %right_ref.1) | copy-start | bytes 393220
  1.6 6.3 %collective-permute-start = (f32[17,8,128]{2,1,0:T(8,128)S(1)}, f32[17,8,128]{2,1,0:T(8,128)S(1)}, u32[]{:S(2)}, u32[]{:S(2)}) collective-permute-start(f32[17,8,128]{2,1,0:T(8,128)S(1)} %pad_maximum_fusion.2), channel_id=1, source_target_pairs={{0,64},{64,128},{128,192},{192,256},{256,320},{320,384},{384,448},... | collective-permute-start | bytes 208904 | tf_op jit(solution)/shard_map/ppermute | solution.py:489
  6.1 6.6 %collective-permute-start.1 = (f32[17,8,128]{2,1,0:T(8,128)S(1)}, f32[17,8,128]{2,1,0:T(8,128)S(1)}, u32[]{:S(2)}, u32[]{:S(2)}) collective-permute-start(f32[17,8,128]{2,1,0:T(8,128)S(1)} %pad_maximum_fusion.3), channel_id=1, source_target_pairs={{64,0},{128,64},{192,128},{256,192},{320,256},{384,320},{448,384},... | collective-permute-start | bytes 208904 | tf_op jit(solution)/shard_map/ppermute | solution.py:489
  12.7 9.6 %collective-permute-start.2 = (f32[10,48,128]{2,1,0:T(8,128)S(1)}, f32[10,48,128]{2,1,0:T(8,128)S(1)}, u32[]{:S(2)}, u32[]{:S(2)}) collective-permute-start(f32[10,48,128]{2,1,0:T(8,128)S(1)} %get-tuple-element.20), channel_id=1, source_target_pairs={{0,1},{1,2},{2,3},{3,4},{4,5},{5,6},{6,7},{7,8},{8,9},{9,10},{10,1... | collective-permute-start | bytes 737288 | tf_op jit(solution)/shard_map/ppermute | solution.py:489
  14.7 9.5 %collective-permute-start.3 = (f32[10,48,128]{2,1,0:T(8,128)S(1)}, f32[10,48,128]{2,1,0:T(8,128)S(1)}, u32[]{:S(2)}, u32[]{:S(2)}) collective-permute-start(f32[10,48,128]{2,1,0:T(8,128)S(1)} %get-tuple-element.21), channel_id=1, source_target_pairs={{1,0},{2,1},{3,2},{4,3},{5,4},{6,5},{7,6},{8,7},{9,8},{10,9},{11,1... | collective-permute-start | bytes 737288 | tf_op jit(solution)/shard_map/ppermute | solution.py:489
  27.1 7.9 %all-to-all-start = ((f32[4,64,128]{2,1,0:T(8,128)}), f32[4,64,128]{2,1,0:T(8,128)S(1)}, u32[]{:S(2)}, u32[]{:S(2)}) async-start(f32[4,64,128]{2,1,0:T(8,128)} %get-tuple-element.22), calls=%async_computation | async-start | bytes 262144 | tf_op jit(solution)/shard_map/all_to_all | solution.py:531
  35.0 8.9 %collective-permute-start.4 = (f32[13,16,128]{2,1,0:T(8,128)S(1)}, f32[13,16,128]{2,1,0:T(8,128)S(1)}, u32[]{:S(2)}, u32[]{:S(2)}) collective-permute-start(f32[13,16,128]{2,1,0:T(8,128)S(1)} %get-tuple-element.36), channel_id=1, source_target_pairs={{0,7},{1,6},{2,5},{3,4},{4,11},{5,10},{6,9},{7,8},{8,15},{9,14},{1... | collective-permute-start | bytes 319496 | tf_op jit(solution)/shard_map/ppermute | solution.py:489
  38.1 7.7 %collective-permute-start.5 = (f32[13,16,128]{2,1,0:T(8,128)S(1)}, f32[13,16,128]{2,1,0:T(8,128)S(1)}, u32[]{:S(2)}, u32[]{:S(2)}) collective-permute-start(f32[13,16,128]{2,1,0:T(8,128)S(1)} %get-tuple-element.37), channel_id=1, source_target_pairs={{7,0},{6,1},{5,2},{4,3},{11,4},{10,5},{9,6},{8,7},{15,8},{14,9},{1... | collective-permute-start | bytes 319496 | tf_op jit(solution)/shard_map/ppermute | solution.py:489
  45.9 15.3 %collective-permute-start.6 = (f32[400,128]{1,0:T(8,128)S(1)}, f32[400,128]{1,0:T(8,128)S(1)}, u32[]{:S(2)}, u32[]{:S(2)}) collective-permute-start(f32[400,128]{1,0:T(8,128)S(1)} %constant_dynamic-update-slice_fusion), channel_id=1, source_target_pairs={{0,64},{64,128},{128,192},{192,256},{256,320},{320,384},{384,448},... | collective-permute-start | bytes 614408 | tf_op jit(solution)/shard_map/ppermute | solution.py:489
  50.2 11.0 %collective-permute-start.7 = (f32[400,128]{1,0:T(8,128)S(1)}, f32[400,128]{1,0:T(8,128)S(1)}, u32[]{:S(2)}, u32[]{:S(2)}) collective-permute-start(f32[400,128]{1,0:T(8,128)S(1)} %constant_dynamic-update-slice_fusion.7), channel_id=1, source_target_pairs={{64,0},{128,64},{192,128},{256,192},{320,256},{384,320},{448,384},... | collective-permute-start | bytes 614408 | tf_op jit(solution)/shard_map/ppermute | solution.py:489
  51.6 7.8 %collective-permute-start.8 = (f32[3,48,128]{2,1,0:T(8,128)S(1)}, f32[3,48,128]{2,1,0:T(8,128)S(1)}, u32[]{:S(2)}, u32[]{:S(2)}) collective-permute-start(f32[3,48,128]{2,1,0:T(8,128)S(1)} %get-tuple-element.23), channel_id=1, source_target_pairs={{0,1},{1,2},{2,3},{3,4},{4,5},{5,6},{6,7},{7,8},{8,9},{9,10},{10,1... | collective-permute-start | bytes 221192 | tf_op jit(solution)/shard_map/ppermute | solution.py:489
  53.7 7.5 %collective-permute-start.9 = (f32[3,48,128]{2,1,0:T(8,128)S(1)}, f32[3,48,128]{2,1,0:T(8,128)S(1)}, u32[]{:S(2)}, u32[]{:S(2)}) collective-permute-start(f32[3,48,128]{2,1,0:T(8,128)S(1)} %get-tuple-element.24), channel_id=1, source_target_pairs={{1,0},{2,1},{3,2},{4,3},{5,4},{6,5},{7,6},{8,7},{9,8},{10,9},{11,1... | collective-permute-start | bytes 221192 | tf_op jit(solution)/shard_map/ppermute | solution.py:489
  67.1 20.8 %all-to-all-start.1 = ((f32[16,8,128]{2,1,0:T(8,128)}), f32[16,8,128]{2,1,0:T(8,128)S(1)}, u32[]{:S(2)}, u32[]{:S(2)}) async-start(f32[16,8,128]{2,1,0:T(8,128)} %get-tuple-element.27), calls=%async_computation.1 | async-start | bytes 131072 | tf_op jit(solution)/shard_map/all_to_all | solution.py:559
  78.3 20.8 %collective-permute-start.10 = (f32[40,128]{1,0:T(8,128)S(1)}, f32[40,128]{1,0:T(8,128)S(1)}, u32[]{:S(2)}, u32[]{:S(2)}) collective-permute-start(f32[40,128]{1,0:T(8,128)S(1)} %get-tuple-element.28), channel_id=1, source_target_pairs={{0,7},{1,6},{2,5},{3,4},{4,11},{5,10},{6,9},{7,8},{8,15},{9,14},{1... | collective-permute-start | bytes 61448 | tf_op jit(solution)/shard_map/ppermute | solution.py:489
  85.0 14.1 %collective-permute-start.11 = (f32[40,128]{1,0:T(8,128)S(1)}, f32[40,128]{1,0:T(8,128)S(1)}, u32[]{:S(2)}, u32[]{:S(2)}) collective-permute-start(f32[40,128]{1,0:T(8,128)S(1)} %get-tuple-element.28), channel_id=1, source_target_pairs={{7,0},{6,1},{5,2},{4,3},{11,4},{10,5},{9,6},{8,7},{15,8},{14,9},{1... | collective-permute-start | bytes 61448 | tf_op jit(solution)/shard_map/ppermute | solution.py:489
  88.6 21.6 %all-to-all-start.2 = ((f32[8,64,128]{2,1,0:T(8,128)}), f32[8,64,128]{2,1,0:T(8,128)S(1)}, u32[]{:S(2)}, u32[]{:S(2)}) async-start(f32[8,64,128]{2,1,0:T(8,128)} %broadcast_in_dim.18), calls=%async_computation.2 | async-start | bytes 524288 | tf_op jit(solution)/shard_map/all_to_all | solution.py:563
  99.1 7.4 %collective-permute-start.13 = (f32[120,128]{1,0:T(8,128)S(1)}, f32[120,128]{1,0:T(8,128)S(1)}, u32[]{:S(2)}, u32[]{:S(2)}) collective-permute-start(f32[120,128]{1,0:T(8,128)S(1)} %constant_dynamic-update-slice_fusion.14), channel_id=1, source_target_pairs={{64,0},{128,64},{192,128},{256,192},{320,256},{384,320},{448,384},... | collective-permute-start | bytes 184328 | tf_op jit(solution)/shard_map/ppermute | solution.py:489
  100.4 6.4 %collective-permute-start.12 = (f32[120,128]{1,0:T(8,128)S(1)}, f32[120,128]{1,0:T(8,128)S(1)}, u32[]{:S(2)}, u32[]{:S(2)}) collective-permute-start(f32[120,128]{1,0:T(8,128)S(1)} %constant_dynamic-update-slice_fusion.14), channel_id=1, source_target_pairs={{0,64},{64,128},{128,192},{192,256},{256,320},{320,384},{384,448},... | collective-permute-start | bytes 184328 | tf_op jit(solution)/shard_map/ppermute | solution.py:489

commit v12 on v11

--- a/solution.py
+++ b/solution.py
@@ -538,7 +538,7 @@
         for rows, planes in FACES:
             part = window[rows.start : rows.stop, 16 - planes :] if up else window[rows.start : rows.stop, :planes]
             parts.append(part.reshape(-1, 128))
-        return jnp.concatenate(parts, axis=0)
+        return jnp.concatenate(parts + [jnp.zeros((8, 128), F32)], axis=0)
 
     before, after = pair(faces(True), faces(False), "gz")
     rims = pair(last_rows, first_rows, "xy")

time: 122 us -> 122 us (level)
  no operation moved by 1% of the time
where the time goes in v12:
time: 122 us; the launch traced here: 121 us
  starting transfers between devices  74.7 us (61%)
  waiting for transfers between devices  23.6 us (19%)
  Pallas kernels  19.8 us (16%)
  local copies, waits for them, and re-layouts  1.83 us (2%)
    ppermute x7, starting transfers between devices, pair(): lax.ppermute(array_up, axis, up)  27.1 us
    ppermute x7, starting transfers between devices, pair(): lax.ppermute(array_down, axis, down)  22.6 us
    ppermute x7, waiting for transfers between devices, pair(): lax.ppermute(array_down, axis, down)  11.6 us
    all_to_all x1, starting transfers between devices, body(): lax.all_to_all(chunks, 'xy', 0, 0, axis_index_groups=peers, tiled=True)  11.2 us
    pallas_call x1, Pallas kernels, body(): pl.pallas_call(partial(way_up, xy), out_shape=[shape(32, 8, 128)] * 2, in...  10.9 us
    all_to_all x1, starting transfers between devices, body(): lax.all_to_all(jnp.broadcast_to(layer, (gz, xy, 128)), 'gz', 0, 0, tiled=...  10.5 us
    pallas_call x1, Pallas kernels, body(): pl.pallas_call(middle_down, out_shape=[shape(xy // GROUP, 8, 128), shape(...  5.85 us
    all_to_all x1, waiting for transfers between devices, body(): lax.all_to_all(chunks, 'xy', 0, 0, axis_index_groups=teams, tiled=True)  4.58 us
  transfers between devices with their start and end apart: 17, of which 12 were waited for; matrix products, arithmetic and copies ran while one was open for 1% of the time, Pallas kernels for 0%

profile of v12, /device:TPU:40, one launch (start us, length us, event | category | flops | bytes accessed | tf_op | source)
XLA Modules:
  0.0 121.2 jit_solution(2423418487719259460)
XLA Ops:
  0.6 0.0 copy-start
  0.6 0.8 fusion.2
  1.5 0.1 copy-done
  1.6 0.0 copy-start.1
  1.6 4.4 %collective-permute-start = (f32[17,8,128]{2,1,0:T(8,128)S(1)}, f32[17,8,128]{2,1,0:T(8,128)S(1)}, u32[]{:S(2)}, u32[]{:S(2)}) collective-permute-start(f32[17,8,128]{2,1,0:T(8,128)S(1)} %pad_maximum_fusion.2), channel_id=1, source_target_pairs={{0,64},{64,128},{128,192},{192,256},{256,320},{320,384},{384,448},... | collective-permute-start | bytes 208904 | tf_op jit(solution)/shard_map/ppermute | solution.py:489
  6.1 1.3 %collective-permute-start.1 = (f32[17,8,128]{2,1,0:T(8,128)S(1)}, f32[17,8,128]{2,1,0:T(8,128)S(1)}, u32[]{:S(2)}, u32[]{:S(2)}) collective-permute-start(f32[17,8,128]{2,1,0:T(8,128)S(1)} %pad_maximum_fusion.3), channel_id=1, source_target_pairs={{64,0},{128,64},{192,128},{256,192},{320,256},{384,320},{448,384},... | collective-permute-start | bytes 208904 | tf_op jit(solution)/shard_map/ppermute | solution.py:489
  7.4 0.6 collective-permute-done.before_ref
  8.0 4.7 %collective-permute-done.1.after_ref = f32[17,8,128]{2,1,0:T(8,128)S(1)} collective-permute-done((f32[17,8,128]{2,1,0:T(8,128)S(1)}, f32[17,8,128]{2,1,0:T(8,128)S(1)}, u32[]{:S(2)}, u32[]{:S(2)}) %collective-permute-start.1) | collective-permute-done | bytes 69664 | tf_op jit(solution)/shard_map/ppermute | solution.py:489
  12.6 0.0 copy-done.1
  12.6 0.1 shard_map.41
  12.7 1.9 %collective-permute-start.2 = (f32[10,48,128]{2,1,0:T(8,128)S(1)}, f32[10,48,128]{2,1,0:T(8,128)S(1)}, u32[]{:S(2)}, u32[]{:S(2)}) collective-permute-start(f32[10,48,128]{2,1,0:T(8,128)S(1)} %get-tuple-element.20), channel_id=1, source_target_pairs={{0,1},{1,2},{2,3},{3,4},{4,5},{5,6},{6,7},{7,8},{8,9},{9,10},{10,1... | collective-permute-start | bytes 737288 | tf_op jit(solution)/shard_map/ppermute | solution.py:489
  14.7 5.8 %collective-permute-start.3 = (f32[10,48,128]{2,1,0:T(8,128)S(1)}, f32[10,48,128]{2,1,0:T(8,128)S(1)}, u32[]{:S(2)}, u32[]{:S(2)}) collective-permute-start(f32[10,48,128]{2,1,0:T(8,128)S(1)} %get-tuple-element.21), channel_id=1, source_target_pairs={{1,0},{2,1},{3,2},{4,3},{5,4},{6,5},{7,6},{8,7},{9,8},{10,9},{11,1... | collective-permute-start | bytes 737288 | tf_op jit(solution)/shard_map/ppermute | solution.py:489
  20.4 1.9 %collective-permute-done.2.before_ref.rim_before_ref = f32[10,48,128]{2,1,0:T(8,128)S(1)} collective-permute-done((f32[10,48,128]{2,1,0:T(8,128)S(1)}, f32[10,48,128]{2,1,0:T(8,128)S(1)}, u32[]{:S(2)}, u32[]{:S(2)}) %collective-permute-start.2) | collective-permute-done | bytes 245792 | tf_op jit(solution)/shard_map/ppermute | solution.py:489
  22.4 1.8 %collective-permute-done.3.after_ref.rim_after_ref = f32[10,48,128]{2,1,0:T(8,128)S(1)} collective-permute-done((f32[10,48,128]{2,1,0:T(8,128)S(1)}, f32[10,48,128]{2,1,0:T(8,128)S(1)}, u32[]{:S(2)}, u32[]{:S(2)}) %collective-permute-start.3) | collective-permute-done | bytes 245792 | tf_op jit(solution)/shard_map/ppermute | solution.py:489
  24.1 3.0 %shard_map.42 = (f32[4,64,128]{2,1,0:T(8,128)}, f32[3,48,128]{2,1,0:T(8,128)S(1)}, f32[3,48,128]{2,1,0:T(8,128)S(1)}, f32[4,64,128]{2,1,0:T(8,128)S(1)}) custom-call(f32[8,64,128]{2,1,0:T(8,128)S(1)} %get-tuple-element.18.s_ref, f32[8,64,128]{2,1,0:T(8,128)S(1)} %get-tuple-element.19.d_ref, ...), custom_call_target="tpu_custom_call" | custom-call | tf_op jit(solution)/shard_map/pallas_call | solution.py:523
  27.1 3.3 %all-to-all-start = ((f32[4,64,128]{2,1,0:T(8,128)}), f32[4,64,128]{2,1,0:T(8,128)S(1)}, u32[]{:S(2)}, u32[]{:S(2)}) async-start(f32[4,64,128]{2,1,0:T(8,128)} %get-tuple-element.22), calls=%async_computation | async-start | bytes 262144 | tf_op jit(solution)/shard_map/all_to_all | solution.py:531
  30.4 4.6 %all-to-all-done = f32[4,64,128]{2,1,0:T(8,128)S(1)} async-done(((f32[4,64,128]{2,1,0:T(8,128)}), f32[4,64,128]{2,1,0:T(8,128)S(1)}, u32[]{:S(2)}, u32[]{:S(2)}) %all-to-all-start) | async-done | bytes 131104 | tf_op jit(solution)/shard_map/all_to_all | solution.py:531
  35.0 3.0 %collective-permute-start.4 = (f32[13,16,128]{2,1,0:T(8,128)S(1)}, f32[13,16,128]{2,1,0:T(8,128)S(1)}, u32[]{:S(2)}, u32[]{:S(2)}) collective-permute-start(f32[13,16,128]{2,1,0:T(8,128)S(1)} %get-tuple-element.36), channel_id=1, source_target_pairs={{0,7},{1,6},{2,5},{3,4},{4,11},{5,10},{6,9},{7,8},{8,15},{9,14},{1... | collective-permute-start | bytes 319496 | tf_op jit(solution)/shard_map/ppermute | solution.py:489
  38.1 4.7 %collective-permute-start.5 = (f32[13,16,128]{2,1,0:T(8,128)S(1)}, f32[13,16,128]{2,1,0:T(8,128)S(1)}, u32[]{:S(2)}, u32[]{:S(2)}) collective-permute-start(f32[13,16,128]{2,1,0:T(8,128)S(1)} %get-tuple-element.37), channel_id=1, source_target_pairs={{7,0},{6,1},{5,2},{4,3},{11,4},{10,5},{9,6},{8,7},{15,8},{14,9},{1... | collective-permute-start | bytes 319496 | tf_op jit(solution)/shard_map/ppermute | solution.py:489
  42.8 1.2 collective-permute-done.4
  44.0 1.7 %collective-permute-done.5 = f32[13,16,128]{2,1,0:T(8,128)S(1)} collective-permute-done((f32[13,16,128]{2,1,0:T(8,128)S(1)}, f32[13,16,128]{2,1,0:T(8,128)S(1)}, u32[]{:S(2)}, u32[]{:S(2)}) %collective-permute-start.5) | collective-permute-done | bytes 106528 | tf_op jit(solution)/shard_map/ppermute | solution.py:489
  45.9 4.3 %collective-permute-start.6 = (f32[408,128]{1,0:T(8,128)S(1)}, f32[408,128]{1,0:T(8,128)S(1)}, u32[]{:S(2)}, u32[]{:S(2)}) collective-permute-start(f32[408,128]{1,0:T(8,128)S(1)} %constant_dynamic-update-slice_fusion), channel_id=1, source_target_pairs={{0,64},{64,128},{128,192},{192,256},{256,320},{320,384},{384,448},... | collective-permute-start | bytes 626696 | tf_op jit(solution)/shard_map/ppermute | solution.py:489
  50.2 1.3 %collective-permute-start.7 = (f32[408,128]{1,0:T(8,128)S(1)}, f32[408,128]{1,0:T(8,128)S(1)}, u32[]{:S(2)}, u32[]{:S(2)}) collective-permute-start(f32[408,128]{1,0:T(8,128)S(1)} %constant_dynamic-update-slice_fusion.8), channel_id=1, source_target_pairs={{64,0},{128,64},{192,128},{256,192},{320,256},{384,320},{448,384},... | collective-permute-start | bytes 626696 | tf_op jit(solution)/shard_map/ppermute | solution.py:489
  51.5 0.1 pad_add_fusion.place_ref
  51.6 2.2 %collective-permute-start.8 = (f32[3,48,128]{2,1,0:T(8,128)S(1)}, f32[3,48,128]{2,1,0:T(8,128)S(1)}, u32[]{:S(2)}, u32[]{:S(2)}) collective-permute-start(f32[3,48,128]{2,1,0:T(8,128)S(1)} %get-tuple-element.23), channel_id=1, source_target_pairs={{0,1},{1,2},{2,3},{3,4},{4,5},{5,6},{6,7},{7,8},{8,9},{9,10},{10,1... | collective-permute-start | bytes 221192 | tf_op jit(solution)/shard_map/ppermute | solution.py:489
  53.7 5.5 %collective-permute-start.9 = (f32[3,48,128]{2,1,0:T(8,128)S(1)}, f32[3,48,128]{2,1,0:T(8,128)S(1)}, u32[]{:S(2)}, u32[]{:S(2)}) collective-permute-start(f32[3,48,128]{2,1,0:T(8,128)S(1)} %get-tuple-element.24), channel_id=1, source_target_pairs={{1,0},{2,1},{3,2},{4,3},{5,4},{6,5},{7,6},{8,7},{9,8},{10,9},{11,1... | collective-permute-start | bytes 221192 | tf_op jit(solution)/shard_map/ppermute | solution.py:489
  59.3 0.1 collective-permute-done.8.before_ref
  59.3 1.9 %collective-permute-done.9.after_ref = f32[3,48,128]{2,1,0:T(8,128)S(1)} collective-permute-done((f32[3,48,128]{2,1,0:T(8,128)S(1)}, f32[3,48,128]{2,1,0:T(8,128)S(1)}, u32[]{:S(2)}, u32[]{:S(2)}) %collective-permute-start.9) | collective-permute-done | bytes 73760 | tf_op jit(solution)/shard_map/ppermute | solution.py:489
  61.2 0.0 collective-permute-done.6.before_ref
  61.2 0.0 collective-permute-done.7.after_ref
  61.3 5.9 %shard_map.43 = (f32[16,8,128]{2,1,0:T(8,128)}, f32[40,128]{1,0:T(8,128)S(1)}, f32[20,48,128]{2,1,0:T(8,128)S(1)}, f32[10,24,128]{2,1,0:T(8,128)S(1)}) custom-call(s32[3]{0:T(128)S(1)} %pad_add_fusion.place_ref, f32[42,16,128]{2,1,0:T(8,128)S(1)} %pad_maximum_fusion.window_ref, f32[408,128]{1,0:T(8,128)S(1)} %collective-permute-done.6.before_ref, ...), custom_call_target="tpu_custom_call" | custom-call | tf_op jit(solution)/shard_map/pallas_call | solution.py:546
  67.1 11.2 %all-to-all-start.1 = ((f32[16,8,128]{2,1,0:T(8,128)}), f32[16,8,128]{2,1,0:T(8,128)S(1)}, u32[]{:S(2)}, u32[]{:S(2)}) async-start(f32[16,8,128]{2,1,0:T(8,128)} %get-tuple-element.27), calls=%async_computation.1 | async-start | bytes 131072 | tf_op jit(solution)/shard_map/all_to_all | solution.py:559
  78.3 6.7 %collective-permute-start.10 = (f32[40,128]{1,0:T(8,128)S(1)}, f32[40,128]{1,0:T(8,128)S(1)}, u32[]{:S(2)}, u32[]{:S(2)}) collective-permute-start(f32[40,128]{1,0:T(8,128)S(1)} %get-tuple-element.28), channel_id=1, source_target_pairs={{0,7},{1,6},{2,5},{3,4},{4,11},{5,10},{6,9},{7,8},{8,15},{9,14},{1... | collective-permute-start | bytes 61448 | tf_op jit(solution)/shard_map/ppermute | solution.py:489
  85.1 2.8 %collective-permute-start.11 = (f32[40,128]{1,0:T(8,128)S(1)}, f32[40,128]{1,0:T(8,128)S(1)}, u32[]{:S(2)}, u32[]{:S(2)}) collective-permute-start(f32[40,128]{1,0:T(8,128)S(1)} %get-tuple-element.28), channel_id=1, source_target_pairs={{7,0},{6,1},{5,2},{4,3},{11,4},{10,5},{9,6},{8,7},{15,8},{14,9},{1... | collective-permute-start | bytes 61448 | tf_op jit(solution)/shard_map/ppermute | solution.py:489
  87.9 0.0 all-to-all-done.1
  87.9 0.7 broadcast_in_dim.18
  88.6 10.5 %all-to-all-start.2 = ((f32[8,64,128]{2,1,0:T(8,128)}), f32[8,64,128]{2,1,0:T(8,128)S(1)}, u32[]{:S(2)}, u32[]{:S(2)}) async-start(f32[8,64,128]{2,1,0:T(8,128)} %broadcast_in_dim.18), calls=%async_computation.2 | async-start | bytes 524288 | tf_op jit(solution)/shard_map/all_to_all | solution.py:563
  99.1 0.0 collective-permute-done.10
  99.1 0.0 collective-permute-done.11
  99.2 1.3 %collective-permute-start.13 = (f32[120,128]{1,0:T(8,128)S(1)}, f32[120,128]{1,0:T(8,128)S(1)}, u32[]{:S(2)}, u32[]{:S(2)}) collective-permute-start(f32[120,128]{1,0:T(8,128)S(1)} %constant_dynamic-update-slice_fusion.16), channel_id=1, source_target_pairs={{64,0},{128,64},{192,128},{256,192},{320,256},{384,320},{448,384},... | collective-permute-start | bytes 184328 | tf_op jit(solution)/shard_map/ppermute | solution.py:489
  100.5 4.5 %collective-permute-start.12 = (f32[120,128]{1,0:T(8,128)S(1)}, f32[120,128]{1,0:T(8,128)S(1)}, u32[]{:S(2)}, u32[]{:S(2)}) collective-permute-start(f32[120,128]{1,0:T(8,128)S(1)} %constant_dynamic-update-slice_fusion.16), channel_id=1, source_target_pairs={{0,64},{64,128},{128,192},{192,256},{256,320},{320,384},{384,448},... | collective-permute-start | bytes 184328 | tf_op jit(solution)/shard_map/ppermute | solution.py:489
  105.0 1.5 %collective-permute-done.13 = f32[120,128]{1,0:T(8,128)S(1)} collective-permute-done((f32[120,128]{1,0:T(8,128)S(1)}, f32[120,128]{1,0:T(8,128)S(1)}, u32[]{:S(2)}, u32[]{:S(2)}) %collective-permute-start.13) | collective-permute-done | bytes 61472 | tf_op jit(solution)/shard_map/ppermute | solution.py:489
  106.5 0.3 collective-permute-done.12
  106.9 3.4 %all-to-all-done.2.gathered_ref = f32[8,64,128]{2,1,0:T(8,128)S(1)} async-done(((f32[8,64,128]{2,1,0:T(8,128)}), f32[8,64,128]{2,1,0:T(8,128)S(1)}, u32[]{:S(2)}, u32[]{:S(2)}) %all-to-all-start.2) | async-done | bytes 262176 | tf_op jit(solution)/shard_map/all_to_all | solution.py:563
  110.3 10.9 %shard_map.44 = (f32[32,8,128]{2,1,0:T(8,128)}, f32[32,8,128]{2,1,0:T(8,128)}) custom-call(s32[3]{0:T(128)S(1)} %pad_add_fusion.place_ref, f32[8,64,128]{2,1,0:T(8,128)S(1)} %all-to-all-done.2.gathered_ref, f32[15,24,128]{2,1,0:T(8,128)S(1)} %pad_maximum_fusion.1.halo_ref, f32[20,48,128]{2,1,0:T(8,128)S(1)} %get-tuple-element.29.kept_ref, ...), custom_call_target="tpu_custom_call" | custom-call | tf_op jit(solution)/shard_map/pallas_call | solution.py:567
  (35 shorter events, 0.3 us)
Async XLA Ops:
  0.6 0.9 copy-start
  1.6 11.0 %copy-start.1 = (f32[32,8,128]{2,1,0:T(8,128)S(1)}, f32[32,8,128]{2,1,0:T(8,128)}, u32[]{:S(2)}) copy-start(f32[32,8,128]{2,1,0:T(8,128)} %right_ref.1) | copy-start | bytes 393220
  1.6 6.3 %collective-permute-start = (f32[17,8,128]{2,1,0:T(8,128)S(1)}, f32[17,8,128]{2,1,0:T(8,128)S(1)}, u32[]{:S(2)}, u32[]{:S(2)}) collective-permute-start(f32[17,8,128]{2,1,0:T(8,128)S(1)} %pad_maximum_fusion.2), channel_id=1, source_target_pairs={{0,64},{64,128},{128,192},{192,256},{256,320},{320,384},{384,448},... | collective-permute-start | bytes 208904 | tf_op jit(solution)/shard_map/ppermute | solution.py:489
  6.1 6.6 %collective-permute-start.1 = (f32[17,8,128]{2,1,0:T(8,128)S(1)}, f32[17,8,128]{2,1,0:T(8,128)S(1)}, u32[]{:S(2)}, u32[]{:S(2)}) collective-permute-start(f32[17,8,128]{2,1,0:T(8,128)S(1)} %pad_maximum_fusion.3), channel_id=1, source_target_pairs={{64,0},{128,64},{192,128},{256,192},{320,256},{384,320},{448,384},... | collective-permute-start | bytes 208904 | tf_op jit(solution)/shard_map/ppermute | solution.py:489
  12.7 9.6 %collective-permute-start.2 = (f32[10,48,128]{2,1,0:T(8,128)S(1)}, f32[10,48,128]{2,1,0:T(8,128)S(1)}, u32[]{:S(2)}, u32[]{:S(2)}) collective-permute-start(f32[10,48,128]{2,1,0:T(8,128)S(1)} %get-tuple-element.20), channel_id=1, source_target_pairs={{0,1},{1,2},{2,3},{3,4},{4,5},{5,6},{6,7},{7,8},{8,9},{9,10},{10,1... | collective-permute-start | bytes 737288 | tf_op jit(solution)/shard_map/ppermute | solution.py:489
  14.7 9.5 %collective-permute-start.3 = (f32[10,48,128]{2,1,0:T(8,128)S(1)}, f32[10,48,128]{2,1,0:T(8,128)S(1)}, u32[]{:S(2)}, u32[]{:S(2)}) collective-permute-start(f32[10,48,128]{2,1,0:T(8,128)S(1)} %get-tuple-element.21), channel_id=1, source_target_pairs={{1,0},{2,1},{3,2},{4,3},{5,4},{6,5},{7,6},{8,7},{9,8},{10,9},{11,1... | collective-permute-start | bytes 737288 | tf_op jit(solution)/shard_map/ppermute | solution.py:489
  27.1 7.9 %all-to-all-start = ((f32[4,64,128]{2,1,0:T(8,128)}), f32[4,64,128]{2,1,0:T(8,128)S(1)}, u32[]{:S(2)}, u32[]{:S(2)}) async-start(f32[4,64,128]{2,1,0:T(8,128)} %get-tuple-element.22), calls=%async_computation | async-start | bytes 262144 | tf_op jit(solution)/shard_map/all_to_all | solution.py:531
  35.0 8.9 %collective-permute-start.4 = (f32[13,16,128]{2,1,0:T(8,128)S(1)}, f32[13,16,128]{2,1,0:T(8,128)S(1)}, u32[]{:S(2)}, u32[]{:S(2)}) collective-permute-start(f32[13,16,128]{2,1,0:T(8,128)S(1)} %get-tuple-element.36), channel_id=1, source_target_pairs={{0,7},{1,6},{2,5},{3,4},{4,11},{5,10},{6,9},{7,8},{8,15},{9,14},{1... | collective-permute-start | bytes 319496 | tf_op jit(solution)/shard_map/ppermute | solution.py:489
  38.1 7.7 %collective-permute-start.5 = (f32[13,16,128]{2,1,0:T(8,128)S(1)}, f32[13,16,128]{2,1,0:T(8,128)S(1)}, u32[]{:S(2)}, u32[]{:S(2)}) collective-permute-start(f32[13,16,128]{2,1,0:T(8,128)S(1)} %get-tuple-element.37), channel_id=1, source_target_pairs={{7,0},{6,1},{5,2},{4,3},{11,4},{10,5},{9,6},{8,7},{15,8},{14,9},{1... | collective-permute-start | bytes 319496 | tf_op jit(solution)/shard_map/ppermute | solution.py:489
  45.9 15.3 %collective-permute-start.6 = (f32[408,128]{1,0:T(8,128)S(1)}, f32[408,128]{1,0:T(8,128)S(1)}, u32[]{:S(2)}, u32[]{:S(2)}) collective-permute-start(f32[408,128]{1,0:T(8,128)S(1)} %constant_dynamic-update-slice_fusion), channel_id=1, source_target_pairs={{0,64},{64,128},{128,192},{192,256},{256,320},{320,384},{384,448},... | collective-permute-start | bytes 626696 | tf_op jit(solution)/shard_map/ppermute | solution.py:489
  50.2 11.1 %collective-permute-start.7 = (f32[408,128]{1,0:T(8,128)S(1)}, f32[408,128]{1,0:T(8,128)S(1)}, u32[]{:S(2)}, u32[]{:S(2)}) collective-permute-start(f32[408,128]{1,0:T(8,128)S(1)} %constant_dynamic-update-slice_fusion.8), channel_id=1, source_target_pairs={{64,0},{128,64},{192,128},{256,192},{320,256},{384,320},{448,384},... | collective-permute-start | bytes 626696 | tf_op jit(solution)/shard_map/ppermute | solution.py:489
  51.6 7.8 %collective-permute-start.8 = (f32[3,48,128]{2,1,0:T(8,128)S(1)}, f32[3,48,128]{2,1,0:T(8,128)S(1)}, u32[]{:S(2)}, u32[]{:S(2)}) collective-permute-start(f32[3,48,128]{2,1,0:T(8,128)S(1)} %get-tuple-element.23), channel_id=1, source_target_pairs={{0,1},{1,2},{2,3},{3,4},{4,5},{5,6},{6,7},{7,8},{8,9},{9,10},{10,1... | collective-permute-start | bytes 221192 | tf_op jit(solution)/shard_map/ppermute | solution.py:489
  53.7 7.5 %collective-permute-start.9 = (f32[3,48,128]{2,1,0:T(8,128)S(1)}, f32[3,48,128]{2,1,0:T(8,128)S(1)}, u32[]{:S(2)}, u32[]{:S(2)}) collective-permute-start(f32[3,48,128]{2,1,0:T(8,128)S(1)} %get-tuple-element.24), channel_id=1, source_target_pairs={{1,0},{2,1},{3,2},{4,3},{5,4},{6,5},{7,6},{8,7},{9,8},{10,9},{11,1... | collective-permute-start | bytes 221192 | tf_op jit(solution)/shard_map/ppermute | solution.py:489
  67.1 20.8 %all-to-all-start.1 = ((f32[16,8,128]{2,1,0:T(8,128)}), f32[16,8,128]{2,1,0:T(8,128)S(1)}, u32[]{:S(2)}, u32[]{:S(2)}) async-start(f32[16,8,128]{2,1,0:T(8,128)} %get-tuple-element.27), calls=%async_computation.1 | async-start | bytes 131072 | tf_op jit(solution)/shard_map/all_to_all | solution.py:559
  78.3 20.8 %collective-permute-start.10 = (f32[40,128]{1,0:T(8,128)S(1)}, f32[40,128]{1,0:T(8,128)S(1)}, u32[]{:S(2)}, u32[]{:S(2)}) collective-permute-start(f32[40,128]{1,0:T(8,128)S(1)} %get-tuple-element.28), channel_id=1, source_target_pairs={{0,7},{1,6},{2,5},{3,4},{4,11},{5,10},{6,9},{7,8},{8,15},{9,14},{1... | collective-permute-start | bytes 61448 | tf_op jit(solution)/shard_map/ppermute | solution.py:489
  85.1 14.1 %collective-permute-start.11 = (f32[40,128]{1,0:T(8,128)S(1)}, f32[40,128]{1,0:T(8,128)S(1)}, u32[]{:S(2)}, u32[]{:S(2)}) collective-permute-start(f32[40,128]{1,0:T(8,128)S(1)} %get-tuple-element.28), channel_id=1, source_target_pairs={{7,0},{6,1},{5,2},{4,3},{11,4},{10,5},{9,6},{8,7},{15,8},{14,9},{1... | collective-permute-start | bytes 61448 | tf_op jit(solution)/shard_map/ppermute | solution.py:489
  88.6 21.6 %all-to-all-start.2 = ((f32[8,64,128]{2,1,0:T(8,128)}), f32[8,64,128]{2,1,0:T(8,128)S(1)}, u32[]{:S(2)}, u32[]{:S(2)}) async-start(f32[8,64,128]{2,1,0:T(8,128)} %broadcast_in_dim.18), calls=%async_computation.2 | async-start | bytes 524288 | tf_op jit(solution)/shard_map/all_to_all | solution.py:563
  99.2 7.4 %collective-permute-start.13 = (f32[120,128]{1,0:T(8,128)S(1)}, f32[120,128]{1,0:T(8,128)S(1)}, u32[]{:S(2)}, u32[]{:S(2)}) collective-permute-start(f32[120,128]{1,0:T(8,128)S(1)} %constant_dynamic-update-slice_fusion.16), channel_id=1, source_target_pairs={{64,0},{128,64},{192,128},{256,192},{320,256},{384,320},{448,384},... | collective-permute-start | bytes 184328 | tf_op jit(solution)/shard_map/ppermute | solution.py:489
  100.5 6.4 %collective-permute-start.12 = (f32[120,128]{1,0:T(8,128)S(1)}, f32[120,128]{1,0:T(8,128)S(1)}, u32[]{:S(2)}, u32[]{:S(2)}) collective-permute-start(f32[120,128]{1,0:T(8,128)S(1)} %constant_dynamic-update-slice_fusion.16), channel_id=1, source_target_pairs={{0,64},{64,128},{128,192},{192,256},{256,320},{320,384},{384,448},... | collective-permute-start | bytes 184328 | tf_op jit(solution)/shard_map/ppermute | solution.py:489
